TPU v7x, 32 devices: a whole 2x2x4 slice. The times are simulated.
32 devices in a mesh: row: 4 (over y, x), col: 8 (over z, core).
Axes of the slice: x: 2, y: 2, z: 4, core: 2. Of those that a mesh axis runs over, the one named last changes fastest.
Arguments:
- alignment_embedding: bfloat16 [16, 768, 64], P('row', 'col'), may hold values from -6 to 6
- coupling_embedding: bfloat16 [768, 768, 128], P('row', 'col'), may hold values from -16 to 16
- amino_validity: int32 [768], replicated, may hold values 0 or 1
- alignment_validity: int32 [16, 768], replicated, may hold values 0 or 1
- alignment_matrix: bfloat16 [64, 576], replicated, may hold values from -0.75 to 0.75
- tensor_final_matrix: bfloat16 [1024, 128], replicated, may hold values from -0.1875 to 0.1875
- coupling_logit_matrix: bfloat16 [128, 8], replicated, may hold values from -10 to 10
- mean_final_matrix: bfloat16 [256, 64], replicated, may hold values from -3 to 3
- trimul_matrices: bfloat16 [128, 640], replicated, may hold values from -0.5 to 0.5
- trimul_final_matrix: bfloat16 [128, 128], replicated, may hold values from -0.5 to 0.5
Outputs:
- alignment_updated_embedding: bfloat16 [16, 768, 64], P('row', 'col')
- pair_output: bfloat16 [768, 768, 128], P('row', 'col')
All inputs are finite; a program needn't handle non-finite values.
Results may differ from a plain program's by a relative error of at most 0.019.
The roundings to bfloat16 on the way count: a program that leaves them out, or rounds other values in their place, can miss the bound.
Values may be sent and summed in bfloat16 or wider, within the bound.
No kernel may reach another device: no remote copies, remote signals or barrier semaphores. Data moves between devices by JAX's collectives and lax.ppermute only.
A program may use at most 256 MiB of HBM per device.

v0:
```python
import jax
import jax.numpy as jnp
from jax import lax
from jax.sharding import PartitionSpec as P

TENSOR_FEATURES = 32
MEAN_GROUPS = 8
GROUP_FEATURES = 32
CTRI = 128


EPS = 1e-05
MASK_PENALTY = 10000.0


def standardize_features(values_in, axis):
    centre = values_in - jnp.mean(values_in, axis=axis, keepdims=True)
    spread = jnp.mean(centre * centre, axis=axis, keepdims=True)
    return centre * lax.rsqrt(spread + EPS)


def on_device(
    alignment_embedding,
    coupling_embedding,
    amino_validity,
    alignment_validity,
    alignment_matrix,
    tensor_final_matrix,
    coupling_logit_matrix,
    mean_final_matrix,
    trimul_matrices,
    trimul_final_matrix,
):
    alignments_each_shard, module_number, alignment_feature_count = alignment_embedding.shape
    rows = coupling_embedding.shape[0]
    row_count = lax.axis_size("row")
    row_index = lax.axis_index("row")
    col_index = lax.axis_index("col")
    alignment_range = alignments_each_shard * row_count
    active_entries = amino_validity.astype(jnp.float32)
    sequence_index = lax.broadcasted_iota(jnp.int32, alignment_validity.shape, 0)
    present_entries = (
        jnp.where(sequence_index == 0, jnp.float32(1.0), alignment_validity.astype(jnp.float32))
        * active_entries[None, :]
    )
    row_start = row_index * rows
    col_start = col_index * module_number
    present_own = lax.dynamic_slice(
        present_entries,
        (row_index * alignments_each_shard, col_start),
        (alignments_each_shard, module_number),
    )
    present_rows = lax.dynamic_slice_in_dim(present_entries, row_start, rows, 1)
    present_cols = lax.dynamic_slice_in_dim(present_entries, col_start, module_number, 1)
    live_rows = lax.dynamic_slice_in_dim(active_entries, row_start, rows, 0)
    live_cols = lax.dynamic_slice_in_dim(active_entries, col_start, module_number, 0)
    alignment_standardized = standardize_features(
        alignment_embedding.astype(jnp.float32), 2
    ).astype(jnp.bfloat16)
    projected_rows = jnp.dot(
        alignment_standardized.reshape(
            alignments_each_shard * module_number, alignment_feature_count
        ),
        alignment_matrix,
        preferred_element_type=jnp.float32,
    ).reshape(alignments_each_shard, module_number, -1)
    own_weight = present_own[:, :, None]
    left = (projected_rows[:, :, :TENSOR_FEATURES] * own_weight).astype(jnp.bfloat16)
    right = (projected_rows[:, :, TENSOR_FEATURES : 2 * TENSOR_FEATURES] * own_weight).astype(
        jnp.bfloat16
    )
    values = projected_rows[
        :, :, 2 * TENSOR_FEATURES : 2 * TENSOR_FEATURES + MEAN_GROUPS * GROUP_FEATURES
    ].astype(jnp.bfloat16)
    sequence_gate = jax.nn.sigmoid(
        projected_rows[:, :, 2 * TENSOR_FEATURES + MEAN_GROUPS * GROUP_FEATURES :]
    )
    carry_width = TENSOR_FEATURES
    carried = left.reshape(alignments_each_shard, module_number * TENSOR_FEATURES)
    right_flat = right.reshape(alignments_each_shard, module_number * TENSOR_FEATURES)
    everything = lax.all_gather(carried, "col", axis=1, tiled=True)
    local = lax.all_to_all(everything, "row", split_axis=1, concat_axis=0, tiled=True)
    right_all = lax.all_gather(right_flat, "row", axis=0, tiled=True)
    gathered = local.reshape(alignment_range, rows, carry_width)
    right_all = right_all.reshape(alignment_range, module_number, TENSOR_FEATURES)
    count = jnp.dot(present_rows.T, present_cols, precision=lax.Precision.HIGHEST)
    divisor = jnp.maximum(count, 1.0)
    w_outer = tensor_final_matrix.reshape(TENSOR_FEATURES, TENSOR_FEATURES, -1)
    w_front = jnp.concatenate([coupling_logit_matrix, trimul_matrices], axis=1)
    size = rows // 4
    mid_parts, logit_parts, left_parts, right_parts, gate_parts = ([], [], [], [], [])
    for part_index in range(4):
        low = part_index * size
        outer = jnp.einsum(
            "sic,sjd->icjd",
            gathered[:, low : low + size],
            right_all,
            preferred_element_type=jnp.float32,
        ).astype(jnp.bfloat16)
        update = jnp.einsum("icjd,cde->ije", outer, w_outer, preferred_element_type=jnp.float32)
        mid = (
            coupling_embedding[low : low + size].astype(jnp.float32)
            + update / divisor[low : low + size, :, None]
        ).astype(jnp.bfloat16)
        normed = standardize_features(mid.astype(jnp.float32), 2).astype(jnp.bfloat16)
        front = jnp.dot(
            normed.reshape(size * module_number, -1), w_front, preferred_element_type=jnp.float32
        ).reshape(size, module_number, -1)
        logit_parts.append(
            front[:, :, :MEAN_GROUPS]
            + MASK_PENALTY * (live_rows[low : low + size] - 1.0)[:, None, None]
        )
        tri = front[:, :, MEAN_GROUPS:]
        pair_live = (live_rows[low : low + size, None] * live_cols[None, :])[:, :, None]
        tri_left = (
            jax.nn.sigmoid(tri[:, :, :CTRI]) * tri[:, :, CTRI : 2 * CTRI] * pair_live
        ).astype(jnp.bfloat16)
        tri_right = (
            jax.nn.sigmoid(tri[:, :, 2 * CTRI : 3 * CTRI])
            * tri[:, :, 3 * CTRI : 4 * CTRI]
            * pair_live
        ).astype(jnp.bfloat16)
        left_parts.append(jnp.transpose(tri_left, (2, 0, 1)))
        right_parts.append(jnp.transpose(tri_right, (2, 0, 1)))
        gate_parts.append(jax.nn.sigmoid(tri[:, :, 4 * CTRI :]))
        mid_parts.append(mid)
    pair_mid = jnp.concatenate(mid_parts, axis=0)
    logits = jnp.concatenate(logit_parts, axis=0)
    tri_left_all = jnp.concatenate(left_parts, axis=1)
    tri_right_all = jnp.concatenate(right_parts, axis=1)
    tri_gate = jnp.concatenate(gate_parts, axis=0)
    logits_all = lax.all_gather(logits, "row", axis=0, tiled=True)
    values_all = lax.all_gather(values, "col", axis=1, tiled=True)
    top_all = jnp.max(logits_all, axis=0)
    expd = jnp.exp(logits_all - top_all[None])
    weights_all = (expd / jnp.sum(expd, axis=0)[None]).astype(jnp.bfloat16)
    value_all_heads = values_all.reshape(alignments_each_shard, -1, MEAN_GROUPS, GROUP_FEATURES)
    summed = jnp.einsum(
        "jih,sjhd->sihd", weights_all, value_all_heads, preferred_element_type=jnp.float32
    )
    head_averaged = summed.reshape(
        alignments_each_shard, module_number, MEAN_GROUPS * GROUP_FEATURES
    )
    gated_result = (sequence_gate * head_averaged).astype(jnp.bfloat16)
    blended_update = jnp.dot(
        gated_result.reshape(alignments_each_shard * module_number, -1),
        mean_final_matrix,
        preferred_element_type=jnp.float32,
    ).reshape(alignments_each_shard, module_number, -1)
    alignment_updated_embedding = (alignment_embedding.astype(jnp.float32) + blended_update).astype(
        jnp.bfloat16
    )
    first_all, second_all = (
        lax.all_to_all(
            lax.all_to_all(tri_left_all, "row", split_axis=0, concat_axis=1, tiled=True),
            "col",
            split_axis=0,
            concat_axis=2,
            tiled=True,
        ),
        lax.all_to_all(
            lax.all_to_all(tri_right_all, "row", split_axis=0, concat_axis=1, tiled=True),
            "col",
            split_axis=0,
            concat_axis=2,
            tiled=True,
        ),
    )
    product = jnp.einsum(
        "cik,cjk->cij", first_all, second_all, preferred_element_type=jnp.float32
    ).astype(jnp.bfloat16)
    returned = lax.all_to_all(
        lax.all_to_all(product, "col", split_axis=2, concat_axis=0, tiled=True),
        "row",
        split_axis=1,
        concat_axis=0,
        tiled=True,
    )
    product_normed = standardize_features(returned.astype(jnp.float32), 0).astype(jnp.bfloat16)
    out = jnp.einsum(
        "crb,ce->rbe", product_normed, trimul_final_matrix, preferred_element_type=jnp.float32
    )
    pair_output = (pair_mid.astype(jnp.float32) + tri_gate * out).astype(jnp.bfloat16)
    return (alignment_updated_embedding, pair_output)


def solution(mesh):
    in_specs = (
        P("row", "col", None),
        P("row", "col", None),
        P(),
        P(),
        P(),
        P(),
        P(),
        P(),
        P(),
        P(),
    )
    out_specs = (P("row", "col", None), P("row", "col", None))
    return jax.shard_map(
        on_device, mesh=mesh, in_specs=in_specs, out_specs=out_specs, check_vma=False
    )
```

profile of v0, /device:TPU:0, one launch (start us, length us, event | category | flops | bytes accessed | tf_op | source)
XLA Modules:
  0.0 859.3 jit_solution(5599205345968899717)
XLA Ops:
  12.3 16.9 %all_gather.13 = bf16[4,24576]{1,0:T(4,128)(2,1)} all-gather(bf16[4,3072]{1,0:T(4,128)(2,1)S(1)} %reshape.250), channel_id=1, replica_groups=mesh['row'=4,'col'=8] {'col'}, dimensions={1}, use_global_device_ids=true | all-gather | bytes 221184 | tf_op jit(solution)/shard_map/all_gather | solution.py:81
  34.6 8.9 %all-gather = bf16[4,4,3072]{2,1,0:T(4,128)(2,1)S(1)} all-gather(bf16[1,4,3072]{2,1,0:T(4,128)(2,1)S(1)} %reshape.259), channel_id=1, replica_groups=mesh['row'=4,'col'=8] {'row'}, dimensions={0}, use_global_device_ids=true | all-gather | bytes 122880 | tf_op jit(solution)/shard_map/all_gather | solution.py:83
  49.1 9.7 %convert_reduce_fusion = (f32[48,96]{1,0:T(8,128)S(1)}, bf16[48,96,128]{2,1,0:T(8,128)(2,1)S(1)}) fusion(f32[48,96]{1,0:T(8,128)S(1)} %get-tuple-element.21, bf16[32,32,128,1]{2,1,0,3:T(8,128)(2,1)S(1)} %bitcast.144, bf16[48,32,96,32]{2,0,3,1:T(8,128)(2,1)S(1)} %convolution_convert_fusion, bf16[192,96,128]{2,1,0:T(8,128)(2,1)} %param.11), kind=kOutput, calls=%fused_computation.26 | convolution fusion | flops 1211493888 | bytes 12095488 | tf_op jit(solution)/shard_map/icjd,cde->ije/dot_general | solution.py:100
  64.2 9.7 %convert_reduce_fusion.2 = (f32[48,96]{1,0:T(8,128)S(1)}, bf16[48,96,128]{2,1,0:T(8,128)(2,1)S(1)}) fusion(f32[48,96]{1,0:T(8,128)S(1)} %get-tuple-element.23, bf16[32,32,128,1]{2,1,0,3:T(8,128)(2,1)S(1)} %bitcast.142, bf16[48,32,96,32]{2,0,3,1:T(8,128)(2,1)S(1)} %convolution_convert_fusion.2, bf16[192,96,128]{2,1,0:T(8,128)(2,1)} %param.11), kind=kOutput, calls=%fused_computation.30 | convolution fusion | flops 1211493888 | bytes 12095488 | tf_op jit(solution)/shard_map/icjd,cde->ije/dot_general | solution.py:100
  79.3 10.2 %convert_reduce_fusion.1 = (f32[48,96]{1,0:T(8,128)S(1)}, bf16[48,96,128]{2,1,0:T(8,128)(2,1)S(1)}) fusion(f32[48,96]{1,0:T(8,128)S(1)} %get-tuple-element.22, bf16[32,32,128,1]{2,1,0,3:T(8,128)(2,1)S(1)} %bitcast.143, bf16[48,32,96,32]{2,0,3,1:T(8,128)(2,1)S(1)} %convolution_convert_fusion.1, bf16[192,96,128]{2,1,0:T(8,128)(2,1)} %param.11), kind=kOutput, calls=%fused_computation.28 | convolution fusion | flops 1211493888 | bytes 12095488 | tf_op jit(solution)/shard_map/icjd,cde->ije/dot_general | solution.py:100
  94.9 9.7 %convert_reduce_fusion.3 = (f32[48,96]{1,0:T(8,128)S(1)}, bf16[48,96,128]{2,1,0:T(8,128)(2,1)S(1)}) fusion(f32[48,96]{1,0:T(8,128)S(1)} %get-tuple-element.20, bf16[32,32,128,1]{2,1,0,3:T(8,128)(2,1)S(1)} %bitcast.141, bf16[48,32,96,32]{2,0,3,1:T(8,128)(2,1)S(1)} %convolution_convert_fusion.3, bf16[192,96,128]{2,1,0:T(8,128)(2,1)} %param.11), kind=kOutput, calls=%fused_computation.32 | convolution fusion | flops 1211493888 | bytes 12095488 | tf_op jit(solution)/shard_map/icjd,cde->ije/dot_general | solution.py:100
  108.9 6.9 fusion.114
  115.8 6.6 fusion.112
  122.4 6.4 fusion.116
  128.8 14.8 %fusion.130 = (bf16[128,48,96]{0,2,1:T(8,128)(2,1)}, bf16[128,48,96]{0,2,1:T(8,128)(2,1)S(1)}, f32[48,96,128]{2,1,0:T(8,128)}, f32[48,96,128]{2,1,0:T(8,128)}, b...) fusion(f32[48,96]{1,0:T(8,128)S(1)} %get-tuple-element.32, f32[48,96,648]{2,1,0:T(8,128)S(1)} %fusion.110, ...), kind=kLoop, calls=%fused_computation.156 | loop fusion | flops 17694720 | bytes 33067008 | tf_op jit(solution)/shard_map/transpose | solution.py:124
  143.6 20.8 %fusion.132 = (bf16[128,48,96]{0,2,1:T(8,128)(2,1)S(1)}, bf16[128,48,96]{0,2,1:T(8,128)(2,1)}, f32[48,96,128]{2,1,0:T(8,128)}, f32[48,96,128]{2,1,0:T(8,128)}, b...) fusion(f32[48,96]{1,0:T(8,128)S(1)} %get-tuple-element.34, f32[48,96,648]{2,1,0:T(8,128)} %fusion.114, ...), kind=kLoop, calls=%fused_computation.158 | loop fusion | flops 17694720 | bytes 33067008 | tf_op jit(solution)/shard_map/transpose | solution.py:124
  166.9 8.4 copy.107
  185.0 8.5 copy.104
  193.5 55.2 %all-to-all-done.3 = bf16[128,192,96]{2,1,0:T(8,128)(2,1)} async-done(((bf16[128,192,96]{2,1,0:T(8,128)(2,1)}), bf16[128,192,96]{2,1,0:T(8,128)(2,1)}, u32[]{:S(2)}, u32[]{:S(2)}) %all-to-all-start.3) | async-done | bytes 4718624 | tf_op jit(solution)/shard_map/all_to_all | solution.py:162
  253.9 12.6 %copy.108 = bf16[32,4,192,96]{2,1,3,0:T(4,128)(2,1)} copy(bf16[32,4,192,96]{3,2,0,1:T(8,128)(2,1)} %bitcast.46) | data formatting | bytes 9437184 | tf_op jit(solution)/shard_map/all_to_all | solution.py:162
  266.5 11.6 %all_to_all.98 = bf16[32,768,96]{1,2,0:T(8,128)(2,1)} reshape(bf16[32,4,192,96]{2,1,3,0:T(4,128)(2,1)} %copy.108) | data formatting | bytes 9437184 | tf_op jit(solution)/shard_map/all_to_all | solution.py:162
  278.1 45.2 %all-to-all-done.1 = bf16[128,192,96]{2,1,0:T(8,128)(2,1)} async-done(((bf16[128,192,96]{2,1,0:T(8,128)(2,1)}), bf16[128,192,96]{2,1,0:T(8,128)(2,1)}, u32[]{:S(2)}, u32[]{:S(2)}) %all-to-all-start.1) | async-done | bytes 4718624 | tf_op jit(solution)/shard_map/all_to_all | solution.py:155
  328.1 12.5 %copy.105 = bf16[32,4,192,96]{2,1,3,0:T(4,128)(2,1)} copy(bf16[32,4,192,96]{3,2,0,1:T(8,128)(2,1)} %bitcast.37) | data formatting | bytes 9437184 | tf_op jit(solution)/shard_map/all_to_all | solution.py:155
  340.6 11.6 %all_to_all.90 = bf16[32,768,96]{1,2,0:T(8,128)(2,1)} reshape(bf16[32,4,192,96]{2,1,3,0:T(4,128)(2,1)} %copy.105) | data formatting | bytes 9437184 | tf_op jit(solution)/shard_map/all_to_all | solution.py:155
  352.2 81.1 %all-to-all-done.4 = bf16[32,768,96]{1,2,0:T(8,128)(2,1)} async-done(((bf16[32,768,96]{1,2,0:T(8,128)(2,1)}), bf16[32,768,96]{1,2,0:T(8,128)(2,1)}, u32[]{:S(2)}, u32[]{:S(2)}) %all-to-all-start.4) | async-done | bytes 4718624 | tf_op jit(solution)/shard_map/all_to_all | solution.py:161
  442.9 100.4 %all-to-all-done.2 = bf16[32,768,96]{1,2,0:T(8,128)(2,1)} async-done(((bf16[32,768,96]{1,2,0:T(8,128)(2,1)}), bf16[32,768,96]{1,2,0:T(8,128)(2,1)}, u32[]{:S(2)}, u32[]{:S(2)}) %all-to-all-start.2) | async-done | bytes 4718624 | tf_op jit(solution)/shard_map/all_to_all | solution.py:154
  552.7 8.5 copy.112
  582.0 101.7 %all-to-all-done.5 = bf16[4,768,768]{1,0,2:T(4,128)(2,1)} async-done(((bf16[4,768,768]{1,0,2:T(4,128)(2,1)}), bf16[4,768,768]{1,0,2:T(4,128)(2,1)}, u32[]{:S(2)}, u32[]{:S(2)}) %all-to-all-start.5) | async-done | bytes 4718624 | tf_op jit(solution)/shard_map/all_to_all | solution.py:173
  689.2 8.7 %copy.115 = bf16[32,768,96]{2,0,1:T(8,128)(2,1)} copy(bf16[32,768,96]{1,2,0:T(8,128)(2,1)} %bitcast.147) | data formatting | bytes 9437184 | tf_op jit(solution)/shard_map/all_to_all | solution.py:173
  714.2 59.3 %all-to-all-done.6 = bf16[32,768,96]{2,0,1:T(8,128)(2,1)} async-done(((bf16[32,768,96]{2,0,1:T(8,128)(2,1)}), bf16[32,768,96]{2,0,1:T(8,128)(2,1)}, u32[]{:S(2)}, u32[]{:S(2)}) %all-to-all-start.6) | async-done | bytes 4718624 | tf_op jit(solution)/shard_map/all_to_all | solution.py:172
  773.5 8.4 copy.116
  781.9 13.5 %reshape.258 = f32[32,4,192,96]{2,1,3,0:T(4,128)} reshape(bf16[32,768,96]{1,2,0:T(8,128)(2,1)} %copy.116) | data formatting | bytes 14155776 | tf_op jit(solution)/shard_map/convert_element_type | solution.py:179
  795.5 6.5 bitcast_reduce_fusion
  802.0 8.4 multiply_reduce_fusion
  810.6 16.3 %copy.117 = f32[4,32,192,96]{3,2,1,0:T(8,128)} copy(f32[4,32,192,96]{2,0,3,1:T(4,128)} %bitcast.145) | data formatting | bytes 18874368 | tf_op jit(solution)/shard_map/convert_element_type | solution.py:179
  827.0 9.2 %fusion.1 = bf16[128,192,96]{2,1,0:T(8,128)(2,1)} fusion(f32[4,32,192,96]{3,2,1,0:T(8,128)} %copy.117, f32[192,96]{1,0:T(8,128)S(1)} %copy.119, f32[192,96]{1,0:T(8,128)S(1)} %copy.118), kind=kLoop, calls=%fused_computation.2 | loop fusion | flops 7077888 | bytes 14303232 | tf_op jit(solution)/shard_map/convert_element_type | solution.py:179
  836.2 16.0 %fusion.11 = bf16[192,96,128]{2,1,0:T(8,128)(2,1)} fusion(f32[48,96,128]{2,1,0:T(8,128)} %get-tuple-element.51, f32[48,96,128]{2,1,0:T(8,128)} %get-tuple-element.12, f32[48,96,128]{2,1,0:T(8,128)} %get-tuple-element.48, f32[48,96,128]{2,1,0:T(8,128)} %get-tuple-element.10, bf16[48,96,128]{2,1,0:T(8,128)(2,1)S(1)} %copy-done.7, ...), kind=kOutput, calls=%fused_computation.14 | convolution fusion | flops 627572736 | bytes 23625728 | tf_op jit(solution)/shard_map/crb,ce->rbe/dot_general | solution.py:180
  (141 shorter events, 120.2 us)
Async XLA Ops:
  7.2 42.0 %copy-start = (bf16[1024,128]{1,0:T(8,128)(2,1)S(1)}, bf16[1024,128]{1,0:T(8,128)(2,1)}, u32[]{:S(2)}) copy-start(bf16[1024,128]{1,0:T(8,128)(2,1)} %param.15) | copy-start | bytes 786436
  7.2 27.1 %copy-start.17 = (bf16[128,640]{1,0:T(8,128)(2,1)S(1)}, bf16[128,640]{1,0:T(8,128)(2,1)}, u32[]{:S(2)}) copy-start(bf16[128,640]{1,0:T(8,128)(2,1)} %param.18) | copy-start | bytes 491524
  29.3 14.7 %all-to-all-start = ((bf16[4,4,6144]{2,0,1:T(4,128)(2,1)}), bf16[4,4,6144]{2,0,1:T(4,128)(2,1)S(1)}, u32[]{:S(2)}, u32[]{:S(2)}) async-start(bf16[4,4,6144]{2,0,1:T(4,128)(2,1)} %bitcast.2), calls=%async_computation | async-start | bytes 393216 | tf_op jit(solution)/shard_map/all_to_all | solution.py:82
  58.8 63.6 %copy-start.6 = (bf16[48,96,128]{2,1,0:T(8,128)(2,1)}, bf16[48,96,128]{2,1,0:T(8,128)(2,1)S(1)}, u32[]{:S(2)}) copy-start(bf16[48,96,128]{2,1,0:T(8,128)(2,1)S(1)} %get-tuple-element.37) | copy-start | bytes 3538948
  73.9 41.9 %copy-start.8 = (bf16[48,96,128]{2,1,0:T(8,128)(2,1)}, bf16[48,96,128]{2,1,0:T(8,128)(2,1)S(1)}, u32[]{:S(2)}) copy-start(bf16[48,96,128]{2,1,0:T(8,128)(2,1)S(1)} %get-tuple-element.41) | copy-start | bytes 3538948
  89.4 5.4 copy-start.10
  94.8 11.4 %copy-start.18 = (bf16[128,8]{0,1:T(8,128)(2,1)S(1)}, bf16[128,8]{0,1:T(8,128)(2,1)}, u32[]{:S(2)}) copy-start(bf16[128,8]{0,1:T(8,128)(2,1)} %param.16) | copy-start | bytes 6148
  104.5 4.4 copy-start.12
  106.2 2.7 copy-start.11
  108.9 19.9 %copy-start.2 = (f32[48,96,648]{2,1,0:T(8,128)}, f32[48,96,648]{2,1,0:T(8,128)S(1)}, u32[]{:S(2)}) copy-start(f32[48,96,648]{2,1,0:T(8,128)S(1)} %fusion.110) | copy-start | bytes 35831812
  143.6 20.8 %copy-start.4 = (bf16[128,48,96]{0,2,1:T(8,128)(2,1)S(1)}, bf16[128,48,96]{0,2,1:T(8,128)(2,1)}, u32[]{:S(2)}) copy-start(bf16[128,48,96]{0,2,1:T(8,128)(2,1)} %get-tuple-element.2) | copy-start | bytes 3538948
  143.6 20.8 %copy-start.5 = (bf16[128,48,96]{0,2,1:T(8,128)(2,1)S(1)}, bf16[128,48,96]{0,2,1:T(8,128)(2,1)}, u32[]{:S(2)}) copy-start(bf16[128,48,96]{0,2,1:T(8,128)(2,1)} %get-tuple-element.50) | copy-start | bytes 3538948
  175.3 73.3 %all-to-all-start.3 = ((bf16[128,192,96]{2,1,0:T(8,128)(2,1)}), bf16[128,192,96]{2,1,0:T(8,128)(2,1)}, u32[]{:S(2)}, u32[]{:S(2)}) async-start(bf16[128,192,96]{2,1,0:T(8,128)(2,1)} %copy.107), calls=%async_computation.3 | async-start | bytes 12582912 | tf_op jit(solution)/shard_map/all_to_all | solution.py:162
  248.7 74.5 %all-to-all-start.1 = ((bf16[128,192,96]{2,1,0:T(8,128)(2,1)}), bf16[128,192,96]{2,1,0:T(8,128)(2,1)}, u32[]{:S(2)}, u32[]{:S(2)}) async-start(bf16[128,192,96]{2,1,0:T(8,128)(2,1)} %copy.104), calls=%async_computation.1 | async-start | bytes 12582912 | tf_op jit(solution)/shard_map/all_to_all | solution.py:155
  323.2 110.1 %all-to-all-start.4 = ((bf16[32,768,96]{1,2,0:T(8,128)(2,1)}), bf16[32,768,96]{1,2,0:T(8,128)(2,1)}, u32[]{:S(2)}, u32[]{:S(2)}) async-start(bf16[32,768,96]{1,2,0:T(8,128)(2,1)} %all_to_all.98), calls=%async_computation.4 | async-start | bytes 9437184 | tf_op jit(solution)/shard_map/all_to_all | solution.py:161
  433.3 109.9 %all-to-all-start.2 = ((bf16[32,768,96]{1,2,0:T(8,128)(2,1)}), bf16[32,768,96]{1,2,0:T(8,128)(2,1)}, u32[]{:S(2)}, u32[]{:S(2)}) async-start(bf16[32,768,96]{1,2,0:T(8,128)(2,1)} %all_to_all.90), calls=%async_computation.2 | async-start | bytes 9437184 | tf_op jit(solution)/shard_map/all_to_all | solution.py:154
  543.2 3.8 copy-start.13
  561.2 122.5 %all-to-all-start.5 = ((bf16[4,768,768]{1,0,2:T(4,128)(2,1)}), bf16[4,768,768]{1,0,2:T(4,128)(2,1)}, u32[]{:S(2)}, u32[]{:S(2)}) async-start(bf16[4,768,768]{1,0,2:T(4,128)(2,1)} %copy.112), calls=%async_computation.5 | async-start | bytes 9437184 | tf_op jit(solution)/shard_map/all_to_all | solution.py:173
  565.8 137.8 %all-gather.4.cloned.1.call-start = ((), (), s32[]{:S(2)}) async-start(), calls=%async_computation.7 | async-start | bytes 1769472 | tf_op jit(solution)/shard_map/all_gather | solution.py:133
  567.7 138.4 %all-gather.6.cloned.1.call-start = ((), (), s32[]{:S(2)}) async-start(), calls=%async_computation.8 | async-start | bytes 3932160 | tf_op jit(solution)/shard_map/all_gather | solution.py:132
  571.0 3.4 slice-start
  575.1 2.6 slice-start.1
  577.6 3.0 copy-start.21
  577.6 3.0 copy-start.22
  577.6 3.2 copy-start.19
  577.6 3.2 copy-start.20
  697.9 75.6 %all-to-all-start.6 = ((bf16[32,768,96]{2,0,1:T(8,128)(2,1)}), bf16[32,768,96]{2,0,1:T(8,128)(2,1)}, u32[]{:S(2)}, u32[]{:S(2)}) async-start(bf16[32,768,96]{2,0,1:T(8,128)(2,1)} %copy.115), calls=%async_computation.6 | async-start | bytes 12582912 | tf_op jit(solution)/shard_map/all_to_all | solution.py:172
  706.2 2.9 copy-start.3
  826.9 9.3 %copy-start.7 = (bf16[48,96,128]{2,1,0:T(8,128)(2,1)S(1)}, bf16[48,96,128]{2,1,0:T(8,128)(2,1)}, u32[]{:S(2)}) copy-start(bf16[48,96,128]{2,1,0:T(8,128)(2,1)} %copy-done.6) | copy-start | bytes 3538948
  827.0 9.3 %copy-start.9 = (bf16[48,96,128]{2,1,0:T(8,128)(2,1)S(1)}, bf16[48,96,128]{2,1,0:T(8,128)(2,1)}, u32[]{:S(2)}) copy-start(bf16[48,96,128]{2,1,0:T(8,128)(2,1)} %copy-done.8) | copy-start | bytes 3538948
  827.0 9.2 %copy-start.24 = (bf16[128,128]{1,0:T(8,128)(2,1)S(1)}, bf16[128,128]{1,0:T(8,128)(2,1)}, u32[]{:S(2)}) copy-start(bf16[128,128]{1,0:T(8,128)(2,1)} %param.19) | copy-start | bytes 98308
  836.2 16.0 %copy-start.1 = (bf16[1024,128]{1,0:T(8,128)(2,1)S(1)}, bf16[1024,128]{1,0:T(8,128)(2,1)}, u32[]{:S(2)}) copy-start(bf16[1024,128]{1,0:T(8,128)(2,1)} %param.15) | copy-start | bytes 786436
  (4 other events, 4.2 us)
Sparse Core Ops, SparseCore 0:
  568.2 40.0 all-gather.3
  610.1 53.0 all-gather.5
where the time goes:
time: 866 us; the launch traced here: 859 us
  waiting for transfers between devices  443 us (51%)
  local copies, waits for them, and re-layouts  156 us (18%)
  matrix products  103 us (12%)
  other arithmetic  83.1 us (10%)
  starting transfers between devices  34 us (4%)
  blocking collectives  25.8 us (3%)
  between operations  14.9 us (2%)
    all_to_all x1, waiting for transfers between devices, on_device(): lax.all_to_all(product, 'col', split_axis=2, concat_axis=0, tiled=True)  102 us
    all_to_all x1, waiting for transfers between devices, on_device(): lax.all_to_all(lax.all_to_all(tri_left_all, 'row', split_axis=0, concat_a...  100 us
    all_to_all x1, waiting for transfers between devices, on_device(): lax.all_to_all(lax.all_to_all(tri_right_all, 'row', split_axis=0, concat_...  81.1 us
    all_to_all x1, waiting for transfers between devices, on_device(): lax.all_to_all(lax.all_to_all(product, 'col', split_axis=2, concat_axis=0...  59.3 us
    all_to_all x1, waiting for transfers between devices, on_device(): lax.all_to_all(tri_right_all, 'row', split_axis=0, concat_axis=1, tiled=T...  55.2 us
    all_to_all x1, waiting for transfers between devices, on_device(): lax.all_to_all(tri_left_all, 'row', split_axis=0, concat_axis=1, tiled=True)  45.2 us
    dot_general x4, matrix products, on_device(): jnp.einsum('icjd,cde->ije', outer, w_outer, preferred_element_type=jnp.fl...  39.2 us
    transpose x2, other arithmetic, on_device(): right_parts.append(jnp.transpose(tri_right, (2, 0, 1)))  35.5 us
  transfers between devices with their start and end apart: 9, of which 6 were waited for; matrix products, arithmetic and copies ran while one was open for 10% of the time, Pallas kernels for 0%

commit v1 on v0

v1 whole, which is shorter than its diff:
```python
import functools

import jax
import jax.numpy as jnp
from jax import lax
from jax.experimental import pallas as pl
from jax.experimental.pallas import tpu as pltpu
from jax.sharding import Mesh, PartitionSpec as P

TENSOR_FEATURES = 32
MEAN_GROUPS = 8
GROUP_FEATURES = 32
CTRI = 128

EPS = 1e-05
MASK_PENALTY = 10000.0
QUAD = 4
LANES = 128
VMEM_LIMIT = 60 * 1024 * 1024
AXES = ("row", "half", "pos")
GROUP = ("row", "pos")
F32 = jnp.float32
BF16 = jnp.bfloat16
NT = (((1,), (1,)), ((), ()))
TN = (((0,), (0,)), ((), ()))


def standardize_features(values_in, axis):
    centre = values_in - jnp.mean(values_in, axis=axis, keepdims=True)
    spread = jnp.mean(centre * centre, axis=axis, keepdims=True)
    return centre * lax.rsqrt(spread + EPS)


def sigmoid(x):
    return 0.5 * jnp.tanh(0.5 * x) + 0.5


def params(grid_dims=1):
    return pltpu.CompilerParams(
        vmem_limit_bytes=VMEM_LIMIT, dimension_semantics=("arbitrary",) * grid_dims
    )


def whole(shape):
    zeros = (0,) * len(shape)
    return pl.BlockSpec(shape, lambda *_: zeros, pipeline_mode=pl.Buffered(1))


def pack_rows(rows):
    unit = rows[0].shape[0] // 3
    return jnp.concatenate([r[: 2 * unit] for r in rows] + [r[2 * unit :] for r in rows], axis=0)


def unpack_rows(packed):
    unit = packed.shape[0] // 12
    return [
        jnp.concatenate(
            [
                packed[2 * unit * a : 2 * unit * (a + 1)],
                packed[8 * unit + unit * a : 8 * unit + unit * (a + 1)],
            ],
            axis=0,
        )
        for a in range(QUAD)
    ]


def swap_blocks(first, second, width, lane):
    low = (lane // width) % 2 == 0
    size = first.shape[1]
    return (
        jnp.where(low, first, pltpu.roll(second, width, 1)),
        jnp.where(low, pltpu.roll(first, size - width, 1), second),
    )


def exchange_blocks(packed):
    part = packed
    unit = LANES // 4
    lane = lax.broadcasted_iota(jnp.int32, part[0][0].shape, 1)
    out = [[None] * 3 for _ in range(4)]
    for pair in range(2):
        one, two = part[2 * pair], part[2 * pair + 1]
        for t in range(2):
            out[2 * t][pair], out[2 * t + 1][pair] = swap_blocks(one[t], two[t], 2 * unit, lane)
    u0, u2 = swap_blocks(part[0][2], part[2][2], 2 * unit, lane)
    u1, u3 = swap_blocks(part[1][2], part[3][2], 2 * unit, lane)
    out[0][2], out[1][2] = swap_blocks(u0, u1, unit, lane)
    out[2][2], out[3][2] = swap_blocks(u2, u3, unit, lane)
    return out


def front_kernel(left_ref, present_ref, coup_ref, weight_ref, right_ref, pcol_ref, mid_ref, normed_ref, tmp_ref):
    block = coup_ref.shape[0]
    seqs = left_ref.shape[0] // block
    wide = coup_ref.shape[2]
    features = weight_ref.shape[1] // wide
    step = 4
    for low in range(0, features, step):
        part = jnp.dot(
            left_ref[...], weight_ref[:, low * wide : (low + step) * wide], preferred_element_type=F32
        ).astype(BF16)
        for i in range(block):
            for d in range(step):
                tmp_ref[
                    i // 2,
                    (low + d) * seqs : (low + d + 1) * seqs,
                    (i % 2) * wide : (i % 2 + 1) * wide,
                ] = part[i * seqs : (i + 1) * seqs, d * wide : (d + 1) * wide]
    for pair in range(block // 2):
        update = jnp.dot(right_ref[...], tmp_ref[pair], preferred_element_type=F32)
        count = jnp.dot(pcol_ref[...], present_ref[pair], preferred_element_type=F32)
        update = update / jnp.maximum(count, 1.0)
        for e in range(2):
            i = 2 * pair + e
            mid = (coup_ref[i].astype(F32) + update[:, e * wide : (e + 1) * wide]).astype(BF16)
            mid_ref[i] = mid
            normed_ref[i] = standardize_features(mid.astype(F32), 1).astype(BF16)


def front(left_rows, present_pairs, coupling, w_tensor, right_cols, present_cols):
    rows, cols, wide = coupling.shape
    seqs = left_rows.shape[0] // rows
    block = 8
    tile = pl.BlockSpec((block, cols, wide), lambda i: (i, 0, 0))
    return pl.pallas_call(
        front_kernel,
        grid=(rows // block,),
        in_specs=[
            pl.BlockSpec((block * seqs, left_rows.shape[1]), lambda i: (i, 0)),
            pl.BlockSpec((block // 2, seqs, 2 * wide), lambda i: (i, 0, 0)),
            tile,
            whole(w_tensor.shape),
            whole(right_cols.shape),
            whole(present_cols.shape),
        ],
        out_specs=[tile, tile],
        out_shape=[jax.ShapeDtypeStruct(coupling.shape, BF16)] * 2,
        scratch_shapes=[pltpu.VMEM((block // 2, right_cols.shape[1], 2 * wide), BF16)],
        compiler_params=params(),
        name="front",
    )(left_rows, present_pairs, coupling, w_tensor, right_cols, present_cols)


def project_kernel(normed_ref, live_ref, weight_ref, out_ref, tmp_ref):
    quads = normed_ref.shape[0] // QUAD
    dests = out_ref.shape[0]
    each = out_ref.shape[1] // quads
    count = dests * each
    for m in range(quads):
        packed = pack_rows([normed_ref[QUAD * m + a] for a in range(QUAD)])
        both = lax.dot_general(weight_ref[...], packed, NT, preferred_element_type=F32)
        gated = sigmoid(both[:count]) * both[count:] * live_ref[m]
        for dest in range(dests):
            tmp_ref[dest, m * each : (m + 1) * each] = gated[dest * each : (dest + 1) * each]
    out_ref[...] = tmp_ref[...].astype(BF16)


def project(normed, live, weight, dests):
    rows, cols, wide = normed.shape
    quads = 8
    each = weight.shape[0] // (2 * dests)
    lanes = QUAD * cols
    total = rows // QUAD
    return pl.pallas_call(
        project_kernel,
        grid=(total // quads,),
        in_specs=[
            pl.BlockSpec((quads * QUAD, cols, wide), lambda i: (i, 0, 0)),
            pl.BlockSpec((quads, 1, lanes), lambda i: (i, 0, 0)),
            whole(weight.shape),
        ],
        out_specs=pl.BlockSpec((dests, quads * each, lanes), lambda i: (0, i, 0)),
        out_shape=jax.ShapeDtypeStruct((dests, total * each, lanes), BF16),
        scratch_shapes=[pltpu.VMEM((dests, quads * each, lanes), F32)],
        compiler_params=params(),
        name="project",
    )(normed, live, weight)


def assemble_kernel(half_ref, recv_ref, left_ref, own_ref, send_ref, flat_ref, right_ref, *, row_count, pos_count):
    channel = pl.program_id(0)
    lanes = recv_ref.shape[2]
    unit = lanes // 12
    cols = 3 * unit
    each = send_ref.shape[1] // (row_count * QUAD)
    stride = recv_ref.shape[1] // each
    groups = pos_count // 4
    tiles = lanes // LANES
    per_row = each * QUAD // cols

    @pl.when(channel == 0)
    def _():
        for src in range(row_count * pos_count):
            value = recv_ref[src].astype(F32)
            for t in range(tiles):
                flat_ref[src, t] = value[:, t * LANES : (t + 1) * LANES]

    def block(row, group, index):
        packed = []
        for p in range(4):
            src = row * pos_count + group * 4 + p
            packed.append(
                [flat_ref[src, t, pl.ds(index, each, stride=stride), :] for t in range(tiles)]
            )
        return exchange_blocks(packed)

    for row in range(row_count):
        for group in range(groups):
            span = slice(group * lanes, (group + 1) * lanes)
            left = block(row, group, channel)
            for a in range(QUAD):
                start = (row * QUAD + a) * each
                left_ref[0, start : start + each, span] = jnp.concatenate(left[a], axis=1).astype(
                    BF16
                )
            right = block(row, group, channel + stride // 2)
            for a in range(QUAD):
                for piece in range(per_row):
                    place = row * per_row + piece
                    base = (place // 4) * lanes
                    low = piece * (cols // QUAD)
                    mid = low + 2 * unit // QUAD
                    high = low + cols // QUAD
                    first = base + (place % 4) * 2 * unit + a
                    second = base + 8 * unit + (place % 4) * unit + a
                    for t in range(tiles):
                        value = right[a][t]
                        at = group * tiles + t
                        right_ref[at, pl.ds(first, mid - low, stride=QUAD), :] = value[low:mid]
                        right_ref[at, pl.ds(second, high - mid, stride=QUAD), :] = value[mid:high]
    width = pos_count * cols
    own = pl.multiple_of(half_ref[0] * width, width)
    other = pl.multiple_of((1 - half_ref[0]) * width, width)
    theirs = []
    for at in range(groups * tiles):
        span = slice(at * LANES, (at + 1) * LANES)
        own_ref[0, :, span] = right_ref[at, pl.ds(own, width), :].astype(BF16)
        theirs.append(right_ref[at, pl.ds(other, width), :].astype(BF16))
    theirs = jnp.concatenate(theirs, axis=1)
    for row in range(row_count):
        span = slice(row * QUAD * each, (row + 1) * QUAD * each)
        send_ref[0, span] = lax.dot_general(
            left_ref[0, span], theirs, NT, preferred_element_type=F32
        ).astype(BF16)


def assemble(half, received, row_count, pos_count, cols):
    sources, height, lanes = received.shape
    each = (2 * pos_count * cols) // (row_count * QUAD)
    stride = height // each
    channels = stride // 2
    depth = pos_count * cols
    rows = 2 * depth
    return pl.pallas_call(
        functools.partial(assemble_kernel, row_count=row_count, pos_count=pos_count),
        grid=(channels,),
        in_specs=[pl.BlockSpec(memory_space=pltpu.SMEM), whole(received.shape)],
        out_specs=[
            pl.BlockSpec((1, rows, depth), lambda c: (c, 0, 0)),
            pl.BlockSpec((1, depth, depth), lambda c: (c, 0, 0)),
            pl.BlockSpec((1, rows, depth), lambda c: (c, 0, 0)),
        ],
        out_shape=[
            jax.ShapeDtypeStruct((channels, rows, depth), BF16),
            jax.ShapeDtypeStruct((channels, depth, depth), BF16),
            jax.ShapeDtypeStruct((channels, rows, depth), BF16),
        ],
        scratch_shapes=[
            pltpu.VMEM((sources, lanes // LANES, height, LANES), F32),
            pltpu.VMEM((depth // LANES, rows, LANES), F32),
        ],
        compiler_params=params(),
        name="assemble",
    )(half, received)


def combine_kernel(left_ref, own_ref, recv_ref, out_ref, tmp_ref, *, row_count, pos_count):
    channel = pl.program_id(0)
    channels = pl.num_programs(0)
    lanes = out_ref.shape[2]
    each = left_ref.shape[1] // (row_count * QUAD)
    stride = out_ref.shape[1] // each
    tiles = lanes // LANES
    for row in range(row_count):
        for group in range(pos_count // 4):
            cols = slice(group * lanes, (group + 1) * lanes)
            blocks = []
            for a in range(QUAD):
                span = slice((row * QUAD + a) * each, (row * QUAD + a + 1) * each)
                value = lax.dot_general(
                    left_ref[0, span], own_ref[0, cols], NT, preferred_element_type=F32
                )
                value = value + recv_ref[0, span, cols].astype(F32)
                blocks.append([value[:, t * LANES : (t + 1) * LANES] for t in range(tiles)])
            for p, value in enumerate(exchange_blocks(blocks)):
                dest = row * pos_count + group * 4 + p
                for t in range(tiles):
                    tmp_ref[dest, t, pl.ds(channel, each, stride=stride), :] = value[t]

    @pl.when(channel == channels - 1)
    def _():
        for dest in range(row_count * pos_count):
            for t in range(tiles):
                out_ref[dest, :, t * LANES : (t + 1) * LANES] = tmp_ref[dest, t].astype(BF16)


def combine(left, own, received, row_count, pos_count, cols):
    channels, rows, depth = left.shape
    each = rows // (row_count * QUAD)
    shape = (row_count * pos_count, each * channels, QUAD * cols)
    return pl.pallas_call(
        functools.partial(combine_kernel, row_count=row_count, pos_count=pos_count),
        grid=(channels,),
        in_specs=[
            pl.BlockSpec((1, rows, depth), lambda c: (c, 0, 0)),
            pl.BlockSpec((1, depth, depth), lambda c: (c, 0, 0)),
            pl.BlockSpec((1, rows, depth), lambda c: (c, 0, 0)),
        ],
        out_specs=whole(shape),
        out_shape=jax.ShapeDtypeStruct(shape, BF16),
        scratch_shapes=[pltpu.VMEM((shape[0], shape[2] // LANES, shape[1], LANES), F32)],
        compiler_params=params(),
        name="combine",
    )(left, own, received)


def finish_kernel(*refs, chunks):
    parts = refs[:chunks]
    mid_ref, normed_ref, gate_ref, weight_ref, out_ref, tmp_ref = refs[chunks:]
    quads = mid_ref.shape[0] // QUAD
    sources = parts[0].shape[0]
    each = parts[0].shape[1] // quads
    total = sources * each * chunks
    for g, part in enumerate(parts):
        for src in range(sources):
            value = part[src].astype(F32)
            for m in range(quads):
                start = m * total + (src * chunks + g) * each
                tmp_ref[start : start + each] = value[m * each : (m + 1) * each]
    for m in range(quads):
        product = tmp_ref[m * total : (m + 1) * total]
        normed = standardize_features(product, 0).astype(BF16)
        out = lax.dot_general(normed, weight_ref[...], TN, preferred_element_type=F32)
        for a, value in enumerate(unpack_rows(out)):
            i = QUAD * m + a
            gate = sigmoid(jnp.dot(normed_ref[i], gate_ref[...], preferred_element_type=F32))
            out_ref[i] = (mid_ref[i].astype(F32) + gate * value).astype(BF16)


def finish(parts, mid, normed, w_gate, w_final):
    rows, cols, wide = mid.shape
    chunks = len(parts)
    sources, height, lanes = parts[0].shape
    total = rows // QUAD
    each = height // total
    quads = 8
    tile = pl.BlockSpec((quads * QUAD, cols, wide), lambda i: (i, 0, 0))
    return pl.pallas_call(
        functools.partial(finish_kernel, chunks=chunks),
        grid=(total // quads,),
        in_specs=[pl.BlockSpec((sources, quads * each, lanes), lambda i: (0, i, 0))] * chunks
        + [tile, tile, whole(w_gate.shape), whole(w_final.shape)],
        out_specs=tile,
        out_shape=jax.ShapeDtypeStruct(mid.shape, BF16),
        scratch_shapes=[pltpu.VMEM((quads * sources * each * chunks, lanes), F32)],
        compiler_params=params(),
        name="finish",
    )(*parts, mid, normed, w_gate, w_final)


def on_device(
    alignment_embedding,
    coupling_embedding,
    amino_validity,
    alignment_validity,
    alignment_matrix,
    tensor_final_matrix,
    coupling_logit_matrix,
    mean_final_matrix,
    trimul_matrices,
    trimul_final_matrix,
):
    seq_each, module_number, feature_count = alignment_embedding.shape
    rows, _, wide = coupling_embedding.shape
    row_count = lax.axis_size("row")
    pos_count = lax.axis_size("pos")
    col_count = 2 * pos_count
    row_index = lax.axis_index("row")
    half = lax.axis_index("half")
    col_index = half * pos_count + lax.axis_index("pos")
    seqs = seq_each * row_count
    active_entries = amino_validity.astype(F32)
    sequence_index = lax.broadcasted_iota(jnp.int32, alignment_validity.shape, 0)
    present_entries = (
        jnp.where(sequence_index == 0, F32(1.0), alignment_validity.astype(F32))
        * active_entries[None, :]
    )
    row_start = row_index * rows
    col_start = col_index * module_number
    present_rows = lax.dynamic_slice_in_dim(present_entries, row_start, rows, 1)
    present_cols = lax.dynamic_slice_in_dim(present_entries, col_start, module_number, 1)
    live_rows = lax.dynamic_slice_in_dim(active_entries, row_start, rows, 0)
    live_cols = lax.dynamic_slice_in_dim(active_entries, col_start, module_number, 0)

    gathered = lax.all_gather(alignment_embedding, AXES, axis=0, tiled=False)
    gathered = gathered.reshape(row_count, col_count, seq_each, module_number, feature_count)
    per_row = rows // module_number
    row_part = lax.dynamic_slice_in_dim(gathered, row_index * per_row, per_row, 1)
    row_part = jnp.transpose(row_part, (1, 3, 0, 2, 4)).reshape(rows * seqs, feature_count)
    col_part = lax.dynamic_slice_in_dim(gathered, col_index, 1, 1)
    col_part = col_part.reshape(seqs * module_number, feature_count)

    def project_msa(part, matrix):
        normed = standardize_features(part.astype(F32), 1).astype(BF16)
        return jnp.dot(normed, matrix, preferred_element_type=F32)

    left_rows = (
        project_msa(row_part, alignment_matrix[:, :TENSOR_FEATURES])
        * present_rows.T.reshape(rows * seqs, 1)
    ).astype(BF16)
    right = project_msa(col_part, alignment_matrix[:, TENSOR_FEATURES : 2 * TENSOR_FEATURES])
    right = (right * present_cols.reshape(seqs * module_number, 1)).astype(BF16)
    right_cols = jnp.transpose(
        right.reshape(seqs, module_number, TENSOR_FEATURES), (1, 2, 0)
    ).reshape(module_number, TENSOR_FEATURES * seqs)
    present_pairs = jnp.broadcast_to(
        jnp.transpose(present_rows.reshape(seqs, rows // 2, 2), (1, 0, 2))[..., None],
        (rows // 2, seqs, 2, wide),
    ).reshape(rows // 2, seqs, 2 * wide).astype(BF16)
    w_tensor = tensor_final_matrix.reshape(TENSOR_FEATURES, TENSOR_FEATURES * wide)
    pair_mid, pair_normed = front(
        left_rows,
        present_pairs,
        coupling_embedding,
        w_tensor,
        right_cols,
        present_cols.T.astype(BF16),
    )

    unit = module_number // 3
    pair_live = live_rows[:, None] * live_cols[None, :]
    quad_live = pair_live.reshape(rows // QUAD, QUAD, module_number)
    live_packed = jnp.concatenate(
        [
            quad_live[:, :, : 2 * unit].reshape(rows // QUAD, -1),
            quad_live[:, :, 2 * unit :].reshape(rows // QUAD, -1),
        ],
        axis=1,
    )[:, None, :]

    devices = row_count * pos_count
    channels = CTRI // devices
    each = min(4, channels)
    chunks = channels // each
    w_kinds = trimul_matrices[:, : 4 * CTRI].T.reshape(2, 2, devices, chunks, each, wide)
    half_scalar = half.astype(jnp.int32).reshape(1)
    pos_half = pos_count
    swap = [(0, 1), (1, 0)]
    returned = []
    for g in range(chunks):
        weight = jnp.transpose(w_kinds[:, :, :, g], (1, 2, 0, 3, 4)).reshape(-1, wide)
        sent = project(pair_normed, live_packed, weight, devices)
        received = lax.all_to_all(sent, GROUP, split_axis=0, concat_axis=0, tiled=True)
        left, own, theirs = assemble(half_scalar, received, row_count, pos_half, module_number)
        partial = lax.ppermute(theirs, "half", swap)
        product = combine(left, own, partial, row_count, pos_half, module_number)
        returned.append(lax.all_to_all(product, GROUP, split_axis=0, concat_axis=0, tiled=True))

    own_rows = project_msa(
        alignment_embedding.reshape(seq_each * module_number, feature_count),
        alignment_matrix[:, 2 * TENSOR_FEATURES :],
    ).reshape(seq_each, module_number, -1)
    values = own_rows[:, :, : MEAN_GROUPS * GROUP_FEATURES].astype(BF16)
    sequence_gate = jax.nn.sigmoid(own_rows[:, :, MEAN_GROUPS * GROUP_FEATURES :])
    logits = (
        jnp.dot(
            pair_normed.reshape(rows * module_number, wide),
            coupling_logit_matrix,
            preferred_element_type=F32,
        ).reshape(rows, module_number, MEAN_GROUPS)
        + MASK_PENALTY * (live_rows - 1.0)[:, None, None]
    )
    logits_all = lax.all_gather(logits, "row", axis=0, tiled=True)
    values_all = lax.all_gather(values, ("half", "pos"), axis=1, tiled=True)
    top_all = jnp.max(logits_all, axis=0)
    expd = jnp.exp(logits_all - top_all[None])
    weights_all = (expd / jnp.sum(expd, axis=0)[None]).astype(BF16)
    value_all_heads = values_all.reshape(seq_each, -1, MEAN_GROUPS, GROUP_FEATURES)
    summed = jnp.einsum("jih,sjhd->sihd", weights_all, value_all_heads, preferred_element_type=F32)
    head_averaged = summed.reshape(seq_each, module_number, MEAN_GROUPS * GROUP_FEATURES)
    gated_result = (sequence_gate * head_averaged).astype(BF16)
    blended_update = jnp.dot(
        gated_result.reshape(seq_each * module_number, -1),
        mean_final_matrix,
        preferred_element_type=F32,
    ).reshape(seq_each, module_number, -1)
    alignment_updated_embedding = (alignment_embedding.astype(F32) + blended_update).astype(BF16)

    pair_output = finish(
        returned, pair_mid, pair_normed, trimul_matrices[:, 4 * CTRI :], trimul_final_matrix
    )
    return (alignment_updated_embedding, pair_output)


def solution(mesh):
    rows, cols = mesh.devices.shape
    inner = Mesh(mesh.devices.reshape(rows, 2, cols // 2), AXES)
    tile = P("row", ("half", "pos"), None)
    in_specs = (tile, tile) + (P(),) * 8
    return jax.shard_map(
        on_device, mesh=inner, in_specs=in_specs, out_specs=(tile, tile), check_vma=False
    )
```

time: 866 us -> 510 us (0.59)
  local copies, waits for them, and re-layouts: 156 us -> 21 us
  waiting for transfers between devices: 443 us -> 336 us
  matrix products: 103 us -> 10.7 us
  Pallas kernels: 0 us -> 90.8 us
  other arithmetic: 83.1 us -> 12.1 us
  blocking collectives: 25.8 us -> 0 us
  starting transfers between devices: 34 us -> 21.8 us
    all_to_all x7 -> x4, waiting for transfers between devices: 443 us -> 70.2 us  [the longest x2 50.2 us: on_device(): lax.all_to_all(sent, GROUP, split_axis=0, concat_axis=0, tiled=True)]
    ppermute x0 -> x2, waiting for transfers between devices: none -> 213 us  [on_device(): partial = lax.ppermute(theirs, 'half', swap)]
    dot_general x17 -> x5, matrix products: 102 us -> 10.1 us  [the longest x1 6.2 us: on_device(): jnp.dot(pair_normed.reshape(rows * module_number, wide), coupling_logit_m...]
    pallas_call x0 -> x8, Pallas kernels: none -> 90.8 us  [the longest x1 25.5 us: front(): pl.pallas_call(front_kernel, grid=(rows // block,), in_specs=[pl.BlockSpe...]
    all_to_all x10 -> x0, local copies, waits for them, and re-layouts: 78.6 us -> none  [the longest x2 24.2 us: on_device(): lax.all_to_all(tri_right_all, 'row', split_axis=0, concat_axis=1, tiled=T...]
    all_gather x1 -> x2, waiting for transfers between devices: 0.02 us -> 52.5 us  [the longest x1 52.5 us: on_device(): gathered = lax.all_gather(alignment_embedding, AXES, axis=0, tiled=False)]
    convert_element_type x3 -> x4, local copies, waits for them, and re-layouts: 38.3 us -> 2.49 us  [the longest x3 2.04 us: on_device(): present_pairs = jnp.broadcast_to(jnp.transpose(present_rows.reshape(seqs,...]
    transpose x2 -> x0, other arithmetic: 35.5 us -> none  [on_device(): right_parts.append(jnp.transpose(tri_right, (2, 0, 1)))]
  transfers between devices with their start and end apart: 9 -> 9, of which waited for: 6 -> 5; matrix products, arithmetic and copies ran while one was open for 10% -> 5% of each run, Pallas kernels for 0% -> 9%
where the time goes in v1:
time: 510 us; the launch traced here: 508 us
  waiting for transfers between devices  336 us (66%)
  Pallas kernels  90.8 us (18%)
  starting transfers between devices  21.8 us (4%)
  local copies, waits for them, and re-layouts  21 us (4%)
  between operations  15.9 us (3%)
  other arithmetic  12.1 us (2%)
  matrix products  10.7 us (2%)
    ppermute x2, waiting for transfers between devices, on_device(): partial = lax.ppermute(theirs, 'half', swap)  213 us
    all_gather x1, waiting for transfers between devices, on_device(): gathered = lax.all_gather(alignment_embedding, AXES, axis=0, tiled=False)  52.5 us
    all_to_all x2, waiting for transfers between devices, on_device(): lax.all_to_all(sent, GROUP, split_axis=0, concat_axis=0, tiled=True)  50.2 us
    pallas_call x1, Pallas kernels, front(): pl.pallas_call(front_kernel, grid=(rows // block,), in_specs=[pl.BlockSpe...  25.5 us
    pallas_call x2, Pallas kernels, combine(): pl.pallas_call(functools.partial(combine_kernel, row_count=row_count, pos...  20.7 us
    all_to_all x2, waiting for transfers between devices, on_device(): lax.all_to_all(product, GROUP, split_axis=0, concat_axis=0, tiled=True)  20 us
    pallas_call x2, Pallas kernels, assemble(): pl.pallas_call(functools.partial(assemble_kernel, row_count=row_count, po...  18.6 us
    pallas_call x2, Pallas kernels, project(): pl.pallas_call(project_kernel, grid=(total // quads,), in_specs=[pl.Block...  15.1 us
  transfers between devices with their start and end apart: 9, of which 5 were waited for; matrix products, arithmetic and copies ran while one was open for 5% of the time, Pallas kernels for 9%

profile of v1, /device:TPU:0, one launch (start us, length us, event | category | flops | bytes accessed | tf_op | source)
XLA Modules:
  0.0 508.4 jit_solution(11645943054003466668)
XLA Ops:
  12.7 1.9 broadcast_in_dim.9
  14.6 1.4 convert_element_type.90.present_ref
  18.5 52.5 %all-gather.9.cloned.1.call-done = bf16[128,96,64]{1,2,0:T(8,128)(2,1)} async-done(((bf16[4,96,64]{1,2,0:T(8,128)(2,1)}), bf16[128,96,64]{1,2,0:T(8,128)(2,1)}) %all-gather.9.cloned.1.call-update) | async-done | bytes 1572880 | tf_op jit(solution)/shard_map/all_gather | solution.py:406
  71.0 1.0 constant_dynamic-slice_fusion.1
  72.8 1.2 dynamic-slice_convert_fusion
  74.0 1.1 copy.90
  75.1 1.2 bitcast_reduce_fusion
  76.4 1.9 fusion.6
  81.0 2.4 fusion.left_ref
  83.3 25.5 %front.1 = (bf16[192,96,128]{2,1,0:T(8,128)(2,1)}, bf16[192,96,128]{2,1,0:T(8,128)(2,1)}) custom-call(bf16[3072,32]{1,0:T(8,128)(2,1)} %fusion.left_ref, bf16[96,16,256]{2,1,0:T(8,128)(2,1)} %convert_element_type.90.present_ref, bf16[192,96,128]{2,1,0:T(8,128)(2,1)} %coup_ref.1, bf16[32,4096]{1,0:T(8,128)(2,1)} %reshape.189.weight_ref, ...), custom_call_target="tpu_custom_call" | custom-call | tf_op jit(solution)/shard_map/front/pallas_call | solution.py:126
  108.8 7.6 %project.3 = bf16[16,384,384]{2,1,0:T(8,128)(2,1)} custom-call(bf16[192,96,128]{2,1,0:T(8,128)(2,1)} %get-tuple-element.10.normed_ref.refs_3_, f32[48,1,384]{2,1,0:T(1,128)} %broadcast_in_dim.10.live_ref, bf16[256,128]{1,0:T(8,128)(2,1)} %bitcast.64), custom_call_target="tpu_custom_call" | custom-call | tf_op jit(solution)/shard_map/project/pallas_call | solution.py:165
  116.4 4.6 all-to-all-start.2
  121.6 7.5 %project.2 = bf16[16,384,384]{2,1,0:T(8,128)(2,1)} custom-call(bf16[192,96,128]{2,1,0:T(8,128)(2,1)} %get-tuple-element.10.normed_ref.refs_3_, f32[48,1,384]{2,1,0:T(1,128)} %broadcast_in_dim.10.live_ref, bf16[256,128]{1,0:T(8,128)(2,1)} %bitcast.65), custom_call_target="tpu_custom_call" | custom-call | tf_op jit(solution)/shard_map/project/pallas_call | solution.py:165
  129.1 50.2 %all-to-all-done.2.recv_ref = bf16[16,384,384]{2,1,0:T(8,128)(2,1)} async-done(((bf16[16,384,384]{2,1,0:T(8,128)(2,1)}), bf16[16,384,384]{2,1,0:T(8,128)(2,1)}, u32[]{:S(2)}, u32[]{:S(2)}) %all-to-all-start.2) | async-done | bytes 4718624 | tf_op jit(solution)/shard_map/all_to_all | solution.py:464
  179.3 5.7 %all-to-all-start = ((bf16[16,384,384]{2,1,0:T(8,128)(2,1)}), bf16[16,384,384]{2,1,0:T(8,128)(2,1)}, u32[]{:S(2)}, u32[]{:S(2)}) async-start(bf16[16,384,384]{2,1,0:T(8,128)(2,1)} %project.2), calls=%async_computation | async-start | bytes 9437184 | tf_op jit(solution)/shard_map/all_to_all | solution.py:464
  185.0 9.3 %assemble.3 = (bf16[4,768,384]{2,1,0:T(8,128)(2,1)}, bf16[4,384,384]{2,1,0:T(8,128)(2,1)}, bf16[4,768,384]{2,1,0:T(8,128)(2,1)}) custom-call(s32[1]{0:T(128)} %bitcast.16.half_ref, bf16[16,384,384]{2,1,0:T(8,128)(2,1)} %all-to-all-done.2.recv_ref), custom_call_target="tpu_custom_call" | custom-call | tf_op jit(solution)/shard_map/assemble/pallas_call | solution.py:255
  195.2 104.4 %collective-permute-done.1.recv_ref = bf16[4,768,384]{2,1,0:T(8,128)(2,1)S(1)} collective-permute-done((bf16[4,768,384]{2,1,0:T(8,128)(2,1)}, bf16[4,768,384]{2,1,0:T(8,128)(2,1)S(1)}, u32[]{:S(2)}, u32[]{:S(2)}) %collective-permute-start.1) | collective-permute-done | bytes 2359328 | tf_op jit(solution)/shard_map/ppermute | solution.py:466
  299.6 1.4 copy-done.3
  301.0 10.4 %combine.3 = bf16[16,192,384]{2,1,0:T(8,128)(2,1)} custom-call(bf16[4,768,384]{2,1,0:T(8,128)(2,1)} %get-tuple-element.14.left_ref, bf16[4,384,384]{2,1,0:T(8,128)(2,1)} %get-tuple-element.15.own_ref, bf16[4,768,384]{2,1,0:T(8,128)(2,1)} %copy-done.3), custom_call_target="tpu_custom_call" | custom-call | tf_op jit(solution)/shard_map/combine/pallas_call | solution.py:312
  311.4 4.1 all-to-all-start.3
  317.6 9.3 %assemble.2 = (bf16[4,768,384]{2,1,0:T(8,128)(2,1)}, bf16[4,384,384]{2,1,0:T(8,128)(2,1)}, bf16[4,768,384]{2,1,0:T(8,128)(2,1)}) custom-call(s32[1]{0:T(128)} %bitcast.16.half_ref, bf16[16,384,384]{2,1,0:T(8,128)(2,1)} %all-to-all-done.recv_ref), custom_call_target="tpu_custom_call" | custom-call | tf_op jit(solution)/shard_map/assemble/pallas_call | solution.py:255
  326.9 1.7 collective-permute-start
  328.6 6.2 %convolution_add_fusion = f32[192,96,8]{1,2,0:T(8,128)} fusion(bf16[192,96,128]{2,1,0:T(8,128)(2,1)} %get-tuple-element.10.normed_ref.refs_3_, f32[192]{0:T(256)S(1)} %get-tuple-element.18, bf16[128,8]{0,1:T(8,128)(2,1)S(1)} %copy-done.11), kind=kOutput, calls=%fused_computation.16 | convolution fusion | flops 37896192 | bytes 5311232 | tf_op jit(solution)/shard_map/dot_general | solution.py:477
  334.9 108.4 %collective-permute-done.recv_ref = bf16[4,768,384]{2,1,0:T(8,128)(2,1)} collective-permute-done((bf16[4,768,384]{2,1,0:T(8,128)(2,1)}, bf16[4,768,384]{2,1,0:T(8,128)(2,1)}, u32[]{:S(2)}, u32[]{:S(2)}) %collective-permute-start) | collective-permute-done | bytes 2359328 | tf_op jit(solution)/shard_map/ppermute | solution.py:466
  443.3 10.3 %combine.2 = bf16[16,192,384]{2,1,0:T(8,128)(2,1)} custom-call(bf16[4,768,384]{2,1,0:T(8,128)(2,1)} %get-tuple-element.11.left_ref, bf16[4,384,384]{2,1,0:T(8,128)(2,1)} %get-tuple-element.12.own_ref, bf16[4,768,384]{2,1,0:T(8,128)(2,1)} %collective-permute-done.recv_ref), custom_call_target="tpu_custom_call" | custom-call | tf_op jit(solution)/shard_map/combine/pallas_call | solution.py:312
  453.6 1.4 copy-done.2
  455.0 4.7 all-to-all-start.1
  460.4 2.6 copy.63
  462.9 2.9 reduce_max.9
  469.2 0.9 fusion.14
  470.0 20.0 %all-to-all-done.1.refs_0_ = bf16[16,192,384]{2,1,0:T(8,128)(2,1)} async-done(((bf16[16,192,384]{2,1,0:T(8,128)(2,1)}), bf16[16,192,384]{2,1,0:T(8,128)(2,1)}, u32[]{:S(2)}, u32[]{:S(2)}) %all-to-all-start.1) | async-done | bytes 2359328 | tf_op jit(solution)/shard_map/all_to_all | solution.py:468
  490.0 11.0 %finish.1 = bf16[192,96,128]{2,1,0:T(8,128)(2,1)} custom-call(bf16[16,192,384]{2,1,0:T(8,128)(2,1)} %all-to-all-done.1.refs_0_, bf16[16,192,384]{2,1,0:T(8,128)(2,1)} %copy-done.2, bf16[192,96,128]{2,1,0:T(8,128)(2,1)} %get-tuple-element.17.refs_2_, bf16[192,96,128]{2,1,0:T(8,128)(2,1)} %get-tuple-element.10.normed_ref.refs_3_, ...), custom_call_target="tpu_custom_call" | custom-call | tf_op jit(solution)/shard_map/finish/pallas_call | solution.py:359
  (90 shorter events, 18.1 us)
Async XLA Ops:
  8.0 460.9 %copy-start = (bf16[256,64]{0,1:T(8,128)(2,1)S(1)}, bf16[256,64]{0,1:T(8,128)(2,1)}, u32[]{:S(2)}) copy-start(bf16[256,64]{0,1:T(8,128)(2,1)} %param.17) | copy-start | bytes 98308
  8.0 63.0 %all-gather.9.cloned.1.call-start = ((), (), s32[]{:S(2)}) async-start(), calls=%async_computation.6 | async-start | bytes 2162688 | tf_op jit(solution)/shard_map/all_gather | solution.py:406
  11.0 5.0 copy-start.9
  11.9 5.7 %slice-start = ((bf16[128,640]{1,0:T(8,128)(2,1)}), bf16[128,512]{1,0:T(8,128)(2,1)S(1)}, s32[]{:S(2)}) async-start(bf16[128,640]{1,0:T(8,128)(2,1)} %param.18), calls=%async_computation.7 | async-start | bytes 262144 | tf_op jit(solution)/shard_map/slice | solution.py:456
  76.3 3.0 copy-start.10
  116.4 62.9 %all-to-all-start.2 = ((bf16[16,384,384]{2,1,0:T(8,128)(2,1)}), bf16[16,384,384]{2,1,0:T(8,128)(2,1)}, u32[]{:S(2)}, u32[]{:S(2)}) async-start(bf16[16,384,384]{2,1,0:T(8,128)(2,1)} %project.3), calls=%async_computation.2 | async-start | bytes 9437184 | tf_op jit(solution)/shard_map/all_to_all | solution.py:464
  179.3 132.1 %all-to-all-start = ((bf16[16,384,384]{2,1,0:T(8,128)(2,1)}), bf16[16,384,384]{2,1,0:T(8,128)(2,1)}, u32[]{:S(2)}, u32[]{:S(2)}) async-start(bf16[16,384,384]{2,1,0:T(8,128)(2,1)} %project.2), calls=%async_computation | async-start | bytes 9437184 | tf_op jit(solution)/shard_map/all_to_all | solution.py:464
  194.4 105.2 %collective-permute-start.1 = (bf16[4,768,384]{2,1,0:T(8,128)(2,1)}, bf16[4,768,384]{2,1,0:T(8,128)(2,1)S(1)}, u32[]{:S(2)}, u32[]{:S(2)}) collective-permute-start(bf16[4,768,384]{2,1,0:T(8,128)(2,1)} %get-tuple-element.16), channel_id=1, source_target_pairs={{0,4},{4,0},{1,5},{5,1},{2,6},{6,2},{3,7},{7,3},{8,12},{12,8},{9,1... | collective-permute-start | bytes 7077896 | tf_op jit(solution)/shard_map/ppermute | solution.py:466
  299.6 1.4 copy-start.3
  311.4 4.1 copy-start.7
  311.4 142.2 %all-to-all-start.3 = ((bf16[16,192,384]{2,1,0:T(8,128)(2,1)}), bf16[16,192,384]{2,1,0:T(8,128)(2,1)S(1)}, u32[]{:S(2)}, u32[]{:S(2)}) async-start(bf16[16,192,384]{2,1,0:T(8,128)(2,1)} %combine.3), calls=%async_computation.3 | async-start | bytes 4718592 | tf_op jit(solution)/shard_map/all_to_all | solution.py:468
  315.4 144.9 %all-gather.5.cloned.1.call-start = ((), (), s32[]{:S(2)}) async-start(), calls=%async_computation.4 | async-start | bytes 1769472 | tf_op jit(solution)/shard_map/all_gather | solution.py:485
  315.9 0.9 copy-start.5
  317.5 11.1 %copy-start.11 = (bf16[128,8]{0,1:T(8,128)(2,1)S(1)}, bf16[128,8]{0,1:T(8,128)(2,1)}, u32[]{:S(2)}) copy-start(bf16[128,8]{0,1:T(8,128)(2,1)} %param.16) | copy-start | bytes 6148
  317.6 145.4 %all-gather.7.cloned.1.call-start = ((), (), s32[]{:S(2)}) async-start(), calls=%async_computation.5 | async-start | bytes 3932160 | tf_op jit(solution)/shard_map/all_gather | solution.py:484
  326.9 116.4 %collective-permute-start = (bf16[4,768,384]{2,1,0:T(8,128)(2,1)}, bf16[4,768,384]{2,1,0:T(8,128)(2,1)}, u32[]{:S(2)}, u32[]{:S(2)}) collective-permute-start(bf16[4,768,384]{2,1,0:T(8,128)(2,1)} %get-tuple-element.13), channel_id=1, source_target_pairs={{0,4},{4,0},{1,5},{5,1},{2,6},{6,2},{3,7},{7,3},{8,12},{12,8},{9,1... | collective-permute-start | bytes 7077896 | tf_op jit(solution)/shard_map/ppermute | solution.py:466
  453.6 6.1 %copy-start.8 = (bf16[128,640]{1,0:T(8,128)(2,1)S(1)}, bf16[128,640]{1,0:T(8,128)(2,1)}, u32[]{:S(2)}) copy-start(bf16[128,640]{1,0:T(8,128)(2,1)} %param.18) | copy-start | bytes 491524
  453.6 1.4 copy-start.2
  455.0 35.0 %all-to-all-start.1 = ((bf16[16,192,384]{2,1,0:T(8,128)(2,1)}), bf16[16,192,384]{2,1,0:T(8,128)(2,1)}, u32[]{:S(2)}, u32[]{:S(2)}) async-start(bf16[16,192,384]{2,1,0:T(8,128)(2,1)} %combine.2), calls=%async_computation.1 | async-start | bytes 4718592 | tf_op jit(solution)/shard_map/all_to_all | solution.py:468
  462.9 2.9 copy-start.1
  466.6 1.4 copy-start.4
  468.0 1.1 copy-start.6
Sparse Core Ops, SparseCore 0:
  11.8 59.1 all-gather.8
Sparse Core Ops, SparseCore 1:
  317.6 50.2 all-gather.4
  369.6 42.3 all-gather.6

commit v2 on v1

--- a/solution.py
+++ b/solution.py
@@ -44,6 +44,10 @@
 def whole(shape):
     zeros = (0,) * len(shape)
     return pl.BlockSpec(shape, lambda *_: zeros, pipeline_mode=pl.Buffered(1))
+
+
+def anywhere(after):
+    return [pl.BlockSpec(memory_space=pl.ANY)] * len(after)
 
 
 def pack_rows(rows):
@@ -90,15 +94,41 @@
     return out
 
 
-def front_kernel(left_ref, present_ref, coup_ref, weight_ref, right_ref, pcol_ref, mid_ref, normed_ref, tmp_ref):
-    block = coup_ref.shape[0]
-    seqs = left_ref.shape[0] // block
-    wide = coup_ref.shape[2]
+def front_kernel(place_ref, *refs, row_count, col_count):
+    lefts, rights = refs[:col_count], refs[col_count : col_count + row_count]
+    refs = refs[col_count + row_count :]
+    present_ref, coup_ref, weight_ref, pcol_ref, mid_ref, normed_ref = refs[:6]
+    sides_ref, right_ref, tmp_ref = refs[6:]
+    block, cols, wide = coup_ref.shape
+    seq_each, _, width = lefts[0].shape
+    seqs = seq_each * row_count
+    per_row = col_count // row_count
+
+    @pl.when(pl.program_id(0) == 0)
+    def _():
+        for t, part in enumerate(lefts):
+            index = lax.rem(t + place_ref[1], col_count)
+            first = lax.rem(index, per_row) * (cols * seqs) + index // per_row * seq_each
+            for k in range(seq_each):
+                sides_ref[pl.ds(first + k, cols, stride=seqs), 0:width] = part[k].astype(F32)
+        right = jnp.zeros(right_ref.shape, F32)
+        feature = lax.broadcasted_iota(jnp.int32, (width, width * seqs), 0)
+        target = lax.broadcasted_iota(jnp.int32, (width, width * seqs), 1)
+        for t, part in enumerate(rights):
+            first = lax.rem(t + place_ref[0], row_count) * seq_each
+            for k in range(seq_each):
+                spread = (target == feature * seqs + (first + k)).astype(F32).astype(BF16)
+                right += jnp.dot(part[k], spread, preferred_element_type=F32)
+        right_ref[...] = right.astype(BF16)
+
+    span = block * seqs
+    start = pl.multiple_of(pl.program_id(0) * span, span)
+    left = sides_ref[pl.ds(start, span), 0:width].astype(BF16)
     features = weight_ref.shape[1] // wide
     step = 4
     for low in range(0, features, step):
         part = jnp.dot(
-            left_ref[...], weight_ref[:, low * wide : (low + step) * wide], preferred_element_type=F32
+            left, weight_ref[:, low * wide : (low + step) * wide], preferred_element_type=F32
         ).astype(BF16)
         for i in range(block):
             for d in range(step):
@@ -118,48 +148,60 @@
             normed_ref[i] = standardize_features(mid.astype(F32), 1).astype(BF16)
 
 
-def front(left_rows, present_pairs, coupling, w_tensor, right_cols, present_cols):
+def front(place, lefts, rights, present_pairs, coupling, w_tensor, present_cols):
     rows, cols, wide = coupling.shape
-    seqs = left_rows.shape[0] // rows
+    seqs, width = present_pairs.shape[1], lefts[0].shape[2]
     block = 8
     tile = pl.BlockSpec((block, cols, wide), lambda i: (i, 0, 0))
     return pl.pallas_call(
-        front_kernel,
+        functools.partial(front_kernel, row_count=len(rights), col_count=len(lefts)),
         grid=(rows // block,),
-        in_specs=[
-            pl.BlockSpec((block * seqs, left_rows.shape[1]), lambda i: (i, 0)),
+        in_specs=[pl.BlockSpec(memory_space=pltpu.SMEM)]
+        + [whole(part.shape) for part in lefts + rights]
+        + [
             pl.BlockSpec((block // 2, seqs, 2 * wide), lambda i: (i, 0, 0)),
             tile,
             whole(w_tensor.shape),
-            whole(right_cols.shape),
             whole(present_cols.shape),
         ],
         out_specs=[tile, tile],
         out_shape=[jax.ShapeDtypeStruct(coupling.shape, BF16)] * 2,
-        scratch_shapes=[pltpu.VMEM((block // 2, right_cols.shape[1], 2 * wide), BF16)],
+        scratch_shapes=[
+            pltpu.VMEM((rows * seqs, LANES), F32),
+            pltpu.VMEM((cols, width * seqs), BF16),
+            pltpu.VMEM((block // 2, width * seqs, 2 * wide), BF16),
+        ],
         compiler_params=params(),
         name="front",
-    )(left_rows, present_pairs, coupling, w_tensor, right_cols, present_cols)
+    )(place, *lefts, *rights, present_pairs, coupling, w_tensor, present_cols)
 
 
 def project_kernel(normed_ref, live_ref, weight_ref, out_ref, tmp_ref):
     quads = normed_ref.shape[0] // QUAD
-    dests = out_ref.shape[0]
-    each = out_ref.shape[1] // quads
+    dests, height, lanes = out_ref.shape
+    each = height // quads
     count = dests * each
     for m in range(quads):
         packed = pack_rows([normed_ref[QUAD * m + a] for a in range(QUAD)])
         both = lax.dot_general(weight_ref[...], packed, NT, preferred_element_type=F32)
         gated = sigmoid(both[:count]) * both[count:] * live_ref[m]
-        for dest in range(dests):
-            tmp_ref[dest, m * each : (m + 1) * each] = gated[dest * each : (dest + 1) * each]
-    out_ref[...] = tmp_ref[...].astype(BF16)
+        for k in range(each):
+            value = gated[k * dests : (k + 1) * dests]
+            for t in range(lanes // LANES):
+                tmp_ref[t, pl.ds(m * each + k, dests, stride=height), :] = value[
+                    :, t * LANES : (t + 1) * LANES
+                ]
+    for dest in range(dests):
+        for t in range(lanes // LANES):
+            out_ref[dest, :, t * LANES : (t + 1) * LANES] = tmp_ref[
+                t, dest * height : (dest + 1) * height
+            ].astype(BF16)
 
 
 def project(normed, live, weight, dests):
     rows, cols, wide = normed.shape
-    quads = 8
     each = weight.shape[0] // (2 * dests)
+    quads = max(8, 16 // each)
     lanes = QUAD * cols
     total = rows // QUAD
     return pl.pallas_call(
@@ -172,13 +214,14 @@
         ],
         out_specs=pl.BlockSpec((dests, quads * each, lanes), lambda i: (0, i, 0)),
         out_shape=jax.ShapeDtypeStruct((dests, total * each, lanes), BF16),
-        scratch_shapes=[pltpu.VMEM((dests, quads * each, lanes), F32)],
+        scratch_shapes=[pltpu.VMEM((lanes // LANES, dests * quads * each, LANES), F32)],
         compiler_params=params(),
         name="project",
     )(normed, live, weight)
 
 
-def assemble_kernel(half_ref, recv_ref, left_ref, own_ref, send_ref, flat_ref, right_ref, *, row_count, pos_count):
+def assemble_kernel(half_ref, recv_ref, *refs, row_count, pos_count):
+    left_ref, own_ref, send_ref, flat_ref, right_ref = refs[-5:]
     channel = pl.program_id(0)
     lanes = recv_ref.shape[2]
     unit = lanes // 12
@@ -245,7 +288,7 @@
         ).astype(BF16)
 
 
-def assemble(half, received, row_count, pos_count, cols):
+def assemble(half, received, after, row_count, pos_count, cols):
     sources, height, lanes = received.shape
     each = (2 * pos_count * cols) // (row_count * QUAD)
     stride = height // each
@@ -255,7 +298,7 @@
     return pl.pallas_call(
         functools.partial(assemble_kernel, row_count=row_count, pos_count=pos_count),
         grid=(channels,),
-        in_specs=[pl.BlockSpec(memory_space=pltpu.SMEM), whole(received.shape)],
+        in_specs=[pl.BlockSpec(memory_space=pltpu.SMEM), whole(received.shape)] + anywhere(after),
         out_specs=[
             pl.BlockSpec((1, rows, depth), lambda c: (c, 0, 0)),
             pl.BlockSpec((1, depth, depth), lambda c: (c, 0, 0)),
@@ -272,10 +315,11 @@
         ],
         compiler_params=params(),
         name="assemble",
-    )(half, received)
-
-
-def combine_kernel(left_ref, own_ref, recv_ref, out_ref, tmp_ref, *, row_count, pos_count):
+    )(half, received, *after)
+
+
+def combine_kernel(left_ref, own_ref, recv_ref, *refs, row_count, pos_count):
+    out_ref, tmp_ref = refs[-2:]
     channel = pl.program_id(0)
     channels = pl.num_programs(0)
     lanes = out_ref.shape[2]
@@ -305,7 +349,7 @@
                 out_ref[dest, :, t * LANES : (t + 1) * LANES] = tmp_ref[dest, t].astype(BF16)
 
 
-def combine(left, own, received, row_count, pos_count, cols):
+def combine(left, own, received, after, row_count, pos_count, cols):
     channels, rows, depth = left.shape
     each = rows // (row_count * QUAD)
     shape = (row_count * pos_count, each * channels, QUAD * cols)
@@ -316,31 +360,41 @@
             pl.BlockSpec((1, rows, depth), lambda c: (c, 0, 0)),
             pl.BlockSpec((1, depth, depth), lambda c: (c, 0, 0)),
             pl.BlockSpec((1, rows, depth), lambda c: (c, 0, 0)),
-        ],
+        ]
+        + anywhere(after),
         out_specs=whole(shape),
         out_shape=jax.ShapeDtypeStruct(shape, BF16),
         scratch_shapes=[pltpu.VMEM((shape[0], shape[2] // LANES, shape[1], LANES), F32)],
         compiler_params=params(),
         name="combine",
-    )(left, own, received)
+    )(left, own, received, *after)
 
 
 def finish_kernel(*refs, chunks):
     parts = refs[:chunks]
-    mid_ref, normed_ref, gate_ref, weight_ref, out_ref, tmp_ref = refs[chunks:]
+    mid_ref, normed_ref, gate_ref, weight_ref, out_ref = refs[chunks : chunks + 5]
+    flat = refs[chunks + 5 :]
     quads = mid_ref.shape[0] // QUAD
-    sources = parts[0].shape[0]
-    each = parts[0].shape[1] // quads
-    total = sources * each * chunks
-    for g, part in enumerate(parts):
+    sources, _, lanes = parts[0].shape
+    tiles = range(lanes // LANES)
+    for part, tmp in zip(parts, flat):
+        height = part.shape[1]
         for src in range(sources):
             value = part[src].astype(F32)
-            for m in range(quads):
-                start = m * total + (src * chunks + g) * each
-                tmp_ref[start : start + each] = value[m * each : (m + 1) * each]
+            for t in tiles:
+                tmp[t, src * height : (src + 1) * height] = value[:, t * LANES : (t + 1) * LANES]
     for m in range(quads):
-        product = tmp_ref[m * total : (m + 1) * total]
-        normed = standardize_features(product, 0).astype(BF16)
+        pieces = []
+        for part, tmp in zip(parts, flat):
+            height = part.shape[1]
+            each = height // quads
+            for k in range(each):
+                pieces.append(
+                    jnp.concatenate(
+                        [tmp[t, pl.ds(m * each + k, sources, stride=height), :] for t in tiles], axis=1
+                    )
+                )
+        normed = standardize_features(jnp.concatenate(pieces, axis=0), 0).astype(BF16)
         out = lax.dot_general(normed, weight_ref[...], TN, preferred_element_type=F32)
         for a, value in enumerate(unpack_rows(out)):
             i = QUAD * m + a
@@ -350,23 +404,31 @@
 
 def finish(parts, mid, normed, w_gate, w_final):
     rows, cols, wide = mid.shape
-    chunks = len(parts)
-    sources, height, lanes = parts[0].shape
+    sources, _, lanes = parts[0].shape
     total = rows // QUAD
-    each = height // total
-    quads = 8
+    heights = [part.shape[1] // total for part in parts]
+    quads = max(8, 16 // min(heights))
     tile = pl.BlockSpec((quads * QUAD, cols, wide), lambda i: (i, 0, 0))
     return pl.pallas_call(
-        functools.partial(finish_kernel, chunks=chunks),
+        functools.partial(finish_kernel, chunks=len(parts)),
         grid=(total // quads,),
-        in_specs=[pl.BlockSpec((sources, quads * each, lanes), lambda i: (0, i, 0))] * chunks
+        in_specs=[
+            pl.BlockSpec((sources, quads * each, lanes), lambda i: (0, i, 0)) for each in heights
+        ]
         + [tile, tile, whole(w_gate.shape), whole(w_final.shape)],
         out_specs=tile,
         out_shape=jax.ShapeDtypeStruct(mid.shape, BF16),
-        scratch_shapes=[pltpu.VMEM((quads * sources * each * chunks, lanes), F32)],
+        scratch_shapes=[
+            pltpu.VMEM((lanes // LANES, sources * quads * each, LANES), F32) for each in heights
+        ],
         compiler_params=params(),
         name="finish",
     )(*parts, mid, normed, w_gate, w_final)
+
+
+def chunk_sizes(channels):
+    each = min(2, channels)
+    return [each] * (channels // each)
 
 
 def on_device(
@@ -403,38 +465,46 @@
     live_rows = lax.dynamic_slice_in_dim(active_entries, row_start, rows, 0)
     live_cols = lax.dynamic_slice_in_dim(active_entries, col_start, module_number, 0)
 
-    gathered = lax.all_gather(alignment_embedding, AXES, axis=0, tiled=False)
-    gathered = gathered.reshape(row_count, col_count, seq_each, module_number, feature_count)
+    own_start = (row_index * seq_each, col_start)
+    present_own = lax.dynamic_slice(present_entries, own_start, (seq_each, module_number))
+    own_normed = standardize_features(alignment_embedding.astype(F32), 2).astype(BF16)
+    own_normed = own_normed.reshape(seq_each * module_number, feature_count)
+
+    def project_msa(matrix):
+        return jnp.dot(own_normed, matrix, preferred_element_type=F32).reshape(
+            seq_each, module_number, -1
+        )
+
+    own_sides = project_msa(alignment_matrix[:, : 2 * TENSOR_FEATURES])
+    own_sides = (own_sides * present_own[:, :, None]).astype(BF16)
+    own_left = own_sides[:, :, :TENSOR_FEATURES]
+    own_right = own_sides[:, :, TENSOR_FEATURES:]
     per_row = rows // module_number
-    row_part = lax.dynamic_slice_in_dim(gathered, row_index * per_row, per_row, 1)
-    row_part = jnp.transpose(row_part, (1, 3, 0, 2, 4)).reshape(rows * seqs, feature_count)
-    col_part = lax.dynamic_slice_in_dim(gathered, col_index, 1, 1)
-    col_part = col_part.reshape(seqs * module_number, feature_count)
-
-    def project_msa(part, matrix):
-        normed = standardize_features(part.astype(F32), 1).astype(BF16)
-        return jnp.dot(normed, matrix, preferred_element_type=F32)
-
-    left_rows = (
-        project_msa(row_part, alignment_matrix[:, :TENSOR_FEATURES])
-        * present_rows.T.reshape(rows * seqs, 1)
-    ).astype(BF16)
-    right = project_msa(col_part, alignment_matrix[:, TENSOR_FEATURES : 2 * TENSOR_FEATURES])
-    right = (right * present_cols.reshape(seqs * module_number, 1)).astype(BF16)
-    right_cols = jnp.transpose(
-        right.reshape(seqs, module_number, TENSOR_FEATURES), (1, 2, 0)
-    ).reshape(module_number, TENSOR_FEATURES * seqs)
+    lefts = []
+    for t in range(col_count):
+        pairs = []
+        for r in range(row_count):
+            for q in range(col_count):
+                to = (r * per_row + q % per_row - t) % col_count
+                pairs.append((r * col_count + q, q // per_row * col_count + to))
+        lefts.append(lax.ppermute(own_left, AXES, pairs))
+    rights = [own_right]
+    for t in range(1, row_count):
+        pairs = [(r, (r - t) % row_count) for r in range(row_count)]
+        rights.append(lax.ppermute(own_right, "row", pairs))
+
     present_pairs = jnp.broadcast_to(
         jnp.transpose(present_rows.reshape(seqs, rows // 2, 2), (1, 0, 2))[..., None],
         (rows // 2, seqs, 2, wide),
     ).reshape(rows // 2, seqs, 2 * wide).astype(BF16)
     w_tensor = tensor_final_matrix.reshape(TENSOR_FEATURES, TENSOR_FEATURES * wide)
     pair_mid, pair_normed = front(
-        left_rows,
+        jnp.stack([row_index, col_index]).astype(jnp.int32),
+        lefts,
+        rights,
         present_pairs,
         coupling_embedding,
         w_tensor,
-        right_cols,
         present_cols.T.astype(BF16),
     )
 
@@ -450,29 +520,28 @@
     )[:, None, :]
 
     devices = row_count * pos_count
-    channels = CTRI // devices
-    each = min(4, channels)
-    chunks = channels // each
-    w_kinds = trimul_matrices[:, : 4 * CTRI].T.reshape(2, 2, devices, chunks, each, wide)
+    sizes = chunk_sizes(CTRI // devices)
+    w_kinds = trimul_matrices[:, : 4 * CTRI].T.reshape(2, 2, devices, -1, wide)
     half_scalar = half.astype(jnp.int32).reshape(1)
-    pos_half = pos_count
     swap = [(0, 1), (1, 0)]
-    returned = []
-    for g in range(chunks):
-        weight = jnp.transpose(w_kinds[:, :, :, g], (1, 2, 0, 3, 4)).reshape(-1, wide)
-        sent = project(pair_normed, live_packed, weight, devices)
+    shape_of = (row_count, pos_count, module_number)
+    stages = []
+    start = 0
+    for g, each in enumerate(sizes):
+        weight = jnp.transpose(w_kinds[:, :, :, start : start + each], (1, 0, 3, 2, 4))
+        start += each
+        sent = project(pair_normed, live_packed, weight.reshape(-1, wide), devices)
         received = lax.all_to_all(sent, GROUP, split_axis=0, concat_axis=0, tiled=True)
-        left, own, theirs = assemble(half_scalar, received, row_count, pos_half, module_number)
-        partial = lax.ppermute(theirs, "half", swap)
-        product = combine(left, own, partial, row_count, pos_half, module_number)
-        returned.append(lax.all_to_all(product, GROUP, split_axis=0, concat_axis=0, tiled=True))
-
-    own_rows = project_msa(
-        alignment_embedding.reshape(seq_each * module_number, feature_count),
-        alignment_matrix[:, 2 * TENSOR_FEATURES :],
-    ).reshape(seq_each, module_number, -1)
-    values = own_rows[:, :, : MEAN_GROUPS * GROUP_FEATURES].astype(BF16)
-    sequence_gate = jax.nn.sigmoid(own_rows[:, :, MEAN_GROUPS * GROUP_FEATURES :])
+        after = (stages[g - 2][2],) if g >= 2 else ()
+        left, own, theirs = assemble(half_scalar, received, after, *shape_of)
+        stages.append((left, own, lax.ppermute(theirs, "half", swap), theirs))
+
+    values = project_msa(
+        alignment_matrix[:, 2 * TENSOR_FEATURES : 2 * TENSOR_FEATURES + MEAN_GROUPS * GROUP_FEATURES]
+    ).astype(BF16)
+    sequence_gate = jax.nn.sigmoid(
+        project_msa(alignment_matrix[:, 2 * TENSOR_FEATURES + MEAN_GROUPS * GROUP_FEATURES :])
+    )
     logits = (
         jnp.dot(
             pair_normed.reshape(rows * module_number, wide),
@@ -497,8 +566,14 @@
     ).reshape(seq_each, module_number, -1)
     alignment_updated_embedding = (alignment_embedding.astype(F32) + blended_update).astype(BF16)
 
+    returned = []
+    for g, (left, own, partial, _) in enumerate(stages):
+        after = (stages[g + 1][3],) if g + 1 < len(stages) else (alignment_updated_embedding,)
+        product = combine(left, own, partial, after, *shape_of)
+        returned.append(lax.all_to_all(product, GROUP, split_axis=0, concat_axis=0, tiled=True))
+    w_final = jnp.transpose(trimul_final_matrix.reshape(devices, -1, wide), (1, 0, 2))
     pair_output = finish(
-        returned, pair_mid, pair_normed, trimul_matrices[:, 4 * CTRI :], trimul_final_matrix
+        returned, pair_mid, pair_normed, trimul_matrices[:, 4 * CTRI :], w_final.reshape(-1, wide)
     )
     return (alignment_updated_embedding, pair_output)
 

time: 510 us -> 525 us (1.029)
  waiting for transfers between devices: 336 us -> 275 us
  starting transfers between devices: 21.8 us -> 73.1 us
  Pallas kernels: 90.8 us -> 121 us
    all_gather x1 -> x0, waiting for transfers between devices: 52.5 us -> none  [on_device(): gathered = lax.all_gather(alignment_embedding, AXES, axis=0, tiled=False)]
    ppermute x2 -> x15, starting transfers between devices: 2.58 us -> 36.8 us  [the longest x8 17.9 us: on_device(): lefts.append(lax.ppermute(own_left, AXES, pairs))]
    pallas_call x2 -> x4, Pallas kernels: 15.1 us -> 35.7 us  [project(): pl.pallas_call(project_kernel, grid=(total // quads,), in_specs=[pl.Block...]
    ppermute x2 -> x15, waiting for transfers between devices: 213 us -> 196 us  [the longest x4 196 us: on_device(): stages.append((left, own, lax.ppermute(theirs, 'half', swap), theirs))]
    all_to_all x2 -> x4, waiting for transfers between devices: 50.2 us -> 62.8 us  [on_device(): lax.all_to_all(sent, GROUP, split_axis=0, concat_axis=0, tiled=True)]
    all_to_all x2 -> x4, starting transfers between devices: 8.75 us -> 17.4 us  [on_device(): lax.all_to_all(product, GROUP, split_axis=0, concat_axis=0, tiled=True)]
    all_to_all x2 -> x4, starting transfers between devices: 10.3 us -> 18.6 us  [on_device(): lax.all_to_all(sent, GROUP, split_axis=0, concat_axis=0, tiled=True)]
    all_to_all x2 -> x4, waiting for transfers between devices: 20 us -> 15.7 us  [on_device(): lax.all_to_all(product, GROUP, split_axis=0, concat_axis=0, tiled=True)]
  transfers between devices with their start and end apart: 9 -> 25, of which waited for: 5 -> 8; matrix products, arithmetic and copies ran while one was open for 5% -> 5% of each run, Pallas kernels for 9% -> 14%
where the time goes in v2:
time: 525 us; the launch traced here: 522 us
  waiting for transfers between devices  275 us (52%)
  Pallas kernels  121 us (23%)
  starting transfers between devices  73.1 us (14%)
  local copies, waits for them, and re-layouts  22.8 us (4%)
  between operations  14.5 us (3%)
  matrix products  9.17 us (2%)
  other arithmetic  7.13 us (1%)
    ppermute x4, waiting for transfers between devices, on_device(): stages.append((left, own, lax.ppermute(theirs, 'half', swap), theirs))  196 us
    all_to_all x4, waiting for transfers between devices, on_device(): lax.all_to_all(sent, GROUP, split_axis=0, concat_axis=0, tiled=True)  62.8 us
    pallas_call x4, Pallas kernels, project(): pl.pallas_call(project_kernel, grid=(total // quads,), in_specs=[pl.Block...  35.7 us
    pallas_call x1, Pallas kernels, front(): pl.pallas_call(functools.partial(front_kernel, row_count=len(rights), col...  27.1 us
    pallas_call x4, Pallas kernels, combine(): pl.pallas_call(functools.partial(combine_kernel, row_count=row_count, pos...  24.6 us
    pallas_call x4, Pallas kernels, assemble(): pl.pallas_call(functools.partial(assemble_kernel, row_count=row_count, po...  21.5 us
    all_to_all x4, starting transfers between devices, on_device(): lax.all_to_all(sent, GROUP, split_axis=0, concat_axis=0, tiled=True)  18.6 us
    ppermute x8, starting transfers between devices, on_device(): lefts.append(lax.ppermute(own_left, AXES, pairs))  17.9 us
  transfers between devices with their start and end apart: 25, of which 8 were waited for; matrix products, arithmetic and copies ran while one was open for 5% of the time, Pallas kernels for 14%

profile of v2, /device:TPU:0, one launch (start us, length us, event | category | flops | bytes accessed | tf_op | source)
XLA Modules:
  0.0 522.2 jit_solution(13784566390537423643)
XLA Ops:
  11.8 7.6 %collective-permute-start.1 = (bf16[4,96,32]{2,1,0:T(8,128)(2,1)S(1)}, bf16[4,96,32]{2,1,0:T(8,128)(2,1)S(1)}, u32[]{:S(2)}, u32[]{:S(2)}) collective-permute-start(bf16[4,96,32]{2,1,0:T(8,128)(2,1)S(1)} %get-tuple-element.45), channel_id=1, source_target_pairs={{0,7},{1,0},{2,15},{3,8},{4,23},{5,16},{6,31},{7,24},{8,1},{9,2},{... | collective-permute-start | bytes 73736 | tf_op jit(solution)/shard_map/ppermute | solution.py:490
  30.6 4.7 collective-permute-start.8
  49.3 27.1 %front.1 = (bf16[192,96,128]{2,1,0:T(8,128)(2,1)}, bf16[192,96,128]{2,1,0:T(8,128)(2,1)}) custom-call(s32[2]{0:T(128)} %pad_add_fusion.place_ref, bf16[4,96,32]{2,1,0:T(8,128)(2,1)} %copy-done.14, bf16[4,96,32]{2,1,0:T(8,128)(2,1)} %copy-done.15, bf16[4,96,32]{2,1,0:T(8,128)(2,1)} %copy-done.16, bf16[4,96,32]{2,1,0:T(8,128)(2,1)} %copy-done.17, ...), custom_call_target="tpu_custom_call" | custom-call | tf_op jit(solution)/shard_map/front/pallas_call | solution.py:156
  76.5 8.9 %project.4 = bf16[16,192,384]{2,1,0:T(8,128)(2,1)} custom-call(bf16[192,96,128]{2,1,0:T(8,128)(2,1)} %get-tuple-element.16.normed_ref.refs_5_, f32[48,1,384]{2,1,0:T(1,128)} %broadcast_in_dim.10.live_ref, bf16[128,128]{1,0:T(8,128)(2,1)} %bitcast.59), custom_call_target="tpu_custom_call" | custom-call | tf_op jit(solution)/shard_map/project/pallas_call | solution.py:207
  89.7 8.9 %project.5 = bf16[16,192,384]{2,1,0:T(8,128)(2,1)} custom-call(bf16[192,96,128]{2,1,0:T(8,128)(2,1)} %get-tuple-element.16.normed_ref.refs_5_, f32[48,1,384]{2,1,0:T(1,128)} %broadcast_in_dim.10.live_ref, bf16[128,128]{1,0:T(8,128)(2,1)} %bitcast.62), custom_call_target="tpu_custom_call" | custom-call | tf_op jit(solution)/shard_map/project/pallas_call | solution.py:207
  98.6 20.9 %all-to-all-done.recv_ref = bf16[16,192,384]{2,1,0:T(8,128)(2,1)S(1)} async-done(((bf16[16,192,384]{2,1,0:T(8,128)(2,1)}), bf16[16,192,384]{2,1,0:T(8,128)(2,1)S(1)}, u32[]{:S(2)}, u32[]{:S(2)}) %all-to-all-start) | async-done | bytes 2359328 | tf_op jit(solution)/shard_map/all_to_all | solution.py:534
  121.0 4.9 all-to-all-start.1
  126.5 8.9 %project.6 = bf16[16,192,384]{2,1,0:T(8,128)(2,1)} custom-call(bf16[192,96,128]{2,1,0:T(8,128)(2,1)} %get-tuple-element.16.normed_ref.refs_5_, f32[48,1,384]{2,1,0:T(1,128)} %broadcast_in_dim.10.live_ref, bf16[128,128]{1,0:T(8,128)(2,1)} %bitcast.63), custom_call_target="tpu_custom_call" | custom-call | tf_op jit(solution)/shard_map/project/pallas_call | solution.py:207
  135.4 21.0 %all-to-all-done.1.recv_ref = bf16[16,192,384]{2,1,0:T(8,128)(2,1)S(1)} async-done(((bf16[16,192,384]{2,1,0:T(8,128)(2,1)}), bf16[16,192,384]{2,1,0:T(8,128)(2,1)S(1)}, u32[]{:S(2)}, u32[]{:S(2)}) %all-to-all-start.1) | async-done | bytes 2359328 | tf_op jit(solution)/shard_map/all_to_all | solution.py:534
  157.8 5.0 all-to-all-start.3
  163.4 8.9 %project.7 = bf16[16,192,384]{2,1,0:T(8,128)(2,1)} custom-call(bf16[192,96,128]{2,1,0:T(8,128)(2,1)} %get-tuple-element.16.normed_ref.refs_5_, f32[48,1,384]{2,1,0:T(1,128)} %broadcast_in_dim.10.live_ref, bf16[128,128]{1,0:T(8,128)(2,1)} %bitcast.61), custom_call_target="tpu_custom_call" | custom-call | tf_op jit(solution)/shard_map/project/pallas_call | solution.py:207
  172.3 20.9 %all-to-all-done.3.recv_ref = bf16[16,192,384]{2,1,0:T(8,128)(2,1)S(1)} async-done(((bf16[16,192,384]{2,1,0:T(8,128)(2,1)}), bf16[16,192,384]{2,1,0:T(8,128)(2,1)S(1)}, u32[]{:S(2)}, u32[]{:S(2)}) %all-to-all-start.3) | async-done | bytes 2359328 | tf_op jit(solution)/shard_map/all_to_all | solution.py:534
  194.6 5.0 all-to-all-start.5
  199.8 5.4 %assemble.4 = (bf16[2,768,384]{2,1,0:T(8,128)(2,1)}, bf16[2,384,384]{2,1,0:T(8,128)(2,1)}, bf16[2,768,384]{2,1,0:T(8,128)(2,1)}) custom-call(s32[1]{0:T(128)} %bitcast.14.half_ref, bf16[16,192,384]{2,1,0:T(8,128)(2,1)} %copy-done.5), custom_call_target="tpu_custom_call" | custom-call | tf_op jit(solution)/shard_map/assemble/pallas_call | solution.py:298
  207.3 5.4 %assemble.5 = (bf16[2,768,384]{2,1,0:T(8,128)(2,1)}, bf16[2,384,384]{2,1,0:T(8,128)(2,1)}, bf16[2,768,384]{2,1,0:T(8,128)(2,1)}) custom-call(s32[1]{0:T(128)} %bitcast.14.half_ref, bf16[16,192,384]{2,1,0:T(8,128)(2,1)} %copy-done.4), custom_call_target="tpu_custom_call" | custom-call | tf_op jit(solution)/shard_map/assemble/pallas_call | solution.py:298
  212.7 60.0 %collective-permute-done.11.recv_ref.refs_0_ = bf16[2,768,384]{2,1,0:T(8,128)(2,1)} collective-permute-done((bf16[2,768,384]{2,1,0:T(8,128)(2,1)}, bf16[2,768,384]{2,1,0:T(8,128)(2,1)}, u32[]{:S(2)}, u32[]{:S(2)}) %collective-permute-start.11) | collective-permute-done | bytes 1179680 | tf_op jit(solution)/shard_map/ppermute | solution.py:537
  272.7 6.1 %combine.4 = bf16[16,96,384]{2,1,0:T(8,128)(2,1)} custom-call(bf16[2,768,384]{2,1,0:T(8,128)(2,1)} %get-tuple-element.17.left_ref, bf16[2,384,384]{2,1,0:T(8,128)(2,1)} %get-tuple-element.18.own_ref, bf16[2,768,384]{2,1,0:T(8,128)(2,1)} %collective-permute-done.11.recv_ref.refs_0_, bf16[2,768,384]{2,1,0:T(8,128)(2,1)} %get-tuple-element.20.refs_0_), custom_call_target="tpu_custom_call" | custom-call | tf_op jit(solution)/shard_map/combine/pallas_call | solution.py:356
  278.9 4.4 all-to-all-start.2
  285.0 6.2 %convolution_add_fusion = f32[192,96,8]{1,2,0:T(8,128)} fusion(bf16[192,96,128]{2,1,0:T(8,128)(2,1)} %get-tuple-element.16.normed_ref.refs_5_, f32[192]{0:T(256)S(1)} %get-tuple-element.38, bf16[128,8]{0,1:T(8,128)(2,1)S(1)} %copy-done.27), kind=kOutput, calls=%fused_computation.7 | convolution fusion | flops 37896192 | bytes 5311232 | tf_op jit(solution)/shard_map/dot_general | solution.py:546
  291.2 5.4 %assemble.6 = (bf16[2,768,384]{2,1,0:T(8,128)(2,1)}, bf16[2,384,384]{2,1,0:T(8,128)(2,1)}, bf16[2,768,384]{2,1,0:T(8,128)(2,1)}) custom-call(s32[1]{0:T(128)} %bitcast.14.half_ref, bf16[16,192,384]{2,1,0:T(8,128)(2,1)} %copy-done.3, bf16[2,768,384]{2,1,0:T(8,128)(2,1)} %collective-permute-done.11.recv_ref.refs_0_), custom_call_target="tpu_custom_call" | custom-call | tf_op jit(solution)/shard_map/assemble/pallas_call | solution.py:298
  296.6 41.4 %collective-permute-done.12.recv_ref.refs_0_ = bf16[2,768,384]{2,1,0:T(8,128)(2,1)} collective-permute-done((bf16[2,768,384]{2,1,0:T(8,128)(2,1)}, bf16[2,768,384]{2,1,0:T(8,128)(2,1)}, u32[]{:S(2)}, u32[]{:S(2)}) %collective-permute-start.12) | collective-permute-done | bytes 1179680 | tf_op jit(solution)/shard_map/ppermute | solution.py:537
  338.0 6.2 %combine.5 = bf16[16,96,384]{2,1,0:T(8,128)(2,1)} custom-call(bf16[2,768,384]{2,1,0:T(8,128)(2,1)} %get-tuple-element.21.left_ref, bf16[2,384,384]{2,1,0:T(8,128)(2,1)} %get-tuple-element.22.own_ref, bf16[2,768,384]{2,1,0:T(8,128)(2,1)} %collective-permute-done.12.recv_ref.refs_0_, bf16[2,768,384]{2,1,0:T(8,128)(2,1)} %get-tuple-element.23.refs_0_), custom_call_target="tpu_custom_call" | custom-call | tf_op jit(solution)/shard_map/combine/pallas_call | solution.py:356
  344.2 4.2 all-to-all-start.4
  351.0 5.3 %assemble.7 = (bf16[2,768,384]{2,1,0:T(8,128)(2,1)}, bf16[2,384,384]{2,1,0:T(8,128)(2,1)}, bf16[2,768,384]{2,1,0:T(8,128)(2,1)}) custom-call(s32[1]{0:T(128)} %bitcast.14.half_ref, bf16[16,192,384]{2,1,0:T(8,128)(2,1)} %copy-done.2, bf16[2,768,384]{2,1,0:T(8,128)(2,1)} %collective-permute-done.12.recv_ref.refs_0_), custom_call_target="tpu_custom_call" | custom-call | tf_op jit(solution)/shard_map/assemble/pallas_call | solution.py:298
  356.3 46.8 %collective-permute-done.13.recv_ref = bf16[2,768,384]{2,1,0:T(8,128)(2,1)} collective-permute-done((bf16[2,768,384]{2,1,0:T(8,128)(2,1)S(1)}, bf16[2,768,384]{2,1,0:T(8,128)(2,1)}, u32[]{:S(2)}, u32[]{:S(2)}) %collective-permute-start.13) | collective-permute-done | bytes 1179680 | tf_op jit(solution)/shard_map/ppermute | solution.py:537
  403.1 6.2 %combine.6 = bf16[16,96,384]{2,1,0:T(8,128)(2,1)} custom-call(bf16[2,768,384]{2,1,0:T(8,128)(2,1)} %get-tuple-element.24.left_ref, bf16[2,384,384]{2,1,0:T(8,128)(2,1)} %get-tuple-element.25.own_ref, bf16[2,768,384]{2,1,0:T(8,128)(2,1)} %collective-permute-done.13.recv_ref, bf16[2,768,384]{2,1,0:T(8,128)(2,1)} %get-tuple-element.26.refs_0_), custom_call_target="tpu_custom_call" | custom-call | tf_op jit(solution)/shard_map/combine/pallas_call | solution.py:356
  409.2 4.6 all-to-all-start.6
  426.4 47.9 %collective-permute-done.14.recv_ref = bf16[2,768,384]{2,1,0:T(8,128)(2,1)} collective-permute-done((bf16[2,768,384]{2,1,0:T(8,128)(2,1)}, bf16[2,768,384]{2,1,0:T(8,128)(2,1)}, u32[]{:S(2)}, u32[]{:S(2)}) %collective-permute-start.14) | collective-permute-done | bytes 1179680 | tf_op jit(solution)/shard_map/ppermute | solution.py:537
  474.3 6.1 %combine.7 = bf16[16,96,384]{2,1,0:T(8,128)(2,1)} custom-call(bf16[2,768,384]{2,1,0:T(8,128)(2,1)} %get-tuple-element.27.left_ref, bf16[2,384,384]{2,1,0:T(8,128)(2,1)} %get-tuple-element.28.own_ref, bf16[2,768,384]{2,1,0:T(8,128)(2,1)} %collective-permute-done.14.recv_ref, bf16[4,96,64]{2,1,0:T(8,128)(2,1)} %fusion.17.refs_0_), custom_call_target="tpu_custom_call" | custom-call | tf_op jit(solution)/shard_map/combine/pallas_call | solution.py:356
  480.5 4.3 all-to-all-start.7
  486.7 15.7 %all-to-all-done.7.refs_3_ = bf16[16,96,384]{2,1,0:T(8,128)(2,1)S(1)} async-done(((bf16[16,96,384]{2,1,0:T(8,128)(2,1)}), bf16[16,96,384]{2,1,0:T(8,128)(2,1)S(1)}, u32[]{:S(2)}, u32[]{:S(2)}) %all-to-all-start.7) | async-done | bytes 1179680 | tf_op jit(solution)/shard_map/all_to_all | solution.py:573
  503.4 12.0 %finish.1 = bf16[192,96,128]{2,1,0:T(8,128)(2,1)} custom-call(bf16[16,96,384]{2,1,0:T(8,128)(2,1)} %all-to-all-done.2.refs_0_, bf16[16,96,384]{2,1,0:T(8,128)(2,1)} %copy-done.6, bf16[16,96,384]{2,1,0:T(8,128)(2,1)} %all-to-all-done.6.refs_2_, bf16[16,96,384]{2,1,0:T(8,128)(2,1)} %copy-done.7, bf16[192,96,128]{2,1,0:T(8,128)(2,1)} %get-tuple-element.29.refs_4_, ...), custom_call_target="tpu_custom_call" | custom-call | tf_op jit(solution)/shard_map/finish/pallas_call | solution.py:412
  (143 shorter events, 61.5 us)
Async XLA Ops:
  7.2 418.1 %copy-start = (bf16[256,64]{0,1:T(8,128)(2,1)S(1)}, bf16[256,64]{0,1:T(8,128)(2,1)}, u32[]{:S(2)}) copy-start(bf16[256,64]{0,1:T(8,128)(2,1)} %param.17) | copy-start | bytes 98308
  9.2 14.0 %slice-start = ((bf16[128,640]{1,0:T(8,128)(2,1)}), bf16[128,512]{1,0:T(8,128)(2,1)S(1)}, s32[]{:S(2)}) async-start(bf16[128,640]{1,0:T(8,128)(2,1)} %param.18), calls=%async_computation.10 | async-start | bytes 262144 | tf_op jit(solution)/shard_map/slice | solution.py:524
  11.1 33.3 %copy-start.12 = (bf16[4,96,32]{2,1,0:T(8,128)(2,1)}, bf16[4,96,32]{2,1,0:T(8,128)(2,1)S(1)}, u32[]{:S(2)}) copy-start(bf16[4,96,32]{2,1,0:T(8,128)(2,1)S(1)} %get-tuple-element.44.refs_8_) | copy-start | bytes 73732
  11.1 12.4 %collective-permute-start = (bf16[4,96,32]{2,1,0:T(8,128)(2,1)S(1)}, bf16[4,96,32]{2,1,0:T(8,128)(2,1)S(1)}, u32[]{:S(2)}, u32[]{:S(2)}) collective-permute-start(bf16[4,96,32]{2,1,0:T(8,128)(2,1)S(1)} %get-tuple-element.45), channel_id=1, source_target_pairs={{0,0},{1,1},{2,8},{3,9},{4,16},{5,17},{6,24},{7,25},{8,2},{9,3},{1... | collective-permute-start | bytes 73736 | tf_op jit(solution)/shard_map/ppermute | solution.py:490
  11.8 14.6 %collective-permute-start.1 = (bf16[4,96,32]{2,1,0:T(8,128)(2,1)S(1)}, bf16[4,96,32]{2,1,0:T(8,128)(2,1)S(1)}, u32[]{:S(2)}, u32[]{:S(2)}) collective-permute-start(bf16[4,96,32]{2,1,0:T(8,128)(2,1)S(1)} %get-tuple-element.45), channel_id=1, source_target_pairs={{0,7},{1,0},{2,15},{3,8},{4,23},{5,16},{6,31},{7,24},{8,1},{9,2},{... | collective-permute-start | bytes 73736 | tf_op jit(solution)/shard_map/ppermute | solution.py:490
  19.4 8.6 %collective-permute-start.2 = (bf16[4,96,32]{2,1,0:T(8,128)(2,1)S(1)}, bf16[4,96,32]{2,1,0:T(8,128)(2,1)S(1)}, u32[]{:S(2)}, u32[]{:S(2)}) collective-permute-start(bf16[4,96,32]{2,1,0:T(8,128)(2,1)S(1)} %get-tuple-element.45), channel_id=1, source_target_pairs={{0,6},{1,7},{2,14},{3,15},{4,22},{5,23},{6,30},{7,31},{8,0},{9,1},... | collective-permute-start | bytes 73736 | tf_op jit(solution)/shard_map/ppermute | solution.py:490
  20.3 10.3 %collective-permute-start.3 = (bf16[4,96,32]{2,1,0:T(8,128)(2,1)S(1)}, bf16[4,96,32]{2,1,0:T(8,128)(2,1)S(1)}, u32[]{:S(2)}, u32[]{:S(2)}) collective-permute-start(bf16[4,96,32]{2,1,0:T(8,128)(2,1)S(1)} %get-tuple-element.45), channel_id=1, source_target_pairs={{0,5},{1,6},{2,13},{3,14},{4,21},{5,22},{6,29},{7,30},{8,7},{9,0},... | collective-permute-start | bytes 73736 | tf_op jit(solution)/shard_map/ppermute | solution.py:490
  22.0 13.2 %collective-permute-start.4 = (bf16[4,96,32]{2,1,0:T(8,128)(2,1)S(1)}, bf16[4,96,32]{2,1,0:T(8,128)(2,1)S(1)}, u32[]{:S(2)}, u32[]{:S(2)}) collective-permute-start(bf16[4,96,32]{2,1,0:T(8,128)(2,1)S(1)} %get-tuple-element.45), channel_id=1, source_target_pairs={{0,4},{1,5},{2,12},{3,13},{4,20},{5,21},{6,28},{7,29},{8,6},{9,7},... | collective-permute-start | bytes 73736 | tf_op jit(solution)/shard_map/ppermute | solution.py:490
  23.5 22.3 %copy-start.14 = (bf16[4,96,32]{2,1,0:T(8,128)(2,1)}, bf16[4,96,32]{2,1,0:T(8,128)(2,1)S(1)}, u32[]{:S(2)}) copy-start(bf16[4,96,32]{2,1,0:T(8,128)(2,1)S(1)} %collective-permute-done.refs_0_) | copy-start | bytes 73732
  23.5 14.3 %collective-permute-start.5 = (bf16[4,96,32]{2,1,0:T(8,128)(2,1)S(1)}, bf16[4,96,32]{2,1,0:T(8,128)(2,1)S(1)}, u32[]{:S(2)}, u32[]{:S(2)}) collective-permute-start(bf16[4,96,32]{2,1,0:T(8,128)(2,1)S(1)} %get-tuple-element.45), channel_id=1, source_target_pairs={{0,3},{1,4},{2,11},{3,12},{4,19},{5,20},{6,27},{7,28},{8,5},{9,6},... | collective-permute-start | bytes 73736 | tf_op jit(solution)/shard_map/ppermute | solution.py:490
  26.4 19.4 %copy-start.15 = (bf16[4,96,32]{2,1,0:T(8,128)(2,1)}, bf16[4,96,32]{2,1,0:T(8,128)(2,1)S(1)}, u32[]{:S(2)}) copy-start(bf16[4,96,32]{2,1,0:T(8,128)(2,1)S(1)} %collective-permute-done.1.refs_1_) | copy-start | bytes 73732
  26.4 21.5 %collective-permute-start.6 = (bf16[4,96,32]{2,1,0:T(8,128)(2,1)S(1)}, bf16[4,96,32]{2,1,0:T(8,128)(2,1)S(1)}, u32[]{:S(2)}, u32[]{:S(2)}) collective-permute-start(bf16[4,96,32]{2,1,0:T(8,128)(2,1)S(1)} %get-tuple-element.45), channel_id=1, source_target_pairs={{0,2},{1,3},{2,10},{3,11},{4,18},{5,19},{6,26},{7,27},{8,4},{9,5},... | collective-permute-start | bytes 73736 | tf_op jit(solution)/shard_map/ppermute | solution.py:490
  28.0 17.8 %copy-start.16 = (bf16[4,96,32]{2,1,0:T(8,128)(2,1)}, bf16[4,96,32]{2,1,0:T(8,128)(2,1)S(1)}, u32[]{:S(2)}) copy-start(bf16[4,96,32]{2,1,0:T(8,128)(2,1)S(1)} %collective-permute-done.2.refs_2_) | copy-start | bytes 73732
  28.0 20.0 %collective-permute-start.7 = (bf16[4,96,32]{2,1,0:T(8,128)(2,1)S(1)}, bf16[4,96,32]{2,1,0:T(8,128)(2,1)S(1)}, u32[]{:S(2)}, u32[]{:S(2)}) collective-permute-start(bf16[4,96,32]{2,1,0:T(8,128)(2,1)S(1)} %get-tuple-element.45), channel_id=1, source_target_pairs={{0,1},{1,2},{2,9},{3,10},{4,17},{5,18},{6,25},{7,26},{8,3},{9,4},{... | collective-permute-start | bytes 73736 | tf_op jit(solution)/shard_map/ppermute | solution.py:490
  30.6 15.2 %copy-start.17 = (bf16[4,96,32]{2,1,0:T(8,128)(2,1)}, bf16[4,96,32]{2,1,0:T(8,128)(2,1)S(1)}, u32[]{:S(2)}) copy-start(bf16[4,96,32]{2,1,0:T(8,128)(2,1)S(1)} %collective-permute-done.3.refs_3_) | copy-start | bytes 73732
  30.6 17.4 %collective-permute-start.8 = (bf16[4,96,32]{2,1,0:T(8,128)(2,1)S(1)}, bf16[4,96,32]{2,1,0:T(8,128)(2,1)S(1)}, u32[]{:S(2)}, u32[]{:S(2)}) collective-permute-start(bf16[4,96,32]{2,1,0:T(8,128)(2,1)S(1)} %get-tuple-element.44.refs_8_), channel_id=1, source_target_pairs={{0,24},{8,0},{16,8},{24,16},{1,25},{9,1},{17,9},{25,17},{2,26},{10... | collective-permute-start | bytes 73736 | tf_op jit(solution)/shard_map/ppermute | solution.py:494
  35.2 12.8 %collective-permute-start.9 = (bf16[4,96,32]{2,1,0:T(8,128)(2,1)S(1)}, bf16[4,96,32]{2,1,0:T(8,128)(2,1)S(1)}, u32[]{:S(2)}, u32[]{:S(2)}) collective-permute-start(bf16[4,96,32]{2,1,0:T(8,128)(2,1)S(1)} %get-tuple-element.44.refs_8_), channel_id=1, source_target_pairs={{0,16},{8,24},{16,0},{24,8},{1,17},{9,25},{17,1},{25,9},{2,18},{10... | collective-permute-start | bytes 73736 | tf_op jit(solution)/shard_map/ppermute | solution.py:494
  37.8 10.2 %collective-permute-start.10 = (bf16[4,96,32]{2,1,0:T(8,128)(2,1)S(1)}, bf16[4,96,32]{2,1,0:T(8,128)(2,1)S(1)}, u32[]{:S(2)}, u32[]{:S(2)}) collective-permute-start(bf16[4,96,32]{2,1,0:T(8,128)(2,1)S(1)} %get-tuple-element.44.refs_8_), channel_id=1, source_target_pairs={{0,8},{8,16},{16,24},{24,0},{1,9},{9,17},{17,25},{25,1},{2,10},{10... | collective-permute-start | bytes 73736 | tf_op jit(solution)/shard_map/ppermute | solution.py:494
  85.3 34.2 %all-to-all-start = ((bf16[16,192,384]{2,1,0:T(8,128)(2,1)}), bf16[16,192,384]{2,1,0:T(8,128)(2,1)S(1)}, u32[]{:S(2)}, u32[]{:S(2)}) async-start(bf16[16,192,384]{2,1,0:T(8,128)(2,1)} %project.4), calls=%async_computation | async-start | bytes 4718592 | tf_op jit(solution)/shard_map/all_to_all | solution.py:534
  121.0 35.4 %all-to-all-start.1 = ((bf16[16,192,384]{2,1,0:T(8,128)(2,1)}), bf16[16,192,384]{2,1,0:T(8,128)(2,1)S(1)}, u32[]{:S(2)}, u32[]{:S(2)}) async-start(bf16[16,192,384]{2,1,0:T(8,128)(2,1)} %project.5), calls=%async_computation.1 | async-start | bytes 4718592 | tf_op jit(solution)/shard_map/all_to_all | solution.py:534
  157.8 35.5 %all-to-all-start.3 = ((bf16[16,192,384]{2,1,0:T(8,128)(2,1)}), bf16[16,192,384]{2,1,0:T(8,128)(2,1)S(1)}, u32[]{:S(2)}, u32[]{:S(2)}) async-start(bf16[16,192,384]{2,1,0:T(8,128)(2,1)} %project.6), calls=%async_computation.3 | async-start | bytes 4718592 | tf_op jit(solution)/shard_map/all_to_all | solution.py:534
  194.6 84.2 %all-to-all-start.5 = ((bf16[16,192,384]{2,1,0:T(8,128)(2,1)}), bf16[16,192,384]{2,1,0:T(8,128)(2,1)S(1)}, u32[]{:S(2)}, u32[]{:S(2)}) async-start(bf16[16,192,384]{2,1,0:T(8,128)(2,1)} %project.7), calls=%async_computation.5 | async-start | bytes 4718592 | tf_op jit(solution)/shard_map/all_to_all | solution.py:534
  199.6 214.2 %all-gather.3.cloned.1.call-start = ((), (), s32[]{:S(2)}) async-start(), calls=%async_computation.8 | async-start | bytes 1769472 | tf_op jit(solution)/shard_map/all_gather | solution.py:554
  205.2 67.5 %collective-permute-start.11 = (bf16[2,768,384]{2,1,0:T(8,128)(2,1)}, bf16[2,768,384]{2,1,0:T(8,128)(2,1)}, u32[]{:S(2)}, u32[]{:S(2)}) collective-permute-start(bf16[2,768,384]{2,1,0:T(8,128)(2,1)} %get-tuple-element.19), channel_id=1, source_target_pairs={{0,4},{4,0},{1,5},{5,1},{2,6},{6,2},{3,7},{7,3},{8,12},{12,8},{9,1... | collective-permute-start | bytes 3538952 | tf_op jit(solution)/shard_map/ppermute | solution.py:537
  278.9 65.3 %all-to-all-start.2 = ((bf16[16,96,384]{2,1,0:T(8,128)(2,1)}), bf16[16,96,384]{2,1,0:T(8,128)(2,1)}, u32[]{:S(2)}, u32[]{:S(2)}) async-start(bf16[16,96,384]{2,1,0:T(8,128)(2,1)} %combine.4), calls=%async_computation.2 | async-start | bytes 2359296 | tf_op jit(solution)/shard_map/all_to_all | solution.py:573
  283.3 133.2 %all-gather.5.cloned.1.call-start = ((), (), s32[]{:S(2)}) async-start(), calls=%async_computation.9 | async-start | bytes 3932160 | tf_op jit(solution)/shard_map/all_gather | solution.py:553
  283.3 54.7 %collective-permute-start.12 = (bf16[2,768,384]{2,1,0:T(8,128)(2,1)}, bf16[2,768,384]{2,1,0:T(8,128)(2,1)}, u32[]{:S(2)}, u32[]{:S(2)}) collective-permute-start(bf16[2,768,384]{2,1,0:T(8,128)(2,1)} %get-tuple-element.20.refs_0_), channel_id=1, source_target_pairs={{0,4},{4,0},{1,5},{5,1},{2,6},{6,2},{3,7},{7,3},{8,12},{12,8},{9,1... | collective-permute-start | bytes 3538952 | tf_op jit(solution)/shard_map/ppermute | solution.py:537
  344.2 65.0 %all-to-all-start.4 = ((bf16[16,96,384]{2,1,0:T(8,128)(2,1)}), bf16[16,96,384]{2,1,0:T(8,128)(2,1)S(1)}, u32[]{:S(2)}, u32[]{:S(2)}) async-start(bf16[16,96,384]{2,1,0:T(8,128)(2,1)} %combine.5), calls=%async_computation.4 | async-start | bytes 2359296 | tf_op jit(solution)/shard_map/all_to_all | solution.py:573
  348.4 54.7 %collective-permute-start.13 = (bf16[2,768,384]{2,1,0:T(8,128)(2,1)S(1)}, bf16[2,768,384]{2,1,0:T(8,128)(2,1)}, u32[]{:S(2)}, u32[]{:S(2)}) collective-permute-start(bf16[2,768,384]{2,1,0:T(8,128)(2,1)S(1)} %copy-done.9), channel_id=1, source_target_pairs={{0,4},{4,0},{1,5},{5,1},{2,6},{6,2},{3,7},{7,3},{8,12},{12,8},{9,1... | collective-permute-start | bytes 3538952 | tf_op jit(solution)/shard_map/ppermute | solution.py:537
  409.2 71.3 %all-to-all-start.6 = ((bf16[16,96,384]{2,1,0:T(8,128)(2,1)}), bf16[16,96,384]{2,1,0:T(8,128)(2,1)}, u32[]{:S(2)}, u32[]{:S(2)}) async-start(bf16[16,96,384]{2,1,0:T(8,128)(2,1)} %combine.6), calls=%async_computation.6 | async-start | bytes 2359296 | tf_op jit(solution)/shard_map/all_to_all | solution.py:573
  419.3 55.0 %collective-permute-start.14 = (bf16[2,768,384]{2,1,0:T(8,128)(2,1)}, bf16[2,768,384]{2,1,0:T(8,128)(2,1)}, u32[]{:S(2)}, u32[]{:S(2)}) collective-permute-start(bf16[2,768,384]{2,1,0:T(8,128)(2,1)} %get-tuple-element.26.refs_0_), channel_id=1, source_target_pairs={{0,4},{4,0},{1,5},{5,1},{2,6},{6,2},{3,7},{7,3},{8,12},{12,8},{9,1... | collective-permute-start | bytes 3538952 | tf_op jit(solution)/shard_map/ppermute | solution.py:537
  480.5 21.9 %all-to-all-start.7 = ((bf16[16,96,384]{2,1,0:T(8,128)(2,1)}), bf16[16,96,384]{2,1,0:T(8,128)(2,1)S(1)}, u32[]{:S(2)}, u32[]{:S(2)}) async-start(bf16[16,96,384]{2,1,0:T(8,128)(2,1)} %combine.7), calls=%async_computation.7 | async-start | bytes 2359296 | tf_op jit(solution)/shard_map/all_to_all | solution.py:573
  (22 other events, 86.3 us)
Sparse Core Ops, SparseCore 0:
  207.5 63.1 all-gather.2
  291.4 47.2 all-gather.4

commit v3 on v2

--- a/solution.py
+++ b/solution.py
@@ -16,7 +16,7 @@
 MASK_PENALTY = 10000.0
 QUAD = 4
 LANES = 128
-VMEM_LIMIT = 60 * 1024 * 1024
+MIB = 1024 * 1024
 AXES = ("row", "half", "pos")
 GROUP = ("row", "pos")
 F32 = jnp.float32
@@ -35,10 +35,14 @@
     return 0.5 * jnp.tanh(0.5 * x) + 0.5
 
 
-def params(grid_dims=1):
+def params(need):
+    limit = min(need + 12 * MIB, 60 * MIB)
     return pltpu.CompilerParams(
-        vmem_limit_bytes=VMEM_LIMIT, dimension_semantics=("arbitrary",) * grid_dims
-    )
+        vmem_limit_bytes=limit, dimension_semantics=("arbitrary",)
+    )
+
+
+LIGHT = pl.CostEstimate(flops=1000, bytes_accessed=1000, transcendentals=0)
 
 
 def whole(shape):
@@ -97,7 +101,7 @@
 def front_kernel(place_ref, *refs, row_count, col_count):
     lefts, rights = refs[:col_count], refs[col_count : col_count + row_count]
     refs = refs[col_count + row_count :]
-    present_ref, coup_ref, weight_ref, pcol_ref, mid_ref, normed_ref = refs[:6]
+    prow_ref, coup_ref, weight_ref, pcol_ref, mid_ref, normed_ref = refs[:6]
     sides_ref, right_ref, tmp_ref = refs[6:]
     block, cols, wide = coup_ref.shape
     seq_each, _, width = lefts[0].shape
@@ -137,9 +141,17 @@
                     (low + d) * seqs : (low + d + 1) * seqs,
                     (i % 2) * wide : (i % 2 + 1) * wide,
                 ] = part[i * seqs : (i + 1) * seqs, d * wide : (d + 1) * wide]
+    row_lane = lax.broadcasted_iota(jnp.int32, prow_ref.shape, 1)
     for pair in range(block // 2):
         update = jnp.dot(right_ref[...], tmp_ref[pair], preferred_element_type=F32)
-        count = jnp.dot(pcol_ref[...], present_ref[pair], preferred_element_type=F32)
+        here = pl.program_id(0) * block + 2 * pair
+        wanted = [jnp.where(row_lane == here + e, prow_ref[...], 0.0) for e in range(2)]
+        wanted = [
+            jnp.broadcast_to(jnp.sum(w, axis=1, keepdims=True), (seqs, wide)) for w in wanted
+        ]
+        count = jnp.dot(
+            pcol_ref[...], jnp.concatenate(wanted, axis=1).astype(BF16), preferred_element_type=F32
+        )
         update = update / jnp.maximum(count, 1.0)
         for e in range(2):
             i = 2 * pair + e
@@ -148,9 +160,9 @@
             normed_ref[i] = standardize_features(mid.astype(F32), 1).astype(BF16)
 
 
-def front(place, lefts, rights, present_pairs, coupling, w_tensor, present_cols):
+def front(place, lefts, rights, present_rows, coupling, w_tensor, present_cols):
     rows, cols, wide = coupling.shape
-    seqs, width = present_pairs.shape[1], lefts[0].shape[2]
+    seqs, width = present_rows.shape[0], lefts[0].shape[2]
     block = 8
     tile = pl.BlockSpec((block, cols, wide), lambda i: (i, 0, 0))
     return pl.pallas_call(
@@ -159,7 +171,7 @@
         in_specs=[pl.BlockSpec(memory_space=pltpu.SMEM)]
         + [whole(part.shape) for part in lefts + rights]
         + [
-            pl.BlockSpec((block // 2, seqs, 2 * wide), lambda i: (i, 0, 0)),
+            whole(present_rows.shape),
             tile,
             whole(w_tensor.shape),
             whole(present_cols.shape),
@@ -171,34 +183,60 @@
             pltpu.VMEM((cols, width * seqs), BF16),
             pltpu.VMEM((block // 2, width * seqs, 2 * wide), BF16),
         ],
-        compiler_params=params(),
+        compiler_params=params(4 * rows * seqs * LANES + 16 * MIB),
+        cost_estimate=LIGHT,
         name="front",
-    )(place, *lefts, *rights, present_pairs, coupling, w_tensor, present_cols)
-
-
-def project_kernel(normed_ref, live_ref, weight_ref, out_ref, tmp_ref):
+    )(place, *lefts, *rights, present_rows, coupling, w_tensor, present_cols)
+
+
+def exchange_rows(values):
+    values = list(values)
+    count = len(values)
+    step = count // 2
+    row = lax.broadcasted_iota(jnp.int32, values[0].shape, 0)
+    size = values[0].shape[0]
+    while step:
+        width = 8 // count * step
+        low = (row // width) % 2 == 0
+        for m in range(count):
+            if m & step == 0:
+                one, two = values[m], values[m + step]
+                values[m] = jnp.where(low, one, pltpu.roll(two, width, 0))
+                values[m + step] = jnp.where(low, pltpu.roll(one, size - width, 0), two)
+        step //= 2
+    return values
+
+
+def project_kernel(live_ref, normed_ref, cols_ref, weight_ref, *refs):
+    out_ref, tmp_ref = refs[-2:]
     quads = normed_ref.shape[0] // QUAD
     dests, height, lanes = out_ref.shape
     each = height // quads
     count = dests * each
-    for m in range(quads):
-        packed = pack_rows([normed_ref[QUAD * m + a] for a in range(QUAD)])
-        both = lax.dot_general(weight_ref[...], packed, NT, preferred_element_type=F32)
-        gated = sigmoid(both[:count]) * both[count:] * live_ref[m]
-        for k in range(each):
-            value = gated[k * dests : (k + 1) * dests]
-            for t in range(lanes // LANES):
-                tmp_ref[t, pl.ds(m * each + k, dests, stride=height), :] = value[
-                    :, t * LANES : (t + 1) * LANES
+    unit = lanes // 12
+    lane = lax.broadcasted_iota(jnp.int32, (1, lanes), 1)
+    place = jnp.where(lane < 8 * unit, lane // (2 * unit), (lane - 8 * unit) // unit)
+    group = max(1, 8 // each)
+    for first in range(0, quads, group):
+        values = []
+        for m in range(first, first + group):
+            packed = pack_rows([normed_ref[QUAD * m + a] for a in range(QUAD)])
+            both = lax.dot_general(weight_ref[...], packed, NT, preferred_element_type=F32)
+            row = (pl.program_id(0) * quads + m) * QUAD
+            live = cols_ref[...]
+            for a in range(QUAD):
+                live = jnp.where(place == a, live * live_ref[row + a], live)
+            values.append(sigmoid(both[:count]) * both[count:] * live)
+        for b, value in enumerate(exchange_rows(values)):
+            size = each * group
+            for v in range(count // size):
+                tmp_ref[v * group + b, first * each : first * each + size] = value[
+                    v * size : (v + 1) * size
                 ]
-    for dest in range(dests):
-        for t in range(lanes // LANES):
-            out_ref[dest, :, t * LANES : (t + 1) * LANES] = tmp_ref[
-                t, dest * height : (dest + 1) * height
-            ].astype(BF16)
-
-
-def project(normed, live, weight, dests):
+    out_ref[...] = tmp_ref[...].astype(BF16)
+
+
+def project(live_rows, normed, live_cols, weight, after, dests):
     rows, cols, wide = normed.shape
     each = weight.shape[0] // (2 * dests)
     quads = max(8, 16 // each)
@@ -208,16 +246,19 @@
         project_kernel,
         grid=(total // quads,),
         in_specs=[
+            pl.BlockSpec(memory_space=pltpu.SMEM),
             pl.BlockSpec((quads * QUAD, cols, wide), lambda i: (i, 0, 0)),
-            pl.BlockSpec((quads, 1, lanes), lambda i: (i, 0, 0)),
+            whole(live_cols.shape),
             whole(weight.shape),
-        ],
+        ]
+        + anywhere(after),
         out_specs=pl.BlockSpec((dests, quads * each, lanes), lambda i: (0, i, 0)),
         out_shape=jax.ShapeDtypeStruct((dests, total * each, lanes), BF16),
-        scratch_shapes=[pltpu.VMEM((lanes // LANES, dests * quads * each, LANES), F32)],
-        compiler_params=params(),
+        scratch_shapes=[pltpu.VMEM((dests, quads * each, lanes), F32)],
+        compiler_params=params(8 * dests * quads * each * lanes + 2 * MIB),
+        cost_estimate=LIGHT,
         name="project",
-    )(normed, live, weight)
+    )(live_rows, normed, live_cols, weight, *after)
 
 
 def assemble_kernel(half_ref, recv_ref, *refs, row_count, pos_count):
@@ -313,7 +354,10 @@
             pltpu.VMEM((sources, lanes // LANES, height, LANES), F32),
             pltpu.VMEM((depth // LANES, rows, LANES), F32),
         ],
-        compiler_params=params(),
+        compiler_params=params(
+            6 * received.size + 4 * rows * depth + 4 * (2 * rows + depth) * depth
+        ),
+        cost_estimate=LIGHT,
         name="assemble",
     )(half, received, *after)
 
@@ -365,7 +409,10 @@
         out_specs=whole(shape),
         out_shape=jax.ShapeDtypeStruct(shape, BF16),
         scratch_shapes=[pltpu.VMEM((shape[0], shape[2] // LANES, shape[1], LANES), F32)],
-        compiler_params=params(),
+        compiler_params=params(
+            4 * (2 * rows + depth) * depth + 6 * shape[0] * shape[1] * shape[2]
+        ),
+        cost_estimate=LIGHT,
         name="combine",
     )(left, own, received, *after)
 
@@ -421,7 +468,10 @@
         scratch_shapes=[
             pltpu.VMEM((lanes // LANES, sources * quads * each, LANES), F32) for each in heights
         ],
-        compiler_params=params(),
+        compiler_params=params(
+            8 * sources * quads * sum(heights) * lanes + 12 * quads * QUAD * cols * wide
+        ),
+        cost_estimate=LIGHT,
         name="finish",
     )(*parts, mid, normed, w_gate, w_final)
 
@@ -493,31 +543,21 @@
         pairs = [(r, (r - t) % row_count) for r in range(row_count)]
         rights.append(lax.ppermute(own_right, "row", pairs))
 
-    present_pairs = jnp.broadcast_to(
-        jnp.transpose(present_rows.reshape(seqs, rows // 2, 2), (1, 0, 2))[..., None],
-        (rows // 2, seqs, 2, wide),
-    ).reshape(rows // 2, seqs, 2 * wide).astype(BF16)
     w_tensor = tensor_final_matrix.reshape(TENSOR_FEATURES, TENSOR_FEATURES * wide)
     pair_mid, pair_normed = front(
         jnp.stack([row_index, col_index]).astype(jnp.int32),
         lefts,
         rights,
-        present_pairs,
+        present_rows,
         coupling_embedding,
         w_tensor,
         present_cols.T.astype(BF16),
     )
 
     unit = module_number // 3
-    pair_live = live_rows[:, None] * live_cols[None, :]
-    quad_live = pair_live.reshape(rows // QUAD, QUAD, module_number)
     live_packed = jnp.concatenate(
-        [
-            quad_live[:, :, : 2 * unit].reshape(rows // QUAD, -1),
-            quad_live[:, :, 2 * unit :].reshape(rows // QUAD, -1),
-        ],
-        axis=1,
-    )[:, None, :]
+        [live_cols[: 2 * unit]] * QUAD + [live_cols[2 * unit :]] * QUAD
+    )[None]
 
     devices = row_count * pos_count
     sizes = chunk_sizes(CTRI // devices)
@@ -528,9 +568,12 @@
     stages = []
     start = 0
     for g, each in enumerate(sizes):
-        weight = jnp.transpose(w_kinds[:, :, :, start : start + each], (1, 0, 3, 2, 4))
+        weight = jnp.transpose(w_kinds[:, :, :, start : start + each], (1, 2, 0, 3, 4))
         start += each
-        sent = project(pair_normed, live_packed, weight.reshape(-1, wide), devices)
+        after = (stages[g - 2][3],) if g >= 2 else ()
+        sent = project(
+            live_rows, pair_normed, live_packed, weight.reshape(-1, wide), after, devices
+        )
         received = lax.all_to_all(sent, GROUP, split_axis=0, concat_axis=0, tiled=True)
         after = (stages[g - 2][2],) if g >= 2 else ()
         left, own, theirs = assemble(half_scalar, received, after, *shape_of)

time: 525 us -> 506 us (0.964)
  Pallas kernels: 121 us -> 86 us
  local copies, waits for them, and re-layouts: 22.8 us -> 45.5 us
  waiting for transfers between devices: 275 us -> 265 us
    ppermute x4, waiting for transfers between devices: 196 us -> 146 us  [on_device(): stages.append((left, own, lax.ppermute(theirs, 'half', swap), theirs))]
    unnamed x59 -> x87, local copies, waits for them, and re-layouts: 9.3 us -> 40.8 us
    all_to_all x4, waiting for transfers between devices: 62.8 us -> 87.9 us  [on_device(): lax.all_to_all(sent, GROUP, split_axis=0, concat_axis=0, tiled=True)]
    pallas_call x4, Pallas kernels: 35.7 us -> 17.4 us  [project(): pl.pallas_call(project_kernel, grid=(total // quads,), in_specs=[pl.Block...]
    all_to_all x4, waiting for transfers between devices: 15.7 us -> 27.2 us  [on_device(): lax.all_to_all(product, GROUP, split_axis=0, concat_axis=0, tiled=True)]
    pallas_call x4, Pallas kernels: 21.5 us -> 14.7 us  [assemble(): pl.pallas_call(functools.partial(assemble_kernel, row_count=row_count, po...]
  transfers between devices with their start and end apart: 25 -> 25, of which waited for: 8 -> 11; matrix products, arithmetic and copies ran while one was open for 5% -> 4% of each run, Pallas kernels for 14% -> 8%
where the time goes in v3:
time: 506 us; the launch traced here: 505 us
  waiting for transfers between devices  265 us (52%)
  Pallas kernels  86 us (17%)
  starting transfers between devices  75.6 us (15%)
  local copies, waits for them, and re-layouts  45.5 us (9%)
  between operations  14.6 us (3%)
  matrix products  9.57 us (2%)
  other arithmetic  8.27 us (2%)
    ppermute x4, waiting for transfers between devices, on_device(): stages.append((left, own, lax.ppermute(theirs, 'half', swap), theirs))  146 us
    all_to_all x4, waiting for transfers between devices, on_device(): lax.all_to_all(sent, GROUP, split_axis=0, concat_axis=0, tiled=True)  87.9 us
    unnamed x87, local copies, waits for them, and re-layouts  40.8 us
    all_to_all x4, waiting for transfers between devices, on_device(): lax.all_to_all(product, GROUP, split_axis=0, concat_axis=0, tiled=True)  27.2 us
    pallas_call x1, Pallas kernels, front(): pl.pallas_call(functools.partial(front_kernel, row_count=len(rights), col...  24.3 us
    pallas_call x4, Pallas kernels, combine(): pl.pallas_call(functools.partial(combine_kernel, row_count=row_count, pos...  19.5 us
    all_to_all x4, starting transfers between devices, on_device(): lax.all_to_all(product, GROUP, split_axis=0, concat_axis=0, tiled=True)  19.1 us
    ppermute x8, starting transfers between devices, on_device(): lefts.append(lax.ppermute(own_left, AXES, pairs))  18.5 us
  transfers between devices with their start and end apart: 25, of which 11 were waited for; matrix products, arithmetic and copies ran while one was open for 4% of the time, Pallas kernels for 8%

profile of v3, /device:TPU:0, one launch (start us, length us, event | category | flops | bytes accessed | tf_op | source)
XLA Modules:
  0.0 504.7 jit_solution(1622963396413670865)
XLA Ops:
  11.8 7.6 %collective-permute-start.1 = (bf16[4,96,32]{2,1,0:T(8,128)(2,1)S(1)}, bf16[4,96,32]{2,1,0:T(8,128)(2,1)S(1)}, u32[]{:S(2)}, u32[]{:S(2)}) collective-permute-start(bf16[4,96,32]{2,1,0:T(8,128)(2,1)S(1)} %get-tuple-element.45), channel_id=1, source_target_pairs={{0,7},{1,0},{2,15},{3,8},{4,23},{5,16},{6,31},{7,24},{8,1},{9,2},{... | collective-permute-start | bytes 73736 | tf_op jit(solution)/shard_map/ppermute | solution.py:540
  30.1 5.2 %collective-permute-start.8 = (bf16[4,96,32]{2,1,0:T(8,128)(2,1)S(1)}, bf16[4,96,32]{2,1,0:T(8,128)(2,1)S(1)}, u32[]{:S(2)}, u32[]{:S(2)}) collective-permute-start(bf16[4,96,32]{2,1,0:T(8,128)(2,1)S(1)} %get-tuple-element.44.refs_8_), channel_id=1, source_target_pairs={{0,24},{8,0},{16,8},{24,16},{1,25},{9,1},{17,9},{25,17},{2,26},{10... | collective-permute-start | bytes 73736 | tf_op jit(solution)/shard_map/ppermute | solution.py:544
  47.7 24.3 %front.1 = (bf16[192,96,128]{2,1,0:T(8,128)(2,1)S(1)}, bf16[192,96,128]{2,1,0:T(8,128)(2,1)S(1)}) custom-call(s32[2]{0:T(128)S(1)} %pad_add_fusion.place_ref, bf16[4,96,32]{2,1,0:T(8,128)(2,1)S(1)} %collective-permute-done.refs_0_, bf16[4,96,32]{2,1,0:T(8,128)(2,1)S(1)} %collective-permute-done.1.refs_1_, ...), custom_call_target="tpu_custom_call" | custom-call | flops 1000 | bytes 1000 | tf_op jit(solution)/shard_map/front/pallas_call | solution.py:168
  74.2 3.8 project.4
  81.6 3.7 all-to-all-start
  87.7 3.8 project.5
  92.9 22.9 %all-to-all-done.recv_ref = bf16[16,192,384]{2,1,0:T(8,128)(2,1)S(1)} async-done(((bf16[16,192,384]{2,1,0:T(8,128)(2,1)}), bf16[16,192,384]{2,1,0:T(8,128)(2,1)S(1)}, u32[]{:S(2)}, u32[]{:S(2)}) %all-to-all-start) | async-done | bytes 2359328 | tf_op jit(solution)/shard_map/all_to_all | solution.py:577
  115.8 5.0 all-to-all-start.1
  127.4 43.0 %all-to-all-done.1.recv_ref = bf16[16,192,384]{2,1,0:T(8,128)(2,1)} async-done(((bf16[16,192,384]{2,1,0:T(8,128)(2,1)}), bf16[16,192,384]{2,1,0:T(8,128)(2,1)}, u32[]{:S(2)}, u32[]{:S(2)}) %all-to-all-start.1) | async-done | bytes 2359328 | tf_op jit(solution)/shard_map/all_to_all | solution.py:577
  170.4 4.5 assemble.5
  176.0 5.0 %collective-permute-done.11.recv_ref.refs_0_ = bf16[2,768,384]{2,1,0:T(8,128)(2,1)S(1)} collective-permute-done((bf16[2,768,384]{2,1,0:T(8,128)(2,1)}, bf16[2,768,384]{2,1,0:T(8,128)(2,1)S(1)}, u32[]{:S(2)}, u32[]{:S(2)}) %collective-permute-start.11) | collective-permute-done | bytes 1179680 | tf_op jit(solution)/shard_map/ppermute | solution.py:580
  181.1 4.9 combine.4
  187.0 4.0 all-to-all-start.2
  193.3 4.9 project.6
  198.3 10.3 %all-to-all-done.2.refs_0_ = bf16[16,96,384]{2,1,0:T(8,128)(2,1)S(1)} async-done(((bf16[16,96,384]{2,1,0:T(8,128)(2,1)}), bf16[16,96,384]{2,1,0:T(8,128)(2,1)S(1)}, u32[]{:S(2)}, u32[]{:S(2)}) %all-to-all-start.2) | async-done | bytes 1179680 | tf_op jit(solution)/shard_map/all_to_all | solution.py:616
  209.6 3.7 all-to-all-start.3
  217.0 4.9 project.7
  221.9 22.0 %all-to-all-done.3.recv_ref = bf16[16,192,384]{2,1,0:T(8,128)(2,1)S(1)} async-done(((bf16[16,192,384]{2,1,0:T(8,128)(2,1)}), bf16[16,192,384]{2,1,0:T(8,128)(2,1)S(1)}, u32[]{:S(2)}, u32[]{:S(2)}) %all-to-all-start.3) | async-done | bytes 2359328 | tf_op jit(solution)/shard_map/all_to_all | solution.py:577
  245.3 4.9 all-to-all-start.5
  253.6 6.2 %convolution_add_fusion = f32[192,96,8]{1,2,0:T(8,128)} fusion(bf16[192,96,128]{2,1,0:T(8,128)(2,1)} %copy-done.1, f32[192]{0:T(256)S(1)} %get-tuple-element.38, bf16[128,8]{0,1:T(8,128)(2,1)S(1)} %copy-done.41), kind=kOutput, calls=%fused_computation.7 | convolution fusion | flops 37896192 | bytes 5311232 | tf_op jit(solution)/shard_map/dot_general | solution.py:589
  267.5 49.2 %collective-permute-done.12.recv_ref.refs_0_ = bf16[2,768,384]{2,1,0:T(8,128)(2,1)} collective-permute-done((bf16[2,768,384]{2,1,0:T(8,128)(2,1)}, bf16[2,768,384]{2,1,0:T(8,128)(2,1)}, u32[]{:S(2)}, u32[]{:S(2)}) %collective-permute-start.12) | collective-permute-done | bytes 1179680 | tf_op jit(solution)/shard_map/ppermute | solution.py:580
  316.7 4.9 combine.5
  323.7 6.4 %all-to-all-start.4 = ((bf16[16,96,384]{2,1,0:T(8,128)(2,1)}), bf16[16,96,384]{2,1,0:T(8,128)(2,1)}, u32[]{:S(2)}, u32[]{:S(2)}) async-start(bf16[16,96,384]{2,1,0:T(8,128)(2,1)} %copy-done.15), calls=%async_computation.4 | async-start | bytes 2359296 | tf_op jit(solution)/shard_map/all_to_all | solution.py:616
  333.0 3.7 assemble.7
  337.7 47.3 %collective-permute-done.13.recv_ref = bf16[2,768,384]{2,1,0:T(8,128)(2,1)S(1)} collective-permute-done((bf16[2,768,384]{2,1,0:T(8,128)(2,1)}, bf16[2,768,384]{2,1,0:T(8,128)(2,1)S(1)}, u32[]{:S(2)}, u32[]{:S(2)}) %collective-permute-start.13) | collective-permute-done | bytes 1179680 | tf_op jit(solution)/shard_map/ppermute | solution.py:580
  385.0 4.9 combine.6
  389.9 4.2 all-to-all-start.6
  410.1 44.9 %collective-permute-done.14.recv_ref = bf16[2,768,384]{2,1,0:T(8,128)(2,1)} collective-permute-done((bf16[2,768,384]{2,1,0:T(8,128)(2,1)}, bf16[2,768,384]{2,1,0:T(8,128)(2,1)}, u32[]{:S(2)}, u32[]{:S(2)}) %collective-permute-start.14) | collective-permute-done | bytes 1179680 | tf_op jit(solution)/shard_map/ppermute | solution.py:580
  455.0 4.9 combine.7
  460.9 4.5 all-to-all-start.7
  466.2 16.9 %all-to-all-done.7.refs_3_ = bf16[16,96,384]{2,1,0:T(8,128)(2,1)} async-done(((bf16[16,96,384]{2,1,0:T(8,128)(2,1)}), bf16[16,96,384]{2,1,0:T(8,128)(2,1)}, u32[]{:S(2)}, u32[]{:S(2)}) %all-to-all-start.7) | async-done | bytes 1179680 | tf_op jit(solution)/shard_map/all_to_all | solution.py:616
  487.7 10.1 %finish.1 = bf16[192,96,128]{2,1,0:T(8,128)(2,1)} custom-call(bf16[16,96,384]{2,1,0:T(8,128)(2,1)S(1)} %copy-done.11, bf16[16,96,384]{2,1,0:T(8,128)(2,1)} %all-to-all-done.4.refs_1_, bf16[16,96,384]{2,1,0:T(8,128)(2,1)S(1)} %all-to-all-done.6.refs_2_, bf16[16,96,384]{2,1,0:T(8,128)(2,1)} %all-to-all-done.7.refs_3_, bf16[192,96,128]{2,1,0:T(8,128)(2,1)S(1)} %copy-done.18, ...), custom_call_target="tpu_custom_call" | custom-call | flops 1000 | bytes 1000 | tf_op jit(solution)/shard_map/finish/pallas_call | solution.py:459
  (163 shorter events, 93.6 us)
Async XLA Ops:
  7.2 401.4 %copy-start = (bf16[256,64]{0,1:T(8,128)(2,1)S(1)}, bf16[256,64]{0,1:T(8,128)(2,1)}, u32[]{:S(2)}) copy-start(bf16[256,64]{0,1:T(8,128)(2,1)} %param.17) | copy-start | bytes 98308
  8.2 242.1 %copy-start.36 = (bf16[4,96,64]{2,1,0:T(8,128)(2,1)}, bf16[4,96,64]{2,1,0:T(8,128)(2,1)S(1)}, u32[]{:S(2)}) copy-start(bf16[4,96,64]{2,1,0:T(8,128)(2,1)S(1)} %copy.78) | copy-start | bytes 147460
  11.2 11.8 %collective-permute-start = (bf16[4,96,32]{2,1,0:T(8,128)(2,1)S(1)}, bf16[4,96,32]{2,1,0:T(8,128)(2,1)S(1)}, u32[]{:S(2)}, u32[]{:S(2)}) collective-permute-start(bf16[4,96,32]{2,1,0:T(8,128)(2,1)S(1)} %get-tuple-element.45), channel_id=1, source_target_pairs={{0,0},{1,1},{2,8},{3,9},{4,16},{5,17},{6,24},{7,25},{8,2},{9,3},{1... | collective-permute-start | bytes 73736 | tf_op jit(solution)/shard_map/ppermute | solution.py:540
  11.8 13.4 %collective-permute-start.1 = (bf16[4,96,32]{2,1,0:T(8,128)(2,1)S(1)}, bf16[4,96,32]{2,1,0:T(8,128)(2,1)S(1)}, u32[]{:S(2)}, u32[]{:S(2)}) collective-permute-start(bf16[4,96,32]{2,1,0:T(8,128)(2,1)S(1)} %get-tuple-element.45), channel_id=1, source_target_pairs={{0,7},{1,0},{2,15},{3,8},{4,23},{5,16},{6,31},{7,24},{8,1},{9,2},{... | collective-permute-start | bytes 73736 | tf_op jit(solution)/shard_map/ppermute | solution.py:540
  19.5 7.4 %collective-permute-start.2 = (bf16[4,96,32]{2,1,0:T(8,128)(2,1)S(1)}, bf16[4,96,32]{2,1,0:T(8,128)(2,1)S(1)}, u32[]{:S(2)}, u32[]{:S(2)}) collective-permute-start(bf16[4,96,32]{2,1,0:T(8,128)(2,1)S(1)} %get-tuple-element.45), channel_id=1, source_target_pairs={{0,6},{1,7},{2,14},{3,15},{4,22},{5,23},{6,30},{7,31},{8,0},{9,1},... | collective-permute-start | bytes 73736 | tf_op jit(solution)/shard_map/ppermute | solution.py:540
  20.4 9.7 %collective-permute-start.3 = (bf16[4,96,32]{2,1,0:T(8,128)(2,1)S(1)}, bf16[4,96,32]{2,1,0:T(8,128)(2,1)S(1)}, u32[]{:S(2)}, u32[]{:S(2)}) collective-permute-start(bf16[4,96,32]{2,1,0:T(8,128)(2,1)S(1)} %get-tuple-element.45), channel_id=1, source_target_pairs={{0,5},{1,6},{2,13},{3,14},{4,21},{5,22},{6,29},{7,30},{8,7},{9,0},... | collective-permute-start | bytes 73736 | tf_op jit(solution)/shard_map/ppermute | solution.py:540
  22.1 13.2 %collective-permute-start.4 = (bf16[4,96,32]{2,1,0:T(8,128)(2,1)S(1)}, bf16[4,96,32]{2,1,0:T(8,128)(2,1)S(1)}, u32[]{:S(2)}, u32[]{:S(2)}) collective-permute-start(bf16[4,96,32]{2,1,0:T(8,128)(2,1)S(1)} %get-tuple-element.45), channel_id=1, source_target_pairs={{0,4},{1,5},{2,12},{3,13},{4,20},{5,21},{6,28},{7,29},{8,6},{9,7},... | collective-permute-start | bytes 73736 | tf_op jit(solution)/shard_map/ppermute | solution.py:540
  22.9 14.8 %collective-permute-start.5 = (bf16[4,96,32]{2,1,0:T(8,128)(2,1)S(1)}, bf16[4,96,32]{2,1,0:T(8,128)(2,1)S(1)}, u32[]{:S(2)}, u32[]{:S(2)}) collective-permute-start(bf16[4,96,32]{2,1,0:T(8,128)(2,1)S(1)} %get-tuple-element.45), channel_id=1, source_target_pairs={{0,3},{1,4},{2,11},{3,12},{4,19},{5,20},{6,27},{7,28},{8,5},{9,6},... | collective-permute-start | bytes 73736 | tf_op jit(solution)/shard_map/ppermute | solution.py:540
  25.3 16.5 %collective-permute-start.6 = (bf16[4,96,32]{2,1,0:T(8,128)(2,1)S(1)}, bf16[4,96,32]{2,1,0:T(8,128)(2,1)S(1)}, u32[]{:S(2)}, u32[]{:S(2)}) collective-permute-start(bf16[4,96,32]{2,1,0:T(8,128)(2,1)S(1)} %get-tuple-element.45), channel_id=1, source_target_pairs={{0,2},{1,3},{2,10},{3,11},{4,18},{5,19},{6,26},{7,27},{8,4},{9,5},... | collective-permute-start | bytes 73736 | tf_op jit(solution)/shard_map/ppermute | solution.py:540
  26.8 14.9 %collective-permute-start.7 = (bf16[4,96,32]{2,1,0:T(8,128)(2,1)S(1)}, bf16[4,96,32]{2,1,0:T(8,128)(2,1)S(1)}, u32[]{:S(2)}, u32[]{:S(2)}) collective-permute-start(bf16[4,96,32]{2,1,0:T(8,128)(2,1)S(1)} %get-tuple-element.45), channel_id=1, source_target_pairs={{0,1},{1,2},{2,9},{3,10},{4,17},{5,18},{6,25},{7,26},{8,3},{9,4},{... | collective-permute-start | bytes 73736 | tf_op jit(solution)/shard_map/ppermute | solution.py:540
  30.1 11.7 %collective-permute-start.8 = (bf16[4,96,32]{2,1,0:T(8,128)(2,1)S(1)}, bf16[4,96,32]{2,1,0:T(8,128)(2,1)S(1)}, u32[]{:S(2)}, u32[]{:S(2)}) collective-permute-start(bf16[4,96,32]{2,1,0:T(8,128)(2,1)S(1)} %get-tuple-element.44.refs_8_), channel_id=1, source_target_pairs={{0,24},{8,0},{16,8},{24,16},{1,25},{9,1},{17,9},{25,17},{2,26},{10... | collective-permute-start | bytes 73736 | tf_op jit(solution)/shard_map/ppermute | solution.py:544
  35.3 8.0 %collective-permute-start.9 = (bf16[4,96,32]{2,1,0:T(8,128)(2,1)S(1)}, bf16[4,96,32]{2,1,0:T(8,128)(2,1)S(1)}, u32[]{:S(2)}, u32[]{:S(2)}) collective-permute-start(bf16[4,96,32]{2,1,0:T(8,128)(2,1)S(1)} %get-tuple-element.44.refs_8_), channel_id=1, source_target_pairs={{0,16},{8,24},{16,0},{24,8},{1,17},{9,25},{17,1},{25,9},{2,18},{10... | collective-permute-start | bytes 73736 | tf_op jit(solution)/shard_map/ppermute | solution.py:544
  37.7 7.6 %collective-permute-start.10 = (bf16[4,96,32]{2,1,0:T(8,128)(2,1)S(1)}, bf16[4,96,32]{2,1,0:T(8,128)(2,1)S(1)}, u32[]{:S(2)}, u32[]{:S(2)}) collective-permute-start(bf16[4,96,32]{2,1,0:T(8,128)(2,1)S(1)} %get-tuple-element.44.refs_8_), channel_id=1, source_target_pairs={{0,8},{8,16},{16,24},{24,0},{1,9},{9,17},{17,25},{25,1},{2,10},{10... | collective-permute-start | bytes 73736 | tf_op jit(solution)/shard_map/ppermute | solution.py:544
  81.6 34.2 %all-to-all-start = ((bf16[16,192,384]{2,1,0:T(8,128)(2,1)}), bf16[16,192,384]{2,1,0:T(8,128)(2,1)S(1)}, u32[]{:S(2)}, u32[]{:S(2)}) async-start(bf16[16,192,384]{2,1,0:T(8,128)(2,1)} %copy-done.9), calls=%async_computation | async-start | bytes 4718592 | tf_op jit(solution)/shard_map/all_to_all | solution.py:577
  115.8 54.6 %all-to-all-start.1 = ((bf16[16,192,384]{2,1,0:T(8,128)(2,1)}), bf16[16,192,384]{2,1,0:T(8,128)(2,1)}, u32[]{:S(2)}, u32[]{:S(2)}) async-start(bf16[16,192,384]{2,1,0:T(8,128)(2,1)} %copy-done.8), calls=%async_computation.1 | async-start | bytes 4718592 | tf_op jit(solution)/shard_map/all_to_all | solution.py:577
  126.4 54.7 %copy-start.29 = (bf16[2,768,384]{2,1,0:T(8,128)(2,1)S(1)}, bf16[2,768,384]{2,1,0:T(8,128)(2,1)}, u32[]{:S(2)}) copy-start(bf16[2,768,384]{2,1,0:T(8,128)(2,1)} %copy-done.28) | copy-start | bytes 3538948
  126.4 54.7 %collective-permute-start.11 = (bf16[2,768,384]{2,1,0:T(8,128)(2,1)}, bf16[2,768,384]{2,1,0:T(8,128)(2,1)S(1)}, u32[]{:S(2)}, u32[]{:S(2)}) collective-permute-start(bf16[2,768,384]{2,1,0:T(8,128)(2,1)} %get-tuple-element.19.refs_0_), channel_id=1, source_target_pairs={{0,4},{4,0},{1,5},{5,1},{2,6},{6,2},{3,7},{7,3},{8,12},{12,8},{9,1... | collective-permute-start | bytes 3538952 | tf_op jit(solution)/shard_map/ppermute | solution.py:580
  187.0 21.6 %all-to-all-start.2 = ((bf16[16,96,384]{2,1,0:T(8,128)(2,1)}), bf16[16,96,384]{2,1,0:T(8,128)(2,1)S(1)}, u32[]{:S(2)}, u32[]{:S(2)}) async-start(bf16[16,96,384]{2,1,0:T(8,128)(2,1)} %combine.4), calls=%async_computation.2 | async-start | bytes 2359296 | tf_op jit(solution)/shard_map/all_to_all | solution.py:616
  209.6 34.2 %all-to-all-start.3 = ((bf16[16,192,384]{2,1,0:T(8,128)(2,1)}), bf16[16,192,384]{2,1,0:T(8,128)(2,1)S(1)}, u32[]{:S(2)}, u32[]{:S(2)}) async-start(bf16[16,192,384]{2,1,0:T(8,128)(2,1)} %project.6), calls=%async_computation.3 | async-start | bytes 4718592 | tf_op jit(solution)/shard_map/all_to_all | solution.py:577
  245.3 78.4 %all-to-all-start.5 = ((bf16[16,192,384]{2,1,0:T(8,128)(2,1)}), bf16[16,192,384]{2,1,0:T(8,128)(2,1)S(1)}, u32[]{:S(2)}, u32[]{:S(2)}) async-start(bf16[16,192,384]{2,1,0:T(8,128)(2,1)} %project.7), calls=%async_computation.5 | async-start | bytes 4718592 | tf_op jit(solution)/shard_map/all_to_all | solution.py:577
  250.3 143.8 %all-gather.3.cloned.1.call-start = ((), (), s32[]{:S(2)}) async-start(), calls=%async_computation.8 | async-start | bytes 1769472 | tf_op jit(solution)/shard_map/all_gather | solution.py:597
  251.4 145.4 %all-gather.5.cloned.1.call-start = ((), (), s32[]{:S(2)}) async-start(), calls=%async_computation.9 | async-start | bytes 3932160 | tf_op jit(solution)/shard_map/all_gather | solution.py:596
  251.6 65.2 %collective-permute-start.12 = (bf16[2,768,384]{2,1,0:T(8,128)(2,1)}, bf16[2,768,384]{2,1,0:T(8,128)(2,1)}, u32[]{:S(2)}, u32[]{:S(2)}) collective-permute-start(bf16[2,768,384]{2,1,0:T(8,128)(2,1)} %copy-done.12), channel_id=1, source_target_pairs={{0,4},{4,0},{1,5},{5,1},{2,6},{6,2},{3,7},{7,3},{8,12},{12,8},{9,1... | collective-permute-start | bytes 3538952 | tf_op jit(solution)/shard_map/ppermute | solution.py:580
  262.8 54.0 %copy-start.22 = (bf16[2,768,384]{2,1,0:T(8,128)(2,1)S(1)}, bf16[2,768,384]{2,1,0:T(8,128)(2,1)}, u32[]{:S(2)}) copy-start(bf16[2,768,384]{2,1,0:T(8,128)(2,1)} %copy-done.21) | copy-start | bytes 3538948
  323.7 66.2 %all-to-all-start.4 = ((bf16[16,96,384]{2,1,0:T(8,128)(2,1)}), bf16[16,96,384]{2,1,0:T(8,128)(2,1)}, u32[]{:S(2)}, u32[]{:S(2)}) async-start(bf16[16,96,384]{2,1,0:T(8,128)(2,1)} %copy-done.15), calls=%async_computation.4 | async-start | bytes 2359296 | tf_op jit(solution)/shard_map/all_to_all | solution.py:616
  330.1 54.9 %copy-start.26 = (bf16[2,768,384]{2,1,0:T(8,128)(2,1)S(1)}, bf16[2,768,384]{2,1,0:T(8,128)(2,1)}, u32[]{:S(2)}) copy-start(bf16[2,768,384]{2,1,0:T(8,128)(2,1)} %copy-done.25) | copy-start | bytes 3538948
  330.1 54.9 %copy-start.31 = (bf16[2,384,384]{2,1,0:T(8,128)(2,1)S(1)}, bf16[2,384,384]{2,1,0:T(8,128)(2,1)}, u32[]{:S(2)}) copy-start(bf16[2,384,384]{2,1,0:T(8,128)(2,1)} %copy-done.30) | copy-start | bytes 1769476
  330.1 54.9 %collective-permute-start.13 = (bf16[2,768,384]{2,1,0:T(8,128)(2,1)}, bf16[2,768,384]{2,1,0:T(8,128)(2,1)S(1)}, u32[]{:S(2)}, u32[]{:S(2)}) collective-permute-start(bf16[2,768,384]{2,1,0:T(8,128)(2,1)} %copy-done.27), channel_id=1, source_target_pairs={{0,4},{4,0},{1,5},{5,1},{2,6},{6,2},{3,7},{7,3},{8,12},{12,8},{9,1... | collective-permute-start | bytes 3538952 | tf_op jit(solution)/shard_map/ppermute | solution.py:580
  389.9 71.0 %all-to-all-start.6 = ((bf16[16,96,384]{2,1,0:T(8,128)(2,1)}), bf16[16,96,384]{2,1,0:T(8,128)(2,1)S(1)}, u32[]{:S(2)}, u32[]{:S(2)}) async-start(bf16[16,96,384]{2,1,0:T(8,128)(2,1)} %combine.6), calls=%async_computation.6 | async-start | bytes 2359296 | tf_op jit(solution)/shard_map/all_to_all | solution.py:616
  399.4 55.5 %collective-permute-start.14 = (bf16[2,768,384]{2,1,0:T(8,128)(2,1)}, bf16[2,768,384]{2,1,0:T(8,128)(2,1)}, u32[]{:S(2)}, u32[]{:S(2)}) collective-permute-start(bf16[2,768,384]{2,1,0:T(8,128)(2,1)} %get-tuple-element.26.refs_0_), channel_id=1, source_target_pairs={{0,4},{4,0},{1,5},{5,1},{2,6},{6,2},{3,7},{7,3},{8,12},{12,8},{9,1... | collective-permute-start | bytes 3538952 | tf_op jit(solution)/shard_map/ppermute | solution.py:580
  407.6 47.4 %copy-start.24 = (bf16[2,768,384]{2,1,0:T(8,128)(2,1)S(1)}, bf16[2,768,384]{2,1,0:T(8,128)(2,1)}, u32[]{:S(2)}) copy-start(bf16[2,768,384]{2,1,0:T(8,128)(2,1)} %copy-done.23) | copy-start | bytes 3538948
  460.9 22.2 %all-to-all-start.7 = ((bf16[16,96,384]{2,1,0:T(8,128)(2,1)}), bf16[16,96,384]{2,1,0:T(8,128)(2,1)}, u32[]{:S(2)}, u32[]{:S(2)}) async-start(bf16[16,96,384]{2,1,0:T(8,128)(2,1)} %copy-done.16), calls=%async_computation.7 | async-start | bytes 2359296 | tf_op jit(solution)/shard_map/all_to_all | solution.py:616
  (36 other events, 175.4 us)
Sparse Core Ops, SparseCore 0:
  252.7 49.6 all-gather.2
  304.3 73.6 all-gather.4

commit v4 on v3

--- a/solution.py
+++ b/solution.py
@@ -35,10 +35,9 @@
     return 0.5 * jnp.tanh(0.5 * x) + 0.5
 
 
-def params(need):
-    limit = min(need + 12 * MIB, 60 * MIB)
+def params():
     return pltpu.CompilerParams(
-        vmem_limit_bytes=limit, dimension_semantics=("arbitrary",)
+        vmem_limit_bytes=60 * MIB, dimension_semantics=("arbitrary",)
     )
 
 
@@ -52,6 +51,19 @@
 
 def anywhere(after):
     return [pl.BlockSpec(memory_space=pl.ANY)] * len(after)
+
+
+def fence(values, after):
+    return pl.pallas_call(
+        lambda *refs: None,
+        in_specs=anywhere(values) + anywhere(after),
+        out_specs=anywhere(values),
+        out_shape=[jax.ShapeDtypeStruct(v.shape, v.dtype) for v in values],
+        input_output_aliases={i: i for i in range(len(values))},
+        compiler_params=pltpu.CompilerParams(vmem_limit_bytes=60 * MIB),
+        cost_estimate=LIGHT,
+        name="fence",
+    )(*values, *after)
 
 
 def pack_rows(rows):
@@ -183,7 +195,7 @@
             pltpu.VMEM((cols, width * seqs), BF16),
             pltpu.VMEM((block // 2, width * seqs, 2 * wide), BF16),
         ],
-        compiler_params=params(4 * rows * seqs * LANES + 16 * MIB),
+        compiler_params=params(),
         cost_estimate=LIGHT,
         name="front",
     )(place, *lefts, *rights, present_rows, coupling, w_tensor, present_cols)
@@ -255,7 +267,7 @@
         out_specs=pl.BlockSpec((dests, quads * each, lanes), lambda i: (0, i, 0)),
         out_shape=jax.ShapeDtypeStruct((dests, total * each, lanes), BF16),
         scratch_shapes=[pltpu.VMEM((dests, quads * each, lanes), F32)],
-        compiler_params=params(8 * dests * quads * each * lanes + 2 * MIB),
+        compiler_params=params(),
         cost_estimate=LIGHT,
         name="project",
     )(live_rows, normed, live_cols, weight, *after)
@@ -329,7 +341,7 @@
         ).astype(BF16)
 
 
-def assemble(half, received, after, row_count, pos_count, cols):
+def assemble(half, received, row_count, pos_count, cols):
     sources, height, lanes = received.shape
     each = (2 * pos_count * cols) // (row_count * QUAD)
     stride = height // each
@@ -339,7 +351,7 @@
     return pl.pallas_call(
         functools.partial(assemble_kernel, row_count=row_count, pos_count=pos_count),
         grid=(channels,),
-        in_specs=[pl.BlockSpec(memory_space=pltpu.SMEM), whole(received.shape)] + anywhere(after),
+        in_specs=[pl.BlockSpec(memory_space=pltpu.SMEM), whole(received.shape)],
         out_specs=[
             pl.BlockSpec((1, rows, depth), lambda c: (c, 0, 0)),
             pl.BlockSpec((1, depth, depth), lambda c: (c, 0, 0)),
@@ -354,12 +366,10 @@
             pltpu.VMEM((sources, lanes // LANES, height, LANES), F32),
             pltpu.VMEM((depth // LANES, rows, LANES), F32),
         ],
-        compiler_params=params(
-            6 * received.size + 4 * rows * depth + 4 * (2 * rows + depth) * depth
-        ),
+        compiler_params=params(),
         cost_estimate=LIGHT,
         name="assemble",
-    )(half, received, *after)
+    )(half, received)
 
 
 def combine_kernel(left_ref, own_ref, recv_ref, *refs, row_count, pos_count):
@@ -409,9 +419,7 @@
         out_specs=whole(shape),
         out_shape=jax.ShapeDtypeStruct(shape, BF16),
         scratch_shapes=[pltpu.VMEM((shape[0], shape[2] // LANES, shape[1], LANES), F32)],
-        compiler_params=params(
-            4 * (2 * rows + depth) * depth + 6 * shape[0] * shape[1] * shape[2]
-        ),
+        compiler_params=params(),
         cost_estimate=LIGHT,
         name="combine",
     )(left, own, received, *after)
@@ -468,9 +476,7 @@
         scratch_shapes=[
             pltpu.VMEM((lanes // LANES, sources * quads * each, LANES), F32) for each in heights
         ],
-        compiler_params=params(
-            8 * sources * quads * sum(heights) * lanes + 12 * quads * QUAD * cols * wide
-        ),
+        compiler_params=params(),
         cost_estimate=LIGHT,
         name="finish",
     )(*parts, mid, normed, w_gate, w_final)
@@ -565,20 +571,6 @@
     half_scalar = half.astype(jnp.int32).reshape(1)
     swap = [(0, 1), (1, 0)]
     shape_of = (row_count, pos_count, module_number)
-    stages = []
-    start = 0
-    for g, each in enumerate(sizes):
-        weight = jnp.transpose(w_kinds[:, :, :, start : start + each], (1, 2, 0, 3, 4))
-        start += each
-        after = (stages[g - 2][3],) if g >= 2 else ()
-        sent = project(
-            live_rows, pair_normed, live_packed, weight.reshape(-1, wide), after, devices
-        )
-        received = lax.all_to_all(sent, GROUP, split_axis=0, concat_axis=0, tiled=True)
-        after = (stages[g - 2][2],) if g >= 2 else ()
-        left, own, theirs = assemble(half_scalar, received, after, *shape_of)
-        stages.append((left, own, lax.ppermute(theirs, "half", swap), theirs))
-
     values = project_msa(
         alignment_matrix[:, 2 * TENSOR_FEATURES : 2 * TENSOR_FEATURES + MEAN_GROUPS * GROUP_FEATURES]
     ).astype(BF16)
@@ -593,6 +585,42 @@
         ).reshape(rows, module_number, MEAN_GROUPS)
         + MASK_PENALTY * (live_rows - 1.0)[:, None, None]
     )
+    chunks = len(sizes)
+
+    def send(g, after):
+        start = sum(sizes[:g])
+        weight = jnp.transpose(w_kinds[:, :, :, start : start + sizes[g]], (1, 2, 0, 3, 4))
+        return project(
+            live_rows, pair_normed, live_packed, weight.reshape(-1, wide), after, devices
+        )
+
+    def exchange(block):
+        return lax.all_to_all(block, GROUP, split_axis=0, concat_axis=0, tiled=True)
+
+    stages = [assemble(half_scalar, exchange(send(0, ())), *shape_of)]
+    ahead = send(1, ()) if chunks > 1 else None
+    partials, returned = [], []
+
+    def finish_chunk(g, partial, after):
+        left, own, _ = stages[g]
+        returned.append(exchange(combine(left, own, partial, after, *shape_of)))
+
+    for g in range(chunks):
+        carried = [stages[g][2]] + partials[g - 1 :][:1] * (g > 0)
+        if g + 1 < chunks:
+            carried.append(ahead)
+        after = returned[g - 2 : g - 1] if g > 1 else []
+        if g == 1:
+            after = [logits, values]
+        carried = fence(carried, after)
+        partials.append(lax.ppermute(carried[0], "half", swap))
+        if g + 1 < chunks:
+            stages.append(assemble(half_scalar, exchange(carried[-1]), *shape_of))
+        if g + 2 < chunks:
+            ahead = send(g + 2, (stages[g][0],))
+        if g > 0:
+            finish_chunk(g - 1, carried[1], tuple(stages[g + 1][:1]) if g + 1 < chunks else ())
+
     logits_all = lax.all_gather(logits, "row", axis=0, tiled=True)
     values_all = lax.all_gather(values, ("half", "pos"), axis=1, tiled=True)
     top_all = jnp.max(logits_all, axis=0)
@@ -609,11 +637,7 @@
     ).reshape(seq_each, module_number, -1)
     alignment_updated_embedding = (alignment_embedding.astype(F32) + blended_update).astype(BF16)
 
-    returned = []
-    for g, (left, own, partial, _) in enumerate(stages):
-        after = (stages[g + 1][3],) if g + 1 < len(stages) else (alignment_updated_embedding,)
-        product = combine(left, own, partial, after, *shape_of)
-        returned.append(lax.all_to_all(product, GROUP, split_axis=0, concat_axis=0, tiled=True))
+    finish_chunk(chunks - 1, partials[-1], (alignment_updated_embedding,))
     w_final = jnp.transpose(trimul_final_matrix.reshape(devices, -1, wide), (1, 0, 2))
     pair_output = finish(
         returned, pair_mid, pair_normed, trimul_matrices[:, 4 * CTRI :], w_final.reshape(-1, wide)

time: 506 us -> 535 us (1.057)
  blocking collectives: 0 us -> 34.7 us
  Pallas kernels: 86 us -> 112 us
  local copies, waits for them, and re-layouts: 45.5 us -> 27.9 us
  starting transfers between devices: 75.6 us -> 62.1 us
    all_to_all x0 -> x1, blocking collectives: none -> 34.7 us  [exchange(): return lax.all_to_all(block, GROUP, split_axis=0, concat_axis=0, tiled=True)]
    unnamed x87 -> x61, local copies, waits for them, and re-layouts: 40.8 us -> 11.6 us
    pallas_call x4, Pallas kernels: 17.4 us -> 26.7 us  [project(): pl.pallas_call(project_kernel, grid=(total // quads,), in_specs=[pl.Block...]
    all_to_all x8 -> x7, starting transfers between devices: 36.4 us -> 29 us  [exchange(): return lax.all_to_all(block, GROUP, split_axis=0, concat_axis=0, tiled=True)]
    pallas_call x4, Pallas kernels: 14.7 us -> 21.4 us  [assemble(): pl.pallas_call(functools.partial(assemble_kernel, row_count=row_count, po...]
    add x0 -> x1, local copies, waits for them, and re-layouts: none -> 6.32 us  [on_device(): jnp.dot(pair_normed.reshape(rows * module_number, wide), coupling_logit_m...]
    all_to_all x8 -> x7, waiting for transfers between devices: 115 us -> 113 us  [exchange(): return lax.all_to_all(block, GROUP, split_axis=0, concat_axis=0, tiled=True)]
  transfers between devices with their start and end apart: 25 -> 24, of which waited for: 11 -> 8; matrix products, arithmetic and copies ran while one was open for 4% -> 6% of each run, Pallas kernels for 8% -> 9%
where the time goes in v4:
time: 535 us; the launch traced here: 532 us
  waiting for transfers between devices  263 us (49%)
  Pallas kernels  112 us (21%)
  starting transfers between devices  62.1 us (12%)
  blocking collectives  34.7 us (6%)
  local copies, waits for them, and re-layouts  27.9 us (5%)
  between operations  14.5 us (3%)
  matrix products  10.3 us (2%)
  other arithmetic  7.55 us (1%)
    ppermute x4, waiting for transfers between devices, on_device(): partials.append(lax.ppermute(carried[0], 'half', swap))  149 us
    all_to_all x7, waiting for transfers between devices, exchange(): return lax.all_to_all(block, GROUP, split_axis=0, concat_axis=0, tiled=True)  113 us
    all_to_all x1, blocking collectives, exchange(): return lax.all_to_all(block, GROUP, split_axis=0, concat_axis=0, tiled=True)  34.7 us
    all_to_all x7, starting transfers between devices, exchange(): return lax.all_to_all(block, GROUP, split_axis=0, concat_axis=0, tiled=True)  29 us
    pallas_call x1, Pallas kernels, front(): pl.pallas_call(functools.partial(front_kernel, row_count=len(rights), col...  27 us
    pallas_call x4, Pallas kernels, project(): pl.pallas_call(project_kernel, grid=(total // quads,), in_specs=[pl.Block...  26.7 us
    pallas_call x4, Pallas kernels, combine(): pl.pallas_call(functools.partial(combine_kernel, row_count=row_count, pos...  24.8 us
    pallas_call x4, Pallas kernels, assemble(): pl.pallas_call(functools.partial(assemble_kernel, row_count=row_count, po...  21.4 us
  transfers between devices with their start and end apart: 24, of which 8 were waited for; matrix products, arithmetic and copies ran while one was open for 6% of the time, Pallas kernels for 9%

profile of v4, /device:TPU:0, one launch (start us, length us, event | category | flops | bytes accessed | tf_op | source)
XLA Modules:
  0.0 532.4 jit_solution(413392938207714671)
XLA Ops:
  11.8 7.6 %collective-permute-start.1 = (bf16[4,96,32]{2,1,0:T(8,128)(2,1)S(1)}, bf16[4,96,32]{2,1,0:T(8,128)(2,1)S(1)}, u32[]{:S(2)}, u32[]{:S(2)}) collective-permute-start(bf16[4,96,32]{2,1,0:T(8,128)(2,1)S(1)} %get-tuple-element.65), channel_id=1, source_target_pairs={{0,7},{1,0},{2,15},{3,8},{4,23},{5,16},{6,31},{7,24},{8,1},{9,2},{... | collective-permute-start | bytes 73736 | tf_op jit(solution)/shard_map/ppermute | solution.py:546
  30.5 4.6 collective-permute-start.8
  46.1 27.0 %front.1 = (bf16[192,96,128]{2,1,0:T(8,128)(2,1)}, bf16[192,96,128]{2,1,0:T(8,128)(2,1)}) custom-call(s32[2]{0:T(128)} %pad_add_fusion.place_ref, bf16[4,96,32]{2,1,0:T(8,128)(2,1)} %copy-done.15, bf16[4,96,32]{2,1,0:T(8,128)(2,1)} %copy-done.16, bf16[4,96,32]{2,1,0:T(8,128)(2,1)} %copy-done.17, bf16[4,96,32]{2,1,0:T(8,128)(2,1)} %copy-done.18, ...), custom_call_target="tpu_custom_call" | custom-call | flops 1000 | bytes 1000 | tf_op jit(solution)/shard_map/front/pallas_call | solution.py:180
  73.1 6.7 %project.4 = bf16[16,192,384]{2,1,0:T(8,128)(2,1)} custom-call(f32[192]{0:T(256)} %get-tuple-element.59.live_ref, bf16[192,96,128]{2,1,0:T(8,128)(2,1)} %get-tuple-element.26.normed_ref.refs_5_, f32[1,384]{1,0:T(1,128)} %broadcast_in_dim.7.cols_ref, bf16[128,128]{1,0:T(8,128)(2,1)} %bitcast.52), custom_call_target="tpu_custom_call" | custom-call | flops 1000 | bytes 1000 | tf_op jit(solution)/shard_map/project/pallas_call | solution.py:257
  79.7 3.7 all-to-all-start
  84.1 6.7 %project.5.refs_1_ = bf16[16,192,384]{2,1,0:T(8,128)(2,1)} custom-call(f32[192]{0:T(256)} %get-tuple-element.59.live_ref, bf16[192,96,128]{2,1,0:T(8,128)(2,1)} %get-tuple-element.26.normed_ref.refs_5_, f32[1,384]{1,0:T(1,128)} %broadcast_in_dim.7.cols_ref, bf16[128,128]{1,0:T(8,128)(2,1)} %bitcast.56), custom_call_target="tpu_custom_call" | custom-call | flops 1000 | bytes 1000 | tf_op jit(solution)/shard_map/project/pallas_call | solution.py:257
  90.8 23.1 %all-to-all-done.recv_ref = bf16[16,192,384]{2,1,0:T(8,128)(2,1)S(1)} async-done(((bf16[16,192,384]{2,1,0:T(8,128)(2,1)}), bf16[16,192,384]{2,1,0:T(8,128)(2,1)S(1)}, u32[]{:S(2)}, u32[]{:S(2)}) %all-to-all-start) | async-done | bytes 2359328 | tf_op jit(solution)/shard_map/all_to_all | solution.py:598
  115.4 5.4 %assemble.4 = (bf16[2,768,384]{2,1,0:T(8,128)(2,1)}, bf16[2,384,384]{2,1,0:T(8,128)(2,1)}, bf16[2,768,384]{2,1,0:T(8,128)(2,1)}) custom-call(s32[1]{0:T(128)} %bitcast.12.half_ref, bf16[16,192,384]{2,1,0:T(8,128)(2,1)} %copy-done.6), custom_call_target="tpu_custom_call" | custom-call | flops 1000 | bytes 1000 | tf_op jit(solution)/shard_map/assemble/pallas_call | solution.py:351
  120.7 5.1 all-to-all-start.1
  129.0 7.4 %broadcast_add_fusion.refs_3_ = f32[192,96,8]{2,1,0:T(8,128)} fusion(f32[192]{0:T(256)S(1)} %get-tuple-element.58, bf16[192,96,128]{2,1,0:T(8,128)(2,1)} %get-tuple-element.26.normed_ref.refs_5_, bf16[128,8]{0,1:T(8,128)(2,1)S(1)} %copy-done.28), kind=kOutput, calls=%fused_computation | convolution fusion | flops 37896192 | bytes 5311232 | tf_op jit(solution)/shard_map/dot_general | solution.py:581
  136.4 6.7 %project.6.refs_2_ = bf16[16,192,384]{2,1,0:T(8,128)(2,1)} custom-call(f32[192]{0:T(256)} %get-tuple-element.59.live_ref, bf16[192,96,128]{2,1,0:T(8,128)(2,1)} %get-tuple-element.26.normed_ref.refs_5_, f32[1,384]{1,0:T(1,128)} %broadcast_in_dim.7.cols_ref, bf16[128,128]{1,0:T(8,128)(2,1)} %bitcast.54, bf16[2,768,384]{2,1,0:T(8,128)(2,1)} %get-tuple-element.27.refs_0_.left_ref), custom_call_target="tpu_custom_call" | custom-call | flops 1000 | bytes 1000 | tf_op jit(solution)/shard_map/project/pallas_call | solution.py:257
  143.0 38.3 %all-to-all-done.1.recv_ref = bf16[16,192,384]{2,1,0:T(8,128)(2,1)S(1)} async-done(((bf16[16,192,384]{2,1,0:T(8,128)(2,1)}), bf16[16,192,384]{2,1,0:T(8,128)(2,1)S(1)}, u32[]{:S(2)}, u32[]{:S(2)}) %all-to-all-start.1) | async-done | bytes 2359328 | tf_op jit(solution)/shard_map/all_to_all | solution.py:598
  182.8 5.4 %assemble.5 = (bf16[2,768,384]{2,1,0:T(8,128)(2,1)}, bf16[2,384,384]{2,1,0:T(8,128)(2,1)}, bf16[2,768,384]{2,1,0:T(8,128)(2,1)}) custom-call(s32[1]{0:T(128)} %bitcast.12.half_ref, bf16[16,192,384]{2,1,0:T(8,128)(2,1)} %copy-done.5), custom_call_target="tpu_custom_call" | custom-call | flops 1000 | bytes 1000 | tf_op jit(solution)/shard_map/assemble/pallas_call | solution.py:351
  188.2 34.7 %all_to_all.40.recv_ref = bf16[16,192,384]{2,1,0:T(8,128)(2,1)} all-to-all(bf16[16,192,384]{2,1,0:T(8,128)(2,1)} %get-tuple-element.34), channel_id=1, replica_groups=mesh['row'=4,'half'=2,'pos'=4] {'row','pos'}, dimensions={0} | all-to-all | bytes 4718592 | tf_op jit(solution)/shard_map/all_to_all | solution.py:598
  222.8 5.3 %assemble.6 = (bf16[2,768,384]{2,1,0:T(8,128)(2,1)}, bf16[2,384,384]{2,1,0:T(8,128)(2,1)}, bf16[2,768,384]{2,1,0:T(8,128)(2,1)}) custom-call(s32[1]{0:T(128)} %bitcast.12.half_ref, bf16[16,192,384]{2,1,0:T(8,128)(2,1)} %all_to_all.40.recv_ref), custom_call_target="tpu_custom_call" | custom-call | flops 1000 | bytes 1000 | tf_op jit(solution)/shard_map/assemble/pallas_call | solution.py:351
  228.2 6.2 %combine.4 = bf16[16,96,384]{2,1,0:T(8,128)(2,1)} custom-call(bf16[2,768,384]{2,1,0:T(8,128)(2,1)} %get-tuple-element.27.refs_0_.left_ref, bf16[2,384,384]{2,1,0:T(8,128)(2,1)} %get-tuple-element.28.own_ref, bf16[2,768,384]{2,1,0:T(8,128)(2,1)} %get-tuple-element.33.recv_ref, bf16[2,768,384]{2,1,0:T(8,128)(2,1)} %get-tuple-element.35.refs_0_.left_ref), custom_call_target="tpu_custom_call" | custom-call | flops 1000 | bytes 1000 | tf_op jit(solution)/shard_map/combine/pallas_call | solution.py:410
  238.8 6.6 %project.7.refs_2_ = bf16[16,192,384]{2,1,0:T(8,128)(2,1)} custom-call(f32[192]{0:T(256)} %get-tuple-element.59.live_ref, bf16[192,96,128]{2,1,0:T(8,128)(2,1)} %get-tuple-element.26.normed_ref.refs_5_, f32[1,384]{1,0:T(1,128)} %broadcast_in_dim.7.cols_ref, bf16[128,128]{1,0:T(8,128)(2,1)} %bitcast.55, bf16[2,768,384]{2,1,0:T(8,128)(2,1)} %get-tuple-element.36.refs_0_.left_ref), custom_call_target="tpu_custom_call" | custom-call | flops 1000 | bytes 1000 | tf_op jit(solution)/shard_map/project/pallas_call | solution.py:257
  245.4 47.2 %collective-permute-done.12.refs_1_ = bf16[2,768,384]{2,1,0:T(8,128)(2,1)S(1)} collective-permute-done((bf16[2,768,384]{2,1,0:T(8,128)(2,1)}, bf16[2,768,384]{2,1,0:T(8,128)(2,1)S(1)}, u32[]{:S(2)}, u32[]{:S(2)}) %collective-permute-start.12) | collective-permute-done | bytes 1179680 | tf_op jit(solution)/shard_map/ppermute | solution.py:616
  294.1 4.0 all-to-all-start.4
  298.9 6.3 %copy.104 = f32[192,96,8]{1,2,0:T(8,128)} copy(f32[192,96,8]{2,1,0:T(8,128)} %broadcast_add_fusion.refs_3_) | data formatting | bytes 1179648 | tf_op jit(solution)/shard_map/add | solution.py:581
  305.2 35.8 %all-to-all-done.4.recv_ref = bf16[16,192,384]{2,1,0:T(8,128)(2,1)S(1)} async-done(((bf16[16,192,384]{2,1,0:T(8,128)(2,1)}), bf16[16,192,384]{2,1,0:T(8,128)(2,1)S(1)}, u32[]{:S(2)}, u32[]{:S(2)}) %all-to-all-start.4) | async-done | bytes 2359328 | tf_op jit(solution)/shard_map/all_to_all | solution.py:598
  342.4 5.3 %assemble.7 = (bf16[2,768,384]{2,1,0:T(8,128)(2,1)}, bf16[2,384,384]{2,1,0:T(8,128)(2,1)}, bf16[2,768,384]{2,1,0:T(8,128)(2,1)}) custom-call(s32[1]{0:T(128)} %bitcast.12.half_ref, bf16[16,192,384]{2,1,0:T(8,128)(2,1)} %copy-done.4), custom_call_target="tpu_custom_call" | custom-call | flops 1000 | bytes 1000 | tf_op jit(solution)/shard_map/assemble/pallas_call | solution.py:351
  347.8 6.4 %combine.5 = bf16[16,96,384]{2,1,0:T(8,128)(2,1)} custom-call(bf16[2,768,384]{2,1,0:T(8,128)(2,1)} %get-tuple-element.36.refs_0_.left_ref, bf16[2,384,384]{2,1,0:T(8,128)(2,1)} %get-tuple-element.37.own_ref, bf16[2,768,384]{2,1,0:T(8,128)(2,1)} %get-tuple-element.40.recv_ref, bf16[2,768,384]{2,1,0:T(8,128)(2,1)} %get-tuple-element.42.refs_0_.left_ref), custom_call_target="tpu_custom_call" | custom-call | flops 1000 | bytes 1000 | tf_op jit(solution)/shard_map/combine/pallas_call | solution.py:410
  354.1 3.7 all-to-all-start.5
  359.1 53.3 %collective-permute-done.13.refs_1_ = bf16[2,768,384]{2,1,0:T(8,128)(2,1)S(1)} collective-permute-done((bf16[2,768,384]{2,1,0:T(8,128)(2,1)}, bf16[2,768,384]{2,1,0:T(8,128)(2,1)S(1)}, u32[]{:S(2)}, u32[]{:S(2)}) %collective-permute-start.13) | collective-permute-done | bytes 1179680 | tf_op jit(solution)/shard_map/ppermute | solution.py:616
  413.9 6.2 %combine.6 = bf16[16,96,384]{2,1,0:T(8,128)(2,1)} custom-call(bf16[2,768,384]{2,1,0:T(8,128)(2,1)} %get-tuple-element.35.refs_0_.left_ref, bf16[2,384,384]{2,1,0:T(8,128)(2,1)} %get-tuple-element.43.own_ref, bf16[2,768,384]{2,1,0:T(8,128)(2,1)} %get-tuple-element.46.recv_ref), custom_call_target="tpu_custom_call" | custom-call | flops 1000 | bytes 1000 | tf_op jit(solution)/shard_map/combine/pallas_call | solution.py:410
  420.1 4.6 all-to-all-start.6
  436.0 48.7 %collective-permute-done.14.recv_ref = bf16[2,768,384]{2,1,0:T(8,128)(2,1)} collective-permute-done((bf16[2,768,384]{2,1,0:T(8,128)(2,1)}, bf16[2,768,384]{2,1,0:T(8,128)(2,1)}, u32[]{:S(2)}, u32[]{:S(2)}) %collective-permute-start.14) | collective-permute-done | bytes 1179680 | tf_op jit(solution)/shard_map/ppermute | solution.py:616
  484.7 6.1 %combine.7 = bf16[16,96,384]{2,1,0:T(8,128)(2,1)} custom-call(bf16[2,768,384]{2,1,0:T(8,128)(2,1)} %get-tuple-element.42.refs_0_.left_ref, bf16[2,384,384]{2,1,0:T(8,128)(2,1)} %get-tuple-element.47.own_ref, bf16[2,768,384]{2,1,0:T(8,128)(2,1)} %collective-permute-done.14.recv_ref, bf16[4,96,64]{2,1,0:T(8,128)(2,1)} %fusion.17.refs_0_), custom_call_target="tpu_custom_call" | custom-call | flops 1000 | bytes 1000 | tf_op jit(solution)/shard_map/combine/pallas_call | solution.py:410
  490.8 4.2 all-to-all-start.7
  497.0 15.6 %all-to-all-done.7.refs_3_ = bf16[16,96,384]{2,1,0:T(8,128)(2,1)S(1)} async-done(((bf16[16,96,384]{2,1,0:T(8,128)(2,1)}), bf16[16,96,384]{2,1,0:T(8,128)(2,1)S(1)}, u32[]{:S(2)}, u32[]{:S(2)}) %all-to-all-start.7) | async-done | bytes 1179680 | tf_op jit(solution)/shard_map/all_to_all | solution.py:598
  513.6 12.0 %finish.1 = bf16[192,96,128]{2,1,0:T(8,128)(2,1)} custom-call(bf16[16,96,384]{2,1,0:T(8,128)(2,1)} %copy-done.3, bf16[16,96,384]{2,1,0:T(8,128)(2,1)} %copy-done.2, bf16[16,96,384]{2,1,0:T(8,128)(2,1)} %all-to-all-done.6.refs_2_, bf16[16,96,384]{2,1,0:T(8,128)(2,1)} %copy-done.7, bf16[192,96,128]{2,1,0:T(8,128)(2,1)} %get-tuple-element.49.refs_4_, ...), custom_call_target="tpu_custom_call" | custom-call | flops 1000 | bytes 1000 | tf_op jit(solution)/shard_map/finish/pallas_call | solution.py:467
  (141 shorter events, 58.0 us)
Async XLA Ops:
  7.2 427.7 %copy-start = (bf16[256,64]{0,1:T(8,128)(2,1)S(1)}, bf16[256,64]{0,1:T(8,128)(2,1)}, u32[]{:S(2)}) copy-start(bf16[256,64]{0,1:T(8,128)(2,1)} %param.17) | copy-start | bytes 98308
  7.2 15.4 %slice-start = ((bf16[128,640]{1,0:T(8,128)(2,1)}), bf16[128,512]{1,0:T(8,128)(2,1)S(1)}, s32[]{:S(2)}) async-start(bf16[128,640]{1,0:T(8,128)(2,1)} %param.18), calls=%async_computation.10 | async-start | bytes 262144 | tf_op jit(solution)/shard_map/slice | solution.py:570
  9.9 32.6 %copy-start.14 = (bf16[1024,128]{1,0:T(8,128)(2,1)S(1)}, bf16[1024,128]{1,0:T(8,128)(2,1)}, u32[]{:S(2)}) copy-start(bf16[1024,128]{1,0:T(8,128)(2,1)} %param.15) | copy-start | bytes 786436
  11.1 34.2 %copy-start.13 = (bf16[4,96,32]{2,1,0:T(8,128)(2,1)}, bf16[4,96,32]{2,1,0:T(8,128)(2,1)S(1)}, u32[]{:S(2)}) copy-start(bf16[4,96,32]{2,1,0:T(8,128)(2,1)S(1)} %get-tuple-element.64.refs_8_) | copy-start | bytes 73732
  11.1 12.4 %collective-permute-start = (bf16[4,96,32]{2,1,0:T(8,128)(2,1)S(1)}, bf16[4,96,32]{2,1,0:T(8,128)(2,1)S(1)}, u32[]{:S(2)}, u32[]{:S(2)}) collective-permute-start(bf16[4,96,32]{2,1,0:T(8,128)(2,1)S(1)} %get-tuple-element.65), channel_id=1, source_target_pairs={{0,0},{1,1},{2,8},{3,9},{4,16},{5,17},{6,24},{7,25},{8,2},{9,3},{1... | collective-permute-start | bytes 73736 | tf_op jit(solution)/shard_map/ppermute | solution.py:546
  11.8 14.5 %collective-permute-start.1 = (bf16[4,96,32]{2,1,0:T(8,128)(2,1)S(1)}, bf16[4,96,32]{2,1,0:T(8,128)(2,1)S(1)}, u32[]{:S(2)}, u32[]{:S(2)}) collective-permute-start(bf16[4,96,32]{2,1,0:T(8,128)(2,1)S(1)} %get-tuple-element.65), channel_id=1, source_target_pairs={{0,7},{1,0},{2,15},{3,8},{4,23},{5,16},{6,31},{7,24},{8,1},{9,2},{... | collective-permute-start | bytes 73736 | tf_op jit(solution)/shard_map/ppermute | solution.py:546
  19.4 8.5 %collective-permute-start.2 = (bf16[4,96,32]{2,1,0:T(8,128)(2,1)S(1)}, bf16[4,96,32]{2,1,0:T(8,128)(2,1)S(1)}, u32[]{:S(2)}, u32[]{:S(2)}) collective-permute-start(bf16[4,96,32]{2,1,0:T(8,128)(2,1)S(1)} %get-tuple-element.65), channel_id=1, source_target_pairs={{0,6},{1,7},{2,14},{3,15},{4,22},{5,23},{6,30},{7,31},{8,0},{9,1},... | collective-permute-start | bytes 73736 | tf_op jit(solution)/shard_map/ppermute | solution.py:546
  20.3 10.3 %collective-permute-start.3 = (bf16[4,96,32]{2,1,0:T(8,128)(2,1)S(1)}, bf16[4,96,32]{2,1,0:T(8,128)(2,1)S(1)}, u32[]{:S(2)}, u32[]{:S(2)}) collective-permute-start(bf16[4,96,32]{2,1,0:T(8,128)(2,1)S(1)} %get-tuple-element.65), channel_id=1, source_target_pairs={{0,5},{1,6},{2,13},{3,14},{4,21},{5,22},{6,29},{7,30},{8,7},{9,0},... | collective-permute-start | bytes 73736 | tf_op jit(solution)/shard_map/ppermute | solution.py:546
  22.0 13.2 %collective-permute-start.4 = (bf16[4,96,32]{2,1,0:T(8,128)(2,1)S(1)}, bf16[4,96,32]{2,1,0:T(8,128)(2,1)S(1)}, u32[]{:S(2)}, u32[]{:S(2)}) collective-permute-start(bf16[4,96,32]{2,1,0:T(8,128)(2,1)S(1)} %get-tuple-element.65), channel_id=1, source_target_pairs={{0,4},{1,5},{2,12},{3,13},{4,20},{5,21},{6,28},{7,29},{8,6},{9,7},... | collective-permute-start | bytes 73736 | tf_op jit(solution)/shard_map/ppermute | solution.py:546
  23.5 21.8 %copy-start.15 = (bf16[4,96,32]{2,1,0:T(8,128)(2,1)}, bf16[4,96,32]{2,1,0:T(8,128)(2,1)S(1)}, u32[]{:S(2)}) copy-start(bf16[4,96,32]{2,1,0:T(8,128)(2,1)S(1)} %collective-permute-done.refs_0_) | copy-start | bytes 73732
  23.5 14.4 %collective-permute-start.5 = (bf16[4,96,32]{2,1,0:T(8,128)(2,1)S(1)}, bf16[4,96,32]{2,1,0:T(8,128)(2,1)S(1)}, u32[]{:S(2)}, u32[]{:S(2)}) collective-permute-start(bf16[4,96,32]{2,1,0:T(8,128)(2,1)S(1)} %get-tuple-element.65), channel_id=1, source_target_pairs={{0,3},{1,4},{2,11},{3,12},{4,19},{5,20},{6,27},{7,28},{8,5},{9,6},... | collective-permute-start | bytes 73736 | tf_op jit(solution)/shard_map/ppermute | solution.py:546
  26.3 19.0 %copy-start.16 = (bf16[4,96,32]{2,1,0:T(8,128)(2,1)}, bf16[4,96,32]{2,1,0:T(8,128)(2,1)S(1)}, u32[]{:S(2)}) copy-start(bf16[4,96,32]{2,1,0:T(8,128)(2,1)S(1)} %collective-permute-done.1.refs_1_) | copy-start | bytes 73732
  26.3 18.4 %collective-permute-start.6 = (bf16[4,96,32]{2,1,0:T(8,128)(2,1)S(1)}, bf16[4,96,32]{2,1,0:T(8,128)(2,1)S(1)}, u32[]{:S(2)}, u32[]{:S(2)}) collective-permute-start(bf16[4,96,32]{2,1,0:T(8,128)(2,1)S(1)} %get-tuple-element.65), channel_id=1, source_target_pairs={{0,2},{1,3},{2,10},{3,11},{4,18},{5,19},{6,26},{7,27},{8,4},{9,5},... | collective-permute-start | bytes 73736 | tf_op jit(solution)/shard_map/ppermute | solution.py:546
  27.8 17.5 %copy-start.17 = (bf16[4,96,32]{2,1,0:T(8,128)(2,1)}, bf16[4,96,32]{2,1,0:T(8,128)(2,1)S(1)}, u32[]{:S(2)}) copy-start(bf16[4,96,32]{2,1,0:T(8,128)(2,1)S(1)} %collective-permute-done.2.refs_2_) | copy-start | bytes 73732
  27.8 16.8 %collective-permute-start.7 = (bf16[4,96,32]{2,1,0:T(8,128)(2,1)S(1)}, bf16[4,96,32]{2,1,0:T(8,128)(2,1)S(1)}, u32[]{:S(2)}, u32[]{:S(2)}) collective-permute-start(bf16[4,96,32]{2,1,0:T(8,128)(2,1)S(1)} %get-tuple-element.65), channel_id=1, source_target_pairs={{0,1},{1,2},{2,9},{3,10},{4,17},{5,18},{6,25},{7,26},{8,3},{9,4},{... | collective-permute-start | bytes 73736 | tf_op jit(solution)/shard_map/ppermute | solution.py:546
  30.5 14.8 %copy-start.18 = (bf16[4,96,32]{2,1,0:T(8,128)(2,1)}, bf16[4,96,32]{2,1,0:T(8,128)(2,1)S(1)}, u32[]{:S(2)}) copy-start(bf16[4,96,32]{2,1,0:T(8,128)(2,1)S(1)} %collective-permute-done.3.refs_3_) | copy-start | bytes 73732
  30.5 14.2 %collective-permute-start.8 = (bf16[4,96,32]{2,1,0:T(8,128)(2,1)S(1)}, bf16[4,96,32]{2,1,0:T(8,128)(2,1)S(1)}, u32[]{:S(2)}, u32[]{:S(2)}) collective-permute-start(bf16[4,96,32]{2,1,0:T(8,128)(2,1)S(1)} %get-tuple-element.64.refs_8_), channel_id=1, source_target_pairs={{0,24},{8,0},{16,8},{24,16},{1,25},{9,1},{17,9},{25,17},{2,26},{10... | collective-permute-start | bytes 73736 | tf_op jit(solution)/shard_map/ppermute | solution.py:550
  35.2 9.5 %collective-permute-start.9 = (bf16[4,96,32]{2,1,0:T(8,128)(2,1)S(1)}, bf16[4,96,32]{2,1,0:T(8,128)(2,1)S(1)}, u32[]{:S(2)}, u32[]{:S(2)}) collective-permute-start(bf16[4,96,32]{2,1,0:T(8,128)(2,1)S(1)} %get-tuple-element.64.refs_8_), channel_id=1, source_target_pairs={{0,16},{8,24},{16,0},{24,8},{1,17},{9,25},{17,1},{25,9},{2,18},{10... | collective-permute-start | bytes 73736 | tf_op jit(solution)/shard_map/ppermute | solution.py:550
  37.8 7.5 %collective-permute-start.10 = (bf16[4,96,32]{2,1,0:T(8,128)(2,1)S(1)}, bf16[4,96,32]{2,1,0:T(8,128)(2,1)S(1)}, u32[]{:S(2)}, u32[]{:S(2)}) collective-permute-start(bf16[4,96,32]{2,1,0:T(8,128)(2,1)S(1)} %get-tuple-element.64.refs_8_), channel_id=1, source_target_pairs={{0,8},{8,16},{16,24},{24,0},{1,9},{9,17},{17,25},{25,1},{2,10},{10... | collective-permute-start | bytes 73736 | tf_op jit(solution)/shard_map/ppermute | solution.py:550
  79.7 34.2 %all-to-all-start = ((bf16[16,192,384]{2,1,0:T(8,128)(2,1)}), bf16[16,192,384]{2,1,0:T(8,128)(2,1)S(1)}, u32[]{:S(2)}, u32[]{:S(2)}) async-start(bf16[16,192,384]{2,1,0:T(8,128)(2,1)} %project.4), calls=%async_computation | async-start | bytes 4718592 | tf_op jit(solution)/shard_map/all_to_all | solution.py:598
  120.7 60.6 %all-to-all-start.1 = ((bf16[16,192,384]{2,1,0:T(8,128)(2,1)}), bf16[16,192,384]{2,1,0:T(8,128)(2,1)S(1)}, u32[]{:S(2)}, u32[]{:S(2)}) async-start(bf16[16,192,384]{2,1,0:T(8,128)(2,1)} %get-tuple-element.30), calls=%async_computation.1 | async-start | bytes 4718592 | tf_op jit(solution)/shard_map/all_to_all | solution.py:598
  125.8 62.3 %collective-permute-start.11 = (bf16[2,768,384]{2,1,0:T(8,128)(2,1)}, bf16[2,768,384]{2,1,0:T(8,128)(2,1)}, u32[]{:S(2)}, u32[]{:S(2)}) collective-permute-start(bf16[2,768,384]{2,1,0:T(8,128)(2,1)} %get-tuple-element.32), channel_id=1, source_target_pairs={{0,4},{4,0},{1,5},{5,1},{2,6},{6,2},{3,7},{7,3},{8,12},{12,8},{9,1... | collective-permute-start | bytes 3538952 | tf_op jit(solution)/shard_map/ppermute | solution.py:616
  234.3 58.3 %all-to-all-start.3 = ((bf16[16,96,384]{2,1,0:T(8,128)(2,1)}), bf16[16,96,384]{2,1,0:T(8,128)(2,1)S(1)}, u32[]{:S(2)}, u32[]{:S(2)}) async-start(bf16[16,96,384]{2,1,0:T(8,128)(2,1)} %combine.4), calls=%async_computation.3 | async-start | bytes 2359296 | tf_op jit(solution)/shard_map/all_to_all | solution.py:598
  238.0 54.6 %collective-permute-start.12 = (bf16[2,768,384]{2,1,0:T(8,128)(2,1)}, bf16[2,768,384]{2,1,0:T(8,128)(2,1)S(1)}, u32[]{:S(2)}, u32[]{:S(2)}) collective-permute-start(bf16[2,768,384]{2,1,0:T(8,128)(2,1)} %get-tuple-element.39), channel_id=1, source_target_pairs={{0,4},{4,0},{1,5},{5,1},{2,6},{6,2},{3,7},{7,3},{8,12},{12,8},{9,1... | collective-permute-start | bytes 3538952 | tf_op jit(solution)/shard_map/ppermute | solution.py:616
  294.1 47.0 %all-to-all-start.4 = ((bf16[16,192,384]{2,1,0:T(8,128)(2,1)}), bf16[16,192,384]{2,1,0:T(8,128)(2,1)S(1)}, u32[]{:S(2)}, u32[]{:S(2)}) async-start(bf16[16,192,384]{2,1,0:T(8,128)(2,1)} %get-tuple-element.41), calls=%async_computation.4 | async-start | bytes 4718592 | tf_op jit(solution)/shard_map/all_to_all | solution.py:598
  298.1 126.6 %all-gather.3.cloned.1.call-start = ((), (), s32[]{:S(2)}) async-start(), calls=%async_computation.8 | async-start | bytes 1769472 | tf_op jit(solution)/shard_map/all_gather | solution.py:625
  298.8 128.5 %all-gather.5.cloned.1.call-start = ((), (), s32[]{:S(2)}) async-start(), calls=%async_computation.9 | async-start | bytes 3932160 | tf_op jit(solution)/shard_map/all_gather | solution.py:624
  354.1 58.3 %all-to-all-start.5 = ((bf16[16,96,384]{2,1,0:T(8,128)(2,1)}), bf16[16,96,384]{2,1,0:T(8,128)(2,1)S(1)}, u32[]{:S(2)}, u32[]{:S(2)}) async-start(bf16[16,96,384]{2,1,0:T(8,128)(2,1)} %combine.5), calls=%async_computation.5 | async-start | bytes 2359296 | tf_op jit(solution)/shard_map/all_to_all | solution.py:598
  357.8 54.6 %collective-permute-start.13 = (bf16[2,768,384]{2,1,0:T(8,128)(2,1)}, bf16[2,768,384]{2,1,0:T(8,128)(2,1)S(1)}, u32[]{:S(2)}, u32[]{:S(2)}) collective-permute-start(bf16[2,768,384]{2,1,0:T(8,128)(2,1)} %get-tuple-element.45), channel_id=1, source_target_pairs={{0,4},{4,0},{1,5},{5,1},{2,6},{6,2},{3,7},{7,3},{8,12},{12,8},{9,1... | collective-permute-start | bytes 3538952 | tf_op jit(solution)/shard_map/ppermute | solution.py:616
  420.1 70.7 %all-to-all-start.6 = ((bf16[16,96,384]{2,1,0:T(8,128)(2,1)}), bf16[16,96,384]{2,1,0:T(8,128)(2,1)}, u32[]{:S(2)}, u32[]{:S(2)}) async-start(bf16[16,96,384]{2,1,0:T(8,128)(2,1)} %combine.6), calls=%async_computation.6 | async-start | bytes 2359296 | tf_op jit(solution)/shard_map/all_to_all | solution.py:598
  430.2 54.5 %collective-permute-start.14 = (bf16[2,768,384]{2,1,0:T(8,128)(2,1)}, bf16[2,768,384]{2,1,0:T(8,128)(2,1)}, u32[]{:S(2)}, u32[]{:S(2)}) collective-permute-start(bf16[2,768,384]{2,1,0:T(8,128)(2,1)} %get-tuple-element.48), channel_id=1, source_target_pairs={{0,4},{4,0},{1,5},{5,1},{2,6},{6,2},{3,7},{7,3},{8,12},{12,8},{9,1... | collective-permute-start | bytes 3538952 | tf_op jit(solution)/shard_map/ppermute | solution.py:616
  490.8 21.8 %all-to-all-start.7 = ((bf16[16,96,384]{2,1,0:T(8,128)(2,1)}), bf16[16,96,384]{2,1,0:T(8,128)(2,1)S(1)}, u32[]{:S(2)}, u32[]{:S(2)}) async-start(bf16[16,96,384]{2,1,0:T(8,128)(2,1)} %combine.7), calls=%async_computation.7 | async-start | bytes 2359296 | tf_op jit(solution)/shard_map/all_to_all | solution.py:598
  (22 other events, 63.4 us)
Sparse Core Ops, SparseCore 0:
  300.5 33.6 all-gather.2
  336.0 54.7 all-gather.4

commit v5 on v4

--- a/solution.py
+++ b/solution.py
@@ -341,7 +341,7 @@
         ).astype(BF16)
 
 
-def assemble(half, received, row_count, pos_count, cols):
+def assemble(half, received, after, row_count, pos_count, cols):
     sources, height, lanes = received.shape
     each = (2 * pos_count * cols) // (row_count * QUAD)
     stride = height // each
@@ -351,7 +351,7 @@
     return pl.pallas_call(
         functools.partial(assemble_kernel, row_count=row_count, pos_count=pos_count),
         grid=(channels,),
-        in_specs=[pl.BlockSpec(memory_space=pltpu.SMEM), whole(received.shape)],
+        in_specs=[pl.BlockSpec(memory_space=pltpu.SMEM), whole(received.shape)] + anywhere(after),
         out_specs=[
             pl.BlockSpec((1, rows, depth), lambda c: (c, 0, 0)),
             pl.BlockSpec((1, depth, depth), lambda c: (c, 0, 0)),
@@ -369,7 +369,7 @@
         compiler_params=params(),
         cost_estimate=LIGHT,
         name="assemble",
-    )(half, received)
+    )(half, received, *after)
 
 
 def combine_kernel(left_ref, own_ref, recv_ref, *refs, row_count, pos_count):
@@ -483,7 +483,7 @@
 
 
 def chunk_sizes(channels):
-    each = min(2, channels)
+    each = min(4, channels)
     return [each] * (channels // each)
 
 
@@ -597,29 +597,14 @@
     def exchange(block):
         return lax.all_to_all(block, GROUP, split_axis=0, concat_axis=0, tiled=True)
 
-    stages = [assemble(half_scalar, exchange(send(0, ())), *shape_of)]
-    ahead = send(1, ()) if chunks > 1 else None
+    sent = send(0, ())
+    ahead = [send(1, ())] if chunks > 1 else []
+    stages = [assemble(half_scalar, exchange(sent), (logits, values, *ahead), *shape_of)]
     partials, returned = [], []
 
     def finish_chunk(g, partial, after):
         left, own, _ = stages[g]
         returned.append(exchange(combine(left, own, partial, after, *shape_of)))
-
-    for g in range(chunks):
-        carried = [stages[g][2]] + partials[g - 1 :][:1] * (g > 0)
-        if g + 1 < chunks:
-            carried.append(ahead)
-        after = returned[g - 2 : g - 1] if g > 1 else []
-        if g == 1:
-            after = [logits, values]
-        carried = fence(carried, after)
-        partials.append(lax.ppermute(carried[0], "half", swap))
-        if g + 1 < chunks:
-            stages.append(assemble(half_scalar, exchange(carried[-1]), *shape_of))
-        if g + 2 < chunks:
-            ahead = send(g + 2, (stages[g][0],))
-        if g > 0:
-            finish_chunk(g - 1, carried[1], tuple(stages[g + 1][:1]) if g + 1 < chunks else ())
 
     logits_all = lax.all_gather(logits, "row", axis=0, tiled=True)
     values_all = lax.all_gather(values, ("half", "pos"), axis=1, tiled=True)
@@ -637,7 +622,20 @@
     ).reshape(seq_each, module_number, -1)
     alignment_updated_embedding = (alignment_embedding.astype(F32) + blended_update).astype(BF16)
 
-    finish_chunk(chunks - 1, partials[-1], (alignment_updated_embedding,))
+    for g in range(chunks):
+        carried = [stages[g][2], *partials[g - 1 : g], *ahead]
+        after = returned[g - 2 : g - 1] if g > 1 else []
+        if g == 1:
+            after = [alignment_updated_embedding]
+        carried = fence(carried, after)
+        partials.append(lax.ppermute(carried[0], "half", swap))
+        if g + 1 < chunks:
+            stages.append(assemble(half_scalar, exchange(carried[-1]), (), *shape_of))
+            ahead = [send(g + 2, (stages[g][0],))] if g + 2 < chunks else []
+        if g > 0:
+            finish_chunk(g - 1, carried[1], tuple(stages[g + 1][:1]) if g + 1 < chunks else ())
+
+    finish_chunk(chunks - 1, partials[-1], (alignment_updated_embedding, *returned[-1:]))
     w_final = jnp.transpose(trimul_final_matrix.reshape(devices, -1, wide), (1, 0, 2))
     pair_output = finish(
         returned, pair_mid, pair_normed, trimul_matrices[:, 4 * CTRI :], w_final.reshape(-1, wide)

time: 535 us -> 535 us (level)
  waiting for transfers between devices: 263 us -> 333 us
  blocking collectives: 34.7 us -> 0 us
  Pallas kernels: 112 us -> 94.4 us
  starting transfers between devices: 62.1 us -> 50.4 us
  local copies, waits for them, and re-layouts: 27.9 us -> 21.4 us
    all_gather x1, waiting for transfers between devices: 0.02 us -> 115 us  [on_device(): values_all = lax.all_gather(values, ('half', 'pos'), axis=1, tiled=True)]
    ppermute x4 -> x2, waiting for transfers between devices: 149 us -> 103 us  [on_device(): partials.append(lax.ppermute(carried[0], 'half', swap))]
    all_gather x1, waiting for transfers between devices: 0.01 us -> 43.7 us  [on_device(): logits_all = lax.all_gather(logits, 'row', axis=0, tiled=True)]
    all_to_all x7 -> x4, waiting for transfers between devices: 113 us -> 70.5 us  [exchange(): return lax.all_to_all(block, GROUP, split_axis=0, concat_axis=0, tiled=True)]
    all_to_all x1 -> x0, blocking collectives: 34.7 us -> none  [exchange(): return lax.all_to_all(block, GROUP, split_axis=0, concat_axis=0, tiled=True)]
    pallas_call x4 -> x2, Pallas kernels: 26.7 us -> 14.7 us  [project(): pl.pallas_call(project_kernel, grid=(total // quads,), in_specs=[pl.Block...]
    all_to_all x7 -> x4, starting transfers between devices: 29 us -> 18.3 us  [exchange(): return lax.all_to_all(block, GROUP, split_axis=0, concat_axis=0, tiled=True)]
    unnamed x61 -> x49, local copies, waits for them, and re-layouts: 11.6 us -> 6.34 us
  transfers between devices with their start and end apart: 24 -> 19, of which waited for: 8 -> 6; matrix products, arithmetic and copies ran while one was open for 6% -> 6% of each run, Pallas kernels for 9% -> 3%
where the time goes in v5:
time: 535 us; the launch traced here: 532 us
  waiting for transfers between devices  333 us (62%)
  Pallas kernels  94.4 us (18%)
  starting transfers between devices  50.4 us (9%)
  local copies, waits for them, and re-layouts  21.4 us (4%)
  between operations  14.4 us (3%)
  matrix products  11.1 us (2%)
  other arithmetic  7.5 us (1%)
    all_gather x1, waiting for transfers between devices, on_device(): values_all = lax.all_gather(values, ('half', 'pos'), axis=1, tiled=True)  115 us
    ppermute x2, waiting for transfers between devices, on_device(): partials.append(lax.ppermute(carried[0], 'half', swap))  103 us
    all_to_all x4, waiting for transfers between devices, exchange(): return lax.all_to_all(block, GROUP, split_axis=0, concat_axis=0, tiled=True)  70.5 us
    all_gather x1, waiting for transfers between devices, on_device(): logits_all = lax.all_gather(logits, 'row', axis=0, tiled=True)  43.7 us
    pallas_call x1, Pallas kernels, front(): pl.pallas_call(functools.partial(front_kernel, row_count=len(rights), col...  27 us
    pallas_call x2, Pallas kernels, combine(): pl.pallas_call(functools.partial(combine_kernel, row_count=row_count, pos...  20.7 us
    pallas_call x2, Pallas kernels, assemble(): pl.pallas_call(functools.partial(assemble_kernel, row_count=row_count, po...  18.7 us
    all_to_all x4, starting transfers between devices, exchange(): return lax.all_to_all(block, GROUP, split_axis=0, concat_axis=0, tiled=True)  18.3 us
  transfers between devices with their start and end apart: 19, of which 6 were waited for; matrix products, arithmetic and copies ran while one was open for 6% of the time, Pallas kernels for 3%

profile of v5, /device:TPU:0, one launch (start us, length us, event | category | flops | bytes accessed | tf_op | source)
XLA Modules:
  0.0 532.5 jit_solution(8117696587711236103)
XLA Ops:
  12.5 7.6 %collective-permute-start.1 = (bf16[4,96,32]{2,1,0:T(8,128)(2,1)S(1)}, bf16[4,96,32]{2,1,0:T(8,128)(2,1)S(1)}, u32[]{:S(2)}, u32[]{:S(2)}) collective-permute-start(bf16[4,96,32]{2,1,0:T(8,128)(2,1)S(1)} %get-tuple-element.39), channel_id=1, source_target_pairs={{0,7},{1,0},{2,15},{3,8},{4,23},{5,16},{6,31},{7,24},{8,1},{9,2},{... | collective-permute-start | bytes 73736 | tf_op jit(solution)/shard_map/ppermute | solution.py:546
  21.0 1.7 collective-permute-start.3
  24.1 2.2 collective-permute-start.5
  26.9 1.6 collective-permute-start.6
  28.5 2.7 collective-permute-start.7
  31.2 4.7 collective-permute-start.8
  35.9 2.6 collective-permute-start.9
  38.5 3.4 collective-permute-start.10
  46.8 27.0 %front.1 = (bf16[192,96,128]{2,1,0:T(8,128)(2,1)}, bf16[192,96,128]{2,1,0:T(8,128)(2,1)}) custom-call(s32[2]{0:T(128)} %pad_add_fusion.place_ref, bf16[4,96,32]{2,1,0:T(8,128)(2,1)} %copy-done.9, bf16[4,96,32]{2,1,0:T(8,128)(2,1)} %copy-done.10, bf16[4,96,32]{2,1,0:T(8,128)(2,1)} %copy-done.11, bf16[4,96,32]{2,1,0:T(8,128)(2,1)} %copy-done.12, ...), custom_call_target="tpu_custom_call" | custom-call | flops 1000 | bytes 1000 | tf_op jit(solution)/shard_map/front/pallas_call | solution.py:180
  73.8 7.3 %project.2 = bf16[16,384,384]{2,1,0:T(8,128)(2,1)} custom-call(f32[192]{0:T(256)} %get-tuple-element.35.live_ref, bf16[192,96,128]{2,1,0:T(8,128)(2,1)} %get-tuple-element.14.normed_ref.refs_3_, f32[1,384]{1,0:T(1,128)} %broadcast_in_dim.7.cols_ref, bf16[256,128]{1,0:T(8,128)(2,1)} %bitcast.46), custom_call_target="tpu_custom_call" | custom-call | flops 1000 | bytes 1000 | tf_op jit(solution)/shard_map/project/pallas_call | solution.py:257
  81.2 4.7 all-to-all-start
  87.5 7.4 %project.3.refs_2_.refs_1_ = bf16[16,384,384]{2,1,0:T(8,128)(2,1)} custom-call(f32[192]{0:T(256)} %get-tuple-element.35.live_ref, bf16[192,96,128]{2,1,0:T(8,128)(2,1)} %get-tuple-element.14.normed_ref.refs_3_, f32[1,384]{1,0:T(1,128)} %broadcast_in_dim.7.cols_ref, bf16[256,128]{1,0:T(8,128)(2,1)} %bitcast.47), custom_call_target="tpu_custom_call" | custom-call | flops 1000 | bytes 1000 | tf_op jit(solution)/shard_map/project/pallas_call | solution.py:257
  94.9 7.4 %broadcast_add_fusion.refs_0_ = f32[192,96,8]{2,1,0:T(8,128)} fusion(f32[192]{0:T(256)S(1)} %get-tuple-element.34, bf16[192,96,128]{2,1,0:T(8,128)(2,1)} %get-tuple-element.14.normed_ref.refs_3_, bf16[128,8]{0,1:T(8,128)(2,1)S(1)} %copy-done.22), kind=kOutput, calls=%fused_computation | convolution fusion | flops 37896192 | bytes 5311232 | tf_op jit(solution)/shard_map/dot_general | solution.py:581
  102.3 41.9 %all-to-all-done.recv_ref = bf16[16,384,384]{2,1,0:T(8,128)(2,1)} async-done(((bf16[16,384,384]{2,1,0:T(8,128)(2,1)}), bf16[16,384,384]{2,1,0:T(8,128)(2,1)}, u32[]{:S(2)}, u32[]{:S(2)}) %all-to-all-start) | async-done | bytes 4718624 | tf_op jit(solution)/shard_map/all_to_all | solution.py:598
  144.2 9.3 %assemble.2 = (bf16[4,768,384]{2,1,0:T(8,128)(2,1)}, bf16[4,384,384]{2,1,0:T(8,128)(2,1)}, bf16[4,768,384]{2,1,0:T(8,128)(2,1)}) custom-call(s32[1]{0:T(128)} %bitcast.12.half_ref, bf16[16,384,384]{2,1,0:T(8,128)(2,1)} %all-to-all-done.recv_ref, f32[192,96,8]{2,1,0:T(8,128)} %broadcast_add_fusion.refs_0_, ...), custom_call_target="tpu_custom_call" | custom-call | flops 1000 | bytes 1000 | tf_op jit(solution)/shard_map/assemble/pallas_call | solution.py:351
  153.5 5.7 %all-to-all-start.1 = ((bf16[16,384,384]{2,1,0:T(8,128)(2,1)}), bf16[16,384,384]{2,1,0:T(8,128)(2,1)}, u32[]{:S(2)}, u32[]{:S(2)}) async-start(bf16[16,384,384]{2,1,0:T(8,128)(2,1)} %get-tuple-element.18), calls=%async_computation.1 | async-start | bytes 9437184 | tf_op jit(solution)/shard_map/all_to_all | solution.py:598
  160.2 6.3 %copy.92 = f32[192,96,8]{1,2,0:T(8,128)} copy(f32[192,96,8]{2,1,0:T(8,128)} %broadcast_add_fusion.refs_0_) | data formatting | bytes 1179648 | tf_op jit(solution)/shard_map/add | solution.py:581
  167.2 115.0 %all-gather.3.cloned.1.call-done = bf16[4,768,256]{2,1,0:T(8,128)(2,1)} async-done(((bf16[4,96,256]{2,1,0:T(8,128)(2,1)}), bf16[4,768,256]{2,1,0:T(8,128)(2,1)}) %all-gather.3.cloned.1.call-update) | async-done | bytes 1572880 | tf_op jit(solution)/shard_map/all_gather | solution.py:610
  282.3 2.6 copy.83
  284.8 43.7 %all-gather.5.cloned.1.call-done = f32[768,96,8]{1,2,0:T(8,128)} async-done(((f32[192,96,8]{1,2,0:T(8,128)}), f32[768,96,8]{1,2,0:T(8,128)}) %all-gather.5.cloned.1.call-update) | async-done | bytes 2359312 | tf_op jit(solution)/shard_map/all_gather | solution.py:609
  328.5 2.9 reduce_max.9
  335.6 9.4 %assemble.3 = (bf16[4,768,384]{2,1,0:T(8,128)(2,1)}, bf16[4,384,384]{2,1,0:T(8,128)(2,1)}, bf16[4,768,384]{2,1,0:T(8,128)(2,1)}) custom-call(s32[1]{0:T(128)} %bitcast.12.half_ref, bf16[16,384,384]{2,1,0:T(8,128)(2,1)} %all-to-all-done.1.recv_ref), custom_call_target="tpu_custom_call" | custom-call | flops 1000 | bytes 1000 | tf_op jit(solution)/shard_map/assemble/pallas_call | solution.py:351
  345.0 10.4 %combine.2 = bf16[16,192,384]{2,1,0:T(8,128)(2,1)} custom-call(bf16[4,768,384]{2,1,0:T(8,128)(2,1)} %get-tuple-element.15.left_ref, bf16[4,384,384]{2,1,0:T(8,128)(2,1)} %get-tuple-element.16.own_ref, bf16[4,768,384]{2,1,0:T(8,128)(2,1)} %get-tuple-element.21.recv_ref), custom_call_target="tpu_custom_call" | custom-call | flops 1000 | bytes 1000 | tf_op jit(solution)/shard_map/combine/pallas_call | solution.py:410
  355.3 3.8 all-to-all-start.2
  359.1 2.5 collective-permute-start.12
  361.6 102.9 %collective-permute-done.12.recv_ref = bf16[4,768,384]{2,1,0:T(8,128)(2,1)} collective-permute-done((bf16[4,768,384]{2,1,0:T(8,128)(2,1)}, bf16[4,768,384]{2,1,0:T(8,128)(2,1)}, u32[]{:S(2)}, u32[]{:S(2)}) %collective-permute-start.12) | collective-permute-done | bytes 2359328 | tf_op jit(solution)/shard_map/ppermute | solution.py:631
  464.5 1.4 copy-done.2
  466.0 10.3 %combine.3 = bf16[16,192,384]{2,1,0:T(8,128)(2,1)} custom-call(bf16[4,768,384]{2,1,0:T(8,128)(2,1)} %get-tuple-element.22.left_ref, bf16[4,384,384]{2,1,0:T(8,128)(2,1)} %get-tuple-element.23.own_ref, bf16[4,768,384]{2,1,0:T(8,128)(2,1)} %collective-permute-done.12.recv_ref, bf16[4,96,64]{2,1,0:T(8,128)(2,1)} %fusion.17.refs_2_.refs_0_, ...), custom_call_target="tpu_custom_call" | custom-call | flops 1000 | bytes 1000 | tf_op jit(solution)/shard_map/combine/pallas_call | solution.py:410
  476.3 4.1 all-to-all-start.3
  482.4 28.5 %all-to-all-done.3.refs_1_ = bf16[16,192,384]{2,1,0:T(8,128)(2,1)S(1)} async-done(((bf16[16,192,384]{2,1,0:T(8,128)(2,1)}), bf16[16,192,384]{2,1,0:T(8,128)(2,1)S(1)}, u32[]{:S(2)}, u32[]{:S(2)}) %all-to-all-start.3) | async-done | bytes 2359328 | tf_op jit(solution)/shard_map/all_to_all | solution.py:598
  510.9 1.4 copy-done.3
  512.3 13.3 %finish.1 = bf16[192,96,128]{2,1,0:T(8,128)(2,1)} custom-call(bf16[16,192,384]{2,1,0:T(8,128)(2,1)} %copy-done.2, bf16[16,192,384]{2,1,0:T(8,128)(2,1)} %copy-done.3, bf16[192,96,128]{2,1,0:T(8,128)(2,1)} %get-tuple-element.25.refs_2_, bf16[192,96,128]{2,1,0:T(8,128)(2,1)} %get-tuple-element.14.normed_ref.refs_3_, bf16[128,128]{1,0:T(8,128)(2,1)} %slice.44.refs_4_, ...), custom_call_target="tpu_custom_call" | custom-call | flops 1000 | bytes 1000 | tf_op jit(solution)/shard_map/finish/pallas_call | solution.py:467
  (108 shorter events, 22.4 us)
Async XLA Ops:
  7.2 327.3 %copy-start = (bf16[256,64]{0,1:T(8,128)(2,1)S(1)}, bf16[256,64]{0,1:T(8,128)(2,1)}, u32[]{:S(2)}) copy-start(bf16[256,64]{0,1:T(8,128)(2,1)} %param.17) | copy-start | bytes 98308
  7.2 16.1 %slice-start = ((bf16[128,640]{1,0:T(8,128)(2,1)}), bf16[128,512]{1,0:T(8,128)(2,1)S(1)}, s32[]{:S(2)}) async-start(bf16[128,640]{1,0:T(8,128)(2,1)} %param.18), calls=%async_computation.6 | async-start | bytes 262144 | tf_op jit(solution)/shard_map/slice | solution.py:570
  7.2 36.0 %copy-start.8 = (bf16[1024,128]{1,0:T(8,128)(2,1)S(1)}, bf16[1024,128]{1,0:T(8,128)(2,1)}, u32[]{:S(2)}) copy-start(bf16[1024,128]{1,0:T(8,128)(2,1)} %param.15) | copy-start | bytes 786436
  11.8 34.2 %copy-start.7 = (bf16[4,96,32]{2,1,0:T(8,128)(2,1)}, bf16[4,96,32]{2,1,0:T(8,128)(2,1)S(1)}, u32[]{:S(2)}) copy-start(bf16[4,96,32]{2,1,0:T(8,128)(2,1)S(1)} %get-tuple-element.38.refs_8_) | copy-start | bytes 73732
  11.8 12.3 %collective-permute-start = (bf16[4,96,32]{2,1,0:T(8,128)(2,1)S(1)}, bf16[4,96,32]{2,1,0:T(8,128)(2,1)S(1)}, u32[]{:S(2)}, u32[]{:S(2)}) collective-permute-start(bf16[4,96,32]{2,1,0:T(8,128)(2,1)S(1)} %get-tuple-element.39), channel_id=1, source_target_pairs={{0,0},{1,1},{2,8},{3,9},{4,16},{5,17},{6,24},{7,25},{8,2},{9,3},{1... | collective-permute-start | bytes 73736 | tf_op jit(solution)/shard_map/ppermute | solution.py:546
  12.5 14.4 %collective-permute-start.1 = (bf16[4,96,32]{2,1,0:T(8,128)(2,1)S(1)}, bf16[4,96,32]{2,1,0:T(8,128)(2,1)S(1)}, u32[]{:S(2)}, u32[]{:S(2)}) collective-permute-start(bf16[4,96,32]{2,1,0:T(8,128)(2,1)S(1)} %get-tuple-element.39), channel_id=1, source_target_pairs={{0,7},{1,0},{2,15},{3,8},{4,23},{5,16},{6,31},{7,24},{8,1},{9,2},{... | collective-permute-start | bytes 73736 | tf_op jit(solution)/shard_map/ppermute | solution.py:546
  20.1 8.4 %collective-permute-start.2 = (bf16[4,96,32]{2,1,0:T(8,128)(2,1)S(1)}, bf16[4,96,32]{2,1,0:T(8,128)(2,1)S(1)}, u32[]{:S(2)}, u32[]{:S(2)}) collective-permute-start(bf16[4,96,32]{2,1,0:T(8,128)(2,1)S(1)} %get-tuple-element.39), channel_id=1, source_target_pairs={{0,6},{1,7},{2,14},{3,15},{4,22},{5,23},{6,30},{7,31},{8,0},{9,1},... | collective-permute-start | bytes 73736 | tf_op jit(solution)/shard_map/ppermute | solution.py:546
  21.0 10.2 %collective-permute-start.3 = (bf16[4,96,32]{2,1,0:T(8,128)(2,1)S(1)}, bf16[4,96,32]{2,1,0:T(8,128)(2,1)S(1)}, u32[]{:S(2)}, u32[]{:S(2)}) collective-permute-start(bf16[4,96,32]{2,1,0:T(8,128)(2,1)S(1)} %get-tuple-element.39), channel_id=1, source_target_pairs={{0,5},{1,6},{2,13},{3,14},{4,21},{5,22},{6,29},{7,30},{8,7},{9,0},... | collective-permute-start | bytes 73736 | tf_op jit(solution)/shard_map/ppermute | solution.py:546
  22.7 13.2 %collective-permute-start.4 = (bf16[4,96,32]{2,1,0:T(8,128)(2,1)S(1)}, bf16[4,96,32]{2,1,0:T(8,128)(2,1)S(1)}, u32[]{:S(2)}, u32[]{:S(2)}) collective-permute-start(bf16[4,96,32]{2,1,0:T(8,128)(2,1)S(1)} %get-tuple-element.39), channel_id=1, source_target_pairs={{0,4},{1,5},{2,12},{3,13},{4,20},{5,21},{6,28},{7,29},{8,6},{9,7},... | collective-permute-start | bytes 73736 | tf_op jit(solution)/shard_map/ppermute | solution.py:546
  24.1 21.9 %copy-start.9 = (bf16[4,96,32]{2,1,0:T(8,128)(2,1)}, bf16[4,96,32]{2,1,0:T(8,128)(2,1)S(1)}, u32[]{:S(2)}) copy-start(bf16[4,96,32]{2,1,0:T(8,128)(2,1)S(1)} %collective-permute-done.refs_0_) | copy-start | bytes 73732
  24.1 14.4 %collective-permute-start.5 = (bf16[4,96,32]{2,1,0:T(8,128)(2,1)S(1)}, bf16[4,96,32]{2,1,0:T(8,128)(2,1)S(1)}, u32[]{:S(2)}, u32[]{:S(2)}) collective-permute-start(bf16[4,96,32]{2,1,0:T(8,128)(2,1)S(1)} %get-tuple-element.39), channel_id=1, source_target_pairs={{0,3},{1,4},{2,11},{3,12},{4,19},{5,20},{6,27},{7,28},{8,5},{9,6},... | collective-permute-start | bytes 73736 | tf_op jit(solution)/shard_map/ppermute | solution.py:546
  26.9 19.1 %copy-start.10 = (bf16[4,96,32]{2,1,0:T(8,128)(2,1)}, bf16[4,96,32]{2,1,0:T(8,128)(2,1)S(1)}, u32[]{:S(2)}) copy-start(bf16[4,96,32]{2,1,0:T(8,128)(2,1)S(1)} %collective-permute-done.1.refs_1_) | copy-start | bytes 73732
  26.9 18.5 %collective-permute-start.6 = (bf16[4,96,32]{2,1,0:T(8,128)(2,1)S(1)}, bf16[4,96,32]{2,1,0:T(8,128)(2,1)S(1)}, u32[]{:S(2)}, u32[]{:S(2)}) collective-permute-start(bf16[4,96,32]{2,1,0:T(8,128)(2,1)S(1)} %get-tuple-element.39), channel_id=1, source_target_pairs={{0,2},{1,3},{2,10},{3,11},{4,18},{5,19},{6,26},{7,27},{8,4},{9,5},... | collective-permute-start | bytes 73736 | tf_op jit(solution)/shard_map/ppermute | solution.py:546
  28.5 17.5 %copy-start.11 = (bf16[4,96,32]{2,1,0:T(8,128)(2,1)}, bf16[4,96,32]{2,1,0:T(8,128)(2,1)S(1)}, u32[]{:S(2)}) copy-start(bf16[4,96,32]{2,1,0:T(8,128)(2,1)S(1)} %collective-permute-done.2.refs_2_) | copy-start | bytes 73732
  28.5 16.9 %collective-permute-start.7 = (bf16[4,96,32]{2,1,0:T(8,128)(2,1)S(1)}, bf16[4,96,32]{2,1,0:T(8,128)(2,1)S(1)}, u32[]{:S(2)}, u32[]{:S(2)}) collective-permute-start(bf16[4,96,32]{2,1,0:T(8,128)(2,1)S(1)} %get-tuple-element.39), channel_id=1, source_target_pairs={{0,1},{1,2},{2,9},{3,10},{4,17},{5,18},{6,25},{7,26},{8,3},{9,4},{... | collective-permute-start | bytes 73736 | tf_op jit(solution)/shard_map/ppermute | solution.py:546
  31.2 14.8 %copy-start.12 = (bf16[4,96,32]{2,1,0:T(8,128)(2,1)}, bf16[4,96,32]{2,1,0:T(8,128)(2,1)S(1)}, u32[]{:S(2)}) copy-start(bf16[4,96,32]{2,1,0:T(8,128)(2,1)S(1)} %collective-permute-done.3.refs_3_) | copy-start | bytes 73732
  31.2 14.2 %collective-permute-start.8 = (bf16[4,96,32]{2,1,0:T(8,128)(2,1)S(1)}, bf16[4,96,32]{2,1,0:T(8,128)(2,1)S(1)}, u32[]{:S(2)}, u32[]{:S(2)}) collective-permute-start(bf16[4,96,32]{2,1,0:T(8,128)(2,1)S(1)} %get-tuple-element.38.refs_8_), channel_id=1, source_target_pairs={{0,24},{8,0},{16,8},{24,16},{1,25},{9,1},{17,9},{25,17},{2,26},{10... | collective-permute-start | bytes 73736 | tf_op jit(solution)/shard_map/ppermute | solution.py:550
  35.9 10.1 %copy-start.13 = (bf16[4,96,32]{2,1,0:T(8,128)(2,1)}, bf16[4,96,32]{2,1,0:T(8,128)(2,1)S(1)}, u32[]{:S(2)}) copy-start(bf16[4,96,32]{2,1,0:T(8,128)(2,1)S(1)} %collective-permute-done.4.refs_4_) | copy-start | bytes 73732
  35.9 9.5 %collective-permute-start.9 = (bf16[4,96,32]{2,1,0:T(8,128)(2,1)S(1)}, bf16[4,96,32]{2,1,0:T(8,128)(2,1)S(1)}, u32[]{:S(2)}, u32[]{:S(2)}) collective-permute-start(bf16[4,96,32]{2,1,0:T(8,128)(2,1)S(1)} %get-tuple-element.38.refs_8_), channel_id=1, source_target_pairs={{0,16},{8,24},{16,0},{24,8},{1,17},{9,25},{17,1},{25,9},{2,18},{10... | collective-permute-start | bytes 73736 | tf_op jit(solution)/shard_map/ppermute | solution.py:550
  38.5 7.5 %copy-start.14 = (bf16[4,96,32]{2,1,0:T(8,128)(2,1)}, bf16[4,96,32]{2,1,0:T(8,128)(2,1)S(1)}, u32[]{:S(2)}) copy-start(bf16[4,96,32]{2,1,0:T(8,128)(2,1)S(1)} %collective-permute-done.5.refs_5_) | copy-start | bytes 73732
  38.5 7.5 %collective-permute-start.10 = (bf16[4,96,32]{2,1,0:T(8,128)(2,1)S(1)}, bf16[4,96,32]{2,1,0:T(8,128)(2,1)S(1)}, u32[]{:S(2)}, u32[]{:S(2)}) collective-permute-start(bf16[4,96,32]{2,1,0:T(8,128)(2,1)S(1)} %get-tuple-element.38.refs_8_), channel_id=1, source_target_pairs={{0,8},{8,16},{16,24},{24,0},{1,9},{9,17},{17,25},{25,1},{2,10},{10... | collective-permute-start | bytes 73736 | tf_op jit(solution)/shard_map/ppermute | solution.py:550
  81.2 5.4 %copy-start.21 = (bf16[64,576]{1,0:T(8,128)(2,1)S(1)}, bf16[64,576]{1,0:T(8,128)(2,1)}, u32[]{:S(2)}) copy-start(bf16[64,576]{1,0:T(8,128)(2,1)} %param.14) | copy-start | bytes 221188
  81.2 63.0 %all-to-all-start = ((bf16[16,384,384]{2,1,0:T(8,128)(2,1)}), bf16[16,384,384]{2,1,0:T(8,128)(2,1)}, u32[]{:S(2)}, u32[]{:S(2)}) async-start(bf16[16,384,384]{2,1,0:T(8,128)(2,1)} %project.2), calls=%async_computation | async-start | bytes 9437184 | tf_op jit(solution)/shard_map/all_to_all | solution.py:598
  87.5 7.4 %copy-start.22 = (bf16[128,8]{0,1:T(8,128)(2,1)S(1)}, bf16[128,8]{0,1:T(8,128)(2,1)}, u32[]{:S(2)}) copy-start(bf16[128,8]{0,1:T(8,128)(2,1)} %param.16) | copy-start | bytes 6148
  153.5 182.1 %all-to-all-start.1 = ((bf16[16,384,384]{2,1,0:T(8,128)(2,1)}), bf16[16,384,384]{2,1,0:T(8,128)(2,1)}, u32[]{:S(2)}, u32[]{:S(2)}) async-start(bf16[16,384,384]{2,1,0:T(8,128)(2,1)} %get-tuple-element.18), calls=%async_computation.1 | async-start | bytes 9437184 | tf_op jit(solution)/shard_map/all_to_all | solution.py:598
  159.2 123.0 %all-gather.3.cloned.1.call-start = ((), (), s32[]{:S(2)}) async-start(), calls=%async_computation.4 | async-start | bytes 1769472 | tf_op jit(solution)/shard_map/all_gather | solution.py:610
  160.0 168.5 %all-gather.5.cloned.1.call-start = ((), (), s32[]{:S(2)}) async-start(), calls=%async_computation.5 | async-start | bytes 3932160 | tf_op jit(solution)/shard_map/all_gather | solution.py:609
  166.5 178.4 %collective-permute-start.11 = (bf16[4,768,384]{2,1,0:T(8,128)(2,1)}, bf16[4,768,384]{2,1,0:T(8,128)(2,1)}, u32[]{:S(2)}, u32[]{:S(2)}) collective-permute-start(bf16[4,768,384]{2,1,0:T(8,128)(2,1)} %get-tuple-element.20), channel_id=1, source_target_pairs={{0,4},{4,0},{1,5},{5,1},{2,6},{6,2},{3,7},{7,3},{8,12},{12,8},{9,1... | collective-permute-start | bytes 7077896 | tf_op jit(solution)/shard_map/ppermute | solution.py:631
  355.3 109.2 %all-to-all-start.2 = ((bf16[16,192,384]{2,1,0:T(8,128)(2,1)}), bf16[16,192,384]{2,1,0:T(8,128)(2,1)S(1)}, u32[]{:S(2)}, u32[]{:S(2)}) async-start(bf16[16,192,384]{2,1,0:T(8,128)(2,1)} %combine.2), calls=%async_computation.2 | async-start | bytes 4718592 | tf_op jit(solution)/shard_map/all_to_all | solution.py:598
  359.1 105.4 %collective-permute-start.12 = (bf16[4,768,384]{2,1,0:T(8,128)(2,1)}, bf16[4,768,384]{2,1,0:T(8,128)(2,1)}, u32[]{:S(2)}, u32[]{:S(2)}) collective-permute-start(bf16[4,768,384]{2,1,0:T(8,128)(2,1)} %get-tuple-element.24), channel_id=1, source_target_pairs={{0,4},{4,0},{1,5},{5,1},{2,6},{6,2},{3,7},{7,3},{8,12},{12,8},{9,1... | collective-permute-start | bytes 7077896 | tf_op jit(solution)/shard_map/ppermute | solution.py:631
  476.3 5.3 %copy-start.5 = (bf16[4,96,64]{2,1,0:T(8,128)(2,1)S(1)}, bf16[4,96,64]{2,1,0:T(8,128)(2,1)}, u32[]{:S(2)}) copy-start(bf16[4,96,64]{2,1,0:T(8,128)(2,1)} %fusion.17.refs_2_.refs_0_) | copy-start | bytes 147460
  476.3 34.6 %all-to-all-start.3 = ((bf16[16,192,384]{2,1,0:T(8,128)(2,1)}), bf16[16,192,384]{2,1,0:T(8,128)(2,1)S(1)}, u32[]{:S(2)}, u32[]{:S(2)}) async-start(bf16[16,192,384]{2,1,0:T(8,128)(2,1)} %combine.3), calls=%async_computation.3 | async-start | bytes 4718592 | tf_op jit(solution)/shard_map/all_to_all | solution.py:598
  (11 other events, 19.3 us)
Sparse Core Ops, SparseCore 0:
  161.7 120.5 all-gather.2
  284.1 44.3 all-gather.4

commit v6 on v5

v6 whole, which is shorter than its diff:
```python
import functools

import jax
import jax.numpy as jnp
from jax import lax
from jax.experimental import pallas as pl
from jax.experimental.pallas import tpu as pltpu
from jax.sharding import Mesh, PartitionSpec as P

TENSOR_FEATURES = 32
MEAN_GROUPS = 8
GROUP_FEATURES = 32
CTRI = 128

EPS = 1e-05
MASK_PENALTY = 10000.0
QUAD = 4
LANES = 128
MIB = 1024 * 1024
AXES = ("row", "half", "pos")
GROUP = ("row", "pos")
F32 = jnp.float32
BF16 = jnp.bfloat16
NT = (((1,), (1,)), ((), ()))
TN = (((0,), (0,)), ((), ()))


def standardize_features(values_in, axis):
    centre = values_in - jnp.mean(values_in, axis=axis, keepdims=True)
    spread = jnp.mean(centre * centre, axis=axis, keepdims=True)
    return centre * lax.rsqrt(spread + EPS)


def sigmoid(x):
    return 0.5 * jnp.tanh(0.5 * x) + 0.5


def params():
    return pltpu.CompilerParams(
        vmem_limit_bytes=60 * MIB, dimension_semantics=("arbitrary",)
    )


LIGHT = pl.CostEstimate(flops=1000, bytes_accessed=1000, transcendentals=0)


def whole(shape):
    zeros = (0,) * len(shape)
    return pl.BlockSpec(shape, lambda *_: zeros, pipeline_mode=pl.Buffered(1))


def anywhere(after):
    return [pl.BlockSpec(memory_space=pl.ANY)] * len(after)


def fence(values, after):
    return pl.pallas_call(
        lambda *refs: None,
        in_specs=anywhere(values) + anywhere(after),
        out_specs=anywhere(values),
        out_shape=[jax.ShapeDtypeStruct(v.shape, v.dtype) for v in values],
        input_output_aliases={i: i for i in range(len(values))},
        compiler_params=pltpu.CompilerParams(vmem_limit_bytes=60 * MIB),
        cost_estimate=LIGHT,
        name="fence",
    )(*values, *after)


def pack_rows(rows):
    unit = rows[0].shape[0] // 3
    return jnp.concatenate([r[: 2 * unit] for r in rows] + [r[2 * unit :] for r in rows], axis=0)


def unpack_rows(packed):
    unit = packed.shape[0] // 12
    return [
        jnp.concatenate(
            [
                packed[2 * unit * a : 2 * unit * (a + 1)],
                packed[8 * unit + unit * a : 8 * unit + unit * (a + 1)],
            ],
            axis=0,
        )
        for a in range(QUAD)
    ]


def swap_blocks(first, second, width, lane):
    low = (lane // width) % 2 == 0
    size = first.shape[1]
    return (
        jnp.where(low, first, pltpu.roll(second, width, 1)),
        jnp.where(low, pltpu.roll(first, size - width, 1), second),
    )


def exchange_blocks(packed):
    part = packed
    unit = LANES // 4
    lane = lax.broadcasted_iota(jnp.int32, part[0][0].shape, 1)
    out = [[None] * 3 for _ in range(4)]
    for pair in range(2):
        one, two = part[2 * pair], part[2 * pair + 1]
        for t in range(2):
            out[2 * t][pair], out[2 * t + 1][pair] = swap_blocks(one[t], two[t], 2 * unit, lane)
    u0, u2 = swap_blocks(part[0][2], part[2][2], 2 * unit, lane)
    u1, u3 = swap_blocks(part[1][2], part[3][2], 2 * unit, lane)
    out[0][2], out[1][2] = swap_blocks(u0, u1, unit, lane)
    out[2][2], out[3][2] = swap_blocks(u2, u3, unit, lane)
    return out


def front_kernel(place_ref, *refs, row_count, col_count, first_block):
    lefts, rights = refs[:col_count], refs[col_count : col_count + row_count]
    refs = refs[col_count + row_count :]
    prow_ref, coup_ref, weight_ref, pcol_ref = refs[:4]
    sides_ref, right_ref, tmp_ref = refs[-3:]
    mid_ref, normed_ref = refs[-5:-3]
    step_at = pl.program_id(0) + first_block
    block, cols, wide = coup_ref.shape
    seq_each, _, width = lefts[0].shape
    seqs = seq_each * row_count
    per_row = col_count // row_count

    @pl.when(pl.program_id(0) == 0)
    def _():
        for t, part in enumerate(lefts):
            index = lax.rem(t + place_ref[1], col_count)
            first = lax.rem(index, per_row) * (cols * seqs) + index // per_row * seq_each
            for k in range(seq_each):
                sides_ref[pl.ds(first + k, cols, stride=seqs), 0:width] = part[k].astype(F32)
        right = jnp.zeros(right_ref.shape, F32)
        feature = lax.broadcasted_iota(jnp.int32, (width, width * seqs), 0)
        target = lax.broadcasted_iota(jnp.int32, (width, width * seqs), 1)
        for t, part in enumerate(rights):
            first = lax.rem(t + place_ref[0], row_count) * seq_each
            for k in range(seq_each):
                spread = (target == feature * seqs + (first + k)).astype(F32).astype(BF16)
                right += jnp.dot(part[k], spread, preferred_element_type=F32)
        right_ref[...] = right.astype(BF16)

    span = block * seqs
    start = pl.multiple_of(step_at * span, span)
    left = sides_ref[pl.ds(start, span), 0:width].astype(BF16)
    features = weight_ref.shape[1] // wide
    step = 4
    for low in range(0, features, step):
        part = jnp.dot(
            left, weight_ref[:, low * wide : (low + step) * wide], preferred_element_type=F32
        ).astype(BF16)
        for i in range(block):
            for d in range(step):
                tmp_ref[
                    i // 2,
                    (low + d) * seqs : (low + d + 1) * seqs,
                    (i % 2) * wide : (i % 2 + 1) * wide,
                ] = part[i * seqs : (i + 1) * seqs, d * wide : (d + 1) * wide]
    row_lane = lax.broadcasted_iota(jnp.int32, prow_ref.shape, 1)
    for pair in range(block // 2):
        update = jnp.dot(right_ref[...], tmp_ref[pair], preferred_element_type=F32)
        here = step_at * block + 2 * pair
        wanted = [jnp.where(row_lane == here + e, prow_ref[...], 0.0) for e in range(2)]
        wanted = [
            jnp.broadcast_to(jnp.sum(w, axis=1, keepdims=True), (seqs, wide)) for w in wanted
        ]
        count = jnp.dot(
            pcol_ref[...], jnp.concatenate(wanted, axis=1).astype(BF16), preferred_element_type=F32
        )
        update = update / jnp.maximum(count, 1.0)
        for e in range(2):
            i = 2 * pair + e
            mid = (coup_ref[i].astype(F32) + update[:, e * wide : (e + 1) * wide]).astype(BF16)
            mid_ref[i] = mid
            normed_ref[i] = standardize_features(mid.astype(F32), 1).astype(BF16)


def front(chunk, chunks, place, lefts, rights, present_rows, coupling, w_tensor, present_cols, after):
    rows, cols, wide = coupling.shape
    seqs, width = present_rows.shape[0], lefts[0].shape[2]
    block = 8
    steps = rows // block // chunks
    tile = pl.BlockSpec((block, cols, wide), lambda i: (i, 0, 0))
    return pl.pallas_call(
        functools.partial(
            front_kernel,
            row_count=len(rights),
            col_count=len(lefts),
            first_block=chunk * steps,
        ),
        grid=(steps,),
        in_specs=[pl.BlockSpec(memory_space=pltpu.SMEM)]
        + [whole(part.shape) for part in lefts + rights]
        + [
            whole(present_rows.shape),
            pl.BlockSpec((block, cols, wide), lambda i: (i + chunk * steps, 0, 0)),
            whole(w_tensor.shape),
            whole(present_cols.shape),
        ]
        + anywhere(after),
        out_specs=[tile, tile],
        out_shape=[jax.ShapeDtypeStruct((rows // chunks, cols, wide), BF16)] * 2,
        scratch_shapes=[
            pltpu.VMEM((rows * seqs, LANES), F32),
            pltpu.VMEM((cols, width * seqs), BF16),
            pltpu.VMEM((block // 2, width * seqs, 2 * wide), BF16),
        ],
        compiler_params=params(),
        cost_estimate=LIGHT,
        name="front",
    )(place, *lefts, *rights, present_rows, coupling, w_tensor, present_cols, *after)


def exchange_rows(values):
    values = list(values)
    count = len(values)
    step = count // 2
    row = lax.broadcasted_iota(jnp.int32, values[0].shape, 0)
    size = values[0].shape[0]
    while step:
        width = 8 // count * step
        low = (row // width) % 2 == 0
        for m in range(count):
            if m & step == 0:
                one, two = values[m], values[m + step]
                values[m] = jnp.where(low, one, pltpu.roll(two, width, 0))
                values[m + step] = jnp.where(low, pltpu.roll(one, size - width, 0), two)
        step //= 2
    return values


def project_kernel(live_ref, normed_ref, cols_ref, weight_ref, *refs, first_row):
    out_ref, tmp_ref = refs[-2:]
    quads = normed_ref.shape[0] // QUAD
    dests, height, lanes = out_ref.shape
    each = height // quads
    count = dests * each
    unit = lanes // 12
    lane = lax.broadcasted_iota(jnp.int32, (1, lanes), 1)
    place = jnp.where(lane < 8 * unit, lane // (2 * unit), (lane - 8 * unit) // unit)
    group = max(1, 8 // each)
    for first in range(0, quads, group):
        values = []
        for m in range(first, first + group):
            packed = pack_rows([normed_ref[QUAD * m + a] for a in range(QUAD)])
            both = lax.dot_general(weight_ref[...], packed, NT, preferred_element_type=F32)
            row = first_row + (pl.program_id(0) * quads + m) * QUAD
            live = cols_ref[...]
            for a in range(QUAD):
                live = jnp.where(place == a, live * live_ref[row + a], live)
            values.append(sigmoid(both[:count]) * both[count:] * live)
        for b, value in enumerate(exchange_rows(values)):
            size = each * group
            for v in range(count // size):
                tmp_ref[v * group + b, first * each : first * each + size] = value[
                    v * size : (v + 1) * size
                ]
    out_ref[...] = tmp_ref[...].astype(BF16)


def project(first_row, live_rows, normed, live_cols, weight, dests):
    rows, cols, wide = normed.shape
    each = weight.shape[0] // (2 * dests)
    quads = max(8, 16 // each)
    lanes = QUAD * cols
    total = rows // QUAD
    return pl.pallas_call(
        functools.partial(project_kernel, first_row=first_row),
        grid=(total // quads,),
        in_specs=[
            pl.BlockSpec(memory_space=pltpu.SMEM),
            pl.BlockSpec((quads * QUAD, cols, wide), lambda i: (i, 0, 0)),
            whole(live_cols.shape),
            whole(weight.shape),
        ],
        out_specs=pl.BlockSpec((dests, quads * each, lanes), lambda i: (0, i, 0)),
        out_shape=jax.ShapeDtypeStruct((dests, total * each, lanes), BF16),
        scratch_shapes=[pltpu.VMEM((dests, quads * each, lanes), F32)],
        compiler_params=params(),
        cost_estimate=LIGHT,
        name="project",
    )(live_rows, normed, live_cols, weight)


def logit_kernel(live_ref, normed_ref, weight_ref, out_ref, *, first_row):
    block = normed_ref.shape[0]
    for i in range(block):
        live = live_ref[first_row + pl.program_id(0) * block + i]
        out_ref[i] = lax.dot_general(
            weight_ref[...], normed_ref[i], NT, preferred_element_type=F32
        ) + MASK_PENALTY * (live - 1.0)


def logit(first_row, live_rows, normed, weight):
    rows, cols, wide = normed.shape
    block = 16
    heads = weight.shape[0]
    return pl.pallas_call(
        functools.partial(logit_kernel, first_row=first_row),
        grid=(rows // block,),
        in_specs=[
            pl.BlockSpec(memory_space=pltpu.SMEM),
            pl.BlockSpec((block, cols, wide), lambda i: (i, 0, 0)),
            whole(weight.shape),
        ],
        out_specs=pl.BlockSpec((block, heads, cols), lambda i: (i, 0, 0)),
        out_shape=jax.ShapeDtypeStruct((rows, heads, cols), F32),
        compiler_params=params(),
        cost_estimate=LIGHT,
        name="logit",
    )(live_rows, normed, weight)


def assemble_kernel(recv_ref, *refs, row_count, pos_count):
    left_ref, right_ref, flat_ref, rows_ref = refs[-4:]
    channel = pl.program_id(0)
    lanes = recv_ref.shape[2]
    each = left_ref.shape[2]
    stride = recv_ref.shape[1] // each
    groups = pos_count // 4
    tiles = lanes // LANES

    @pl.when(channel == 0)
    def _():
        for src in range(row_count * pos_count):
            value = recv_ref[src].astype(F32)
            for t in range(tiles):
                flat_ref[src, t] = value[:, t * LANES : (t + 1) * LANES]

    def block(row, group, index):
        packed = []
        for p in range(4):
            src = row * pos_count + group * 4 + p
            packed.append(
                [flat_ref[src, t, pl.ds(index, each, stride=stride), :] for t in range(tiles)]
            )
        return exchange_blocks(packed)

    for row in range(row_count):
        for group in range(groups):
            span = slice(group * lanes, (group + 1) * lanes)
            left = block(row, group, channel)
            right = block(row, group, channel + stride // 2)
            for a in range(QUAD):
                left_ref[0, row * QUAD + a, :, span] = jnp.concatenate(left[a], axis=1).astype(BF16)
                for t in range(tiles):
                    rows_ref[t, pl.ds(a, each, stride=QUAD), :] = right[a][t]
            for t in range(tiles):
                at = slice(group * lanes + t * LANES, group * lanes + (t + 1) * LANES)
                right_ref[0, row, 0, :, at] = rows_ref[t].astype(BF16)


def assemble(chunk, chunks, received, sides, row_count, pos_count, cols):
    sources, height, lanes = received.shape
    depth = pos_count * cols
    each = depth // (row_count * QUAD * chunks)
    channels = height // each // 2
    blocks = row_count * QUAD
    shapes = [
        (channels, blocks, each * chunks, depth),
        (channels, row_count, chunks, QUAD * each, depth),
    ]
    return pl.pallas_call(
        functools.partial(assemble_kernel, row_count=row_count, pos_count=pos_count),
        grid=(channels,),
        in_specs=[whole(received.shape)] + anywhere(sides),
        out_specs=[
            pl.BlockSpec((1, blocks, each, depth), lambda c: (c, 0, chunk, 0)),
            pl.BlockSpec((1, row_count, 1, QUAD * each, depth), lambda c: (c, 0, chunk, 0, 0)),
        ],
        out_shape=[jax.ShapeDtypeStruct(shape, BF16) for shape in shapes],
        input_output_aliases={1: 0, 2: 1} if sides else {},
        scratch_shapes=[
            pltpu.VMEM((sources, lanes // LANES, height, LANES), F32),
            pltpu.VMEM((lanes // LANES, QUAD * each, LANES), F32),
        ],
        compiler_params=params(),
        cost_estimate=LIGHT,
        name="assemble",
    )(received, *sides)


def multiply_kernel(left_ref, right_ref, *refs, pos_count):
    out_ref, tmp_ref = refs[-2:]
    channel = pl.program_id(0)
    channels = pl.num_programs(0)
    lanes = out_ref.shape[2]
    _, blocks, each, depth = left_ref.shape
    row_count = blocks // QUAD
    unit = lanes // 12
    stride = out_ref.shape[1] // each
    tiles = lanes // LANES
    for group in range(pos_count // 4):
        starts = [(group * 4 + p) * 3 * unit for p in range(4)]
        wanted = jnp.concatenate(
            [right_ref[0, start : start + 2 * unit] for start in starts]
            + [right_ref[0, start + 2 * unit : start + 3 * unit] for start in starts],
            axis=0,
        )
        for row in range(row_count):
            left = left_ref[0, row * QUAD : (row + 1) * QUAD].reshape(QUAD * each, depth)
            value = lax.dot_general(left, wanted, NT, preferred_element_type=F32)
            packed = [
                [
                    value[a * each : (a + 1) * each, t * LANES : (t + 1) * LANES]
                    for t in range(tiles)
                ]
                for a in range(QUAD)
            ]
            for p, part in enumerate(exchange_blocks(packed)):
                dest = row * pos_count + group * 4 + p
                for t in range(tiles):
                    tmp_ref[dest, t, pl.ds(channel, each, stride=stride), :] = part[t]

    @pl.when(channel == channels - 1)
    def _():
        for dest in range(row_count * pos_count):
            for t in range(tiles):
                out_ref[dest, :, t * LANES : (t + 1) * LANES] = tmp_ref[dest, t].astype(BF16)


def multiply(first, count, left, right, after, pos_count, cols):
    _, blocks, each, depth = left.shape
    lanes = QUAD * cols
    shape = (blocks // QUAD * pos_count, each * count, lanes)
    return pl.pallas_call(
        functools.partial(multiply_kernel, pos_count=pos_count),
        grid=(count,),
        in_specs=[
            pl.BlockSpec((1, blocks, each, depth), lambda c: (c + first, 0, 0, 0)),
            pl.BlockSpec((1, depth, depth), lambda c: (c + first, 0, 0)),
        ]
        + anywhere(after),
        out_specs=whole(shape),
        out_shape=jax.ShapeDtypeStruct(shape, BF16),
        scratch_shapes=[pltpu.VMEM((shape[0], lanes // LANES, shape[1], LANES), F32)],
        compiler_params=params(),
        cost_estimate=LIGHT,
        name="multiply",
    )(left, right, *after)


def finish_kernel(*refs, parts, chunks):
    products = refs[:parts]
    mids = refs[parts : parts + chunks]
    normeds = refs[parts + chunks : parts + 2 * chunks]
    gate_ref, weight_ref, out_ref = refs[parts + 2 * chunks : parts + 2 * chunks + 3]
    flat = refs[parts + 2 * chunks + 3 :]
    quads = out_ref.shape[0] // QUAD
    sources, _, lanes = products[0].shape
    tiles = range(lanes // LANES)
    for product, tmp in zip(products, flat):
        height = product.shape[1]
        for src in range(sources):
            value = product[src].astype(F32)
            for t in tiles:
                tmp[t, src * height : (src + 1) * height] = value[:, t * LANES : (t + 1) * LANES]

    def rows(mid_ref, normed_ref):
        for m in range(quads):
            pieces = []
            for product, tmp in zip(products, flat):
                height = product.shape[1]
                each = height // quads
                for k in range(each):
                    pieces.append(
                        jnp.concatenate(
                            [tmp[t, pl.ds(m * each + k, sources, stride=height), :] for t in tiles],
                            axis=1,
                        )
                    )
            normed = standardize_features(jnp.concatenate(pieces, axis=0), 0).astype(BF16)
            out = lax.dot_general(normed, weight_ref[...], TN, preferred_element_type=F32)
            for a, value in enumerate(unpack_rows(out)):
                i = QUAD * m + a
                gate = sigmoid(jnp.dot(normed_ref[i], gate_ref[...], preferred_element_type=F32))
                out_ref[i] = (mid_ref[i].astype(F32) + gate * value).astype(BF16)

    steps = pl.num_programs(0) // chunks
    for chunk in range(chunks):
        pl.when(pl.program_id(0) // steps == chunk)(
            functools.partial(rows, mids[chunk], normeds[chunk])
        )


def finish(products, mids, normeds, w_gate, w_final):
    rows, cols, wide = mids[0].shape
    chunks = len(mids)
    sources, _, lanes = products[0].shape
    total = rows * chunks // QUAD
    heights = [part.shape[1] // total for part in products]
    quads = max(8, 16 // min(heights))
    steps = rows // QUAD // quads

    def tile(chunk):
        return pl.BlockSpec(
            (quads * QUAD, cols, wide),
            lambda i: (jnp.clip(i - chunk * steps, 0, steps - 1), 0, 0),
        )

    tiles = [tile(chunk) for chunk in range(chunks)]
    return pl.pallas_call(
        functools.partial(finish_kernel, parts=len(products), chunks=chunks),
        grid=(total // quads,),
        in_specs=[
            pl.BlockSpec((sources, quads * each, lanes), lambda i: (0, i, 0)) for each in heights
        ]
        + tiles * 2
        + [whole(w_gate.shape), whole(w_final.shape)],
        out_specs=pl.BlockSpec((quads * QUAD, cols, wide), lambda i: (i, 0, 0)),
        out_shape=jax.ShapeDtypeStruct((rows * chunks, cols, wide), BF16),
        scratch_shapes=[
            pltpu.VMEM((lanes // LANES, sources * quads * each, LANES), F32) for each in heights
        ],
        compiler_params=params(),
        cost_estimate=LIGHT,
        name="finish",
    )(*products, *mids, *normeds, w_gate, w_final)


def chunk_sizes(channels):
    each = min(2, channels)
    return [each] * (channels // each)


def on_device(
    alignment_embedding,
    coupling_embedding,
    amino_validity,
    alignment_validity,
    alignment_matrix,
    tensor_final_matrix,
    coupling_logit_matrix,
    mean_final_matrix,
    trimul_matrices,
    trimul_final_matrix,
):
    seq_each, module_number, feature_count = alignment_embedding.shape
    rows, _, wide = coupling_embedding.shape
    row_count = lax.axis_size("row")
    pos_count = lax.axis_size("pos")
    col_count = 2 * pos_count
    row_index = lax.axis_index("row")
    half = lax.axis_index("half")
    col_index = half * pos_count + lax.axis_index("pos")
    seqs = seq_each * row_count
    active_entries = amino_validity.astype(F32)
    sequence_index = lax.broadcasted_iota(jnp.int32, alignment_validity.shape, 0)
    present_entries = (
        jnp.where(sequence_index == 0, F32(1.0), alignment_validity.astype(F32))
        * active_entries[None, :]
    )
    row_start = row_index * rows
    col_start = col_index * module_number
    present_rows = lax.dynamic_slice_in_dim(present_entries, row_start, rows, 1)
    present_cols = lax.dynamic_slice_in_dim(present_entries, col_start, module_number, 1)
    live_rows = lax.dynamic_slice_in_dim(active_entries, row_start, rows, 0)
    live_cols = lax.dynamic_slice_in_dim(active_entries, col_start, module_number, 0)

    own_start = (row_index * seq_each, col_start)
    present_own = lax.dynamic_slice(present_entries, own_start, (seq_each, module_number))
    own_normed = standardize_features(alignment_embedding.astype(F32), 2).astype(BF16)
    own_normed = own_normed.reshape(seq_each * module_number, feature_count)

    def project_msa(matrix):
        return jnp.dot(own_normed, matrix, preferred_element_type=F32).reshape(
            seq_each, module_number, -1
        )

    own_sides = project_msa(alignment_matrix[:, : 2 * TENSOR_FEATURES])
    own_sides = (own_sides * present_own[:, :, None]).astype(BF16)
    own_left = own_sides[:, :, :TENSOR_FEATURES]
    own_right = own_sides[:, :, TENSOR_FEATURES:]
    per_row = rows // module_number
    lefts = []
    for t in range(col_count):
        pairs = []
        for r in range(row_count):
            for q in range(col_count):
                to = (r * per_row + q % per_row - t) % col_count
                pairs.append((r * col_count + q, q // per_row * col_count + to))
        lefts.append(lax.ppermute(own_left, AXES, pairs))
    rights = [own_right]
    for t in range(1, row_count):
        pairs = [(r, (r - t) % row_count) for r in range(row_count)]
        rights.append(lax.ppermute(own_right, "row", pairs))

    w_tensor = tensor_final_matrix.reshape(TENSOR_FEATURES, TENSOR_FEATURES * wide)
    unit = module_number // 3
    live_packed = jnp.concatenate(
        [live_cols[: 2 * unit]] * QUAD + [live_cols[2 * unit :]] * QUAD
    )[None]
    devices = row_count * col_count
    channels = CTRI // devices
    w_kinds = trimul_matrices[:, : 4 * CTRI].T.reshape(2, 2, devices, channels, wide)
    w_sides = jnp.transpose(w_kinds, (1, 2, 0, 3, 4)).reshape(-1, wide)
    w_logit = coupling_logit_matrix.T

    def exchange(block):
        return lax.all_to_all(block, AXES, split_axis=0, concat_axis=0, tiled=True)

    shape_of = (row_count, col_count, module_number)
    row_chunks = rows // QUAD // 16
    mids, normeds, logits = [], [], []
    sent, sides = (), ()
    for chunk in range(row_chunks):
        mid, normed = front(
            chunk,
            row_chunks,
            jnp.stack([row_index, col_index]).astype(jnp.int32),
            lefts,
            rights,
            present_rows,
            coupling_embedding,
            w_tensor,
            present_cols.T.astype(BF16),
            sent,
        )
        first_row = chunk * (rows // row_chunks)
        block = project(first_row, live_rows, normed, live_packed, w_sides, devices)
        sent = (block,)
        sides = assemble(chunk, row_chunks, exchange(block), sides, *shape_of)
        logits.append(logit(first_row, live_rows, normed, w_logit))
        mids.append(mid)
        normeds.append(normed)

    values = project_msa(
        alignment_matrix[:, 2 * TENSOR_FEATURES : 2 * TENSOR_FEATURES + MEAN_GROUPS * GROUP_FEATURES]
    ).astype(BF16)
    sequence_gate = jax.nn.sigmoid(
        project_msa(alignment_matrix[:, 2 * TENSOR_FEATURES + MEAN_GROUPS * GROUP_FEATURES :])
    )
    logits_all = lax.all_gather(jnp.concatenate(logits, axis=0), "row", axis=0, tiled=True)
    values_all = lax.all_gather(values, ("half", "pos"), axis=1, tiled=True)

    left, right = sides
    right = right.reshape(channels, -1, right.shape[-1])
    returned, first, after = [], 0, ()
    for count in chunk_sizes(channels):
        product = multiply(first, count, left, right, after, *shape_of[1:])
        returned.append(exchange(product))
        after = (product,)
        first += count
    logits_all, values_all = fence([logits_all, values_all], after)
    top_all = jnp.max(logits_all, axis=0)
    expd = jnp.exp(logits_all - top_all[None])
    weights_all = (expd / jnp.sum(expd, axis=0)[None]).astype(BF16)
    value_all_heads = values_all.reshape(seq_each, -1, MEAN_GROUPS, GROUP_FEATURES)
    summed = jnp.einsum("jhi,sjhd->sihd", weights_all, value_all_heads, preferred_element_type=F32)
    head_averaged = summed.reshape(seq_each, module_number, MEAN_GROUPS * GROUP_FEATURES)
    gated_result = (sequence_gate * head_averaged).astype(BF16)
    blended_update = jnp.dot(
        gated_result.reshape(seq_each * module_number, -1),
        mean_final_matrix,
        preferred_element_type=F32,
    ).reshape(seq_each, module_number, -1)
    alignment_updated_embedding = (alignment_embedding.astype(F32) + blended_update).astype(BF16)

    w_final = jnp.transpose(trimul_final_matrix.reshape(devices, -1, wide), (1, 0, 2))
    pair_output = finish(
        returned, mids, normeds, trimul_matrices[:, 4 * CTRI :], w_final.reshape(-1, wide)
    )
    return (alignment_updated_embedding, pair_output)


def solution(mesh):
    rows, cols = mesh.devices.shape
    inner = Mesh(mesh.devices.reshape(rows, 2, cols // 2), AXES)
    tile = P("row", ("half", "pos"), None)
    in_specs = (tile, tile) + (P(),) * 8
    return jax.shard_map(
        on_device, mesh=inner, in_specs=in_specs, out_specs=(tile, tile), check_vma=False
    )
```

time: 535 us -> 470 us (0.88)
  waiting for transfers between devices: 333 us -> 269 us
  Pallas kernels: 94.4 us -> 112 us
  matrix products: 11.1 us -> 3.71 us
  local copies, waits for them, and re-layouts: 21.4 us -> 15.6 us
    all_to_all x4 -> x5, waiting for transfers between devices: 70.5 us -> 229 us  [exchange(): return lax.all_to_all(block, AXES, split_axis=0, concat_axis=0, tiled=True)]
    all_gather x1, waiting for transfers between devices: 115 us -> 0.01 us  [on_device(): values_all = lax.all_gather(values, ('half', 'pos'), axis=1, tiled=True)]
    ppermute x2 -> x0, waiting for transfers between devices: 103 us -> none  [on_device(): partials.append(lax.ppermute(carried[0], 'half', swap))]
    pallas_call x2 -> x3, Pallas kernels: 18.7 us -> 26.2 us  [assemble(): pl.pallas_call(functools.partial(assemble_kernel, row_count=row_count, po...]
    dot_general x2 -> x1, matrix products: 7.99 us -> 0.62 us  [on_device(): jnp.einsum('jhi,sjhd->sihd', weights_all, value_all_heads, preferred_elem...]
    pallas_call x1 -> x3, Pallas kernels: 27 us -> 34.2 us  [front(): pl.pallas_call(functools.partial(front_kernel, row_count=len(rights), col...]
    add x1 -> x0, local copies, waits for them, and re-layouts: 6.3 us -> none  [on_device(): jnp.dot(pair_normed.reshape(rows * module_number, wide), coupling_logit_m...]
    pallas_call x5 -> x9, Pallas kernels: 48.7 us -> 51.6 us  [the longest x2 14 us: multiply(): pl.pallas_call(functools.partial(multiply_kernel, pos_count=pos_count), g...]
  transfers between devices with their start and end apart: 19 -> 18, of which waited for: 6 -> 6; matrix products, arithmetic and copies ran while one was open for 6% -> 4% of each run, Pallas kernels for 3% -> 13%
where the time goes in v6:
time: 470 us; the launch traced here: 469 us
  waiting for transfers between devices  269 us (57%)
  Pallas kernels  112 us (24%)
  starting transfers between devices  46 us (10%)
  local copies, waits for them, and re-layouts  15.6 us (3%)
  between operations  14.4 us (3%)
  other arithmetic  8.26 us (2%)
    all_to_all x5, waiting for transfers between devices, exchange(): return lax.all_to_all(block, AXES, split_axis=0, concat_axis=0, tiled=True)  229 us
    all_gather x1, waiting for transfers between devices, on_device(): lax.all_gather(jnp.concatenate(logits, axis=0), 'row', axis=0, tiled=True)  39.7 us
    pallas_call x3, Pallas kernels, front(): pl.pallas_call(functools.partial(front_kernel, row_count=len(rights), col...  34.2 us
    pallas_call x3, Pallas kernels, assemble(): pl.pallas_call(functools.partial(assemble_kernel, row_count=row_count, po...  26.2 us
    ppermute x8, starting transfers between devices, on_device(): lefts.append(lax.ppermute(own_left, AXES, pairs))  18.8 us
    all_to_all x5, starting transfers between devices, exchange(): return lax.all_to_all(block, AXES, split_axis=0, concat_axis=0, tiled=True)  16 us
    pallas_call x2, Pallas kernels, multiply(): pl.pallas_call(functools.partial(multiply_kernel, pos_count=pos_count), g...  14 us
    pallas_call x3, Pallas kernels, project(): pl.pallas_call(functools.partial(project_kernel, first_row=first_row), gr...  13 us
  transfers between devices with their start and end apart: 18, of which 6 were waited for; matrix products, arithmetic and copies ran while one was open for 4% of the time, Pallas kernels for 13%

profile of v6, /device:TPU:0, one launch (start us, length us, event | category | flops | bytes accessed | tf_op | source)
XLA Modules:
  0.0 468.6 jit_solution(15761589879021128786)
XLA Ops:
  12.9 7.6 %collective-permute-start.1 = (bf16[4,96,32]{2,1,0:T(8,128)(2,1)S(1)}, bf16[4,96,32]{2,1,0:T(8,128)(2,1)S(1)}, u32[]{:S(2)}, u32[]{:S(2)}) collective-permute-start(bf16[4,96,32]{2,1,0:T(8,128)(2,1)S(1)} %get-tuple-element.31), channel_id=1, source_target_pairs={{0,7},{1,0},{2,15},{3,8},{4,23},{5,16},{6,31},{7,24},{8,1},{9,2},{... | collective-permute-start | bytes 73736 | tf_op jit(solution)/shard_map/ppermute | solution.py:581
  23.8 2.2 collective-permute-start.5
  28.5 3.2 collective-permute-start.7
  31.7 5.8 %collective-permute-start.10 = (bf16[4,96,32]{2,1,0:T(8,128)(2,1)S(1)}, bf16[4,96,32]{2,1,0:T(8,128)(2,1)S(1)}, u32[]{:S(2)}, u32[]{:S(2)}) collective-permute-start(bf16[4,96,32]{2,1,0:T(8,128)(2,1)S(1)} %get-tuple-element.30.refs_8_), channel_id=1, source_target_pairs={{0,8},{8,16},{16,24},{24,0},{1,9},{9,17},{17,25},{25,1},{2,10},{10... | collective-permute-start | bytes 73736 | tf_op jit(solution)/shard_map/ppermute | solution.py:585
  37.6 5.3 %collective-permute-start.9 = (bf16[4,96,32]{2,1,0:T(8,128)(2,1)S(1)}, bf16[4,96,32]{2,1,0:T(8,128)(2,1)S(1)}, u32[]{:S(2)}, u32[]{:S(2)}) collective-permute-start(bf16[4,96,32]{2,1,0:T(8,128)(2,1)S(1)} %get-tuple-element.30.refs_8_), channel_id=1, source_target_pairs={{0,16},{8,24},{16,0},{24,8},{1,17},{9,25},{17,1},{25,9},{2,18},{10... | collective-permute-start | bytes 73736 | tf_op jit(solution)/shard_map/ppermute | solution.py:585
  49.6 11.3 %front.3 = (bf16[64,96,128]{2,1,0:T(8,128)(2,1)}, bf16[64,96,128]{2,1,0:T(8,128)(2,1)}) custom-call(s32[2]{0:T(128)} %pad_add_fusion.place_ref, bf16[4,96,32]{2,1,0:T(8,128)(2,1)} %copy-done.8, bf16[4,96,32]{2,1,0:T(8,128)(2,1)} %copy-done.9, bf16[4,96,32]{2,1,0:T(8,128)(2,1)} %copy-done.10, bf16[4,96,32]{2,1,0:T(8,128)(2,1)} %copy-done.11, ...), custom_call_target="tpu_custom_call" | custom-call | flops 1000 | bytes 1000 | tf_op jit(solution)/shard_map/front/pallas_call | solution.py:183
  60.9 4.3 project.3.refs_16_
  65.2 2.8 all-to-all-start.2
  68.0 11.4 %front.4 = (bf16[64,96,128]{2,1,0:T(8,128)(2,1)}, bf16[64,96,128]{2,1,0:T(8,128)(2,1)}) custom-call(s32[2]{0:T(128)} %pad_add_fusion.place_ref, bf16[4,96,32]{2,1,0:T(8,128)(2,1)} %copy-done.8, bf16[4,96,32]{2,1,0:T(8,128)(2,1)} %copy-done.9, bf16[4,96,32]{2,1,0:T(8,128)(2,1)} %copy-done.10, bf16[4,96,32]{2,1,0:T(8,128)(2,1)} %copy-done.11, ...), custom_call_target="tpu_custom_call" | custom-call | flops 1000 | bytes 1000 | tf_op jit(solution)/shard_map/front/pallas_call | solution.py:183
  79.4 4.3 project.4.refs_16_
  83.7 56.9 %all-to-all-done.2.recv_ref = bf16[32,128,384]{2,1,0:T(8,128)(2,1)S(1)} async-done(((bf16[32,128,384]{2,1,0:T(8,128)(2,1)}), bf16[32,128,384]{2,1,0:T(8,128)(2,1)S(1)}, u32[]{:S(2)}, u32[]{:S(2)}) %all-to-all-start.2) | async-done | bytes 3145760 | tf_op jit(solution)/shard_map/all_to_all | solution.py:599
  142.4 3.6 all-to-all-start.1
  145.9 11.4 %front.5 = (bf16[64,96,128]{2,1,0:T(8,128)(2,1)}, bf16[64,96,128]{2,1,0:T(8,128)(2,1)}) custom-call(s32[2]{0:T(128)} %pad_add_fusion.place_ref, bf16[4,96,32]{2,1,0:T(8,128)(2,1)} %copy-done.8, bf16[4,96,32]{2,1,0:T(8,128)(2,1)} %copy-done.9, bf16[4,96,32]{2,1,0:T(8,128)(2,1)} %copy-done.10, bf16[4,96,32]{2,1,0:T(8,128)(2,1)} %copy-done.11, ...), custom_call_target="tpu_custom_call" | custom-call | flops 1000 | bytes 1000 | tf_op jit(solution)/shard_map/front/pallas_call | solution.py:183
  157.3 4.4 project.5
  161.8 56.8 %all-to-all-done.1.recv_ref = bf16[32,128,384]{2,1,0:T(8,128)(2,1)} async-done(((bf16[32,128,384]{2,1,0:T(8,128)(2,1)}), bf16[32,128,384]{2,1,0:T(8,128)(2,1)}, u32[]{:S(2)}, u32[]{:S(2)}) %all-to-all-start.1) | async-done | bytes 3145760 | tf_op jit(solution)/shard_map/all_to_all | solution.py:599
  218.6 3.0 all-to-all-start
  221.5 8.8 %assemble.3 = (bf16[4,16,48,768]{3,2,1,0:T(8,128)(2,1)}, bf16[4,4,3,64,768]{4,3,2,1,0:T(8,128)(2,1)}) custom-call(bf16[32,128,384]{2,1,0:T(8,128)(2,1)} %copy-done.2), custom_call_target="tpu_custom_call" | custom-call | flops 1000 | bytes 1000 | tf_op jit(solution)/shard_map/assemble/pallas_call | solution.py:362
  230.3 8.7 %assemble.4 = (bf16[4,16,48,768]{3,2,1,0:T(8,128)(2,1)}, bf16[4,4,3,64,768]{4,3,2,1,0:T(8,128)(2,1)}) custom-call(bf16[32,128,384]{2,1,0:T(8,128)(2,1)} %all-to-all-done.1.recv_ref, bf16[4,16,48,768]{3,2,1,0:T(8,128)(2,1)} %get-tuple-element.19.refs_0_, ...), custom_call_target="tpu_custom_call", output_to_operand_aliasing={{0}: (1, {}), {1}: (2, {})} | custom-call | flops 1000 | bytes 1000 | tf_op jit(solution)/shard_map/assemble/pallas_call | solution.py:362
  239.0 55.0 %all-to-all-done.recv_ref = bf16[32,128,384]{2,1,0:T(8,128)(2,1)S(1)} async-done(((bf16[32,128,384]{2,1,0:T(8,128)(2,1)}), bf16[32,128,384]{2,1,0:T(8,128)(2,1)S(1)}, u32[]{:S(2)}, u32[]{:S(2)}) %all-to-all-start) | async-done | bytes 3145760 | tf_op jit(solution)/shard_map/all_to_all | solution.py:599
  295.7 8.7 %assemble.5 = (bf16[4,16,48,768]{3,2,1,0:T(8,128)(2,1)}, bf16[4,4,3,64,768]{4,3,2,1,0:T(8,128)(2,1)}) custom-call(bf16[32,128,384]{2,1,0:T(8,128)(2,1)} %copy-done.3, bf16[4,16,48,768]{3,2,1,0:T(8,128)(2,1)} %get-tuple-element.21.refs_0_, bf16[4,4,3,64,768]{4,3,2,1,0:T(8,128)(2,1)} %get-tuple-element.22.refs_1_), custom_call_target="tpu_custom_call", output_to_operand_aliasing={{0}: (1, {}), {1}: (2, {})} | custom-call | flops 1000 | bytes 1000 | tf_op jit(solution)/shard_map/assemble/pallas_call | solution.py:362
  304.4 7.0 %multiply.14.refs_0_ = bf16[32,96,384]{2,1,0:T(8,128)(2,1)} custom-call(bf16[4,16,48,768]{3,2,1,0:T(8,128)(2,1)} %get-tuple-element.23.left_ref, bf16[4,768,768]{2,1,0:T(8,128)(2,1)} %bitcast.37), custom_call_target="tpu_custom_call" | custom-call | flops 1000 | bytes 1000 | tf_op jit(solution)/shard_map/multiply/pallas_call | solution.py:425
  311.4 7.0 %multiply.15.refs_2_ = bf16[32,96,384]{2,1,0:T(8,128)(2,1)} custom-call(bf16[4,16,48,768]{3,2,1,0:T(8,128)(2,1)} %get-tuple-element.23.left_ref, bf16[4,768,768]{2,1,0:T(8,128)(2,1)} %bitcast.38, bf16[32,96,384]{2,1,0:T(8,128)(2,1)} %multiply.14.refs_0_), custom_call_target="tpu_custom_call" | custom-call | flops 1000 | bytes 1000 | tf_op jit(solution)/shard_map/multiply/pallas_call | solution.py:425
  318.4 2.9 all-to-all-start.4
  322.4 3.9 logit.5
  326.3 4.0 logit.4
  330.3 3.9 logit.3
  336.2 53.5 %all-to-all-done.4.refs_1_ = bf16[32,96,384]{2,1,0:T(8,128)(2,1)S(1)} async-done(((bf16[32,96,384]{2,1,0:T(8,128)(2,1)}), bf16[32,96,384]{2,1,0:T(8,128)(2,1)S(1)}, u32[]{:S(2)}, u32[]{:S(2)}) %all-to-all-start.4) | async-done | bytes 2359328 | tf_op jit(solution)/shard_map/all_to_all | solution.py:599
  389.8 3.8 all-to-all-start.3
  394.8 39.7 %all-gather.3.cloned.1.call-done.refs_0_ = f32[768,8,96]{2,1,0:T(8,128)} async-done(((f32[192,8,96]{2,1,0:T(8,128)}), f32[768,8,96]{2,1,0:T(8,128)}) %all-gather.3.cloned.1.call-update) | async-done | bytes 2359312 | tf_op jit(solution)/shard_map/all_gather | solution.py:632
  434.6 2.7 copy.74
  442.3 6.8 %all-to-all-done.3.refs_0_ = bf16[32,96,384]{2,1,0:T(8,128)(2,1)} async-done(((bf16[32,96,384]{2,1,0:T(8,128)(2,1)}), bf16[32,96,384]{2,1,0:T(8,128)(2,1)}, u32[]{:S(2)}, u32[]{:S(2)}) %all-to-all-start.3) | async-done | bytes 2359328 | tf_op jit(solution)/shard_map/all_to_all | solution.py:599
  449.1 12.6 %finish.1 = bf16[192,96,128]{2,1,0:T(8,128)(2,1)} custom-call(bf16[32,96,384]{2,1,0:T(8,128)(2,1)} %all-to-all-done.3.refs_0_, bf16[32,96,384]{2,1,0:T(8,128)(2,1)} %copy-done.4, bf16[64,96,128]{2,1,0:T(8,128)(2,1)} %get-tuple-element.27.refs_2_, bf16[64,96,128]{2,1,0:T(8,128)(2,1)} %get-tuple-element.28.refs_3_, ...), custom_call_target="tpu_custom_call" | custom-call | flops 1000 | bytes 1000 | tf_op jit(solution)/shard_map/finish/pallas_call | solution.py:501
  (107 shorter events, 30.7 us)
Async XLA Ops:
  7.2 434.0 %copy-start = (bf16[256,64]{0,1:T(8,128)(2,1)S(1)}, bf16[256,64]{0,1:T(8,128)(2,1)}, u32[]{:S(2)}) copy-start(bf16[256,64]{0,1:T(8,128)(2,1)} %param.17) | copy-start | bytes 98308
  7.2 40.1 %slice-start = ((bf16[128,640]{1,0:T(8,128)(2,1)}), bf16[128,512]{1,0:T(8,128)(2,1)S(1)}, s32[]{:S(2)}) async-start(bf16[128,640]{1,0:T(8,128)(2,1)} %param.18), calls=%async_computation.7 | async-start | bytes 262144 | tf_op jit(solution)/shard_map/slice | solution.py:594
  12.3 36.0 %copy-start.5 = (bf16[4,96,32]{2,1,0:T(8,128)(2,1)}, bf16[4,96,32]{2,1,0:T(8,128)(2,1)S(1)}, u32[]{:S(2)}) copy-start(bf16[4,96,32]{2,1,0:T(8,128)(2,1)S(1)} %get-tuple-element.30.refs_8_) | copy-start | bytes 73732
  12.3 11.5 %collective-permute-start = (bf16[4,96,32]{2,1,0:T(8,128)(2,1)S(1)}, bf16[4,96,32]{2,1,0:T(8,128)(2,1)S(1)}, u32[]{:S(2)}, u32[]{:S(2)}) collective-permute-start(bf16[4,96,32]{2,1,0:T(8,128)(2,1)S(1)} %get-tuple-element.31), channel_id=1, source_target_pairs={{0,0},{1,1},{2,8},{3,9},{4,16},{5,17},{6,24},{7,25},{8,2},{9,3},{1... | collective-permute-start | bytes 73736 | tf_op jit(solution)/shard_map/ppermute | solution.py:581
  12.9 13.7 %collective-permute-start.1 = (bf16[4,96,32]{2,1,0:T(8,128)(2,1)S(1)}, bf16[4,96,32]{2,1,0:T(8,128)(2,1)S(1)}, u32[]{:S(2)}, u32[]{:S(2)}) collective-permute-start(bf16[4,96,32]{2,1,0:T(8,128)(2,1)S(1)} %get-tuple-element.31), channel_id=1, source_target_pairs={{0,7},{1,0},{2,15},{3,8},{4,23},{5,16},{6,31},{7,24},{8,1},{9,2},{... | collective-permute-start | bytes 73736 | tf_op jit(solution)/shard_map/ppermute | solution.py:581
  20.6 7.9 %collective-permute-start.2 = (bf16[4,96,32]{2,1,0:T(8,128)(2,1)S(1)}, bf16[4,96,32]{2,1,0:T(8,128)(2,1)S(1)}, u32[]{:S(2)}, u32[]{:S(2)}) collective-permute-start(bf16[4,96,32]{2,1,0:T(8,128)(2,1)S(1)} %get-tuple-element.31), channel_id=1, source_target_pairs={{0,6},{1,7},{2,14},{3,15},{4,22},{5,23},{6,30},{7,31},{8,0},{9,1},... | collective-permute-start | bytes 73736 | tf_op jit(solution)/shard_map/ppermute | solution.py:581
  21.5 10.3 %collective-permute-start.3 = (bf16[4,96,32]{2,1,0:T(8,128)(2,1)S(1)}, bf16[4,96,32]{2,1,0:T(8,128)(2,1)S(1)}, u32[]{:S(2)}, u32[]{:S(2)}) collective-permute-start(bf16[4,96,32]{2,1,0:T(8,128)(2,1)S(1)} %get-tuple-element.31), channel_id=1, source_target_pairs={{0,5},{1,6},{2,13},{3,14},{4,21},{5,22},{6,29},{7,30},{8,7},{9,0},... | collective-permute-start | bytes 73736 | tf_op jit(solution)/shard_map/ppermute | solution.py:581
  23.2 14.4 %collective-permute-start.4 = (bf16[4,96,32]{2,1,0:T(8,128)(2,1)S(1)}, bf16[4,96,32]{2,1,0:T(8,128)(2,1)S(1)}, u32[]{:S(2)}, u32[]{:S(2)}) collective-permute-start(bf16[4,96,32]{2,1,0:T(8,128)(2,1)S(1)} %get-tuple-element.31), channel_id=1, source_target_pairs={{0,4},{1,5},{2,12},{3,13},{4,20},{5,21},{6,28},{7,29},{8,6},{9,7},... | collective-permute-start | bytes 73736 | tf_op jit(solution)/shard_map/ppermute | solution.py:581
  23.8 24.5 %copy-start.8 = (bf16[4,96,32]{2,1,0:T(8,128)(2,1)}, bf16[4,96,32]{2,1,0:T(8,128)(2,1)S(1)}, u32[]{:S(2)}) copy-start(bf16[4,96,32]{2,1,0:T(8,128)(2,1)S(1)} %collective-permute-done.refs_0_) | copy-start | bytes 73732
  23.8 13.8 %collective-permute-start.5 = (bf16[4,96,32]{2,1,0:T(8,128)(2,1)S(1)}, bf16[4,96,32]{2,1,0:T(8,128)(2,1)S(1)}, u32[]{:S(2)}, u32[]{:S(2)}) collective-permute-start(bf16[4,96,32]{2,1,0:T(8,128)(2,1)S(1)} %get-tuple-element.31), channel_id=1, source_target_pairs={{0,3},{1,4},{2,11},{3,12},{4,19},{5,20},{6,27},{7,28},{8,5},{9,6},... | collective-permute-start | bytes 73736 | tf_op jit(solution)/shard_map/ppermute | solution.py:581
  26.7 21.6 %copy-start.9 = (bf16[4,96,32]{2,1,0:T(8,128)(2,1)}, bf16[4,96,32]{2,1,0:T(8,128)(2,1)S(1)}, u32[]{:S(2)}) copy-start(bf16[4,96,32]{2,1,0:T(8,128)(2,1)S(1)} %collective-permute-done.1.refs_1_) | copy-start | bytes 73732
  26.7 21.5 %collective-permute-start.6 = (bf16[4,96,32]{2,1,0:T(8,128)(2,1)S(1)}, bf16[4,96,32]{2,1,0:T(8,128)(2,1)S(1)}, u32[]{:S(2)}, u32[]{:S(2)}) collective-permute-start(bf16[4,96,32]{2,1,0:T(8,128)(2,1)S(1)} %get-tuple-element.31), channel_id=1, source_target_pairs={{0,2},{1,3},{2,10},{3,11},{4,18},{5,19},{6,26},{7,27},{8,4},{9,5},... | collective-permute-start | bytes 73736 | tf_op jit(solution)/shard_map/ppermute | solution.py:581
  28.5 19.8 %copy-start.10 = (bf16[4,96,32]{2,1,0:T(8,128)(2,1)}, bf16[4,96,32]{2,1,0:T(8,128)(2,1)S(1)}, u32[]{:S(2)}) copy-start(bf16[4,96,32]{2,1,0:T(8,128)(2,1)S(1)} %collective-permute-done.2.refs_2_) | copy-start | bytes 73732
  28.5 19.7 %collective-permute-start.7 = (bf16[4,96,32]{2,1,0:T(8,128)(2,1)S(1)}, bf16[4,96,32]{2,1,0:T(8,128)(2,1)S(1)}, u32[]{:S(2)}, u32[]{:S(2)}) collective-permute-start(bf16[4,96,32]{2,1,0:T(8,128)(2,1)S(1)} %get-tuple-element.31), channel_id=1, source_target_pairs={{0,1},{1,2},{2,9},{3,10},{4,17},{5,18},{6,25},{7,26},{8,3},{9,4},{... | collective-permute-start | bytes 73736 | tf_op jit(solution)/shard_map/ppermute | solution.py:581
  31.7 16.5 %copy-start.11 = (bf16[4,96,32]{2,1,0:T(8,128)(2,1)}, bf16[4,96,32]{2,1,0:T(8,128)(2,1)S(1)}, u32[]{:S(2)}) copy-start(bf16[4,96,32]{2,1,0:T(8,128)(2,1)S(1)} %collective-permute-done.3.refs_3_) | copy-start | bytes 73732
  31.7 16.4 %collective-permute-start.10 = (bf16[4,96,32]{2,1,0:T(8,128)(2,1)S(1)}, bf16[4,96,32]{2,1,0:T(8,128)(2,1)S(1)}, u32[]{:S(2)}, u32[]{:S(2)}) collective-permute-start(bf16[4,96,32]{2,1,0:T(8,128)(2,1)S(1)} %get-tuple-element.30.refs_8_), channel_id=1, source_target_pairs={{0,8},{8,16},{16,24},{24,0},{1,9},{9,17},{17,25},{25,1},{2,10},{10... | collective-permute-start | bytes 73736 | tf_op jit(solution)/shard_map/ppermute | solution.py:585
  37.5 10.7 %copy-start.12 = (bf16[4,96,32]{2,1,0:T(8,128)(2,1)}, bf16[4,96,32]{2,1,0:T(8,128)(2,1)S(1)}, u32[]{:S(2)}) copy-start(bf16[4,96,32]{2,1,0:T(8,128)(2,1)S(1)} %collective-permute-done.4.refs_4_) | copy-start | bytes 73732
  37.5 10.7 %collective-permute-start.8 = (bf16[4,96,32]{2,1,0:T(8,128)(2,1)S(1)}, bf16[4,96,32]{2,1,0:T(8,128)(2,1)S(1)}, u32[]{:S(2)}, u32[]{:S(2)}) collective-permute-start(bf16[4,96,32]{2,1,0:T(8,128)(2,1)S(1)} %get-tuple-element.30.refs_8_), channel_id=1, source_target_pairs={{0,24},{8,0},{16,8},{24,16},{1,25},{9,1},{17,9},{25,17},{2,26},{10... | collective-permute-start | bytes 73736 | tf_op jit(solution)/shard_map/ppermute | solution.py:585
  37.6 10.7 %copy-start.13 = (bf16[4,96,32]{2,1,0:T(8,128)(2,1)}, bf16[4,96,32]{2,1,0:T(8,128)(2,1)S(1)}, u32[]{:S(2)}) copy-start(bf16[4,96,32]{2,1,0:T(8,128)(2,1)S(1)} %collective-permute-done.5.refs_5_) | copy-start | bytes 73732
  37.6 10.7 %collective-permute-start.9 = (bf16[4,96,32]{2,1,0:T(8,128)(2,1)S(1)}, bf16[4,96,32]{2,1,0:T(8,128)(2,1)S(1)}, u32[]{:S(2)}, u32[]{:S(2)}) collective-permute-start(bf16[4,96,32]{2,1,0:T(8,128)(2,1)S(1)} %get-tuple-element.30.refs_8_), channel_id=1, source_target_pairs={{0,16},{8,24},{16,0},{24,8},{1,17},{9,25},{17,1},{25,9},{2,18},{10... | collective-permute-start | bytes 73736 | tf_op jit(solution)/shard_map/ppermute | solution.py:585
  65.2 75.4 %all-to-all-start.2 = ((bf16[32,128,384]{2,1,0:T(8,128)(2,1)}), bf16[32,128,384]{2,1,0:T(8,128)(2,1)S(1)}, u32[]{:S(2)}, u32[]{:S(2)}) async-start(bf16[32,128,384]{2,1,0:T(8,128)(2,1)} %project.3.refs_16_), calls=%async_computation.2 | async-start | bytes 6291456 | tf_op jit(solution)/shard_map/all_to_all | solution.py:599
  142.4 76.2 %all-to-all-start.1 = ((bf16[32,128,384]{2,1,0:T(8,128)(2,1)}), bf16[32,128,384]{2,1,0:T(8,128)(2,1)}, u32[]{:S(2)}, u32[]{:S(2)}) async-start(bf16[32,128,384]{2,1,0:T(8,128)(2,1)} %project.4.refs_16_), calls=%async_computation.1 | async-start | bytes 6291456 | tf_op jit(solution)/shard_map/all_to_all | solution.py:599
  218.6 75.4 %all-to-all-start = ((bf16[32,128,384]{2,1,0:T(8,128)(2,1)}), bf16[32,128,384]{2,1,0:T(8,128)(2,1)S(1)}, u32[]{:S(2)}, u32[]{:S(2)}) async-start(bf16[32,128,384]{2,1,0:T(8,128)(2,1)} %project.5), calls=%async_computation | async-start | bytes 6291456 | tf_op jit(solution)/shard_map/all_to_all | solution.py:599
  318.4 3.0 copy-start.22
  318.4 71.4 %all-to-all-start.4 = ((bf16[32,96,384]{2,1,0:T(8,128)(2,1)}), bf16[32,96,384]{2,1,0:T(8,128)(2,1)S(1)}, u32[]{:S(2)}, u32[]{:S(2)}) async-start(bf16[32,96,384]{2,1,0:T(8,128)(2,1)} %multiply.15.refs_2_), calls=%async_computation.4 | async-start | bytes 4718592 | tf_op jit(solution)/shard_map/all_to_all | solution.py:599
  321.3 73.6 %all-gather.5.cloned.1.call-start = ((), (), s32[]{:S(2)}) async-start(), calls=%async_computation.6 | async-start | bytes 1769472 | tf_op jit(solution)/shard_map/all_gather | solution.py:633
  322.3 112.2 %all-gather.3.cloned.1.call-start = ((), (), s32[]{:S(2)}) async-start(), calls=%async_computation.5 | async-start | bytes 3932160 | tf_op jit(solution)/shard_map/all_gather | solution.py:632
  326.3 7.9 %copy-start.7 = (f32[64,8,96]{2,1,0:T(8,128)S(1)}, f32[64,8,96]{2,1,0:T(8,128)}, u32[]{:S(2)}) copy-start(f32[64,8,96]{2,1,0:T(8,128)} %logit.5) | copy-start | bytes 589828
  336.2 57.4 %copy-start.20 = (bf16[128,640]{1,0:T(8,128)(2,1)S(1)}, bf16[128,640]{1,0:T(8,128)(2,1)}, u32[]{:S(2)}) copy-start(bf16[128,640]{1,0:T(8,128)(2,1)} %param.18) | copy-start | bytes 491524
  336.2 58.0 %copy-start.21 = (bf16[128,128]{1,0:T(8,128)(2,1)S(1)}, bf16[128,128]{1,0:T(8,128)(2,1)}, u32[]{:S(2)}) copy-start(bf16[128,128]{1,0:T(8,128)(2,1)} %param.19) | copy-start | bytes 98308
  389.8 44.8 %copy-start.4 = (bf16[32,96,384]{2,1,0:T(8,128)(2,1)}, bf16[32,96,384]{2,1,0:T(8,128)(2,1)S(1)}, u32[]{:S(2)}) copy-start(bf16[32,96,384]{2,1,0:T(8,128)(2,1)S(1)} %all-to-all-done.4.refs_1_) | copy-start | bytes 7077892
  389.8 59.4 %all-to-all-start.3 = ((bf16[32,96,384]{2,1,0:T(8,128)(2,1)}), bf16[32,96,384]{2,1,0:T(8,128)(2,1)}, u32[]{:S(2)}, u32[]{:S(2)}) async-start(bf16[32,96,384]{2,1,0:T(8,128)(2,1)} %multiply.14.refs_0_), calls=%async_computation.3 | async-start | bytes 4718592 | tf_op jit(solution)/shard_map/all_to_all | solution.py:599
  (10 other events, 13.9 us)
Sparse Core Ops, SparseCore 0:
  323.7 47.4 all-gather.4
  373.6 60.9 all-gather.2

commit v7 on v6

--- a/solution.py
+++ b/solution.py
@@ -281,7 +281,8 @@
     )(live_rows, normed, live_cols, weight)
 
 
-def logit_kernel(live_ref, normed_ref, weight_ref, out_ref, *, first_row):
+def logit_kernel(live_ref, normed_ref, weight_ref, *refs, first_row):
+    out_ref = refs[-1]
     block = normed_ref.shape[0]
     for i in range(block):
         live = live_ref[first_row + pl.program_id(0) * block + i]
@@ -290,7 +291,7 @@
         ) + MASK_PENALTY * (live - 1.0)
 
 
-def logit(first_row, live_rows, normed, weight):
+def logit(first_row, live_rows, normed, weight, after):
     rows, cols, wide = normed.shape
     block = 16
     heads = weight.shape[0]
@@ -301,21 +302,23 @@
             pl.BlockSpec(memory_space=pltpu.SMEM),
             pl.BlockSpec((block, cols, wide), lambda i: (i, 0, 0)),
             whole(weight.shape),
-        ],
+        ]
+        + anywhere(after),
         out_specs=pl.BlockSpec((block, heads, cols), lambda i: (i, 0, 0)),
         out_shape=jax.ShapeDtypeStruct((rows, heads, cols), F32),
         compiler_params=params(),
         cost_estimate=LIGHT,
         name="logit",
-    )(live_rows, normed, weight)
-
-
-def assemble_kernel(recv_ref, *refs, row_count, pos_count):
+    )(live_rows, normed, weight, *after)
+
+
+def assemble_kernel(recv_ref, *refs, row_count, pos_count, spans):
     left_ref, right_ref, flat_ref, rows_ref = refs[-4:]
     channel = pl.program_id(0)
     lanes = recv_ref.shape[2]
     each = left_ref.shape[2]
-    stride = recv_ref.shape[1] // each
+    height = recv_ref.shape[1] // spans
+    stride = height // each
     groups = pos_count // 4
     tiles = lanes // LANES
 
@@ -328,15 +331,16 @@
 
     def block(row, group, index):
         packed = []
+        index = index + group // groups * height
         for p in range(4):
-            src = row * pos_count + group * 4 + p
+            src = row * pos_count + group % groups * 4 + p
             packed.append(
                 [flat_ref[src, t, pl.ds(index, each, stride=stride), :] for t in range(tiles)]
             )
         return exchange_blocks(packed)
 
     for row in range(row_count):
-        for group in range(groups):
+        for group in range(groups * spans):
             span = slice(group * lanes, (group + 1) * lanes)
             left = block(row, group, channel)
             right = block(row, group, channel + stride // 2)
@@ -349,20 +353,22 @@
                 right_ref[0, row, 0, :, at] = rows_ref[t].astype(BF16)
 
 
-def assemble(chunk, chunks, received, sides, row_count, pos_count, cols):
+def assemble(chunk, chunks, spans, received, sides, after, row_count, pos_count, cols):
     sources, height, lanes = received.shape
-    depth = pos_count * cols
+    depth = spans * pos_count * cols
     each = depth // (row_count * QUAD * chunks)
-    channels = height // each // 2
+    channels = height // spans // each // 2
     blocks = row_count * QUAD
     shapes = [
         (channels, blocks, each * chunks, depth),
         (channels, row_count, chunks, QUAD * each, depth),
     ]
     return pl.pallas_call(
-        functools.partial(assemble_kernel, row_count=row_count, pos_count=pos_count),
+        functools.partial(
+            assemble_kernel, row_count=row_count, pos_count=pos_count, spans=spans
+        ),
         grid=(channels,),
-        in_specs=[whole(received.shape)] + anywhere(sides),
+        in_specs=[whole(received.shape)] + anywhere(sides) + anywhere(after),
         out_specs=[
             pl.BlockSpec((1, blocks, each, depth), lambda c: (c, 0, chunk, 0)),
             pl.BlockSpec((1, row_count, 1, QUAD * each, depth), lambda c: (c, 0, chunk, 0, 0)),
@@ -376,7 +382,7 @@
         compiler_params=params(),
         cost_estimate=LIGHT,
         name="assemble",
-    )(received, *sides)
+    )(received, *sides, *after)
 
 
 def multiply_kernel(left_ref, right_ref, *refs, pos_count):
@@ -418,16 +424,16 @@
                 out_ref[dest, :, t * LANES : (t + 1) * LANES] = tmp_ref[dest, t].astype(BF16)
 
 
-def multiply(first, count, left, right, after, pos_count, cols):
-    _, blocks, each, depth = left.shape
+def multiply(left, right, after, pos_count, cols):
+    count, blocks, each, depth = left.shape
     lanes = QUAD * cols
     shape = (blocks // QUAD * pos_count, each * count, lanes)
     return pl.pallas_call(
         functools.partial(multiply_kernel, pos_count=pos_count),
         grid=(count,),
         in_specs=[
-            pl.BlockSpec((1, blocks, each, depth), lambda c: (c + first, 0, 0, 0)),
-            pl.BlockSpec((1, depth, depth), lambda c: (c + first, 0, 0)),
+            pl.BlockSpec((1, blocks, each, depth), lambda c: (c, 0, 0, 0)),
+            pl.BlockSpec((1, depth, depth), lambda c: (c, 0, 0)),
         ]
         + anywhere(after),
         out_specs=whole(shape),
@@ -439,6 +445,193 @@
     )(left, right, *after)
 
 
+def assemble_half_kernel(half_ref, *refs, row_count, pos_count, parts):
+    recvs = refs[:parts]
+    left_ref, own_ref, send_ref, flat_ref, right_ref = refs[-5:]
+    channel = pl.program_id(0)
+    lanes = recvs[0].shape[2]
+    unit = lanes // 12
+    cols = 3 * unit
+    each = send_ref.shape[1] // (row_count * QUAD)
+    stride = sum(recv.shape[1] for recv in recvs) // each
+    groups = pos_count // 4
+    tiles = lanes // LANES
+    per_row = each * QUAD // cols
+
+    @pl.when(channel == 0)
+    def _():
+        for src in range(row_count * pos_count):
+            start = 0
+            for recv in recvs:
+                value = recv[src].astype(F32)
+                end = start + recv.shape[1]
+                for t in range(tiles):
+                    flat_ref[src, t, start:end] = value[:, t * LANES : (t + 1) * LANES]
+                start = end
+
+    def block(row, group, index):
+        packed = []
+        for p in range(4):
+            src = row * pos_count + group * 4 + p
+            packed.append(
+                [flat_ref[src, t, pl.ds(index, each, stride=stride), :] for t in range(tiles)]
+            )
+        return exchange_blocks(packed)
+
+    for row in range(row_count):
+        for group in range(groups):
+            span = slice(group * lanes, (group + 1) * lanes)
+            left = block(row, group, channel)
+            for a in range(QUAD):
+                start = (row * QUAD + a) * each
+                left_ref[0, start : start + each, span] = jnp.concatenate(left[a], axis=1).astype(
+                    BF16
+                )
+            right = block(row, group, channel + stride // 2)
+            for a in range(QUAD):
+                for piece in range(per_row):
+                    place = row * per_row + piece
+                    base = (place // 4) * lanes
+                    low = piece * (cols // QUAD)
+                    mid = low + 2 * unit // QUAD
+                    high = low + cols // QUAD
+                    first = base + (place % 4) * 2 * unit + a
+                    second = base + 8 * unit + (place % 4) * unit + a
+                    for t in range(tiles):
+                        value = right[a][t]
+                        at = group * tiles + t
+                        right_ref[at, pl.ds(first, mid - low, stride=QUAD), :] = value[low:mid]
+                        right_ref[at, pl.ds(second, high - mid, stride=QUAD), :] = value[mid:high]
+    width = pos_count * cols
+    own = pl.multiple_of(half_ref[0] * width, width)
+    other = pl.multiple_of((1 - half_ref[0]) * width, width)
+    theirs = []
+    for at in range(groups * tiles):
+        span = slice(at * LANES, (at + 1) * LANES)
+        own_ref[0, :, span] = right_ref[at, pl.ds(own, width), :].astype(BF16)
+        theirs.append(right_ref[at, pl.ds(other, width), :].astype(BF16))
+    theirs = jnp.concatenate(theirs, axis=1)
+    for row in range(row_count):
+        span = slice(row * QUAD * each, (row + 1) * QUAD * each)
+        send_ref[0, span] = lax.dot_general(
+            left_ref[0, span], theirs, NT, preferred_element_type=F32
+        ).astype(BF16)
+
+
+def assemble_half(half, received, row_count, pos_count, cols):
+    sources, _, lanes = received[0].shape
+    height = sum(part.shape[1] for part in received)
+    each = (2 * pos_count * cols) // (row_count * QUAD)
+    channels = height // each // 2
+    depth = pos_count * cols
+    rows = 2 * depth
+    return pl.pallas_call(
+        functools.partial(
+            assemble_half_kernel, row_count=row_count, pos_count=pos_count, parts=len(received)
+        ),
+        grid=(channels,),
+        in_specs=[pl.BlockSpec(memory_space=pltpu.SMEM)] + [whole(part.shape) for part in received],
+        out_specs=[
+            pl.BlockSpec((1, rows, depth), lambda c: (c, 0, 0)),
+            pl.BlockSpec((1, depth, depth), lambda c: (c, 0, 0)),
+            pl.BlockSpec((1, rows, depth), lambda c: (c, 0, 0)),
+        ],
+        out_shape=[
+            jax.ShapeDtypeStruct((channels, rows, depth), BF16),
+            jax.ShapeDtypeStruct((channels, depth, depth), BF16),
+            jax.ShapeDtypeStruct((channels, rows, depth), BF16),
+        ],
+        scratch_shapes=[
+            pltpu.VMEM((sources, lanes // LANES, height, LANES), F32),
+            pltpu.VMEM((depth // LANES, rows, LANES), F32),
+        ],
+        compiler_params=params(),
+        cost_estimate=LIGHT,
+        name="assemble_half",
+    )(half, *received)
+
+
+def combine_kernel(left_ref, own_ref, recv_ref, *refs, row_count, pos_count):
+    out_ref, tmp_ref = refs[-2:]
+    channel = pl.program_id(0)
+    channels = pl.num_programs(0)
+    lanes = out_ref.shape[2]
+    each = left_ref.shape[1] // (row_count * QUAD)
+    stride = out_ref.shape[1] // each
+    tiles = lanes // LANES
+    for row in range(row_count):
+        for group in range(pos_count // 4):
+            cols = slice(group * lanes, (group + 1) * lanes)
+            blocks = []
+            for a in range(QUAD):
+                span = slice((row * QUAD + a) * each, (row * QUAD + a + 1) * each)
+                value = lax.dot_general(
+                    left_ref[0, span], own_ref[0, cols], NT, preferred_element_type=F32
+                )
+                value = value + recv_ref[0, span, cols].astype(F32)
+                blocks.append([value[:, t * LANES : (t + 1) * LANES] for t in range(tiles)])
+            for p, value in enumerate(exchange_blocks(blocks)):
+                dest = row * pos_count + group * 4 + p
+                for t in range(tiles):
+                    tmp_ref[dest, t, pl.ds(channel, each, stride=stride), :] = value[t]
+
+    @pl.when(channel == channels - 1)
+    def _():
+        for dest in range(row_count * pos_count):
+            for t in range(tiles):
+                out_ref[dest, :, t * LANES : (t + 1) * LANES] = tmp_ref[dest, t].astype(BF16)
+
+
+def combine(left, own, received, after, row_count, pos_count, cols):
+    channels, rows, depth = left.shape
+    each = rows // (row_count * QUAD)
+    shape = (row_count * pos_count, each * channels, QUAD * cols)
+    return pl.pallas_call(
+        functools.partial(combine_kernel, row_count=row_count, pos_count=pos_count),
+        grid=(channels,),
+        in_specs=[
+            pl.BlockSpec((1, rows, depth), lambda c: (c, 0, 0)),
+            pl.BlockSpec((1, depth, depth), lambda c: (c, 0, 0)),
+            pl.BlockSpec((1, rows, depth), lambda c: (c, 0, 0)),
+        ]
+        + anywhere(after),
+        out_specs=whole(shape),
+        out_shape=jax.ShapeDtypeStruct(shape, BF16),
+        scratch_shapes=[pltpu.VMEM((shape[0], shape[2] // LANES, shape[1], LANES), F32)],
+        compiler_params=params(),
+        cost_estimate=LIGHT,
+        name="combine",
+    )(left, own, received, *after)
+
+
+def merge_kernel(*refs, parts, slots):
+    pieces, (out_ref, sems) = refs[:parts], refs[-2:]
+    copies = []
+    for index, (piece, slot) in enumerate(zip(pieces, slots)):
+        height = piece.shape[1]
+        place = out_ref.at[:, pl.ds(slot * height, height), :]
+        copies.append(pltpu.make_async_copy(piece, place, sems.at[index]))
+    for copy in copies:
+        copy.start()
+    for copy in copies:
+        copy.wait()
+
+
+def merge(pieces, slots, count, into):
+    sources, height, lanes = pieces[0].shape
+    return pl.pallas_call(
+        functools.partial(merge_kernel, parts=len(pieces), slots=slots),
+        in_specs=anywhere(pieces) + anywhere(into),
+        out_specs=pl.BlockSpec(memory_space=pl.ANY),
+        out_shape=jax.ShapeDtypeStruct((sources, height * count, lanes), BF16),
+        input_output_aliases={len(pieces): 0} if into else {},
+        scratch_shapes=[pltpu.SemaphoreType.DMA((len(pieces),))],
+        compiler_params=pltpu.CompilerParams(vmem_limit_bytes=60 * MIB),
+        cost_estimate=LIGHT,
+        name="merge",
+    )(*pieces, *into)
+
+
 def finish_kernel(*refs, parts, chunks):
     products = refs[:parts]
     mids = refs[parts : parts + chunks]
@@ -446,10 +639,10 @@
     gate_ref, weight_ref, out_ref = refs[parts + 2 * chunks : parts + 2 * chunks + 3]
     flat = refs[parts + 2 * chunks + 3 :]
     quads = out_ref.shape[0] // QUAD
-    sources, _, lanes = products[0].shape
+    lanes = products[0].shape[2]
     tiles = range(lanes // LANES)
     for product, tmp in zip(products, flat):
-        height = product.shape[1]
+        sources, height, _ = product.shape
         for src in range(sources):
             value = product[src].astype(F32)
             for t in tiles:
@@ -459,7 +652,7 @@
         for m in range(quads):
             pieces = []
             for product, tmp in zip(products, flat):
-                height = product.shape[1]
+                sources, height, _ = product.shape
                 each = height // quads
                 for k in range(each):
                     pieces.append(
@@ -485,7 +678,7 @@
 def finish(products, mids, normeds, w_gate, w_final):
     rows, cols, wide = mids[0].shape
     chunks = len(mids)
-    sources, _, lanes = products[0].shape
+    lanes = products[0].shape[2]
     total = rows * chunks // QUAD
     heights = [part.shape[1] // total for part in products]
     quads = max(8, 16 // min(heights))
@@ -502,24 +695,21 @@
         functools.partial(finish_kernel, parts=len(products), chunks=chunks),
         grid=(total // quads,),
         in_specs=[
-            pl.BlockSpec((sources, quads * each, lanes), lambda i: (0, i, 0)) for each in heights
+            pl.BlockSpec((part.shape[0], quads * each, lanes), lambda i: (0, i, 0))
+            for part, each in zip(products, heights)
         ]
         + tiles * 2
         + [whole(w_gate.shape), whole(w_final.shape)],
         out_specs=pl.BlockSpec((quads * QUAD, cols, wide), lambda i: (i, 0, 0)),
         out_shape=jax.ShapeDtypeStruct((rows * chunks, cols, wide), BF16),
         scratch_shapes=[
-            pltpu.VMEM((lanes // LANES, sources * quads * each, LANES), F32) for each in heights
+            pltpu.VMEM((lanes // LANES, part.shape[0] * quads * each, LANES), F32)
+            for part, each in zip(products, heights)
         ],
         compiler_params=params(),
         cost_estimate=LIGHT,
         name="finish",
     )(*products, *mids, *normeds, w_gate, w_final)
-
-
-def chunk_sizes(channels):
-    each = min(2, channels)
-    return [each] * (channels // each)
 
 
 def on_device(
@@ -590,22 +780,19 @@
         [live_cols[: 2 * unit]] * QUAD + [live_cols[2 * unit :]] * QUAD
     )[None]
     devices = row_count * col_count
-    channels = CTRI // devices
-    w_kinds = trimul_matrices[:, : 4 * CTRI].T.reshape(2, 2, devices, channels, wide)
-    w_sides = jnp.transpose(w_kinds, (1, 2, 0, 3, 4)).reshape(-1, wide)
+    w_kinds = trimul_matrices[:, : 4 * CTRI].T.reshape(2, 2, CTRI, wide)
     w_logit = coupling_logit_matrix.T
 
-    def exchange(block):
-        return lax.all_to_all(block, AXES, split_axis=0, concat_axis=0, tiled=True)
-
-    shape_of = (row_count, col_count, module_number)
-    row_chunks = rows // QUAD // 16
-    mids, normeds, logits = [], [], []
-    sent, sides = (), ()
-    for chunk in range(row_chunks):
-        mid, normed = front(
+    def side_weights(part):
+        return jnp.transpose(part, (1, 2, 0, 3, 4)).reshape(-1, wide)
+
+    def exchange(block, axes):
+        return lax.all_to_all(block, axes, split_axis=0, concat_axis=0, tiled=True)
+
+    def front_rows(chunk, chunks, after):
+        return front(
             chunk,
-            row_chunks,
+            chunks,
             jnp.stack([row_index, col_index]).astype(jnp.int32),
             lefts,
             rights,
@@ -613,15 +800,77 @@
             coupling_embedding,
             w_tensor,
             present_cols.T.astype(BF16),
-            sent,
+            after,
         )
-        first_row = chunk * (rows // row_chunks)
-        block = project(first_row, live_rows, normed, live_packed, w_sides, devices)
-        sent = (block,)
-        sides = assemble(chunk, row_chunks, exchange(block), sides, *shape_of)
-        logits.append(logit(first_row, live_rows, normed, w_logit))
-        mids.append(mid)
-        normeds.append(normed)
+
+    def project_rows(chunk, normed, weight, dests):
+        first_row = chunk * normed.shape[0]
+        return project(first_row, live_rows, normed, live_packed, weight, dests)
+
+    group = devices // 2
+    shape_of = (row_count, col_count, module_number)
+    half_shape = (row_count, pos_count, module_number)
+    mids, normeds, returned = [], [], []
+    if CTRI // 2 % devices:
+        row_chunks = rows // QUAD // 16
+        sent, sides = (), ()
+        weight = side_weights(w_kinds.reshape(2, 2, devices, -1, wide))
+        for chunk in range(row_chunks):
+            mid, normed = front_rows(chunk, row_chunks, sent)
+            block = project_rows(chunk, normed, weight, devices)
+            sent = (block,)
+            sides = assemble(chunk, row_chunks, 1, exchange(block, AXES), sides, (), *shape_of)
+            mids.append(mid)
+            normeds.append(normed)
+        left, right = sides
+        right = right.reshape(right.shape[0], -1, right.shape[-1])
+        last = multiply(left, right, (), *shape_of[1:])
+        returned.append(exchange(last, AXES))
+        after = (last,)
+        orders = [(0, CTRI, devices)]
+    else:
+        cut = CTRI // 2
+        row_chunks = 2
+        w_half = side_weights(w_kinds[:, :, :cut].reshape(2, 2, group, -1, wide))
+        w_both = w_kinds[:, :, cut:].reshape(2, 2, row_count, 2, pos_count, -1, wide)
+
+        def half_weights(which):
+            part = lax.dynamic_index_in_dim(w_both, which, 3, keepdims=False)
+            return side_weights(part.reshape(2, 2, group, -1, wide))
+
+        w_own, w_other = half_weights(half), half_weights(1 - half)
+        swap = [(0, 1), (1, 0)]
+        received, crossed, kept, ahead = [], [], [], ()
+        for chunk in range(row_chunks):
+            mid, normed = front_rows(chunk, row_chunks, ahead)
+            mids.append(mid)
+            normeds.append(normed)
+            to_half = project_rows(chunk, normed, w_half, group)
+            to_other = project_rows(chunk, normed, w_other, group)
+            to_other, to_half, w_own = fence([to_other, to_half, w_own], received + crossed)
+            crossed.append(lax.ppermute(to_other, "half", swap))
+            received.append(exchange(to_half, GROUP))
+            ahead = (w_own,)
+            kept.append(project_rows(chunk, normed, w_own, group))
+        half_scalar = half.astype(jnp.int32).reshape(1)
+        left, own, theirs = assemble_half(half_scalar, received, *half_shape)
+        merged = merge(kept + crossed[:-1], tuple(range(2 * row_chunks - 1)), 2 * row_chunks, ())
+        merged = merge(crossed[-1:], (2 * row_chunks - 1,), 2 * row_chunks, (merged,))
+        theirs, merged = fence([theirs, merged], ())
+        partial = lax.ppermute(theirs, "half", swap)
+        both = exchange(merged, GROUP)
+        after = (both,)
+        product = combine(left, own, partial, (both,), *half_shape)
+        returned.append(exchange(product, GROUP))
+        left, right = assemble(0, 1, 2, both, (), (product,), *half_shape)
+        right = right.reshape(right.shape[0], -1, right.shape[-1])
+        last = multiply(left, right, (), *shape_of[1:])
+        returned.append(exchange(last, AXES))
+        orders = [(0, cut, group), (cut, CTRI, devices)]
+    logits = [
+        logit(chunk * normed.shape[0], live_rows, normed, w_logit, after)
+        for chunk, normed in enumerate(normeds)
+    ]
 
     values = project_msa(
         alignment_matrix[:, 2 * TENSOR_FEATURES : 2 * TENSOR_FEATURES + MEAN_GROUPS * GROUP_FEATURES]
@@ -632,15 +881,7 @@
     logits_all = lax.all_gather(jnp.concatenate(logits, axis=0), "row", axis=0, tiled=True)
     values_all = lax.all_gather(values, ("half", "pos"), axis=1, tiled=True)
 
-    left, right = sides
-    right = right.reshape(channels, -1, right.shape[-1])
-    returned, first, after = [], 0, ()
-    for count in chunk_sizes(channels):
-        product = multiply(first, count, left, right, after, *shape_of[1:])
-        returned.append(exchange(product))
-        after = (product,)
-        first += count
-    logits_all, values_all = fence([logits_all, values_all], after)
+    logits_all, values_all = fence([logits_all, values_all], (last,))
     top_all = jnp.max(logits_all, axis=0)
     expd = jnp.exp(logits_all - top_all[None])
     weights_all = (expd / jnp.sum(expd, axis=0)[None]).astype(BF16)
@@ -655,10 +896,15 @@
     ).reshape(seq_each, module_number, -1)
     alignment_updated_embedding = (alignment_embedding.astype(F32) + blended_update).astype(BF16)
 
-    w_final = jnp.transpose(trimul_final_matrix.reshape(devices, -1, wide), (1, 0, 2))
-    pair_output = finish(
-        returned, mids, normeds, trimul_matrices[:, 4 * CTRI :], w_final.reshape(-1, wide)
+    w_final = jnp.concatenate(
+        [
+            jnp.transpose(
+                trimul_final_matrix[low:high].reshape(sources, -1, wide), (1, 0, 2)
+            ).reshape(-1, wide)
+            for low, high, sources in orders
+        ]
     )
+    pair_output = finish(returned, mids, normeds, trimul_matrices[:, 4 * CTRI :], w_final)
     return (alignment_updated_embedding, pair_output)
 
 

time: 470 us -> 571 us (1.21)
  Pallas kernels: 112 us -> 261 us
  waiting for transfers between devices: 269 us -> 206 us
  starting transfers between devices: 46 us -> 56.9 us
    all_to_all x5, waiting for transfers between devices: 229 us -> 13.4 us  [exchange(): return lax.all_to_all(block, axes, split_axis=0, concat_axis=0, tiled=True)]
    pallas_call x0 -> x4, Pallas kernels: none -> 165 us  [the longest x2 145 us: merge(): pl.pallas_call(functools.partial(merge_kernel, parts=len(pieces), slots=s...]
    ppermute x0 -> x3, waiting for transfers between devices: none -> 134 us  [the longest x1 108 us: on_device(): partial = lax.ppermute(theirs, 'half', swap)]
    all_gather x1, waiting for transfers between devices: 39.7 us -> 58.7 us  [on_device(): lax.all_gather(jnp.concatenate(logits, axis=0), 'row', axis=0, tiled=True)]
    pallas_call x3 -> x1, Pallas kernels: 26.2 us -> 8.85 us  [assemble(): pl.pallas_call(functools.partial(assemble_kernel, row_count=row_count, po...]
    pallas_call x3 -> x6, Pallas kernels: 13 us -> 26.1 us  [project(): pl.pallas_call(functools.partial(project_kernel, first_row=first_row), gr...]
    all_to_all x5, starting transfers between devices: 16 us -> 23.4 us  [exchange(): return lax.all_to_all(block, axes, split_axis=0, concat_axis=0, tiled=True)]
    pallas_call x2 -> x1, Pallas kernels: 14 us -> 6.98 us  [multiply(): pl.pallas_call(functools.partial(multiply_kernel, pos_count=pos_count), g...]
  transfers between devices with their start and end apart: 18 -> 21, of which waited for: 6 -> 4; matrix products, arithmetic and copies ran while one was open for 4% -> 3% of each run, Pallas kernels for 13% -> 36%
where the time goes in v7:
time: 571 us; the launch traced here: 569 us
  Pallas kernels  261 us (46%)
  waiting for transfers between devices  206 us (36%)
  starting transfers between devices  56.9 us (10%)
  local copies, waits for them, and re-layouts  18.3 us (3%)
  between operations  14.5 us (3%)
  other arithmetic  8.88 us (2%)
    pallas_call x2, Pallas kernels, merge(): pl.pallas_call(functools.partial(merge_kernel, parts=len(pieces), slots=s...  145 us
    ppermute x1, waiting for transfers between devices, on_device(): partial = lax.ppermute(theirs, 'half', swap)  108 us
    all_gather x1, waiting for transfers between devices, on_device(): lax.all_gather(jnp.concatenate(logits, axis=0), 'row', axis=0, tiled=True)  58.7 us
    pallas_call x2, Pallas kernels, front(): pl.pallas_call(functools.partial(front_kernel, row_count=len(rights), col...  30.6 us
    pallas_call x6, Pallas kernels, project(): pl.pallas_call(functools.partial(project_kernel, first_row=first_row), gr...  26.1 us
    ppermute x2, waiting for transfers between devices, on_device(): crossed.append(lax.ppermute(to_other, 'half', swap))  25.7 us
    all_to_all x5, starting transfers between devices, exchange(): return lax.all_to_all(block, axes, split_axis=0, concat_axis=0, tiled=True)  23.4 us
    ppermute x8, starting transfers between devices, on_device(): lefts.append(lax.ppermute(own_left, AXES, pairs))  18.6 us
  transfers between devices with their start and end apart: 21, of which 4 were waited for; matrix products, arithmetic and copies ran while one was open for 3% of the time, Pallas kernels for 36%

profile of v7, /device:TPU:0, one launch (start us, length us, event | category | flops | bytes accessed | tf_op | source)
XLA Modules:
  0.0 569.2 jit_solution(6840355657820046531)
XLA Ops:
  13.0 7.6 %collective-permute-start.1 = (bf16[4,96,32]{2,1,0:T(8,128)(2,1)S(1)}, bf16[4,96,32]{2,1,0:T(8,128)(2,1)S(1)}, u32[]{:S(2)}, u32[]{:S(2)}) collective-permute-start(bf16[4,96,32]{2,1,0:T(8,128)(2,1)S(1)} %get-tuple-element.43), channel_id=1, source_target_pairs={{0,7},{1,0},{2,15},{3,8},{4,23},{5,16},{6,31},{7,24},{8,1},{9,2},{... | collective-permute-start | bytes 73736 | tf_op jit(solution)/shard_map/ppermute | solution.py:771
  24.1 2.2 collective-permute-start.5
  28.5 3.2 collective-permute-start.7
  31.8 5.8 %collective-permute-start.10 = (bf16[4,96,32]{2,1,0:T(8,128)(2,1)S(1)}, bf16[4,96,32]{2,1,0:T(8,128)(2,1)S(1)}, u32[]{:S(2)}, u32[]{:S(2)}) collective-permute-start(bf16[4,96,32]{2,1,0:T(8,128)(2,1)S(1)} %get-tuple-element.42.refs_8_), channel_id=1, source_target_pairs={{0,8},{8,16},{16,24},{24,0},{1,9},{9,17},{17,25},{25,1},{2,10},{10... | collective-permute-start | bytes 73736 | tf_op jit(solution)/shard_map/ppermute | solution.py:775
  37.6 5.3 collective-permute-start.9
  49.7 15.3 %front.2 = (bf16[96,96,128]{2,1,0:T(8,128)(2,1)}, bf16[96,96,128]{2,1,0:T(8,128)(2,1)}) custom-call(s32[2]{0:T(128)} %pad_add_fusion.place_ref, bf16[4,96,32]{2,1,0:T(8,128)(2,1)} %copy-done.10, bf16[4,96,32]{2,1,0:T(8,128)(2,1)} %copy-done.11, bf16[4,96,32]{2,1,0:T(8,128)(2,1)} %copy-done.12, bf16[4,96,32]{2,1,0:T(8,128)(2,1)} %copy-done.13, ...), custom_call_target="tpu_custom_call" | custom-call | flops 1000 | bytes 1000 | tf_op jit(solution)/shard_map/front/pallas_call | solution.py:183
  65.0 4.6 project.7.refs_1_
  69.6 4.2 project.6.refs_0_
  73.8 3.7 all-to-all-start
  78.2 15.4 %front.3 = (bf16[96,96,128]{2,1,0:T(8,128)(2,1)}, bf16[96,96,128]{2,1,0:T(8,128)(2,1)}) custom-call(s32[2]{0:T(128)} %pad_add_fusion.place_ref, bf16[4,96,32]{2,1,0:T(8,128)(2,1)} %copy-done.10, bf16[4,96,32]{2,1,0:T(8,128)(2,1)} %copy-done.11, bf16[4,96,32]{2,1,0:T(8,128)(2,1)} %copy-done.12, bf16[4,96,32]{2,1,0:T(8,128)(2,1)} %copy-done.13, ...), custom_call_target="tpu_custom_call" | custom-call | flops 1000 | bytes 1000 | tf_op jit(solution)/shard_map/front/pallas_call | solution.py:183
  93.6 4.7 project.9.refs_1_
  98.3 4.2 project.8.refs_0_
  102.5 4.2 project.10.refs_0_
  106.7 25.7 %collective-permute-done.11.refs_4_.refs_2_ = bf16[16,96,384]{2,1,0:T(8,128)(2,1)} collective-permute-done((bf16[16,96,384]{2,1,0:T(8,128)(2,1)}, bf16[16,96,384]{2,1,0:T(8,128)(2,1)}, u32[]{:S(2)}, u32[]{:S(2)}) %collective-permute-start.11) | collective-permute-done | bytes 1179680 | tf_op jit(solution)/shard_map/ppermute | solution.py:851
  133.7 5.2 all-to-all-start.1
  140.9 4.2 project.11.refs_1_
  145.1 108.3 %merge.2.refs_1_ = bf16[16,384,384]{2,1,0:T(8,128)(2,1)} custom-call(bf16[16,96,384]{2,1,0:T(8,128)(2,1)} %project.10.refs_0_, bf16[16,96,384]{2,1,0:T(8,128)(2,1)} %project.11.refs_1_, bf16[16,96,384]{2,1,0:T(8,128)(2,1)} %collective-permute-done.11.refs_4_.refs_2_), custom_call_target="tpu_custom_call" | custom-call | flops 1000 | bytes 1000 | tf_op jit(solution)/shard_map/merge/pallas_call | solution.py:622
  253.4 36.8 %merge.3.refs_1_ = bf16[16,384,384]{2,1,0:T(8,128)(2,1)} custom-call(bf16[16,96,384]{2,1,0:T(8,128)(2,1)} %collective-permute-done.12.refs_0_, bf16[16,384,384]{2,1,0:T(8,128)(2,1)} %merge.2.refs_1_), custom_call_target="tpu_custom_call", output_to_operand_aliasing={{}: (1, {})} | custom-call | flops 1000 | bytes 1000 | tf_op jit(solution)/shard_map/merge/pallas_call | solution.py:622
  291.8 9.3 %assemble_half.1 = (bf16[4,768,384]{2,1,0:T(8,128)(2,1)}, bf16[4,384,384]{2,1,0:T(8,128)(2,1)}, bf16[4,768,384]{2,1,0:T(8,128)(2,1)}) custom-call(s32[1]{0:T(128)} %bitcast.6.half_ref, bf16[16,192,384]{2,1,0:T(8,128)(2,1)} %copy-done.2, bf16[16,192,384]{2,1,0:T(8,128)(2,1)} %copy-done.4), custom_call_target="tpu_custom_call" | custom-call | flops 1000 | bytes 1000 | tf_op jit(solution)/shard_map/assemble_half/pallas_call | solution.py:528
  301.1 5.1 all-to-all-start.2
  307.3 107.9 %collective-permute-done.13.recv_ref = bf16[4,768,384]{2,1,0:T(8,128)(2,1)S(1)} collective-permute-done((bf16[4,768,384]{2,1,0:T(8,128)(2,1)}, bf16[4,768,384]{2,1,0:T(8,128)(2,1)S(1)}, u32[]{:S(2)}, u32[]{:S(2)}) %collective-permute-start.13) | collective-permute-done | bytes 2359328 | tf_op jit(solution)/shard_map/ppermute | solution.py:860
  416.6 10.3 %combine.1.refs_0_ = bf16[16,192,384]{2,1,0:T(8,128)(2,1)} custom-call(bf16[4,768,384]{2,1,0:T(8,128)(2,1)} %get-tuple-element.31.left_ref, bf16[4,384,384]{2,1,0:T(8,128)(2,1)} %get-tuple-element.32.own_ref, bf16[4,768,384]{2,1,0:T(8,128)(2,1)} %copy-done.5, bf16[16,384,384]{2,1,0:T(8,128)(2,1)} %all-to-all-done.2.refs_0_.recv_ref), custom_call_target="tpu_custom_call" | custom-call | flops 1000 | bytes 1000 | tf_op jit(solution)/shard_map/combine/pallas_call | solution.py:589
  426.9 5.2 all-to-all-start.3
  433.2 5.3 logit.2
  438.5 5.3 logit.3
  445.8 8.9 %assemble.1 = (bf16[2,16,48,768]{3,2,1,0:T(8,128)(2,1)}, bf16[2,4,1,192,768]{4,3,2,1,0:T(8,128)(2,1)}) custom-call(bf16[16,384,384]{2,1,0:T(8,128)(2,1)} %all-to-all-done.2.refs_0_.recv_ref, bf16[16,192,384]{2,1,0:T(8,128)(2,1)} %combine.1.refs_0_), custom_call_target="tpu_custom_call" | custom-call | flops 1000 | bytes 1000 | tf_op jit(solution)/shard_map/assemble/pallas_call | solution.py:366
  454.7 7.0 %multiply.13.refs_2_ = bf16[32,96,384]{2,1,0:T(8,128)(2,1)} custom-call(bf16[2,16,48,768]{3,2,1,0:T(8,128)(2,1)} %get-tuple-element.34.left_ref, bf16[2,768,768]{2,1,0:T(8,128)(2,1)} %bitcast.52), custom_call_target="tpu_custom_call" | custom-call | flops 1000 | bytes 1000 | tf_op jit(solution)/shard_map/multiply/pallas_call | solution.py:431
  461.7 13.4 %all-to-all-done.3.refs_0_ = bf16[16,192,384]{2,1,0:T(8,128)(2,1)S(1)} async-done(((bf16[16,192,384]{2,1,0:T(8,128)(2,1)}), bf16[16,192,384]{2,1,0:T(8,128)(2,1)S(1)}, u32[]{:S(2)}, u32[]{:S(2)}) %all-to-all-start.3) | async-done | bytes 2359328 | tf_op jit(solution)/shard_map/all_to_all | solution.py:790
  476.5 4.3 all-to-all-start.4
  482.8 58.7 %all-gather.3.cloned.1.call-done.refs_0_ = f32[768,8,96]{2,1,0:T(8,128)} async-done(((f32[192,8,96]{2,1,0:T(8,128)}), f32[768,8,96]{2,1,0:T(8,128)}) %all-gather.3.cloned.1.call-update) | async-done | bytes 2359312 | tf_op jit(solution)/shard_map/all_gather | solution.py:881
  541.5 2.7 copy.108
  549.3 13.1 %finish.1 = bf16[192,96,128]{2,1,0:T(8,128)(2,1)} custom-call(bf16[16,192,384]{2,1,0:T(8,128)(2,1)} %copy-done.3, bf16[32,96,384]{2,1,0:T(8,128)(2,1)} %all-to-all-done.4.refs_1_, bf16[96,96,128]{2,1,0:T(8,128)(2,1)} %get-tuple-element.38.refs_2_, bf16[96,96,128]{2,1,0:T(8,128)(2,1)} %get-tuple-element.39.refs_3_, ...), custom_call_target="tpu_custom_call" | custom-call | flops 1000 | bytes 1000 | tf_op jit(solution)/shard_map/finish/pallas_call | solution.py:694
  (130 shorter events, 37.6 us)
Async XLA Ops:
  7.2 541.0 %copy-start = (bf16[256,64]{0,1:T(8,128)(2,1)S(1)}, bf16[256,64]{0,1:T(8,128)(2,1)}, u32[]{:S(2)}) copy-start(bf16[256,64]{0,1:T(8,128)(2,1)} %param.17) | copy-start | bytes 98308
  7.2 16.6 %copy-start.22 = (bf16[128,640]{1,0:T(8,128)(2,1)S(1)}, bf16[128,640]{1,0:T(8,128)(2,1)}, u32[]{:S(2)}) copy-start(bf16[128,640]{1,0:T(8,128)(2,1)} %param.18) | copy-start | bytes 491524
  7.2 37.6 %copy-start.21 = (bf16[1024,128]{1,0:T(8,128)(2,1)S(1)}, bf16[1024,128]{1,0:T(8,128)(2,1)}, u32[]{:S(2)}) copy-start(bf16[1024,128]{1,0:T(8,128)(2,1)} %param.15) | copy-start | bytes 786436
  12.3 36.1 %copy-start.8 = (bf16[4,96,32]{2,1,0:T(8,128)(2,1)}, bf16[4,96,32]{2,1,0:T(8,128)(2,1)S(1)}, u32[]{:S(2)}) copy-start(bf16[4,96,32]{2,1,0:T(8,128)(2,1)S(1)} %get-tuple-element.42.refs_8_) | copy-start | bytes 73732
  12.3 11.7 %collective-permute-start = (bf16[4,96,32]{2,1,0:T(8,128)(2,1)S(1)}, bf16[4,96,32]{2,1,0:T(8,128)(2,1)S(1)}, u32[]{:S(2)}, u32[]{:S(2)}) collective-permute-start(bf16[4,96,32]{2,1,0:T(8,128)(2,1)S(1)} %get-tuple-element.43), channel_id=1, source_target_pairs={{0,0},{1,1},{2,8},{3,9},{4,16},{5,17},{6,24},{7,25},{8,2},{9,3},{1... | collective-permute-start | bytes 73736 | tf_op jit(solution)/shard_map/ppermute | solution.py:771
  13.0 13.9 %collective-permute-start.1 = (bf16[4,96,32]{2,1,0:T(8,128)(2,1)S(1)}, bf16[4,96,32]{2,1,0:T(8,128)(2,1)S(1)}, u32[]{:S(2)}, u32[]{:S(2)}) collective-permute-start(bf16[4,96,32]{2,1,0:T(8,128)(2,1)S(1)} %get-tuple-element.43), channel_id=1, source_target_pairs={{0,7},{1,0},{2,15},{3,8},{4,23},{5,16},{6,31},{7,24},{8,1},{9,2},{... | collective-permute-start | bytes 73736 | tf_op jit(solution)/shard_map/ppermute | solution.py:771
  20.6 7.9 %collective-permute-start.2 = (bf16[4,96,32]{2,1,0:T(8,128)(2,1)S(1)}, bf16[4,96,32]{2,1,0:T(8,128)(2,1)S(1)}, u32[]{:S(2)}, u32[]{:S(2)}) collective-permute-start(bf16[4,96,32]{2,1,0:T(8,128)(2,1)S(1)} %get-tuple-element.43), channel_id=1, source_target_pairs={{0,6},{1,7},{2,14},{3,15},{4,22},{5,23},{6,30},{7,31},{8,0},{9,1},... | collective-permute-start | bytes 73736 | tf_op jit(solution)/shard_map/ppermute | solution.py:771
  21.5 10.3 %collective-permute-start.3 = (bf16[4,96,32]{2,1,0:T(8,128)(2,1)S(1)}, bf16[4,96,32]{2,1,0:T(8,128)(2,1)S(1)}, u32[]{:S(2)}, u32[]{:S(2)}) collective-permute-start(bf16[4,96,32]{2,1,0:T(8,128)(2,1)S(1)} %get-tuple-element.43), channel_id=1, source_target_pairs={{0,5},{1,6},{2,13},{3,14},{4,21},{5,22},{6,29},{7,30},{8,7},{9,0},... | collective-permute-start | bytes 73736 | tf_op jit(solution)/shard_map/ppermute | solution.py:771
  23.2 14.4 %collective-permute-start.4 = (bf16[4,96,32]{2,1,0:T(8,128)(2,1)S(1)}, bf16[4,96,32]{2,1,0:T(8,128)(2,1)S(1)}, u32[]{:S(2)}, u32[]{:S(2)}) collective-permute-start(bf16[4,96,32]{2,1,0:T(8,128)(2,1)S(1)} %get-tuple-element.43), channel_id=1, source_target_pairs={{0,4},{1,5},{2,12},{3,13},{4,20},{5,21},{6,28},{7,29},{8,6},{9,7},... | collective-permute-start | bytes 73736 | tf_op jit(solution)/shard_map/ppermute | solution.py:771
  24.1 24.3 %copy-start.10 = (bf16[4,96,32]{2,1,0:T(8,128)(2,1)}, bf16[4,96,32]{2,1,0:T(8,128)(2,1)S(1)}, u32[]{:S(2)}) copy-start(bf16[4,96,32]{2,1,0:T(8,128)(2,1)S(1)} %collective-permute-done.refs_0_) | copy-start | bytes 73732
  24.1 13.5 %collective-permute-start.5 = (bf16[4,96,32]{2,1,0:T(8,128)(2,1)S(1)}, bf16[4,96,32]{2,1,0:T(8,128)(2,1)S(1)}, u32[]{:S(2)}, u32[]{:S(2)}) collective-permute-start(bf16[4,96,32]{2,1,0:T(8,128)(2,1)S(1)} %get-tuple-element.43), channel_id=1, source_target_pairs={{0,3},{1,4},{2,11},{3,12},{4,19},{5,20},{6,27},{7,28},{8,5},{9,6},... | collective-permute-start | bytes 73736 | tf_op jit(solution)/shard_map/ppermute | solution.py:771
  26.9 21.5 %copy-start.11 = (bf16[4,96,32]{2,1,0:T(8,128)(2,1)}, bf16[4,96,32]{2,1,0:T(8,128)(2,1)S(1)}, u32[]{:S(2)}) copy-start(bf16[4,96,32]{2,1,0:T(8,128)(2,1)S(1)} %collective-permute-done.1.refs_1_) | copy-start | bytes 73732
  26.9 21.4 %collective-permute-start.6 = (bf16[4,96,32]{2,1,0:T(8,128)(2,1)S(1)}, bf16[4,96,32]{2,1,0:T(8,128)(2,1)S(1)}, u32[]{:S(2)}, u32[]{:S(2)}) collective-permute-start(bf16[4,96,32]{2,1,0:T(8,128)(2,1)S(1)} %get-tuple-element.43), channel_id=1, source_target_pairs={{0,2},{1,3},{2,10},{3,11},{4,18},{5,19},{6,26},{7,27},{8,4},{9,5},... | collective-permute-start | bytes 73736 | tf_op jit(solution)/shard_map/ppermute | solution.py:771
  28.5 19.9 %copy-start.12 = (bf16[4,96,32]{2,1,0:T(8,128)(2,1)}, bf16[4,96,32]{2,1,0:T(8,128)(2,1)S(1)}, u32[]{:S(2)}) copy-start(bf16[4,96,32]{2,1,0:T(8,128)(2,1)S(1)} %collective-permute-done.2.refs_2_) | copy-start | bytes 73732
  28.5 19.8 %collective-permute-start.7 = (bf16[4,96,32]{2,1,0:T(8,128)(2,1)S(1)}, bf16[4,96,32]{2,1,0:T(8,128)(2,1)S(1)}, u32[]{:S(2)}, u32[]{:S(2)}) collective-permute-start(bf16[4,96,32]{2,1,0:T(8,128)(2,1)S(1)} %get-tuple-element.43), channel_id=1, source_target_pairs={{0,1},{1,2},{2,9},{3,10},{4,17},{5,18},{6,25},{7,26},{8,3},{9,4},{... | collective-permute-start | bytes 73736 | tf_op jit(solution)/shard_map/ppermute | solution.py:771
  31.8 16.7 %copy-start.13 = (bf16[4,96,32]{2,1,0:T(8,128)(2,1)}, bf16[4,96,32]{2,1,0:T(8,128)(2,1)S(1)}, u32[]{:S(2)}) copy-start(bf16[4,96,32]{2,1,0:T(8,128)(2,1)S(1)} %collective-permute-done.3.refs_3_) | copy-start | bytes 73732
  31.8 16.6 %collective-permute-start.10 = (bf16[4,96,32]{2,1,0:T(8,128)(2,1)S(1)}, bf16[4,96,32]{2,1,0:T(8,128)(2,1)S(1)}, u32[]{:S(2)}, u32[]{:S(2)}) collective-permute-start(bf16[4,96,32]{2,1,0:T(8,128)(2,1)S(1)} %get-tuple-element.42.refs_8_), channel_id=1, source_target_pairs={{0,8},{8,16},{16,24},{24,0},{1,9},{9,17},{17,25},{25,1},{2,10},{10... | collective-permute-start | bytes 73736 | tf_op jit(solution)/shard_map/ppermute | solution.py:775
  37.6 10.9 %copy-start.14 = (bf16[4,96,32]{2,1,0:T(8,128)(2,1)}, bf16[4,96,32]{2,1,0:T(8,128)(2,1)S(1)}, u32[]{:S(2)}) copy-start(bf16[4,96,32]{2,1,0:T(8,128)(2,1)S(1)} %collective-permute-done.4.refs_4_) | copy-start | bytes 73732
  37.6 10.8 %collective-permute-start.8 = (bf16[4,96,32]{2,1,0:T(8,128)(2,1)S(1)}, bf16[4,96,32]{2,1,0:T(8,128)(2,1)S(1)}, u32[]{:S(2)}, u32[]{:S(2)}) collective-permute-start(bf16[4,96,32]{2,1,0:T(8,128)(2,1)S(1)} %get-tuple-element.42.refs_8_), channel_id=1, source_target_pairs={{0,24},{8,0},{16,8},{24,16},{1,25},{9,1},{17,9},{25,17},{2,26},{10... | collective-permute-start | bytes 73736 | tf_op jit(solution)/shard_map/ppermute | solution.py:775
  37.6 10.8 %copy-start.15 = (bf16[4,96,32]{2,1,0:T(8,128)(2,1)}, bf16[4,96,32]{2,1,0:T(8,128)(2,1)S(1)}, u32[]{:S(2)}) copy-start(bf16[4,96,32]{2,1,0:T(8,128)(2,1)S(1)} %collective-permute-done.5.refs_5_) | copy-start | bytes 73732
  37.6 10.8 %collective-permute-start.9 = (bf16[4,96,32]{2,1,0:T(8,128)(2,1)S(1)}, bf16[4,96,32]{2,1,0:T(8,128)(2,1)S(1)}, u32[]{:S(2)}, u32[]{:S(2)}) collective-permute-start(bf16[4,96,32]{2,1,0:T(8,128)(2,1)S(1)} %get-tuple-element.42.refs_8_), channel_id=1, source_target_pairs={{0,16},{8,24},{16,0},{24,8},{1,17},{9,25},{17,1},{25,9},{2,18},{10... | collective-permute-start | bytes 73736 | tf_op jit(solution)/shard_map/ppermute | solution.py:775
  73.8 58.5 %all-to-all-start = ((bf16[16,192,384]{2,1,0:T(8,128)(2,1)}), bf16[16,192,384]{2,1,0:T(8,128)(2,1)S(1)}, u32[]{:S(2)}, u32[]{:S(2)}) async-start(bf16[16,192,384]{2,1,0:T(8,128)(2,1)} %get-tuple-element.22), calls=%async_computation | async-start | bytes 4718592 | tf_op jit(solution)/shard_map/all_to_all | solution.py:790
  77.5 54.8 %collective-permute-start.11 = (bf16[16,96,384]{2,1,0:T(8,128)(2,1)}, bf16[16,96,384]{2,1,0:T(8,128)(2,1)}, u32[]{:S(2)}, u32[]{:S(2)}) collective-permute-start(bf16[16,96,384]{2,1,0:T(8,128)(2,1)} %get-tuple-element.25), channel_id=1, source_target_pairs={{0,4},{4,0},{1,5},{5,1},{2,6},{6,2},{3,7},{7,3},{8,12},{12,8},{9,1... | collective-permute-start | bytes 3538952 | tf_op jit(solution)/shard_map/ppermute | solution.py:851
  133.7 156.6 %all-to-all-start.1 = ((bf16[16,192,384]{2,1,0:T(8,128)(2,1)}), bf16[16,192,384]{2,1,0:T(8,128)(2,1)S(1)}, u32[]{:S(2)}, u32[]{:S(2)}) async-start(bf16[16,192,384]{2,1,0:T(8,128)(2,1)} %get-tuple-element.26), calls=%async_computation.1 | async-start | bytes 4718592 | tf_op jit(solution)/shard_map/all_to_all | solution.py:790
  138.9 114.5 %collective-permute-start.12 = (bf16[16,96,384]{2,1,0:T(8,128)(2,1)}, bf16[16,96,384]{2,1,0:T(8,128)(2,1)}, u32[]{:S(2)}, u32[]{:S(2)}) collective-permute-start(bf16[16,96,384]{2,1,0:T(8,128)(2,1)} %get-tuple-element.28), channel_id=1, source_target_pairs={{0,4},{4,0},{1,5},{5,1},{2,6},{6,2},{3,7},{7,3},{8,12},{12,8},{9,1... | collective-permute-start | bytes 3538952 | tf_op jit(solution)/shard_map/ppermute | solution.py:851
  301.1 114.1 %all-to-all-start.2 = ((bf16[16,384,384]{2,1,0:T(8,128)(2,1)}), bf16[16,384,384]{2,1,0:T(8,128)(2,1)}, u32[]{:S(2)}, u32[]{:S(2)}) async-start(bf16[16,384,384]{2,1,0:T(8,128)(2,1)} %get-tuple-element.30), calls=%async_computation.2 | async-start | bytes 9437184 | tf_op jit(solution)/shard_map/all_to_all | solution.py:790
  306.1 109.0 %collective-permute-start.13 = (bf16[4,768,384]{2,1,0:T(8,128)(2,1)}, bf16[4,768,384]{2,1,0:T(8,128)(2,1)S(1)}, u32[]{:S(2)}, u32[]{:S(2)}) collective-permute-start(bf16[4,768,384]{2,1,0:T(8,128)(2,1)} %get-tuple-element.33), channel_id=1, source_target_pairs={{0,4},{4,0},{1,5},{5,1},{2,6},{6,2},{3,7},{7,3},{8,12},{12,8},{9,1... | collective-permute-start | bytes 7077896 | tf_op jit(solution)/shard_map/ppermute | solution.py:860
  426.9 48.1 %all-to-all-start.3 = ((bf16[16,192,384]{2,1,0:T(8,128)(2,1)}), bf16[16,192,384]{2,1,0:T(8,128)(2,1)S(1)}, u32[]{:S(2)}, u32[]{:S(2)}) async-start(bf16[16,192,384]{2,1,0:T(8,128)(2,1)} %combine.1.refs_0_), calls=%async_computation.3 | async-start | bytes 4718592 | tf_op jit(solution)/shard_map/all_to_all | solution.py:790
  432.1 50.7 %all-gather.5.cloned.1.call-start = ((), (), s32[]{:S(2)}) async-start(), calls=%async_computation.6 | async-start | bytes 1769472 | tf_op jit(solution)/shard_map/all_gather | solution.py:882
  433.1 108.4 %all-gather.3.cloned.1.call-start = ((), (), s32[]{:S(2)}) async-start(), calls=%async_computation.5 | async-start | bytes 3932160 | tf_op jit(solution)/shard_map/all_gather | solution.py:881
  461.7 20.5 %copy-start.23 = (bf16[128,128]{1,0:T(8,128)(2,1)S(1)}, bf16[128,128]{1,0:T(8,128)(2,1)}, u32[]{:S(2)}) copy-start(bf16[128,128]{1,0:T(8,128)(2,1)} %param.19) | copy-start | bytes 98308
  476.5 72.8 %all-to-all-start.4 = ((bf16[32,96,384]{2,1,0:T(8,128)(2,1)}), bf16[32,96,384]{2,1,0:T(8,128)(2,1)}, u32[]{:S(2)}, u32[]{:S(2)}) async-start(bf16[32,96,384]{2,1,0:T(8,128)(2,1)} %multiply.13.refs_2_), calls=%async_computation.4 | async-start | bytes 4718592 | tf_op jit(solution)/shard_map/all_to_all | solution.py:790
  (14 other events, 29.0 us)
Sparse Core Ops, SparseCore 0:
  434.6 34.3 all-gather.4
  470.8 70.7 all-gather.2

commit v8 on v7

--- a/solution.py
+++ b/solution.py
@@ -281,35 +281,46 @@
     )(live_rows, normed, live_cols, weight)
 
 
-def logit_kernel(live_ref, normed_ref, weight_ref, *refs, first_row):
-    out_ref = refs[-1]
-    block = normed_ref.shape[0]
-    for i in range(block):
-        live = live_ref[first_row + pl.program_id(0) * block + i]
-        out_ref[i] = lax.dot_general(
-            weight_ref[...], normed_ref[i], NT, preferred_element_type=F32
-        ) + MASK_PENALTY * (live - 1.0)
-
-
-def logit(first_row, live_rows, normed, weight, after):
-    rows, cols, wide = normed.shape
-    block = 16
+def logit_kernel(live_ref, *refs, chunks):
+    normeds, weight_ref, out_ref = refs[:chunks], refs[chunks], refs[-1]
+    block = out_ref.shape[0]
+    steps = pl.num_programs(0) // chunks
+
+    def rows(normed_ref):
+        for i in range(block):
+            live = live_ref[pl.program_id(0) * block + i]
+            out_ref[i] = lax.dot_general(
+                weight_ref[...], normed_ref[i], NT, preferred_element_type=F32
+            ) + MASK_PENALTY * (live - 1.0)
+
+    for chunk in range(chunks):
+        pl.when(pl.program_id(0) // steps == chunk)(functools.partial(rows, normeds[chunk]))
+
+
+def chunk_tiles(shape, chunks, steps):
+    def tile(chunk):
+        return pl.BlockSpec(shape, lambda i: (jnp.clip(i - chunk * steps, 0, steps - 1), 0, 0))
+
+    return [tile(chunk) for chunk in range(chunks)]
+
+
+def logit(live_rows, normeds, weight, after):
+    rows, cols, wide = normeds[0].shape
+    block, chunks = 16, len(normeds)
     heads = weight.shape[0]
     return pl.pallas_call(
-        functools.partial(logit_kernel, first_row=first_row),
-        grid=(rows // block,),
-        in_specs=[
-            pl.BlockSpec(memory_space=pltpu.SMEM),
-            pl.BlockSpec((block, cols, wide), lambda i: (i, 0, 0)),
-            whole(weight.shape),
-        ]
+        functools.partial(logit_kernel, chunks=chunks),
+        grid=(rows // block * chunks,),
+        in_specs=[pl.BlockSpec(memory_space=pltpu.SMEM)]
+        + chunk_tiles((block, cols, wide), chunks, rows // block)
+        + [whole(weight.shape)]
         + anywhere(after),
         out_specs=pl.BlockSpec((block, heads, cols), lambda i: (i, 0, 0)),
-        out_shape=jax.ShapeDtypeStruct((rows, heads, cols), F32),
+        out_shape=jax.ShapeDtypeStruct((rows * chunks, heads, cols), F32),
         compiler_params=params(),
         cost_estimate=LIGHT,
         name="logit",
-    )(live_rows, normed, weight, *after)
+    )(live_rows, *normeds, weight, *after)
 
 
 def assemble_kernel(recv_ref, *refs, row_count, pos_count, spans):
@@ -518,7 +529,7 @@
         ).astype(BF16)
 
 
-def assemble_half(half, received, row_count, pos_count, cols):
+def assemble_half(half, received, after, row_count, pos_count, cols):
     sources, _, lanes = received[0].shape
     height = sum(part.shape[1] for part in received)
     each = (2 * pos_count * cols) // (row_count * QUAD)
@@ -530,7 +541,9 @@
             assemble_half_kernel, row_count=row_count, pos_count=pos_count, parts=len(received)
         ),
         grid=(channels,),
-        in_specs=[pl.BlockSpec(memory_space=pltpu.SMEM)] + [whole(part.shape) for part in received],
+        in_specs=[pl.BlockSpec(memory_space=pltpu.SMEM)]
+        + [whole(part.shape) for part in received]
+        + anywhere(after),
         out_specs=[
             pl.BlockSpec((1, rows, depth), lambda c: (c, 0, 0)),
             pl.BlockSpec((1, depth, depth), lambda c: (c, 0, 0)),
@@ -548,7 +561,7 @@
         compiler_params=params(),
         cost_estimate=LIGHT,
         name="assemble_half",
-    )(half, *received)
+    )(half, *received, *after)
 
 
 def combine_kernel(left_ref, own_ref, recv_ref, *refs, row_count, pos_count):
@@ -604,32 +617,76 @@
     )(left, own, received, *after)
 
 
-def merge_kernel(*refs, parts, slots):
-    pieces, (out_ref, sems) = refs[:parts], refs[-2:]
-    copies = []
-    for index, (piece, slot) in enumerate(zip(pieces, slots)):
-        height = piece.shape[1]
-        place = out_ref.at[:, pl.ds(slot * height, height), :]
-        copies.append(pltpu.make_async_copy(piece, place, sems.at[index]))
-    for copy in copies:
-        copy.start()
-    for copy in copies:
-        copy.wait()
-
-
-def merge(pieces, slots, count, into):
+def merge_kernel(*refs, parts):
+    for index, piece in enumerate(refs[:parts]):
+
+        @pl.when(pl.program_id(0) == index)
+        def _():
+            refs[-1][...] = piece[...]
+
+
+def merge(pieces, first, count, into):
     sources, height, lanes = pieces[0].shape
     return pl.pallas_call(
-        functools.partial(merge_kernel, parts=len(pieces), slots=slots),
-        in_specs=anywhere(pieces) + anywhere(into),
-        out_specs=pl.BlockSpec(memory_space=pl.ANY),
+        functools.partial(merge_kernel, parts=len(pieces)),
+        grid=(len(pieces),),
+        in_specs=[whole(piece.shape) for piece in pieces] + anywhere(into),
+        out_specs=pl.BlockSpec((sources, height, lanes), lambda i: (0, i + first, 0)),
         out_shape=jax.ShapeDtypeStruct((sources, height * count, lanes), BF16),
         input_output_aliases={len(pieces): 0} if into else {},
-        scratch_shapes=[pltpu.SemaphoreType.DMA((len(pieces),))],
-        compiler_params=pltpu.CompilerParams(vmem_limit_bytes=60 * MIB),
+        compiler_params=params(),
         cost_estimate=LIGHT,
         name="merge",
     )(*pieces, *into)
+
+
+def average_kernel(place_ref, *refs, row_count, col_count):
+    logits, values = refs[:row_count], refs[row_count : row_count + col_count]
+    gate_ref, align_ref, weight_ref, out_ref, exp_ref, value_ref = refs[row_count + col_count :]
+    rows, heads, cols = logits[0].shape
+    per_row = col_count // row_count
+    for u, value in enumerate(values):
+        value_ref[lax.rem(place_ref[1] + u, col_count)] = value[...]
+    top = jnp.max(logits[0][...], axis=0)
+    for block in logits[1:]:
+        top = jnp.maximum(top, jnp.max(block[...], axis=0))
+    total = jnp.zeros((heads, cols), F32)
+    size = rows * heads
+    for t, block in enumerate(logits):
+        powers = jnp.exp(block[...] - top[None])
+        total = total + jnp.sum(powers, axis=0)
+        exp_ref[t * size : (t + 1) * size, 0:cols] = powers.reshape(size, cols)
+    out = align_ref[...].astype(F32)
+    for h in range(heads):
+        summed = jnp.zeros(gate_ref.shape[1:], F32)
+        for t in range(row_count):
+            first = lax.rem(place_ref[0] + t, row_count) * per_row
+            powers = exp_ref[pl.ds(t * size + h, rows, stride=heads), :][:, :cols]
+            weights = (powers / total[h : h + 1]).astype(BF16)
+            value = jnp.concatenate([value_ref[first + k, h] for k in range(per_row)], axis=0)
+            summed += lax.dot_general(weights, value, TN, preferred_element_type=F32)
+        gated = (gate_ref[h] * summed).astype(BF16)
+        out += jnp.dot(gated, weight_ref[h], preferred_element_type=F32)
+    out_ref[...] = out.astype(BF16)
+
+
+def average(place, logits, values, gate, align, weight):
+    rows, heads, cols = logits[0].shape
+    operands = [*logits, *values, gate, align, weight]
+    return pl.pallas_call(
+        functools.partial(average_kernel, row_count=len(logits), col_count=len(values)),
+        grid=(1,),
+        in_specs=[pl.BlockSpec(memory_space=pltpu.SMEM)] + [whole(v.shape) for v in operands],
+        out_specs=whole(align.shape),
+        out_shape=jax.ShapeDtypeStruct(align.shape, BF16),
+        scratch_shapes=[
+            pltpu.VMEM((len(logits) * rows * heads, LANES), F32),
+            pltpu.VMEM((len(values), *values[0].shape), BF16),
+        ],
+        compiler_params=params(),
+        cost_estimate=LIGHT,
+        name="average",
+    )(place, *operands)
 
 
 def finish_kernel(*refs, parts, chunks):
@@ -684,13 +741,7 @@
     quads = max(8, 16 // min(heights))
     steps = rows // QUAD // quads
 
-    def tile(chunk):
-        return pl.BlockSpec(
-            (quads * QUAD, cols, wide),
-            lambda i: (jnp.clip(i - chunk * steps, 0, steps - 1), 0, 0),
-        )
-
-    tiles = [tile(chunk) for chunk in range(chunks)]
+    tiles = chunk_tiles((quads * QUAD, cols, wide), chunks, steps)
     return pl.pallas_call(
         functools.partial(finish_kernel, parts=len(products), chunks=chunks),
         grid=(total // quads,),
@@ -793,7 +844,7 @@
         return front(
             chunk,
             chunks,
-            jnp.stack([row_index, col_index]).astype(jnp.int32),
+            place,
             lefts,
             rights,
             present_rows,
@@ -806,6 +857,33 @@
     def project_rows(chunk, normed, weight, dests):
         first_row = chunk * normed.shape[0]
         return project(first_row, live_rows, normed, live_packed, weight, dests)
+
+    place = jnp.stack([row_index, col_index]).astype(jnp.int32)
+
+    def by_head(part):
+        part = part.reshape(seq_each, module_number, MEAN_GROUPS, GROUP_FEATURES)
+        return jnp.transpose(part, (2, 1, 0, 3)).reshape(MEAN_GROUPS, module_number, -1)
+
+    first = 2 * TENSOR_FEATURES
+    middle = first + MEAN_GROUPS * GROUP_FEATURES
+    values = by_head(project_msa(alignment_matrix[:, first:middle]).astype(BF16))
+    sequence_gate = by_head(jax.nn.sigmoid(project_msa(alignment_matrix[:, middle:])))
+    w_mean = mean_final_matrix.reshape(MEAN_GROUPS, 1, GROUP_FEATURES, 1, feature_count)
+    same = jnp.eye(seq_each, dtype=BF16).reshape(1, seq_each, 1, seq_each, 1)
+    w_mean = (w_mean * same).reshape(
+        MEAN_GROUPS, seq_each * GROUP_FEATURES, seq_each * feature_count
+    )
+    align = jnp.transpose(alignment_embedding, (1, 0, 2)).reshape(module_number, -1)
+
+    def update_alignment(logits, values):
+        logit_blocks, value_blocks = [logits], [values]
+        for t in range(1, row_count):
+            pairs = [(r, (r - t) % row_count) for r in range(row_count)]
+            logit_blocks.append(lax.ppermute(logits, "row", pairs))
+        for t in range(1, col_count):
+            pairs = [(q, (q - t) % col_count) for q in range(col_count)]
+            value_blocks.append(lax.ppermute(values, ("half", "pos"), pairs))
+        return average(place, logit_blocks, value_blocks, sequence_gate, align, w_mean)
 
     group = devices // 2
     shape_of = (row_count, col_count, module_number)
@@ -826,7 +904,7 @@
         right = right.reshape(right.shape[0], -1, right.shape[-1])
         last = multiply(left, right, (), *shape_of[1:])
         returned.append(exchange(last, AXES))
-        after = (last,)
+        logits = logit(live_rows, normeds, w_logit, ())
         orders = [(0, CTRI, devices)]
     else:
         cut = CTRI // 2
@@ -853,13 +931,15 @@
             ahead = (w_own,)
             kept.append(project_rows(chunk, normed, w_own, group))
         half_scalar = half.astype(jnp.int32).reshape(1)
-        left, own, theirs = assemble_half(half_scalar, received, *half_shape)
-        merged = merge(kept + crossed[:-1], tuple(range(2 * row_chunks - 1)), 2 * row_chunks, ())
-        merged = merge(crossed[-1:], (2 * row_chunks - 1,), 2 * row_chunks, (merged,))
+        logits = logit(live_rows, normeds, w_logit, tuple(kept))
+        merged = merge(kept + crossed[:-1], 0, 2 * row_chunks, ())
+        left, own, theirs = assemble_half(
+            half_scalar, received, (logits, values, merged), *half_shape
+        )
+        merged = merge(crossed[-1:], 2 * row_chunks - 1, 2 * row_chunks, (merged,))
         theirs, merged = fence([theirs, merged], ())
         partial = lax.ppermute(theirs, "half", swap)
         both = exchange(merged, GROUP)
-        after = (both,)
         product = combine(left, own, partial, (both,), *half_shape)
         returned.append(exchange(product, GROUP))
         left, right = assemble(0, 1, 2, both, (), (product,), *half_shape)
@@ -867,35 +947,11 @@
         last = multiply(left, right, (), *shape_of[1:])
         returned.append(exchange(last, AXES))
         orders = [(0, cut, group), (cut, CTRI, devices)]
-    logits = [
-        logit(chunk * normed.shape[0], live_rows, normed, w_logit, after)
-        for chunk, normed in enumerate(normeds)
-    ]
-
-    values = project_msa(
-        alignment_matrix[:, 2 * TENSOR_FEATURES : 2 * TENSOR_FEATURES + MEAN_GROUPS * GROUP_FEATURES]
-    ).astype(BF16)
-    sequence_gate = jax.nn.sigmoid(
-        project_msa(alignment_matrix[:, 2 * TENSOR_FEATURES + MEAN_GROUPS * GROUP_FEATURES :])
+    logits, values = fence([logits, values], (last,))
+    aligned = update_alignment(logits, values)
+    alignment_updated_embedding = jnp.transpose(
+        aligned.reshape(module_number, seq_each, feature_count), (1, 0, 2)
     )
-    logits_all = lax.all_gather(jnp.concatenate(logits, axis=0), "row", axis=0, tiled=True)
-    values_all = lax.all_gather(values, ("half", "pos"), axis=1, tiled=True)
-
-    logits_all, values_all = fence([logits_all, values_all], (last,))
-    top_all = jnp.max(logits_all, axis=0)
-    expd = jnp.exp(logits_all - top_all[None])
-    weights_all = (expd / jnp.sum(expd, axis=0)[None]).astype(BF16)
-    value_all_heads = values_all.reshape(seq_each, -1, MEAN_GROUPS, GROUP_FEATURES)
-    summed = jnp.einsum("jhi,sjhd->sihd", weights_all, value_all_heads, preferred_element_type=F32)
-    head_averaged = summed.reshape(seq_each, module_number, MEAN_GROUPS * GROUP_FEATURES)
-    gated_result = (sequence_gate * head_averaged).astype(BF16)
-    blended_update = jnp.dot(
-        gated_result.reshape(seq_each * module_number, -1),
-        mean_final_matrix,
-        preferred_element_type=F32,
-    ).reshape(seq_each, module_number, -1)
-    alignment_updated_embedding = (alignment_embedding.astype(F32) + blended_update).astype(BF16)
-
     w_final = jnp.concatenate(
         [
             jnp.transpose(

time: 571 us -> 485 us (0.85)
  Pallas kernels: 261 us -> 127 us
  waiting for transfers between devices: 206 us -> 237 us
  starting transfers between devices: 56.9 us -> 83 us
  between operations: 14.5 us -> 1.21 us
  local copies, waits for them, and re-layouts: 18.3 us -> 24.4 us
    pallas_call x4, Pallas kernels: 156 us -> 21.7 us  [the longest x1 9.57 us: logit(): pl.pallas_call(functools.partial(logit_kernel, chunks=chunks), grid=(rows...]
    ppermute x0 -> x10, waiting for transfers between devices: none -> 59.6 us  [the longest x7 59.6 us: update_alignment(): value_blocks.append(lax.ppermute(values, ('half', 'pos'), pairs))]
    all_gather x2 -> x0, waiting for transfers between devices: 58.7 us -> none  [the longest x1 58.7 us: on_device(): lax.all_gather(jnp.concatenate(logits, axis=0), 'row', axis=0, tiled=True)]
    all_to_all x5, waiting for transfers between devices: 13.4 us -> 43.3 us  [exchange(): return lax.all_to_all(block, axes, split_axis=0, concat_axis=0, tiled=True)]
    ppermute x0 -> x10, starting transfers between devices: none -> 25.9 us  [the longest x7 22.3 us: update_alignment(): value_blocks.append(lax.ppermute(values, ('half', 'pos'), pairs))]
  transfers between devices with their start and end apart: 21 -> 29, of which waited for: 4 -> 9; matrix products, arithmetic and copies ran while one was open for 3% -> 5% of each run, Pallas kernels for 36% -> 16%
where the time goes in v8:
time: 485 us; the launch traced here: 482 us
  waiting for transfers between devices  237 us (49%)
  Pallas kernels  127 us (26%)
  starting transfers between devices  83 us (17%)
  local copies, waits for them, and re-layouts  24.4 us (5%)
  other arithmetic  5.66 us (1%)
    ppermute x1, waiting for transfers between devices, on_device(): partial = lax.ppermute(theirs, 'half', swap)  109 us
    ppermute x7, waiting for transfers between devices, update_alignment(): value_blocks.append(lax.ppermute(values, ('half', 'pos'), pairs))  59.6 us
    all_to_all x5, waiting for transfers between devices, exchange(): return lax.all_to_all(block, axes, split_axis=0, concat_axis=0, tiled=True)  43.3 us
    pallas_call x2, Pallas kernels, front(): pl.pallas_call(functools.partial(front_kernel, row_count=len(rights), col...  30.6 us
    pallas_call x6, Pallas kernels, project(): pl.pallas_call(functools.partial(project_kernel, first_row=first_row), gr...  26.1 us
    ppermute x2, waiting for transfers between devices, on_device(): crossed.append(lax.ppermute(to_other, 'half', swap))  25.5 us
    all_to_all x5, starting transfers between devices, exchange(): return lax.all_to_all(block, axes, split_axis=0, concat_axis=0, tiled=True)  24.6 us
    ppermute x7, starting transfers between devices, update_alignment(): value_blocks.append(lax.ppermute(values, ('half', 'pos'), pairs))  22.3 us
  transfers between devices with their start and end apart: 29, of which 9 were waited for; matrix products, arithmetic and copies ran while one was open for 5% of the time, Pallas kernels for 16%

profile of v8, /device:TPU:0, one launch (start us, length us, event | category | flops | bytes accessed | tf_op | source)
XLA Modules:
  0.0 482.3 jit_solution(913786403555688597)
XLA Ops:
  6.4 7.6 %collective-permute-start.1 = (bf16[4,96,32]{2,1,0:T(8,128)(2,1)S(1)}, bf16[4,96,32]{2,1,0:T(8,128)(2,1)S(1)}, u32[]{:S(2)}, u32[]{:S(2)}) collective-permute-start(bf16[4,96,32]{2,1,0:T(8,128)(2,1)S(1)} %get-tuple-element.43), channel_id=1, source_target_pairs={{0,7},{1,0},{2,15},{3,8},{4,23},{5,16},{6,31},{7,24},{8,1},{9,2},{... | collective-permute-start | bytes 73736 | tf_op jit(solution)/shard_map/ppermute | solution.py:822
  25.2 5.8 %collective-permute-start.10 = (bf16[4,96,32]{2,1,0:T(8,128)(2,1)S(1)}, bf16[4,96,32]{2,1,0:T(8,128)(2,1)S(1)}, u32[]{:S(2)}, u32[]{:S(2)}) collective-permute-start(bf16[4,96,32]{2,1,0:T(8,128)(2,1)S(1)} %get-tuple-element.42.refs_8_), channel_id=1, source_target_pairs={{0,8},{8,16},{16,24},{24,0},{1,9},{9,17},{17,25},{25,1},{2,10},{10... | collective-permute-start | bytes 73736 | tf_op jit(solution)/shard_map/ppermute | solution.py:826
  31.0 5.3 %collective-permute-start.9 = (bf16[4,96,32]{2,1,0:T(8,128)(2,1)S(1)}, bf16[4,96,32]{2,1,0:T(8,128)(2,1)S(1)}, u32[]{:S(2)}, u32[]{:S(2)}) collective-permute-start(bf16[4,96,32]{2,1,0:T(8,128)(2,1)S(1)} %get-tuple-element.42.refs_8_), channel_id=1, source_target_pairs={{0,16},{8,24},{16,0},{24,8},{1,17},{9,25},{17,1},{25,9},{2,18},{10... | collective-permute-start | bytes 73736 | tf_op jit(solution)/shard_map/ppermute | solution.py:826
  43.2 15.2 %front.2 = (bf16[96,96,128]{2,1,0:T(8,128)(2,1)}, bf16[96,96,128]{2,1,0:T(8,128)(2,1)}) custom-call(s32[2]{0:T(128)} %pad_add_fusion.place_ref, bf16[4,96,32]{2,1,0:T(8,128)(2,1)} %copy-done.11, bf16[4,96,32]{2,1,0:T(8,128)(2,1)} %copy-done.12, bf16[4,96,32]{2,1,0:T(8,128)(2,1)} %copy-done.13, bf16[4,96,32]{2,1,0:T(8,128)(2,1)} %copy-done.14, ...), custom_call_target="tpu_custom_call" | custom-call | flops 1000 | bytes 1000 | tf_op jit(solution)/shard_map/front/pallas_call | solution.py:183
  58.4 4.6 project.7.refs_1_
  63.1 4.2 project.6.refs_0_
  67.3 3.9 all-to-all-start
  71.9 15.4 %front.3 = (bf16[96,96,128]{2,1,0:T(8,128)(2,1)}, bf16[96,96,128]{2,1,0:T(8,128)(2,1)}) custom-call(s32[2]{0:T(128)} %pad_add_fusion.place_ref, bf16[4,96,32]{2,1,0:T(8,128)(2,1)} %copy-done.11, bf16[4,96,32]{2,1,0:T(8,128)(2,1)} %copy-done.12, bf16[4,96,32]{2,1,0:T(8,128)(2,1)} %copy-done.13, bf16[4,96,32]{2,1,0:T(8,128)(2,1)} %copy-done.14, ...), custom_call_target="tpu_custom_call" | custom-call | flops 1000 | bytes 1000 | tf_op jit(solution)/shard_map/front/pallas_call | solution.py:183
  87.2 4.6 project.10.refs_1_
  91.9 4.2 project.9.refs_0_
  96.1 4.2 project.8.refs_3_.refs_0_
  100.3 25.5 %collective-permute-done.11.refs_4_.refs_2_ = bf16[16,96,384]{2,1,0:T(8,128)(2,1)} collective-permute-done((bf16[16,96,384]{2,1,0:T(8,128)(2,1)S(1)}, bf16[16,96,384]{2,1,0:T(8,128)(2,1)}, u32[]{:S(2)}, u32[]{:S(2)}) %collective-permute-start.11) | collective-permute-done | bytes 1179680 | tf_op jit(solution)/shard_map/ppermute | solution.py:929
  127.4 5.3 %all-to-all-start.1 = ((bf16[16,192,384]{2,1,0:T(8,128)(2,1)}), bf16[16,192,384]{2,1,0:T(8,128)(2,1)S(1)}, u32[]{:S(2)}, u32[]{:S(2)}) async-start(bf16[16,192,384]{2,1,0:T(8,128)(2,1)} %get-tuple-element.27), calls=%async_computation.1 | async-start | bytes 4718592 | tf_op jit(solution)/shard_map/all_to_all | solution.py:841
  141.8 4.2 project.11.refs_4_.refs_1_
  146.0 9.6 %logit.1.refs_2_.refs_0_ = f32[192,8,96]{2,1,0:T(8,128)} custom-call(f32[192]{0:T(256)} %dynamic_slice.22.live_ref, bf16[96,96,128]{2,1,0:T(8,128)(2,1)} %get-tuple-element.21.normed_ref.refs_0_.refs_4_, bf16[96,96,128]{2,1,0:T(8,128)(2,1)} %get-tuple-element.23.normed_ref.refs_1_.refs_5_, bf16[8,128]{1,0:T(8,128)(2,1)} %bitcast.82, ...), custom_call_target="tpu_custom_call" | custom-call | flops 1000 | bytes 1000 | tf_op jit(solution)/shard_map/logit/pallas_call | solution.py:311
  155.6 4.2 merge.2.refs_4_.refs_1_
  159.8 28.5 %all-to-all-done.1.refs_1_ = bf16[16,192,384]{2,1,0:T(8,128)(2,1)S(1)} async-done(((bf16[16,192,384]{2,1,0:T(8,128)(2,1)}), bf16[16,192,384]{2,1,0:T(8,128)(2,1)S(1)}, u32[]{:S(2)}, u32[]{:S(2)}) %all-to-all-start.1) | async-done | bytes 2359328 | tf_op jit(solution)/shard_map/all_to_all | solution.py:841
  189.7 9.4 %assemble_half.1 = (bf16[4,768,384]{2,1,0:T(8,128)(2,1)}, bf16[4,384,384]{2,1,0:T(8,128)(2,1)}, bf16[4,768,384]{2,1,0:T(8,128)(2,1)}) custom-call(s32[1]{0:T(128)} %bitcast.21.half_ref, bf16[16,192,384]{2,1,0:T(8,128)(2,1)} %copy-done, bf16[16,192,384]{2,1,0:T(8,128)(2,1)} %copy-done.2, f32[192,8,96]{2,1,0:T(8,128)} %logit.1.refs_2_.refs_0_, ...), custom_call_target="tpu_custom_call" | custom-call | flops 1000 | bytes 1000 | tf_op jit(solution)/shard_map/assemble_half/pallas_call | solution.py:539
  201.5 4.7 all-to-all-start.2
  206.2 108.7 %collective-permute-done.13.recv_ref = bf16[4,768,384]{2,1,0:T(8,128)(2,1)} collective-permute-done((bf16[4,768,384]{2,1,0:T(8,128)(2,1)S(1)}, bf16[4,768,384]{2,1,0:T(8,128)(2,1)}, u32[]{:S(2)}, u32[]{:S(2)}) %collective-permute-start.13) | collective-permute-done | bytes 2359328 | tf_op jit(solution)/shard_map/ppermute | solution.py:941
  314.9 10.3 %combine.1.refs_0_ = bf16[16,192,384]{2,1,0:T(8,128)(2,1)} custom-call(bf16[4,768,384]{2,1,0:T(8,128)(2,1)} %get-tuple-element.31.left_ref, bf16[4,384,384]{2,1,0:T(8,128)(2,1)} %get-tuple-element.32.own_ref, bf16[4,768,384]{2,1,0:T(8,128)(2,1)} %collective-permute-done.13.recv_ref, bf16[16,384,384]{2,1,0:T(8,128)(2,1)} %all-to-all-done.2.refs_0_.recv_ref), custom_call_target="tpu_custom_call" | custom-call | flops 1000 | bytes 1000 | tf_op jit(solution)/shard_map/combine/pallas_call | solution.py:602
  329.0 8.8 %assemble.1 = (bf16[2,16,48,768]{3,2,1,0:T(8,128)(2,1)}, bf16[2,4,1,192,768]{4,3,2,1,0:T(8,128)(2,1)}) custom-call(bf16[16,384,384]{2,1,0:T(8,128)(2,1)} %all-to-all-done.2.refs_0_.recv_ref, bf16[16,192,384]{2,1,0:T(8,128)(2,1)} %combine.1.refs_0_), custom_call_target="tpu_custom_call" | custom-call | flops 1000 | bytes 1000 | tf_op jit(solution)/shard_map/assemble/pallas_call | solution.py:377
  337.8 7.0 %multiply.13.refs_2_ = bf16[32,96,384]{2,1,0:T(8,128)(2,1)} custom-call(bf16[2,16,48,768]{3,2,1,0:T(8,128)(2,1)} %get-tuple-element.34.left_ref, bf16[2,768,768]{2,1,0:T(8,128)(2,1)} %bitcast.57), custom_call_target="tpu_custom_call" | custom-call | flops 1000 | bytes 1000 | tf_op jit(solution)/shard_map/multiply/pallas_call | solution.py:442
  344.8 14.7 %all-to-all-done.3.refs_0_ = bf16[16,192,384]{2,1,0:T(8,128)(2,1)S(1)} async-done(((bf16[16,192,384]{2,1,0:T(8,128)(2,1)}), bf16[16,192,384]{2,1,0:T(8,128)(2,1)S(1)}, u32[]{:S(2)}, u32[]{:S(2)}) %all-to-all-start.3) | async-done | bytes 2359328 | tf_op jit(solution)/shard_map/all_to_all | solution.py:841
  360.9 7.0 %all-to-all-start.4 = ((bf16[32,96,384]{2,1,0:T(8,128)(2,1)}), bf16[32,96,384]{2,1,0:T(8,128)(2,1)}, u32[]{:S(2)}, u32[]{:S(2)}) async-start(bf16[32,96,384]{2,1,0:T(8,128)(2,1)} %multiply.13.refs_2_), calls=%async_computation.4 | async-start | bytes 4718592 | tf_op jit(solution)/shard_map/all_to_all | solution.py:841
  377.0 34.0 %collective-permute-done.17.refs_5_ = bf16[8,96,128]{2,1,0:T(8,128)(2,1)S(1)} collective-permute-done((bf16[8,96,128]{2,1,0:T(8,128)(2,1)}, bf16[8,96,128]{2,1,0:T(8,128)(2,1)S(1)}, u32[]{:S(2)}, u32[]{:S(2)}) %collective-permute-start.17) | collective-permute-done | bytes 196640 | tf_op jit(solution)/shard_map/ppermute | solution.py:885
  411.0 4.4 collective-permute-start.19
  419.3 11.7 %collective-permute-start.20 = (bf16[8,96,128]{2,1,0:T(8,128)(2,1)S(1)}, bf16[8,96,128]{2,1,0:T(8,128)(2,1)S(1)}, u32[]{:S(2)}, u32[]{:S(2)}) collective-permute-start(bf16[8,96,128]{2,1,0:T(8,128)(2,1)S(1)} %copy-done.5), channel_id=1, source_target_pairs={{0,4},{1,5},{2,6},{3,7},{4,0},{5,1},{6,2},{7,3},{8,12},{9,13},{10,... | collective-permute-start | bytes 589832 | tf_op jit(solution)/shard_map/ppermute | solution.py:885
  435.5 16.4 %collective-permute-done.20.refs_8_ = bf16[8,96,128]{2,1,0:T(8,128)(2,1)S(1)} collective-permute-done((bf16[8,96,128]{2,1,0:T(8,128)(2,1)S(1)}, bf16[8,96,128]{2,1,0:T(8,128)(2,1)S(1)}, u32[]{:S(2)}, u32[]{:S(2)}) %collective-permute-start.20) | collective-permute-done | bytes 196640 | tf_op jit(solution)/shard_map/ppermute | solution.py:885
  452.8 8.2 %collective-permute-done.22.refs_10_ = bf16[8,96,128]{2,1,0:T(8,128)(2,1)S(1)} collective-permute-done((bf16[8,96,128]{2,1,0:T(8,128)(2,1)S(1)}, bf16[8,96,128]{2,1,0:T(8,128)(2,1)S(1)}, u32[]{:S(2)}, u32[]{:S(2)}) %collective-permute-start.22) | collective-permute-done | bytes 196640 | tf_op jit(solution)/shard_map/ppermute | solution.py:885
  462.2 5.5 %average.1 = bf16[96,256]{1,0:T(8,128)(2,1)} custom-call(s32[2]{0:T(128)} %pad_add_fusion.place_ref, f32[192,8,96]{2,1,0:T(8,128)} %get-tuple-element.36.refs_0_, f32[192,8,96]{2,1,0:T(8,128)} %copy-done.9, f32[192,8,96]{2,1,0:T(8,128)} %copy-done.10, f32[192,8,96]{2,1,0:T(8,128)} %collective-permute-done.16.refs_3_, ...), custom_call_target="tpu_custom_call" | custom-call | flops 1000 | bytes 1000 | tf_op jit(solution)/shard_map/average/pallas_call | solution.py:676
  469.2 13.1 %finish.1 = bf16[192,96,128]{2,1,0:T(8,128)(2,1)} custom-call(bf16[16,192,384]{2,1,0:T(8,128)(2,1)} %copy-done.1, bf16[32,96,384]{2,1,0:T(8,128)(2,1)} %all-to-all-done.4.refs_1_, bf16[96,96,128]{2,1,0:T(8,128)(2,1)} %get-tuple-element.38.refs_2_, bf16[96,96,128]{2,1,0:T(8,128)(2,1)} %get-tuple-element.39.refs_3_, ...), custom_call_target="tpu_custom_call" | custom-call | flops 1000 | bytes 1000 | tf_op jit(solution)/shard_map/finish/pallas_call | solution.py:745
  (163 shorter events, 65.1 us)
Async XLA Ops:
  0.6 37.7 %copy-start.22 = (bf16[1024,128]{1,0:T(8,128)(2,1)S(1)}, bf16[1024,128]{1,0:T(8,128)(2,1)}, u32[]{:S(2)}) copy-start(bf16[1024,128]{1,0:T(8,128)(2,1)} %param.15) | copy-start | bytes 786436
  5.8 11.7 %collective-permute-start = (bf16[4,96,32]{2,1,0:T(8,128)(2,1)S(1)}, bf16[4,96,32]{2,1,0:T(8,128)(2,1)S(1)}, u32[]{:S(2)}, u32[]{:S(2)}) collective-permute-start(bf16[4,96,32]{2,1,0:T(8,128)(2,1)S(1)} %get-tuple-element.43), channel_id=1, source_target_pairs={{0,0},{1,1},{2,8},{3,9},{4,16},{5,17},{6,24},{7,25},{8,2},{9,3},{1... | collective-permute-start | bytes 73736 | tf_op jit(solution)/shard_map/ppermute | solution.py:822
  6.4 13.9 %collective-permute-start.1 = (bf16[4,96,32]{2,1,0:T(8,128)(2,1)S(1)}, bf16[4,96,32]{2,1,0:T(8,128)(2,1)S(1)}, u32[]{:S(2)}, u32[]{:S(2)}) collective-permute-start(bf16[4,96,32]{2,1,0:T(8,128)(2,1)S(1)} %get-tuple-element.43), channel_id=1, source_target_pairs={{0,7},{1,0},{2,15},{3,8},{4,23},{5,16},{6,31},{7,24},{8,1},{9,2},{... | collective-permute-start | bytes 73736 | tf_op jit(solution)/shard_map/ppermute | solution.py:822
  14.0 7.9 %collective-permute-start.2 = (bf16[4,96,32]{2,1,0:T(8,128)(2,1)S(1)}, bf16[4,96,32]{2,1,0:T(8,128)(2,1)S(1)}, u32[]{:S(2)}, u32[]{:S(2)}) collective-permute-start(bf16[4,96,32]{2,1,0:T(8,128)(2,1)S(1)} %get-tuple-element.43), channel_id=1, source_target_pairs={{0,6},{1,7},{2,14},{3,15},{4,22},{5,23},{6,30},{7,31},{8,0},{9,1},... | collective-permute-start | bytes 73736 | tf_op jit(solution)/shard_map/ppermute | solution.py:822
  14.9 10.3 %collective-permute-start.3 = (bf16[4,96,32]{2,1,0:T(8,128)(2,1)S(1)}, bf16[4,96,32]{2,1,0:T(8,128)(2,1)S(1)}, u32[]{:S(2)}, u32[]{:S(2)}) collective-permute-start(bf16[4,96,32]{2,1,0:T(8,128)(2,1)S(1)} %get-tuple-element.43), channel_id=1, source_target_pairs={{0,5},{1,6},{2,13},{3,14},{4,21},{5,22},{6,29},{7,30},{8,7},{9,0},... | collective-permute-start | bytes 73736 | tf_op jit(solution)/shard_map/ppermute | solution.py:822
  16.7 14.4 %collective-permute-start.4 = (bf16[4,96,32]{2,1,0:T(8,128)(2,1)S(1)}, bf16[4,96,32]{2,1,0:T(8,128)(2,1)S(1)}, u32[]{:S(2)}, u32[]{:S(2)}) collective-permute-start(bf16[4,96,32]{2,1,0:T(8,128)(2,1)S(1)} %get-tuple-element.43), channel_id=1, source_target_pairs={{0,4},{1,5},{2,12},{3,13},{4,20},{5,21},{6,28},{7,29},{8,6},{9,7},... | collective-permute-start | bytes 73736 | tf_op jit(solution)/shard_map/ppermute | solution.py:822
  17.5 13.5 %collective-permute-start.5 = (bf16[4,96,32]{2,1,0:T(8,128)(2,1)S(1)}, bf16[4,96,32]{2,1,0:T(8,128)(2,1)S(1)}, u32[]{:S(2)}, u32[]{:S(2)}) collective-permute-start(bf16[4,96,32]{2,1,0:T(8,128)(2,1)S(1)} %get-tuple-element.43), channel_id=1, source_target_pairs={{0,3},{1,4},{2,11},{3,12},{4,19},{5,20},{6,27},{7,28},{8,5},{9,6},... | collective-permute-start | bytes 73736 | tf_op jit(solution)/shard_map/ppermute | solution.py:822
  20.4 21.4 %collective-permute-start.6 = (bf16[4,96,32]{2,1,0:T(8,128)(2,1)S(1)}, bf16[4,96,32]{2,1,0:T(8,128)(2,1)S(1)}, u32[]{:S(2)}, u32[]{:S(2)}) collective-permute-start(bf16[4,96,32]{2,1,0:T(8,128)(2,1)S(1)} %get-tuple-element.43), channel_id=1, source_target_pairs={{0,2},{1,3},{2,10},{3,11},{4,18},{5,19},{6,26},{7,27},{8,4},{9,5},... | collective-permute-start | bytes 73736 | tf_op jit(solution)/shard_map/ppermute | solution.py:822
  22.0 19.8 %collective-permute-start.7 = (bf16[4,96,32]{2,1,0:T(8,128)(2,1)S(1)}, bf16[4,96,32]{2,1,0:T(8,128)(2,1)S(1)}, u32[]{:S(2)}, u32[]{:S(2)}) collective-permute-start(bf16[4,96,32]{2,1,0:T(8,128)(2,1)S(1)} %get-tuple-element.43), channel_id=1, source_target_pairs={{0,1},{1,2},{2,9},{3,10},{4,17},{5,18},{6,25},{7,26},{8,3},{9,4},{... | collective-permute-start | bytes 73736 | tf_op jit(solution)/shard_map/ppermute | solution.py:822
  25.2 16.6 %collective-permute-start.10 = (bf16[4,96,32]{2,1,0:T(8,128)(2,1)S(1)}, bf16[4,96,32]{2,1,0:T(8,128)(2,1)S(1)}, u32[]{:S(2)}, u32[]{:S(2)}) collective-permute-start(bf16[4,96,32]{2,1,0:T(8,128)(2,1)S(1)} %get-tuple-element.42.refs_8_), channel_id=1, source_target_pairs={{0,8},{8,16},{16,24},{24,0},{1,9},{9,17},{17,25},{25,1},{2,10},{10... | collective-permute-start | bytes 73736 | tf_op jit(solution)/shard_map/ppermute | solution.py:826
  31.0 10.8 %collective-permute-start.8 = (bf16[4,96,32]{2,1,0:T(8,128)(2,1)S(1)}, bf16[4,96,32]{2,1,0:T(8,128)(2,1)S(1)}, u32[]{:S(2)}, u32[]{:S(2)}) collective-permute-start(bf16[4,96,32]{2,1,0:T(8,128)(2,1)S(1)} %get-tuple-element.42.refs_8_), channel_id=1, source_target_pairs={{0,24},{8,0},{16,8},{24,16},{1,25},{9,1},{17,9},{25,17},{2,26},{10... | collective-permute-start | bytes 73736 | tf_op jit(solution)/shard_map/ppermute | solution.py:826
  31.0 10.8 %collective-permute-start.9 = (bf16[4,96,32]{2,1,0:T(8,128)(2,1)S(1)}, bf16[4,96,32]{2,1,0:T(8,128)(2,1)S(1)}, u32[]{:S(2)}, u32[]{:S(2)}) collective-permute-start(bf16[4,96,32]{2,1,0:T(8,128)(2,1)S(1)} %get-tuple-element.42.refs_8_), channel_id=1, source_target_pairs={{0,16},{8,24},{16,0},{24,8},{1,17},{9,25},{17,1},{25,9},{2,18},{10... | collective-permute-start | bytes 73736 | tf_op jit(solution)/shard_map/ppermute | solution.py:826
  67.3 58.7 %all-to-all-start = ((bf16[16,192,384]{2,1,0:T(8,128)(2,1)}), bf16[16,192,384]{2,1,0:T(8,128)(2,1)S(1)}, u32[]{:S(2)}, u32[]{:S(2)}) async-start(bf16[16,192,384]{2,1,0:T(8,128)(2,1)} %get-tuple-element.24), calls=%async_computation | async-start | bytes 4718592 | tf_op jit(solution)/shard_map/all_to_all | solution.py:841
  71.1 54.7 %collective-permute-start.11 = (bf16[16,96,384]{2,1,0:T(8,128)(2,1)S(1)}, bf16[16,96,384]{2,1,0:T(8,128)(2,1)}, u32[]{:S(2)}, u32[]{:S(2)}) collective-permute-start(bf16[16,96,384]{2,1,0:T(8,128)(2,1)S(1)} %copy-done.4), channel_id=1, source_target_pairs={{0,4},{4,0},{1,5},{5,1},{2,6},{6,2},{3,7},{7,3},{8,12},{12,8},{9,1... | collective-permute-start | bytes 3538952 | tf_op jit(solution)/shard_map/ppermute | solution.py:929
  127.4 60.8 %all-to-all-start.1 = ((bf16[16,192,384]{2,1,0:T(8,128)(2,1)}), bf16[16,192,384]{2,1,0:T(8,128)(2,1)S(1)}, u32[]{:S(2)}, u32[]{:S(2)}) async-start(bf16[16,192,384]{2,1,0:T(8,128)(2,1)} %get-tuple-element.27), calls=%async_computation.1 | async-start | bytes 4718592 | tf_op jit(solution)/shard_map/all_to_all | solution.py:841
  132.7 66.3 %collective-permute-start.12 = (bf16[16,96,384]{2,1,0:T(8,128)(2,1)S(1)}, bf16[16,96,384]{2,1,0:T(8,128)(2,1)}, u32[]{:S(2)}, u32[]{:S(2)}) collective-permute-start(bf16[16,96,384]{2,1,0:T(8,128)(2,1)S(1)} %copy-done.3), channel_id=1, source_target_pairs={{0,4},{4,0},{1,5},{5,1},{2,6},{6,2},{3,7},{7,3},{8,12},{12,8},{9,1... | collective-permute-start | bytes 3538952 | tf_op jit(solution)/shard_map/ppermute | solution.py:929
  201.5 113.5 %all-to-all-start.2 = ((bf16[16,384,384]{2,1,0:T(8,128)(2,1)}), bf16[16,384,384]{2,1,0:T(8,128)(2,1)}, u32[]{:S(2)}, u32[]{:S(2)}) async-start(bf16[16,384,384]{2,1,0:T(8,128)(2,1)} %get-tuple-element.30), calls=%async_computation.2 | async-start | bytes 9437184 | tf_op jit(solution)/shard_map/all_to_all | solution.py:841
  206.2 108.8 %collective-permute-start.13 = (bf16[4,768,384]{2,1,0:T(8,128)(2,1)S(1)}, bf16[4,768,384]{2,1,0:T(8,128)(2,1)}, u32[]{:S(2)}, u32[]{:S(2)}) collective-permute-start(bf16[4,768,384]{2,1,0:T(8,128)(2,1)S(1)} %copy-done.6), channel_id=1, source_target_pairs={{0,4},{4,0},{1,5},{5,1},{2,6},{6,2},{3,7},{7,3},{8,12},{12,8},{9,1... | collective-permute-start | bytes 7077896 | tf_op jit(solution)/shard_map/ppermute | solution.py:941
  325.3 34.2 %all-to-all-start.3 = ((bf16[16,192,384]{2,1,0:T(8,128)(2,1)}), bf16[16,192,384]{2,1,0:T(8,128)(2,1)S(1)}, u32[]{:S(2)}, u32[]{:S(2)}) async-start(bf16[16,192,384]{2,1,0:T(8,128)(2,1)} %combine.1.refs_0_), calls=%async_computation.3 | async-start | bytes 4718592 | tf_op jit(solution)/shard_map/all_to_all | solution.py:841
  360.9 108.3 %all-to-all-start.4 = ((bf16[32,96,384]{2,1,0:T(8,128)(2,1)}), bf16[32,96,384]{2,1,0:T(8,128)(2,1)}, u32[]{:S(2)}, u32[]{:S(2)}) async-start(bf16[32,96,384]{2,1,0:T(8,128)(2,1)} %multiply.13.refs_2_), calls=%async_computation.4 | async-start | bytes 4718592 | tf_op jit(solution)/shard_map/all_to_all | solution.py:841
  367.9 47.4 %copy-start.30 = (bf16[128,128]{1,0:T(8,128)(2,1)S(1)}, bf16[128,128]{1,0:T(8,128)(2,1)}, u32[]{:S(2)}) copy-start(bf16[128,128]{1,0:T(8,128)(2,1)} %param.19) | copy-start | bytes 98308
  367.9 50.0 %copy-start.29 = (bf16[256,64]{0,1:T(8,128)(2,1)S(1)}, bf16[256,64]{0,1:T(8,128)(2,1)}, u32[]{:S(2)}) copy-start(bf16[256,64]{0,1:T(8,128)(2,1)} %param.17) | copy-start | bytes 98308
  367.9 43.0 %collective-permute-start.17 = (bf16[8,96,128]{2,1,0:T(8,128)(2,1)}, bf16[8,96,128]{2,1,0:T(8,128)(2,1)S(1)}, u32[]{:S(2)}, u32[]{:S(2)}) collective-permute-start(bf16[8,96,128]{2,1,0:T(8,128)(2,1)} %get-tuple-element.37.refs_4_), channel_id=1, source_target_pairs={{0,7},{1,0},{2,1},{3,2},{4,3},{5,4},{6,5},{7,6},{8,15},{9,8},{10,9... | collective-permute-start | bytes 589832 | tf_op jit(solution)/shard_map/ppermute | solution.py:885
  372.4 88.5 %collective-permute-start.14 = (f32[192,8,96]{2,1,0:T(8,128)}, f32[192,8,96]{2,1,0:T(8,128)S(1)}, u32[]{:S(2)}, u32[]{:S(2)}) collective-permute-start(f32[192,8,96]{2,1,0:T(8,128)} %get-tuple-element.36.refs_0_), channel_id=1, source_target_pairs={{0,24},{8,0},{16,8},{24,16},{1,25},{9,1},{17,9},{25,17},{2,26},{10... | collective-permute-start | bytes 1769480 | tf_op jit(solution)/shard_map/ppermute | solution.py:882
  374.9 86.1 %collective-permute-start.15 = (f32[192,8,96]{2,1,0:T(8,128)}, f32[192,8,96]{2,1,0:T(8,128)S(1)}, u32[]{:S(2)}, u32[]{:S(2)}) collective-permute-start(f32[192,8,96]{2,1,0:T(8,128)} %get-tuple-element.36.refs_0_), channel_id=1, source_target_pairs={{0,16},{8,24},{16,0},{24,8},{1,17},{9,25},{17,1},{25,9},{2,18},{10... | collective-permute-start | bytes 1769480 | tf_op jit(solution)/shard_map/ppermute | solution.py:882
  375.4 85.6 %collective-permute-start.16 = (f32[192,8,96]{2,1,0:T(8,128)}, f32[192,8,96]{2,1,0:T(8,128)}, u32[]{:S(2)}, u32[]{:S(2)}) collective-permute-start(f32[192,8,96]{2,1,0:T(8,128)} %get-tuple-element.36.refs_0_), channel_id=1, source_target_pairs={{0,8},{8,16},{16,24},{24,0},{1,9},{9,17},{17,25},{25,1},{2,10},{10... | collective-permute-start | bytes 1769480 | tf_op jit(solution)/shard_map/ppermute | solution.py:882
  376.0 43.2 %collective-permute-start.18 = (bf16[8,96,128]{2,1,0:T(8,128)(2,1)}, bf16[8,96,128]{2,1,0:T(8,128)(2,1)}, u32[]{:S(2)}, u32[]{:S(2)}) collective-permute-start(bf16[8,96,128]{2,1,0:T(8,128)(2,1)} %get-tuple-element.37.refs_4_), channel_id=1, source_target_pairs={{0,6},{1,7},{2,0},{3,1},{4,2},{5,3},{6,4},{7,5},{8,14},{9,15},{10,... | collective-permute-start | bytes 589832 | tf_op jit(solution)/shard_map/ppermute | solution.py:885
  411.0 21.0 %collective-permute-start.19 = (bf16[8,96,128]{2,1,0:T(8,128)(2,1)}, bf16[8,96,128]{2,1,0:T(8,128)(2,1)}, u32[]{:S(2)}, u32[]{:S(2)}) collective-permute-start(bf16[8,96,128]{2,1,0:T(8,128)(2,1)} %get-tuple-element.37.refs_4_), channel_id=1, source_target_pairs={{0,5},{1,6},{2,7},{3,0},{4,1},{5,2},{6,3},{7,4},{8,13},{9,14},{10,... | collective-permute-start | bytes 589832 | tf_op jit(solution)/shard_map/ppermute | solution.py:885
  419.3 32.6 %collective-permute-start.20 = (bf16[8,96,128]{2,1,0:T(8,128)(2,1)S(1)}, bf16[8,96,128]{2,1,0:T(8,128)(2,1)S(1)}, u32[]{:S(2)}, u32[]{:S(2)}) collective-permute-start(bf16[8,96,128]{2,1,0:T(8,128)(2,1)S(1)} %copy-done.5), channel_id=1, source_target_pairs={{0,4},{1,5},{2,6},{3,7},{4,0},{5,1},{6,2},{7,3},{8,12},{9,13},{10,... | collective-permute-start | bytes 589832 | tf_op jit(solution)/shard_map/ppermute | solution.py:885
  432.0 19.9 %collective-permute-start.21 = (bf16[8,96,128]{2,1,0:T(8,128)(2,1)S(1)}, bf16[8,96,128]{2,1,0:T(8,128)(2,1)S(1)}, u32[]{:S(2)}, u32[]{:S(2)}) collective-permute-start(bf16[8,96,128]{2,1,0:T(8,128)(2,1)S(1)} %copy-done.5), channel_id=1, source_target_pairs={{0,3},{1,4},{2,5},{3,6},{4,7},{5,0},{6,1},{7,2},{8,11},{9,12},{10,... | collective-permute-start | bytes 589832 | tf_op jit(solution)/shard_map/ppermute | solution.py:885
  451.9 9.1 %collective-permute-start.22 = (bf16[8,96,128]{2,1,0:T(8,128)(2,1)S(1)}, bf16[8,96,128]{2,1,0:T(8,128)(2,1)S(1)}, u32[]{:S(2)}, u32[]{:S(2)}) collective-permute-start(bf16[8,96,128]{2,1,0:T(8,128)(2,1)S(1)} %copy-done.5), channel_id=1, source_target_pairs={{0,2},{1,3},{2,4},{3,5},{4,6},{5,7},{6,0},{7,1},{8,10},{9,11},{10,... | collective-permute-start | bytes 589832 | tf_op jit(solution)/shard_map/ppermute | solution.py:885
  451.9 9.1 %collective-permute-start.23 = (bf16[8,96,128]{2,1,0:T(8,128)(2,1)S(1)}, bf16[8,96,128]{2,1,0:T(8,128)(2,1)S(1)}, u32[]{:S(2)}, u32[]{:S(2)}) collective-permute-start(bf16[8,96,128]{2,1,0:T(8,128)(2,1)S(1)} %copy-done.5), channel_id=1, source_target_pairs={{0,1},{1,2},{2,3},{3,4},{4,5},{5,6},{6,7},{7,0},{8,9},{9,10},{10,1... | collective-permute-start | bytes 589832 | tf_op jit(solution)/shard_map/ppermute | solution.py:885
  (28 other events, 212.2 us)

commit v9 on v8

--- a/solution.py
+++ b/solution.py
@@ -575,14 +575,18 @@
     for row in range(row_count):
         for group in range(pos_count // 4):
             cols = slice(group * lanes, (group + 1) * lanes)
-            blocks = []
-            for a in range(QUAD):
-                span = slice((row * QUAD + a) * each, (row * QUAD + a + 1) * each)
-                value = lax.dot_general(
-                    left_ref[0, span], own_ref[0, cols], NT, preferred_element_type=F32
-                )
-                value = value + recv_ref[0, span, cols].astype(F32)
-                blocks.append([value[:, t * LANES : (t + 1) * LANES] for t in range(tiles)])
+            span = slice(row * QUAD * each, (row + 1) * QUAD * each)
+            value = lax.dot_general(
+                left_ref[0, span], own_ref[0, cols], NT, preferred_element_type=F32
+            )
+            value = value + recv_ref[0, span, cols].astype(F32)
+            blocks = [
+                [
+                    value[a * each : (a + 1) * each, t * LANES : (t + 1) * LANES]
+                    for t in range(tiles)
+                ]
+                for a in range(QUAD)
+            ]
             for p, value in enumerate(exchange_blocks(blocks)):
                 dest = row * pos_count + group * 4 + p
                 for t in range(tiles):
@@ -642,11 +646,15 @@
 
 def average_kernel(place_ref, *refs, row_count, col_count):
     logits, values = refs[:row_count], refs[row_count : row_count + col_count]
-    gate_ref, align_ref, weight_ref, out_ref, exp_ref, value_ref = refs[row_count + col_count :]
+    refs = refs[row_count + col_count :]
+    gate_ref, align_ref, weight_ref, project_ref, out_ref, exp_ref, value_ref = refs
     rows, heads, cols = logits[0].shape
+    wide = gate_ref.shape[2]
     per_row = col_count // row_count
     for u, value in enumerate(values):
-        value_ref[lax.rem(place_ref[1] + u, col_count)] = value[...]
+        value_ref[lax.rem(place_ref[1] + u, col_count)] = jnp.dot(
+            value[...], project_ref[...], preferred_element_type=F32
+        ).astype(BF16)
     top = jnp.max(logits[0][...], axis=0)
     for block in logits[1:]:
         top = jnp.maximum(top, jnp.max(block[...], axis=0))
@@ -663,16 +671,18 @@
             first = lax.rem(place_ref[0] + t, row_count) * per_row
             powers = exp_ref[pl.ds(t * size + h, rows, stride=heads), :][:, :cols]
             weights = (powers / total[h : h + 1]).astype(BF16)
-            value = jnp.concatenate([value_ref[first + k, h] for k in range(per_row)], axis=0)
+            value = jnp.concatenate(
+                [value_ref[first + k, :, h * wide : (h + 1) * wide] for k in range(per_row)], axis=0
+            )
             summed += lax.dot_general(weights, value, TN, preferred_element_type=F32)
         gated = (gate_ref[h] * summed).astype(BF16)
         out += jnp.dot(gated, weight_ref[h], preferred_element_type=F32)
     out_ref[...] = out.astype(BF16)
 
 
-def average(place, logits, values, gate, align, weight):
+def average(place, logits, values, gate, align, weight, w_value):
     rows, heads, cols = logits[0].shape
-    operands = [*logits, *values, gate, align, weight]
+    operands = [*logits, *values, gate, align, weight, w_value]
     return pl.pallas_call(
         functools.partial(average_kernel, row_count=len(logits), col_count=len(values)),
         grid=(1,),
@@ -681,7 +691,7 @@
         out_shape=jax.ShapeDtypeStruct(align.shape, BF16),
         scratch_shapes=[
             pltpu.VMEM((len(logits) * rows * heads, LANES), F32),
-            pltpu.VMEM((len(values), *values[0].shape), BF16),
+            pltpu.VMEM((len(values), cols, w_value.shape[1]), BF16),
         ],
         compiler_params=params(),
         cost_estimate=LIGHT,
@@ -866,7 +876,14 @@
 
     first = 2 * TENSOR_FEATURES
     middle = first + MEAN_GROUPS * GROUP_FEATURES
-    values = by_head(project_msa(alignment_matrix[:, first:middle]).astype(BF16))
+    w_value = alignment_matrix[:, first:middle].reshape(
+        1, feature_count, MEAN_GROUPS, 1, GROUP_FEATURES
+    )
+    apart = jnp.eye(seq_each, dtype=BF16).reshape(seq_each, 1, 1, seq_each, 1)
+    w_value = (w_value * apart).reshape(seq_each * feature_count, -1)
+    own_rows = jnp.transpose(
+        own_normed.reshape(seq_each, module_number, feature_count), (1, 0, 2)
+    ).reshape(module_number, -1)
     sequence_gate = by_head(jax.nn.sigmoid(project_msa(alignment_matrix[:, middle:])))
     w_mean = mean_final_matrix.reshape(MEAN_GROUPS, 1, GROUP_FEATURES, 1, feature_count)
     same = jnp.eye(seq_each, dtype=BF16).reshape(1, seq_each, 1, seq_each, 1)
@@ -875,15 +892,12 @@
     )
     align = jnp.transpose(alignment_embedding, (1, 0, 2)).reshape(module_number, -1)
 
-    def update_alignment(logits, values):
-        logit_blocks, value_blocks = [logits], [values]
-        for t in range(1, row_count):
-            pairs = [(r, (r - t) % row_count) for r in range(row_count)]
-            logit_blocks.append(lax.ppermute(logits, "row", pairs))
-        for t in range(1, col_count):
-            pairs = [(q, (q - t) % col_count) for q in range(col_count)]
-            value_blocks.append(lax.ppermute(values, ("half", "pos"), pairs))
-        return average(place, logit_blocks, value_blocks, sequence_gate, align, w_mean)
+    def blocks_of(own, axes, count):
+        blocks = [own]
+        for t in range(1, count):
+            pairs = [(at, (at - t) % count) for at in range(count)]
+            blocks.append(lax.ppermute(own, axes, pairs))
+        return blocks
 
     group = devices // 2
     shape_of = (row_count, col_count, module_number)
@@ -905,6 +919,8 @@
         last = multiply(left, right, (), *shape_of[1:])
         returned.append(exchange(last, AXES))
         logits = logit(live_rows, normeds, w_logit, ())
+        (logits,) = fence([logits], (last,))
+        logits = blocks_of(logits, "row", row_count)
         orders = [(0, CTRI, devices)]
     else:
         cut = CTRI // 2
@@ -934,21 +950,24 @@
         logits = logit(live_rows, normeds, w_logit, tuple(kept))
         merged = merge(kept + crossed[:-1], 0, 2 * row_chunks, ())
         left, own, theirs = assemble_half(
-            half_scalar, received, (logits, values, merged), *half_shape
+            half_scalar, received, (logits, merged), *half_shape
         )
         merged = merge(crossed[-1:], 2 * row_chunks - 1, 2 * row_chunks, (merged,))
         theirs, merged = fence([theirs, merged], ())
         partial = lax.ppermute(theirs, "half", swap)
         both = exchange(merged, GROUP)
         product = combine(left, own, partial, (both,), *half_shape)
+        (logits,) = fence([logits], (product,))
+        logits = blocks_of(logits, "row", row_count)
         returned.append(exchange(product, GROUP))
         left, right = assemble(0, 1, 2, both, (), (product,), *half_shape)
         right = right.reshape(right.shape[0], -1, right.shape[-1])
-        last = multiply(left, right, (), *shape_of[1:])
+        last = multiply(left, right, tuple(logits[1:]), *shape_of[1:])
         returned.append(exchange(last, AXES))
         orders = [(0, cut, group), (cut, CTRI, devices)]
-    logits, values = fence([logits, values], (last,))
-    aligned = update_alignment(logits, values)
+    (own_rows,) = fence([own_rows], (last,))
+    values = blocks_of(own_rows, ("half", "pos"), col_count)
+    aligned = average(place, logits, values, sequence_gate, align, w_mean, w_value)
     alignment_updated_embedding = jnp.transpose(
         aligned.reshape(module_number, seq_each, feature_count), (1, 0, 2)
     )

time: 485 us -> 495 us (1.021)
  waiting for transfers between devices: 237 us -> 253 us
    ppermute x10, waiting for transfers between devices: 59.6 us -> 82.7 us  [blocks_of(): blocks.append(lax.ppermute(own, axes, pairs))]
    all_to_all x5, waiting for transfers between devices: 43.3 us -> 36.5 us  [exchange(): return lax.all_to_all(block, axes, split_axis=0, concat_axis=0, tiled=True)]
  transfers between devices with their start and end apart: 29 -> 29, of which waited for: 9 -> 8; matrix products, arithmetic and copies ran while one was open for 5% -> 4% of each run, Pallas kernels for 16% -> 16%
where the time goes in v9:
time: 495 us; the launch traced here: 493 us
  waiting for transfers between devices  253 us (51%)
  Pallas kernels  124 us (25%)
  starting transfers between devices  84.2 us (17%)
  local copies, waits for them, and re-layouts  21.9 us (4%)
  other arithmetic  6.91 us (1%)
    ppermute x1, waiting for transfers between devices, on_device(): partial = lax.ppermute(theirs, 'half', swap)  109 us
    ppermute x10, waiting for transfers between devices, blocks_of(): blocks.append(lax.ppermute(own, axes, pairs))  82.7 us
    all_to_all x5, waiting for transfers between devices, exchange(): return lax.all_to_all(block, axes, split_axis=0, concat_axis=0, tiled=True)  36.5 us
    pallas_call x2, Pallas kernels, front(): pl.pallas_call(functools.partial(front_kernel, row_count=len(rights), col...  30.6 us
    ppermute x10, starting transfers between devices, blocks_of(): blocks.append(lax.ppermute(own, axes, pairs))  29.7 us
    pallas_call x6, Pallas kernels, project(): pl.pallas_call(functools.partial(project_kernel, first_row=first_row), gr...  26.2 us
    ppermute x2, waiting for transfers between devices, on_device(): crossed.append(lax.ppermute(to_other, 'half', swap))  25.1 us
    all_to_all x5, starting transfers between devices, exchange(): return lax.all_to_all(block, axes, split_axis=0, concat_axis=0, tiled=True)  22.6 us
  transfers between devices with their start and end apart: 29, of which 8 were waited for; matrix products, arithmetic and copies ran while one was open for 4% of the time, Pallas kernels for 16%

profile of v9, /device:TPU:0, one launch (start us, length us, event | category | flops | bytes accessed | tf_op | source)
XLA Modules:
  0.0 492.5 jit_solution(7500698811981483684)
XLA Ops:
  7.2 7.6 %collective-permute-start.1 = (bf16[4,96,32]{2,1,0:T(8,128)(2,1)S(1)}, bf16[4,96,32]{2,1,0:T(8,128)(2,1)S(1)}, u32[]{:S(2)}, u32[]{:S(2)}) collective-permute-start(bf16[4,96,32]{2,1,0:T(8,128)(2,1)S(1)} %get-tuple-element.39), channel_id=1, source_target_pairs={{0,7},{1,0},{2,15},{3,8},{4,23},{5,16},{6,31},{7,24},{8,1},{9,2},{... | collective-permute-start | bytes 73736 | tf_op jit(solution)/shard_map/ppermute | solution.py:832
  26.0 4.7 collective-permute-start.8
  33.3 3.3 collective-permute-start.10
  43.4 15.3 %front.2 = (bf16[96,96,128]{2,1,0:T(8,128)(2,1)}, bf16[96,96,128]{2,1,0:T(8,128)(2,1)}) custom-call(s32[2]{0:T(128)} %pad_add_fusion.place_ref, bf16[4,96,32]{2,1,0:T(8,128)(2,1)} %copy-done.11, bf16[4,96,32]{2,1,0:T(8,128)(2,1)} %copy-done.12, bf16[4,96,32]{2,1,0:T(8,128)(2,1)} %copy-done.13, bf16[4,96,32]{2,1,0:T(8,128)(2,1)} %copy-done.14, ...), custom_call_target="tpu_custom_call" | custom-call | flops 1000 | bytes 1000 | tf_op jit(solution)/shard_map/front/pallas_call | solution.py:183
  58.7 4.2 project.6.refs_0_
  62.9 4.6 project.7.refs_1_
  67.5 3.9 all-to-all-start
  72.5 4.2 project.8.refs_3_.refs_0_
  76.7 15.4 %front.3 = (bf16[96,96,128]{2,1,0:T(8,128)(2,1)}, bf16[96,96,128]{2,1,0:T(8,128)(2,1)}) custom-call(s32[2]{0:T(128)} %pad_add_fusion.place_ref, bf16[4,96,32]{2,1,0:T(8,128)(2,1)} %copy-done.11, bf16[4,96,32]{2,1,0:T(8,128)(2,1)} %copy-done.12, bf16[4,96,32]{2,1,0:T(8,128)(2,1)} %copy-done.13, bf16[4,96,32]{2,1,0:T(8,128)(2,1)} %copy-done.14, ...), custom_call_target="tpu_custom_call" | custom-call | flops 1000 | bytes 1000 | tf_op jit(solution)/shard_map/front/pallas_call | solution.py:183
  92.1 4.2 project.9.refs_0_
  96.3 4.7 project.10.refs_1_
  101.0 25.1 %collective-permute-done.11.refs_4_.refs_2_ = bf16[16,96,384]{2,1,0:T(8,128)(2,1)} collective-permute-done((bf16[16,96,384]{2,1,0:T(8,128)(2,1)S(1)}, bf16[16,96,384]{2,1,0:T(8,128)(2,1)}, u32[]{:S(2)}, u32[]{:S(2)}) %collective-permute-start.11) | collective-permute-done | bytes 1179680 | tf_op jit(solution)/shard_map/ppermute | solution.py:945
  128.0 5.3 %all-to-all-start.1 = ((bf16[16,192,384]{2,1,0:T(8,128)(2,1)}), bf16[16,192,384]{2,1,0:T(8,128)(2,1)S(1)}, u32[]{:S(2)}, u32[]{:S(2)}) async-start(bf16[16,192,384]{2,1,0:T(8,128)(2,1)} %get-tuple-element.25), calls=%async_computation.1 | async-start | bytes 4718592 | tf_op jit(solution)/shard_map/all_to_all | solution.py:851
  134.9 4.2 project.11.refs_4_.refs_1_
  139.1 9.6 %logit.1.refs_2_.refs_0_ = f32[192,8,96]{2,1,0:T(8,128)} custom-call(f32[192]{0:T(256)} %dynamic_slice.22.live_ref, bf16[96,96,128]{2,1,0:T(8,128)(2,1)} %get-tuple-element.19.normed_ref.refs_0_.refs_4_, bf16[96,96,128]{2,1,0:T(8,128)(2,1)} %get-tuple-element.21.normed_ref.refs_1_.refs_5_, bf16[8,128]{1,0:T(8,128)(2,1)} %bitcast.83, ...), custom_call_target="tpu_custom_call" | custom-call | flops 1000 | bytes 1000 | tf_op jit(solution)/shard_map/logit/pallas_call | solution.py:311
  148.7 4.2 merge.2.refs_3_.refs_1_
  152.9 36.0 %all-to-all-done.1.refs_1_ = bf16[16,192,384]{2,1,0:T(8,128)(2,1)S(1)} async-done(((bf16[16,192,384]{2,1,0:T(8,128)(2,1)}), bf16[16,192,384]{2,1,0:T(8,128)(2,1)S(1)}, u32[]{:S(2)}, u32[]{:S(2)}) %all-to-all-start.1) | async-done | bytes 2359328 | tf_op jit(solution)/shard_map/all_to_all | solution.py:851
  190.3 9.4 %assemble_half.1 = (bf16[4,768,384]{2,1,0:T(8,128)(2,1)}, bf16[4,384,384]{2,1,0:T(8,128)(2,1)}, bf16[4,768,384]{2,1,0:T(8,128)(2,1)}) custom-call(s32[1]{0:T(128)} %bitcast.17.half_ref, bf16[16,192,384]{2,1,0:T(8,128)(2,1)} %copy-done, bf16[16,192,384]{2,1,0:T(8,128)(2,1)} %copy-done.2, f32[192,8,96]{2,1,0:T(8,128)} %logit.1.refs_2_.refs_0_, ...), custom_call_target="tpu_custom_call" | custom-call | flops 1000 | bytes 1000 | tf_op jit(solution)/shard_map/assemble_half/pallas_call | solution.py:539
  202.0 4.9 all-to-all-start.2
  207.0 108.7 %collective-permute-done.13.recv_ref = bf16[4,768,384]{2,1,0:T(8,128)(2,1)} collective-permute-done((bf16[4,768,384]{2,1,0:T(8,128)(2,1)S(1)}, bf16[4,768,384]{2,1,0:T(8,128)(2,1)}, u32[]{:S(2)}, u32[]{:S(2)}) %collective-permute-start.13) | collective-permute-done | bytes 2359328 | tf_op jit(solution)/shard_map/ppermute | solution.py:957
  315.7 6.8 %combine.1.refs_1_.refs_0_ = bf16[16,192,384]{2,1,0:T(8,128)(2,1)} custom-call(bf16[4,768,384]{2,1,0:T(8,128)(2,1)} %get-tuple-element.26.left_ref, bf16[4,384,384]{2,1,0:T(8,128)(2,1)} %get-tuple-element.27.own_ref, bf16[4,768,384]{2,1,0:T(8,128)(2,1)} %collective-permute-done.13.recv_ref, bf16[16,384,384]{2,1,0:T(8,128)(2,1)} %all-to-all-done.2.refs_0_.recv_ref), custom_call_target="tpu_custom_call" | custom-call | flops 1000 | bytes 1000 | tf_op jit(solution)/shard_map/combine/pallas_call | solution.py:606
  322.5 3.7 all-to-all-start.3
  330.2 8.8 %assemble.1 = (bf16[2,16,48,768]{3,2,1,0:T(8,128)(2,1)}, bf16[2,4,1,192,768]{4,3,2,1,0:T(8,128)(2,1)}) custom-call(bf16[16,384,384]{2,1,0:T(8,128)(2,1)} %all-to-all-done.2.refs_0_.recv_ref, bf16[16,192,384]{2,1,0:T(8,128)(2,1)} %combine.1.refs_1_.refs_0_), custom_call_target="tpu_custom_call" | custom-call | flops 1000 | bytes 1000 | tf_op jit(solution)/shard_map/assemble/pallas_call | solution.py:377
  339.0 34.7 %collective-permute-done.14.refs_0_.refs_1_ = f32[192,8,96]{2,1,0:T(8,128)S(1)} collective-permute-done((f32[192,8,96]{2,1,0:T(8,128)}, f32[192,8,96]{2,1,0:T(8,128)S(1)}, u32[]{:S(2)}, u32[]{:S(2)}) %collective-permute-start.14) | collective-permute-done | bytes 589856 | tf_op jit(solution)/shard_map/ppermute | solution.py:899
  373.7 17.4 %collective-permute-done.16.refs_2_.refs_3_ = f32[192,8,96]{2,1,0:T(8,128)} collective-permute-done((f32[192,8,96]{2,1,0:T(8,128)}, f32[192,8,96]{2,1,0:T(8,128)}, u32[]{:S(2)}, u32[]{:S(2)}) %collective-permute-start.16) | collective-permute-done | bytes 589856 | tf_op jit(solution)/shard_map/ppermute | solution.py:899
  391.1 7.0 %multiply.13.refs_1_ = bf16[32,96,384]{2,1,0:T(8,128)(2,1)} custom-call(bf16[2,16,48,768]{3,2,1,0:T(8,128)(2,1)} %get-tuple-element.32.left_ref, bf16[2,768,768]{2,1,0:T(8,128)(2,1)} %bitcast.58, f32[192,8,96]{2,1,0:T(8,128)} %copy-done.5, f32[192,8,96]{2,1,0:T(8,128)} %collective-permute-done.15.refs_1_.refs_2_, ...), custom_call_target="tpu_custom_call" | custom-call | flops 1000 | bytes 1000 | tf_op jit(solution)/shard_map/multiply/pallas_call | solution.py:442
  399.5 4.8 all-to-all-start.4
  408.6 3.4 collective-permute-start.17
  415.0 29.5 %collective-permute-done.17.refs_5_ = bf16[96,256]{1,0:T(8,128)(2,1)S(1)} collective-permute-done((bf16[96,256]{1,0:T(8,128)(2,1)}, bf16[96,256]{1,0:T(8,128)(2,1)S(1)}, u32[]{:S(2)}, u32[]{:S(2)}) %collective-permute-start.17) | collective-permute-done | bytes 49184 | tf_op jit(solution)/shard_map/ppermute | solution.py:899
  445.6 19.4 %collective-permute-start.23 = (bf16[96,256]{1,0:T(8,128)(2,1)}, bf16[96,256]{1,0:T(8,128)(2,1)S(1)}, u32[]{:S(2)}, u32[]{:S(2)}) collective-permute-start(bf16[96,256]{1,0:T(8,128)(2,1)} %fence.9.refs_4_), channel_id=1, source_target_pairs={{0,1},{1,2},{2,3},{3,4},{4,5},{5,6},{6,7},{7,0},{8,9},{9,10},{10,1... | collective-permute-start | bytes 147464 | tf_op jit(solution)/shard_map/ppermute | solution.py:899
  471.8 6.1 %average.1 = bf16[96,256]{1,0:T(8,128)(2,1)} custom-call(s32[2]{0:T(128)} %pad_add_fusion.place_ref, f32[192,8,96]{2,1,0:T(8,128)} %fence.8.refs_0_, f32[192,8,96]{2,1,0:T(8,128)} %copy-done.5, f32[192,8,96]{2,1,0:T(8,128)} %collective-permute-done.15.refs_1_.refs_2_, f32[192,8,96]{2,1,0:T(8,128)} %collective-permute-done.16.refs_2_.refs_3_, ...), custom_call_target="tpu_custom_call" | custom-call | flops 1000 | bytes 1000 | tf_op jit(solution)/shard_map/average/pallas_call | solution.py:686
  479.4 13.1 %finish.1 = bf16[192,96,128]{2,1,0:T(8,128)(2,1)} custom-call(bf16[16,192,384]{2,1,0:T(8,128)(2,1)} %copy-done.1, bf16[32,96,384]{2,1,0:T(8,128)(2,1)} %all-to-all-done.4.refs_1_, bf16[96,96,128]{2,1,0:T(8,128)(2,1)} %get-tuple-element.34.refs_2_, bf16[96,96,128]{2,1,0:T(8,128)(2,1)} %get-tuple-element.35.refs_3_, ...), custom_call_target="tpu_custom_call" | custom-call | flops 1000 | bytes 1000 | tf_op jit(solution)/shard_map/finish/pallas_call | solution.py:755
  (174 shorter events, 57.4 us)
Async XLA Ops:
  0.6 37.9 %copy-start.22 = (bf16[1024,128]{1,0:T(8,128)(2,1)S(1)}, bf16[1024,128]{1,0:T(8,128)(2,1)}, u32[]{:S(2)}) copy-start(bf16[1024,128]{1,0:T(8,128)(2,1)} %param.15) | copy-start | bytes 786436
  4.0 54.6 %copy-start.9 = (bf16[4,96,64]{1,2,0:T(8,128)(2,1)}, bf16[4,96,64]{1,2,0:T(8,128)(2,1)S(1)}, u32[]{:S(2)}) copy-start(bf16[4,96,64]{1,2,0:T(8,128)(2,1)S(1)} %fusion.7) | copy-start | bytes 147460
  6.5 11.7 %collective-permute-start = (bf16[4,96,32]{2,1,0:T(8,128)(2,1)S(1)}, bf16[4,96,32]{2,1,0:T(8,128)(2,1)S(1)}, u32[]{:S(2)}, u32[]{:S(2)}) collective-permute-start(bf16[4,96,32]{2,1,0:T(8,128)(2,1)S(1)} %get-tuple-element.39), channel_id=1, source_target_pairs={{0,0},{1,1},{2,8},{3,9},{4,16},{5,17},{6,24},{7,25},{8,2},{9,3},{1... | collective-permute-start | bytes 73736 | tf_op jit(solution)/shard_map/ppermute | solution.py:832
  7.2 13.9 %collective-permute-start.1 = (bf16[4,96,32]{2,1,0:T(8,128)(2,1)S(1)}, bf16[4,96,32]{2,1,0:T(8,128)(2,1)S(1)}, u32[]{:S(2)}, u32[]{:S(2)}) collective-permute-start(bf16[4,96,32]{2,1,0:T(8,128)(2,1)S(1)} %get-tuple-element.39), channel_id=1, source_target_pairs={{0,7},{1,0},{2,15},{3,8},{4,23},{5,16},{6,31},{7,24},{8,1},{9,2},{... | collective-permute-start | bytes 73736 | tf_op jit(solution)/shard_map/ppermute | solution.py:832
  14.8 7.9 %collective-permute-start.2 = (bf16[4,96,32]{2,1,0:T(8,128)(2,1)S(1)}, bf16[4,96,32]{2,1,0:T(8,128)(2,1)S(1)}, u32[]{:S(2)}, u32[]{:S(2)}) collective-permute-start(bf16[4,96,32]{2,1,0:T(8,128)(2,1)S(1)} %get-tuple-element.39), channel_id=1, source_target_pairs={{0,6},{1,7},{2,14},{3,15},{4,22},{5,23},{6,30},{7,31},{8,0},{9,1},... | collective-permute-start | bytes 73736 | tf_op jit(solution)/shard_map/ppermute | solution.py:832
  15.7 10.3 %collective-permute-start.3 = (bf16[4,96,32]{2,1,0:T(8,128)(2,1)S(1)}, bf16[4,96,32]{2,1,0:T(8,128)(2,1)S(1)}, u32[]{:S(2)}, u32[]{:S(2)}) collective-permute-start(bf16[4,96,32]{2,1,0:T(8,128)(2,1)S(1)} %get-tuple-element.39), channel_id=1, source_target_pairs={{0,5},{1,6},{2,13},{3,14},{4,21},{5,22},{6,29},{7,30},{8,7},{9,0},... | collective-permute-start | bytes 73736 | tf_op jit(solution)/shard_map/ppermute | solution.py:832
  17.4 13.2 %collective-permute-start.4 = (bf16[4,96,32]{2,1,0:T(8,128)(2,1)S(1)}, bf16[4,96,32]{2,1,0:T(8,128)(2,1)S(1)}, u32[]{:S(2)}, u32[]{:S(2)}) collective-permute-start(bf16[4,96,32]{2,1,0:T(8,128)(2,1)S(1)} %get-tuple-element.39), channel_id=1, source_target_pairs={{0,4},{1,5},{2,12},{3,13},{4,20},{5,21},{6,28},{7,29},{8,6},{9,7},... | collective-permute-start | bytes 73736 | tf_op jit(solution)/shard_map/ppermute | solution.py:832
  18.3 15.0 %collective-permute-start.5 = (bf16[4,96,32]{2,1,0:T(8,128)(2,1)S(1)}, bf16[4,96,32]{2,1,0:T(8,128)(2,1)S(1)}, u32[]{:S(2)}, u32[]{:S(2)}) collective-permute-start(bf16[4,96,32]{2,1,0:T(8,128)(2,1)S(1)} %get-tuple-element.39), channel_id=1, source_target_pairs={{0,3},{1,4},{2,11},{3,12},{4,19},{5,20},{6,27},{7,28},{8,5},{9,6},... | collective-permute-start | bytes 73736 | tf_op jit(solution)/shard_map/ppermute | solution.py:832
  21.1 20.9 %collective-permute-start.6 = (bf16[4,96,32]{2,1,0:T(8,128)(2,1)S(1)}, bf16[4,96,32]{2,1,0:T(8,128)(2,1)S(1)}, u32[]{:S(2)}, u32[]{:S(2)}) collective-permute-start(bf16[4,96,32]{2,1,0:T(8,128)(2,1)S(1)} %get-tuple-element.39), channel_id=1, source_target_pairs={{0,2},{1,3},{2,10},{3,11},{4,18},{5,19},{6,26},{7,27},{8,4},{9,5},... | collective-permute-start | bytes 73736 | tf_op jit(solution)/shard_map/ppermute | solution.py:832
  22.7 19.3 %collective-permute-start.7 = (bf16[4,96,32]{2,1,0:T(8,128)(2,1)S(1)}, bf16[4,96,32]{2,1,0:T(8,128)(2,1)S(1)}, u32[]{:S(2)}, u32[]{:S(2)}) collective-permute-start(bf16[4,96,32]{2,1,0:T(8,128)(2,1)S(1)} %get-tuple-element.39), channel_id=1, source_target_pairs={{0,1},{1,2},{2,9},{3,10},{4,17},{5,18},{6,25},{7,26},{8,3},{9,4},{... | collective-permute-start | bytes 73736 | tf_op jit(solution)/shard_map/ppermute | solution.py:832
  26.0 16.1 %collective-permute-start.8 = (bf16[4,96,32]{2,1,0:T(8,128)(2,1)S(1)}, bf16[4,96,32]{2,1,0:T(8,128)(2,1)S(1)}, u32[]{:S(2)}, u32[]{:S(2)}) collective-permute-start(bf16[4,96,32]{2,1,0:T(8,128)(2,1)S(1)} %get-tuple-element.38.refs_8_), channel_id=1, source_target_pairs={{0,24},{8,0},{16,8},{24,16},{1,25},{9,1},{17,9},{25,17},{2,26},{10... | collective-permute-start | bytes 73736 | tf_op jit(solution)/shard_map/ppermute | solution.py:836
  30.6 11.4 %collective-permute-start.9 = (bf16[4,96,32]{2,1,0:T(8,128)(2,1)S(1)}, bf16[4,96,32]{2,1,0:T(8,128)(2,1)S(1)}, u32[]{:S(2)}, u32[]{:S(2)}) collective-permute-start(bf16[4,96,32]{2,1,0:T(8,128)(2,1)S(1)} %get-tuple-element.38.refs_8_), channel_id=1, source_target_pairs={{0,16},{8,24},{16,0},{24,8},{1,17},{9,25},{17,1},{25,9},{2,18},{10... | collective-permute-start | bytes 73736 | tf_op jit(solution)/shard_map/ppermute | solution.py:836
  33.3 8.8 %collective-permute-start.10 = (bf16[4,96,32]{2,1,0:T(8,128)(2,1)S(1)}, bf16[4,96,32]{2,1,0:T(8,128)(2,1)S(1)}, u32[]{:S(2)}, u32[]{:S(2)}) collective-permute-start(bf16[4,96,32]{2,1,0:T(8,128)(2,1)S(1)} %get-tuple-element.38.refs_8_), channel_id=1, source_target_pairs={{0,8},{8,16},{16,24},{24,0},{1,9},{9,17},{17,25},{25,1},{2,10},{10... | collective-permute-start | bytes 73736 | tf_op jit(solution)/shard_map/ppermute | solution.py:836
  67.5 59.1 %all-to-all-start = ((bf16[16,192,384]{2,1,0:T(8,128)(2,1)}), bf16[16,192,384]{2,1,0:T(8,128)(2,1)S(1)}, u32[]{:S(2)}, u32[]{:S(2)}) async-start(bf16[16,192,384]{2,1,0:T(8,128)(2,1)} %get-tuple-element.22), calls=%async_computation | async-start | bytes 4718592 | tf_op jit(solution)/shard_map/all_to_all | solution.py:851
  71.4 54.7 %collective-permute-start.11 = (bf16[16,96,384]{2,1,0:T(8,128)(2,1)S(1)}, bf16[16,96,384]{2,1,0:T(8,128)(2,1)}, u32[]{:S(2)}, u32[]{:S(2)}) collective-permute-start(bf16[16,96,384]{2,1,0:T(8,128)(2,1)S(1)} %copy-done.4), channel_id=1, source_target_pairs={{0,4},{4,0},{1,5},{5,1},{2,6},{6,2},{3,7},{7,3},{8,12},{12,8},{9,1... | collective-permute-start | bytes 3538952 | tf_op jit(solution)/shard_map/ppermute | solution.py:945
  128.0 60.8 %all-to-all-start.1 = ((bf16[16,192,384]{2,1,0:T(8,128)(2,1)}), bf16[16,192,384]{2,1,0:T(8,128)(2,1)S(1)}, u32[]{:S(2)}, u32[]{:S(2)}) async-start(bf16[16,192,384]{2,1,0:T(8,128)(2,1)} %get-tuple-element.25), calls=%async_computation.1 | async-start | bytes 4718592 | tf_op jit(solution)/shard_map/all_to_all | solution.py:851
  133.3 66.3 %collective-permute-start.12 = (bf16[16,96,384]{2,1,0:T(8,128)(2,1)S(1)}, bf16[16,96,384]{2,1,0:T(8,128)(2,1)}, u32[]{:S(2)}, u32[]{:S(2)}) collective-permute-start(bf16[16,96,384]{2,1,0:T(8,128)(2,1)S(1)} %copy-done.3), channel_id=1, source_target_pairs={{0,4},{4,0},{1,5},{5,1},{2,6},{6,2},{3,7},{7,3},{8,12},{12,8},{9,1... | collective-permute-start | bytes 3538952 | tf_op jit(solution)/shard_map/ppermute | solution.py:945
  202.0 113.7 %all-to-all-start.2 = ((bf16[16,384,384]{2,1,0:T(8,128)(2,1)}), bf16[16,384,384]{2,1,0:T(8,128)(2,1)}, u32[]{:S(2)}, u32[]{:S(2)}) async-start(bf16[16,384,384]{2,1,0:T(8,128)(2,1)} %get-tuple-element.31), calls=%async_computation.2 | async-start | bytes 9437184 | tf_op jit(solution)/shard_map/all_to_all | solution.py:851
  206.9 108.8 %collective-permute-start.13 = (bf16[4,768,384]{2,1,0:T(8,128)(2,1)S(1)}, bf16[4,768,384]{2,1,0:T(8,128)(2,1)}, u32[]{:S(2)}, u32[]{:S(2)}) collective-permute-start(bf16[4,768,384]{2,1,0:T(8,128)(2,1)S(1)} %copy-done.6), channel_id=1, source_target_pairs={{0,4},{4,0},{1,5},{5,1},{2,6},{6,2},{3,7},{7,3},{8,12},{12,8},{9,1... | collective-permute-start | bytes 7077896 | tf_op jit(solution)/shard_map/ppermute | solution.py:957
  322.5 75.6 %all-to-all-start.3 = ((bf16[16,192,384]{2,1,0:T(8,128)(2,1)}), bf16[16,192,384]{2,1,0:T(8,128)(2,1)S(1)}, u32[]{:S(2)}, u32[]{:S(2)}) async-start(bf16[16,192,384]{2,1,0:T(8,128)(2,1)} %combine.1.refs_1_.refs_0_), calls=%async_computation.3 | async-start | bytes 4718592 | tf_op jit(solution)/shard_map/all_to_all | solution.py:851
  326.3 47.4 %collective-permute-start.14 = (f32[192,8,96]{2,1,0:T(8,128)}, f32[192,8,96]{2,1,0:T(8,128)S(1)}, u32[]{:S(2)}, u32[]{:S(2)}) collective-permute-start(f32[192,8,96]{2,1,0:T(8,128)} %fence.8.refs_0_), channel_id=1, source_target_pairs={{0,24},{8,0},{16,8},{24,16},{1,25},{9,1},{17,9},{25,17},{2,26},{10... | collective-permute-start | bytes 1769480 | tf_op jit(solution)/shard_map/ppermute | solution.py:899
  329.1 44.6 %collective-permute-start.15 = (f32[192,8,96]{2,1,0:T(8,128)}, f32[192,8,96]{2,1,0:T(8,128)}, u32[]{:S(2)}, u32[]{:S(2)}) collective-permute-start(f32[192,8,96]{2,1,0:T(8,128)} %fence.8.refs_0_), channel_id=1, source_target_pairs={{0,16},{8,24},{16,0},{24,8},{1,17},{9,25},{17,1},{25,9},{2,18},{10... | collective-permute-start | bytes 1769480 | tf_op jit(solution)/shard_map/ppermute | solution.py:899
  329.6 61.5 %collective-permute-start.16 = (f32[192,8,96]{2,1,0:T(8,128)}, f32[192,8,96]{2,1,0:T(8,128)}, u32[]{:S(2)}, u32[]{:S(2)}) collective-permute-start(f32[192,8,96]{2,1,0:T(8,128)} %fence.8.refs_0_), channel_id=1, source_target_pairs={{0,8},{8,16},{16,24},{24,0},{1,9},{9,17},{17,25},{25,1},{2,10},{10... | collective-permute-start | bytes 1769480 | tf_op jit(solution)/shard_map/ppermute | solution.py:899
  399.5 79.9 %all-to-all-start.4 = ((bf16[32,96,384]{2,1,0:T(8,128)(2,1)}), bf16[32,96,384]{2,1,0:T(8,128)(2,1)}, u32[]{:S(2)}, u32[]{:S(2)}) async-start(bf16[32,96,384]{2,1,0:T(8,128)(2,1)} %multiply.13.refs_1_), calls=%async_computation.4 | async-start | bytes 4718592 | tf_op jit(solution)/shard_map/all_to_all | solution.py:851
  408.6 59.5 %copy-start.7 = (bf16[4,96,64]{1,2,0:T(8,128)(2,1)S(1)}, bf16[4,96,64]{1,2,0:T(8,128)(2,1)}, u32[]{:S(2)}) copy-start(bf16[4,96,64]{1,2,0:T(8,128)(2,1)} %param.10) | copy-start | bytes 147460
  408.6 35.9 %collective-permute-start.17 = (bf16[96,256]{1,0:T(8,128)(2,1)}, bf16[96,256]{1,0:T(8,128)(2,1)S(1)}, u32[]{:S(2)}, u32[]{:S(2)}) collective-permute-start(bf16[96,256]{1,0:T(8,128)(2,1)} %fence.9.refs_4_), channel_id=1, source_target_pairs={{0,7},{1,0},{2,1},{3,2},{4,3},{5,4},{6,5},{7,6},{8,15},{9,8},{10,9... | collective-permute-start | bytes 147464 | tf_op jit(solution)/shard_map/ppermute | solution.py:899
  412.0 33.6 %collective-permute-start.18 = (bf16[96,256]{1,0:T(8,128)(2,1)}, bf16[96,256]{1,0:T(8,128)(2,1)S(1)}, u32[]{:S(2)}, u32[]{:S(2)}) collective-permute-start(bf16[96,256]{1,0:T(8,128)(2,1)} %fence.9.refs_4_), channel_id=1, source_target_pairs={{0,6},{1,7},{2,0},{3,1},{4,2},{5,3},{6,4},{7,5},{8,14},{9,15},{10,... | collective-permute-start | bytes 147464 | tf_op jit(solution)/shard_map/ppermute | solution.py:899
  412.5 58.0 %collective-permute-start.19 = (bf16[96,256]{1,0:T(8,128)(2,1)}, bf16[96,256]{1,0:T(8,128)(2,1)S(1)}, u32[]{:S(2)}, u32[]{:S(2)}) collective-permute-start(bf16[96,256]{1,0:T(8,128)(2,1)} %fence.9.refs_4_), channel_id=1, source_target_pairs={{0,5},{1,6},{2,7},{3,0},{4,1},{5,2},{6,3},{7,4},{8,13},{9,14},{10,... | collective-permute-start | bytes 147464 | tf_op jit(solution)/shard_map/ppermute | solution.py:899
  412.6 58.0 %collective-permute-start.20 = (bf16[96,256]{1,0:T(8,128)(2,1)}, bf16[96,256]{1,0:T(8,128)(2,1)S(1)}, u32[]{:S(2)}, u32[]{:S(2)}) collective-permute-start(bf16[96,256]{1,0:T(8,128)(2,1)} %fence.9.refs_4_), channel_id=1, source_target_pairs={{0,4},{1,5},{2,6},{3,7},{4,0},{5,1},{6,2},{7,3},{8,12},{9,13},{10,... | collective-permute-start | bytes 147464 | tf_op jit(solution)/shard_map/ppermute | solution.py:899
  415.0 55.5 %collective-permute-start.21 = (bf16[96,256]{1,0:T(8,128)(2,1)}, bf16[96,256]{1,0:T(8,128)(2,1)S(1)}, u32[]{:S(2)}, u32[]{:S(2)}) collective-permute-start(bf16[96,256]{1,0:T(8,128)(2,1)} %fence.9.refs_4_), channel_id=1, source_target_pairs={{0,3},{1,4},{2,5},{3,6},{4,7},{5,0},{6,1},{7,2},{8,11},{9,12},{10,... | collective-permute-start | bytes 147464 | tf_op jit(solution)/shard_map/ppermute | solution.py:899
  444.5 26.0 %collective-permute-start.22 = (bf16[96,256]{1,0:T(8,128)(2,1)}, bf16[96,256]{1,0:T(8,128)(2,1)S(1)}, u32[]{:S(2)}, u32[]{:S(2)}) collective-permute-start(bf16[96,256]{1,0:T(8,128)(2,1)} %fence.9.refs_4_), channel_id=1, source_target_pairs={{0,2},{1,3},{2,4},{3,5},{4,6},{5,7},{6,0},{7,1},{8,10},{9,11},{10,... | collective-permute-start | bytes 147464 | tf_op jit(solution)/shard_map/ppermute | solution.py:899
  445.6 25.0 %collective-permute-start.23 = (bf16[96,256]{1,0:T(8,128)(2,1)}, bf16[96,256]{1,0:T(8,128)(2,1)S(1)}, u32[]{:S(2)}, u32[]{:S(2)}) collective-permute-start(bf16[96,256]{1,0:T(8,128)(2,1)} %fence.9.refs_4_), channel_id=1, source_target_pairs={{0,1},{1,2},{2,3},{3,4},{4,5},{5,6},{6,7},{7,0},{8,9},{9,10},{10,1... | collective-permute-start | bytes 147464 | tf_op jit(solution)/shard_map/ppermute | solution.py:899
  (31 other events, 271.2 us)

commit v10 on v9

--- a/solution.py
+++ b/solution.py
@@ -113,12 +113,12 @@
 def front_kernel(place_ref, *refs, row_count, col_count, first_block):
     lefts, rights = refs[:col_count], refs[col_count : col_count + row_count]
     refs = refs[col_count + row_count :]
-    prow_ref, coup_ref, weight_ref, pcol_ref = refs[:4]
+    prow_ref, coup_ref, weight_ref, pcol_ref, wleft_ref, pside_ref = refs[:6]
     sides_ref, right_ref, tmp_ref = refs[-3:]
     mid_ref, normed_ref = refs[-5:-3]
     step_at = pl.program_id(0) + first_block
     block, cols, wide = coup_ref.shape
-    seq_each, _, width = lefts[0].shape
+    seq_each, _, width = wleft_ref.shape
     seqs = seq_each * row_count
     per_row = col_count // row_count
 
@@ -126,9 +126,16 @@
     def _():
         for t, part in enumerate(lefts):
             index = lax.rem(t + place_ref[1], col_count)
-            first = lax.rem(index, per_row) * (cols * seqs) + index // per_row * seq_each
+            span = pl.multiple_of(lax.rem(index, per_row) * cols, cols)
+            first = index // per_row * seq_each
+            present = pside_ref[pl.ds(span, cols), :]
+            seq_lane = lax.broadcasted_iota(jnp.int32, present.shape, 1)
             for k in range(seq_each):
-                sides_ref[pl.ds(first + k, cols, stride=seqs), 0:width] = part[k].astype(F32)
+                mask = jnp.sum(
+                    jnp.where(seq_lane == first + k, present, 0.0), axis=1, keepdims=True
+                )
+                left = jnp.dot(part[...], wleft_ref[k], preferred_element_type=F32) * mask
+                sides_ref[pl.ds(span * seqs + first + k, cols, stride=seqs), 0:width] = left
         right = jnp.zeros(right_ref.shape, F32)
         feature = lax.broadcasted_iota(jnp.int32, (width, width * seqs), 0)
         target = lax.broadcasted_iota(jnp.int32, (width, width * seqs), 1)
@@ -174,9 +181,12 @@
             normed_ref[i] = standardize_features(mid.astype(F32), 1).astype(BF16)
 
 
-def front(chunk, chunks, place, lefts, rights, present_rows, coupling, w_tensor, present_cols, after):
+def front(
+    chunk, chunks, place, lefts, rights, present_rows, coupling, w_tensor, present_cols, w_left, after
+):
     rows, cols, wide = coupling.shape
-    seqs, width = present_rows.shape[0], lefts[0].shape[2]
+    seqs, width = present_rows.shape[0], w_left.shape[2]
+    present_sides = present_rows.T
     block = 8
     steps = rows // block // chunks
     tile = pl.BlockSpec((block, cols, wide), lambda i: (i, 0, 0))
@@ -195,6 +205,8 @@
             pl.BlockSpec((block, cols, wide), lambda i: (i + chunk * steps, 0, 0)),
             whole(w_tensor.shape),
             whole(present_cols.shape),
+            whole(w_left.shape),
+            whole(present_sides.shape),
         ]
         + anywhere(after),
         out_specs=[tile, tile],
@@ -207,7 +219,18 @@
         compiler_params=params(),
         cost_estimate=LIGHT,
         name="front",
-    )(place, *lefts, *rights, present_rows, coupling, w_tensor, present_cols, *after)
+    )(
+        place,
+        *lefts,
+        *rights,
+        present_rows,
+        coupling,
+        w_tensor,
+        present_cols,
+        w_left,
+        present_sides,
+        *after,
+    )
 
 
 def exchange_rows(values):
@@ -644,59 +667,97 @@
     )(*pieces, *into)
 
 
-def average_kernel(place_ref, *refs, row_count, col_count):
-    logits, values = refs[:row_count], refs[row_count : row_count + col_count]
-    refs = refs[row_count + col_count :]
-    gate_ref, align_ref, weight_ref, project_ref, out_ref, exp_ref, value_ref = refs
-    rows, heads, cols = logits[0].shape
-    wide = gate_ref.shape[2]
+def partial_kernel(place_ref, logit_ref, *refs, row_count, col_count):
+    sides, refs = refs[:col_count], refs[col_count:]
+    project_ref, outs, exp_ref, value_ref = refs[0], refs[1 : 1 + row_count], *refs[-2:]
+    rows, heads, cols = logit_ref.shape
+    wide = value_ref.shape[2] // heads
     per_row = col_count // row_count
-    for u, value in enumerate(values):
-        value_ref[lax.rem(place_ref[1] + u, col_count)] = jnp.dot(
-            value[...], project_ref[...], preferred_element_type=F32
+    for u, side in enumerate(sides):
+        index = lax.rem(place_ref[1] + u, col_count)
+        part = lax.rem(place_ref[0] + row_count - index // per_row, row_count)
+        span = pl.multiple_of(lax.rem(index, per_row) * cols, cols)
+        value_ref[part, pl.ds(span, cols), :] = jnp.dot(
+            side[...], project_ref[...], preferred_element_type=F32
         ).astype(BF16)
-    top = jnp.max(logits[0][...], axis=0)
-    for block in logits[1:]:
-        top = jnp.maximum(top, jnp.max(block[...], axis=0))
-    total = jnp.zeros((heads, cols), F32)
-    size = rows * heads
-    for t, block in enumerate(logits):
-        powers = jnp.exp(block[...] - top[None])
-        total = total + jnp.sum(powers, axis=0)
-        exp_ref[t * size : (t + 1) * size, 0:cols] = powers.reshape(size, cols)
+    top = jnp.max(logit_ref[...], axis=0)
+    powers = jnp.exp(logit_ref[...] - top[None])
+    total = jnp.sum(powers, axis=0)
+    exp_ref[:, 0:cols] = powers.reshape(rows * heads, cols)
+    for h in range(heads):
+        weights = exp_ref[pl.ds(h, rows, stride=heads), :][:, :cols].astype(BF16)
+        for t, out in enumerate(outs):
+            out[h, :cols] = lax.dot_general(
+                weights,
+                value_ref[t, :, h * wide : (h + 1) * wide],
+                TN,
+                preferred_element_type=F32,
+            )
+            out[h, cols:] = jnp.zeros((out.shape[1] - cols, wide), F32)
+            out[h, cols : cols + 1, 0:cols] = top[h : h + 1]
+            out[h, cols + 1 : cols + 2, 0:cols] = total[h : h + 1]
+
+
+def partial_average(place, logits, sides, w_value):
+    rows, heads, cols = logits.shape
+    wide = w_value.shape[1] // heads
+    row_count = len(sides) * cols // rows
+    shape = (heads, cols + 8, wide)
+    return pl.pallas_call(
+        functools.partial(partial_kernel, row_count=row_count, col_count=len(sides)),
+        grid=(1,),
+        in_specs=[pl.BlockSpec(memory_space=pltpu.SMEM)]
+        + [whole(v.shape) for v in (logits, *sides, w_value)],
+        out_specs=[whole(shape)] * row_count,
+        out_shape=[jax.ShapeDtypeStruct(shape, F32)] * row_count,
+        scratch_shapes=[
+            pltpu.VMEM((rows * heads, LANES), F32),
+            pltpu.VMEM((row_count, rows, w_value.shape[1]), BF16),
+        ],
+        compiler_params=params(),
+        cost_estimate=LIGHT,
+        name="partial",
+    )(place, logits, *sides, w_value)
+
+
+def average_kernel(*refs):
+    parts, (gate_ref, align_ref, weight_ref, out_ref) = refs[:-4], refs[-4:]
+    heads, cols, _ = gate_ref.shape
+    here = lax.broadcasted_iota(jnp.int32, (cols, cols), 0)
+    there = lax.broadcasted_iota(jnp.int32, (cols, cols), 1)
     out = align_ref[...].astype(F32)
     for h in range(heads):
+        tops = [part[h, cols : cols + 1, 0:cols] for part in parts]
+        sums = [part[h, cols + 1 : cols + 2, 0:cols] for part in parts]
+        top = functools.reduce(jnp.maximum, tops)
+        scales = [jnp.exp(t - top) for t in tops]
+        total = sum(scale * each for scale, each in zip(scales, sums))
         summed = jnp.zeros(gate_ref.shape[1:], F32)
-        for t in range(row_count):
-            first = lax.rem(place_ref[0] + t, row_count) * per_row
-            powers = exp_ref[pl.ds(t * size + h, rows, stride=heads), :][:, :cols]
-            weights = (powers / total[h : h + 1]).astype(BF16)
-            value = jnp.concatenate(
-                [value_ref[first + k, :, h * wide : (h + 1) * wide] for k in range(per_row)], axis=0
+        for part, scale in zip(parts, scales):
+            factor = jnp.where(here == there, scale / total, 0.0)
+            summed += jnp.dot(
+                factor,
+                part[h, :cols],
+                precision=lax.Precision.HIGHEST,
+                preferred_element_type=F32,
             )
-            summed += lax.dot_general(weights, value, TN, preferred_element_type=F32)
         gated = (gate_ref[h] * summed).astype(BF16)
         out += jnp.dot(gated, weight_ref[h], preferred_element_type=F32)
     out_ref[...] = out.astype(BF16)
 
 
-def average(place, logits, values, gate, align, weight, w_value):
-    rows, heads, cols = logits[0].shape
-    operands = [*logits, *values, gate, align, weight, w_value]
-    return pl.pallas_call(
-        functools.partial(average_kernel, row_count=len(logits), col_count=len(values)),
+def average(parts, gate, align, weight):
+    operands = [*parts, gate, align, weight]
+    return pl.pallas_call(
+        average_kernel,
         grid=(1,),
-        in_specs=[pl.BlockSpec(memory_space=pltpu.SMEM)] + [whole(v.shape) for v in operands],
+        in_specs=[whole(v.shape) for v in operands],
         out_specs=whole(align.shape),
         out_shape=jax.ShapeDtypeStruct(align.shape, BF16),
-        scratch_shapes=[
-            pltpu.VMEM((len(logits) * rows * heads, LANES), F32),
-            pltpu.VMEM((len(values), cols, w_value.shape[1]), BF16),
-        ],
         compiler_params=params(),
         cost_estimate=LIGHT,
         name="average",
-    )(place, *operands)
+    )(*operands)
 
 
 def finish_kernel(*refs, parts, chunks):
@@ -817,10 +878,14 @@
             seq_each, module_number, -1
         )
 
-    own_sides = project_msa(alignment_matrix[:, : 2 * TENSOR_FEATURES])
-    own_sides = (own_sides * present_own[:, :, None]).astype(BF16)
-    own_left = own_sides[:, :, :TENSOR_FEATURES]
-    own_right = own_sides[:, :, TENSOR_FEATURES:]
+    own_right = project_msa(alignment_matrix[:, TENSOR_FEATURES : 2 * TENSOR_FEATURES])
+    own_right = (own_right * present_own[:, :, None]).astype(BF16)
+    own_rows = jnp.transpose(
+        own_normed.reshape(seq_each, module_number, feature_count), (1, 0, 2)
+    ).reshape(module_number, -1)
+    apart = jnp.eye(seq_each, dtype=BF16)
+    w_left = apart[:, :, None, None] * alignment_matrix[:, :TENSOR_FEATURES]
+    w_left = w_left.reshape(seq_each, seq_each * feature_count, TENSOR_FEATURES)
     per_row = rows // module_number
     lefts = []
     for t in range(col_count):
@@ -829,7 +894,7 @@
             for q in range(col_count):
                 to = (r * per_row + q % per_row - t) % col_count
                 pairs.append((r * col_count + q, q // per_row * col_count + to))
-        lefts.append(lax.ppermute(own_left, AXES, pairs))
+        lefts.append(lax.ppermute(own_rows, AXES, pairs))
     rights = [own_right]
     for t in range(1, row_count):
         pairs = [(r, (r - t) % row_count) for r in range(row_count)]
@@ -861,6 +926,7 @@
             coupling_embedding,
             w_tensor,
             present_cols.T.astype(BF16),
+            w_left,
             after,
         )
 
@@ -879,25 +945,22 @@
     w_value = alignment_matrix[:, first:middle].reshape(
         1, feature_count, MEAN_GROUPS, 1, GROUP_FEATURES
     )
-    apart = jnp.eye(seq_each, dtype=BF16).reshape(seq_each, 1, 1, seq_each, 1)
-    w_value = (w_value * apart).reshape(seq_each * feature_count, -1)
-    own_rows = jnp.transpose(
-        own_normed.reshape(seq_each, module_number, feature_count), (1, 0, 2)
-    ).reshape(module_number, -1)
+    w_value = (w_value * apart.reshape(seq_each, 1, 1, seq_each, 1)).reshape(
+        seq_each * feature_count, -1
+    )
     sequence_gate = by_head(jax.nn.sigmoid(project_msa(alignment_matrix[:, middle:])))
     w_mean = mean_final_matrix.reshape(MEAN_GROUPS, 1, GROUP_FEATURES, 1, feature_count)
-    same = jnp.eye(seq_each, dtype=BF16).reshape(1, seq_each, 1, seq_each, 1)
-    w_mean = (w_mean * same).reshape(
+    w_mean = (w_mean * apart.reshape(1, seq_each, 1, seq_each, 1)).reshape(
         MEAN_GROUPS, seq_each * GROUP_FEATURES, seq_each * feature_count
     )
     align = jnp.transpose(alignment_embedding, (1, 0, 2)).reshape(module_number, -1)
 
-    def blocks_of(own, axes, count):
-        blocks = [own]
-        for t in range(1, count):
-            pairs = [(at, (at - t) % count) for at in range(count)]
-            blocks.append(lax.ppermute(own, axes, pairs))
-        return blocks
+    def gather_parts(parts):
+        gathered = list(parts[:1])
+        for t in range(1, row_count):
+            pairs = [(r, (r - t) % row_count) for r in range(row_count)]
+            gathered.append(lax.ppermute(parts[t], "row", pairs))
+        return gathered
 
     group = devices // 2
     shape_of = (row_count, col_count, module_number)
@@ -919,8 +982,8 @@
         last = multiply(left, right, (), *shape_of[1:])
         returned.append(exchange(last, AXES))
         logits = logit(live_rows, normeds, w_logit, ())
-        (logits,) = fence([logits], (last,))
-        logits = blocks_of(logits, "row", row_count)
+        parts = partial_average(place, logits, lefts, w_value)
+        parts = gather_parts(fence(parts, (last,)))
         orders = [(0, CTRI, devices)]
     else:
         cut = CTRI // 2
@@ -948,26 +1011,25 @@
             kept.append(project_rows(chunk, normed, w_own, group))
         half_scalar = half.astype(jnp.int32).reshape(1)
         logits = logit(live_rows, normeds, w_logit, tuple(kept))
+        parts = partial_average(place, logits, lefts, w_value)
         merged = merge(kept + crossed[:-1], 0, 2 * row_chunks, ())
         left, own, theirs = assemble_half(
-            half_scalar, received, (logits, merged), *half_shape
+            half_scalar, received, (parts[0], merged), *half_shape
         )
         merged = merge(crossed[-1:], 2 * row_chunks - 1, 2 * row_chunks, (merged,))
-        theirs, merged = fence([theirs, merged], ())
+        theirs, merged, *parts = fence([theirs, merged, *parts], ())
         partial = lax.ppermute(theirs, "half", swap)
         both = exchange(merged, GROUP)
-        product = combine(left, own, partial, (both,), *half_shape)
-        (logits,) = fence([logits], (product,))
-        logits = blocks_of(logits, "row", row_count)
+        parts = gather_parts(parts)
+        product = combine(left, own, partial, (both, *parts[1:]), *half_shape)
         returned.append(exchange(product, GROUP))
         left, right = assemble(0, 1, 2, both, (), (product,), *half_shape)
         right = right.reshape(right.shape[0], -1, right.shape[-1])
-        last = multiply(left, right, tuple(logits[1:]), *shape_of[1:])
+        last = multiply(left, right, (), *shape_of[1:])
         returned.append(exchange(last, AXES))
         orders = [(0, cut, group), (cut, CTRI, devices)]
-    (own_rows,) = fence([own_rows], (last,))
-    values = blocks_of(own_rows, ("half", "pos"), col_count)
-    aligned = average(place, logits, values, sequence_gate, align, w_mean, w_value)
+    parts = fence(parts, (last,))
+    aligned = average(parts, sequence_gate, align, w_mean)
     alignment_updated_embedding = jnp.transpose(
         aligned.reshape(module_number, seq_each, feature_count), (1, 0, 2)
     )

time: 495 us -> 432 us (0.87)
  waiting for transfers between devices: 253 us -> 209 us
  starting transfers between devices: 84.2 us -> 53.8 us
  local copies, waits for them, and re-layouts: 21.9 us -> 27.6 us
    ppermute x1, waiting for transfers between devices: 109 us -> 60.3 us  [on_device(): partial = lax.ppermute(theirs, 'half', swap)]
    all_to_all x5, waiting for transfers between devices: 36.5 us -> 77.2 us  [exchange(): return lax.all_to_all(block, axes, split_axis=0, concat_axis=0, tiled=True)]
    ppermute x18 -> x11, waiting for transfers between devices: 82.7 us -> 44.8 us  [the longest x3 44.8 us: gather_parts(): gathered.append(lax.ppermute(parts[t], 'row', pairs))]
    ppermute x18 -> x11, starting transfers between devices: 48.3 us -> 19.2 us  [the longest x8 15.4 us: on_device(): lefts.append(lax.ppermute(own_rows, AXES, pairs))]
  transfers between devices with their start and end apart: 29 -> 22, of which waited for: 8 -> 7; matrix products, arithmetic and copies ran while one was open for 4% -> 6% of each run, Pallas kernels for 16% -> 19%
where the time goes in v10:
time: 432 us; the launch traced here: 429 us
  waiting for transfers between devices  209 us (48%)
  Pallas kernels  127 us (29%)
  starting transfers between devices  53.8 us (12%)
  local copies, waits for them, and re-layouts  27.6 us (6%)
  other arithmetic  9.65 us (2%)
    all_to_all x5, waiting for transfers between devices, exchange(): return lax.all_to_all(block, axes, split_axis=0, concat_axis=0, tiled=True)  77.2 us
    ppermute x1, waiting for transfers between devices, on_device(): partial = lax.ppermute(theirs, 'half', swap)  60.3 us
    ppermute x3, waiting for transfers between devices, gather_parts(): gathered.append(lax.ppermute(parts[t], 'row', pairs))  44.8 us
    pallas_call x2, Pallas kernels, front(): pl.pallas_call(functools.partial(front_kernel, row_count=len(rights), col...  30.5 us
    ppermute x2, waiting for transfers between devices, on_device(): crossed.append(lax.ppermute(to_other, 'half', swap))  26.8 us
    pallas_call x6, Pallas kernels, project(): pl.pallas_call(functools.partial(project_kernel, first_row=first_row), gr...  26.1 us
    all_to_all x5, starting transfers between devices, exchange(): return lax.all_to_all(block, axes, split_axis=0, concat_axis=0, tiled=True)  25.1 us
    ppermute x8, starting transfers between devices, on_device(): lefts.append(lax.ppermute(own_rows, AXES, pairs))  15.4 us
  transfers between devices with their start and end apart: 22, of which 7 were waited for; matrix products, arithmetic and copies ran while one was open for 6% of the time, Pallas kernels for 19%

profile of v10, /device:TPU:0, one launch (start us, length us, event | category | flops | bytes accessed | tf_op | source)
XLA Modules:
  0.0 429.4 jit_solution(4934210718677671489)
XLA Ops:
  13.2 3.5 collective-permute-start.1
  28.1 3.5 collective-permute-start.7
  38.3 15.2 %front.2 = (bf16[96,96,128]{2,1,0:T(8,128)(2,1)}, bf16[96,96,128]{2,1,0:T(8,128)(2,1)}) custom-call(s32[2]{0:T(128)} %pad_add_fusion.place_ref, bf16[96,256]{1,0:T(8,128)(2,1)} %copy-done.12, bf16[96,256]{1,0:T(8,128)(2,1)} %copy-done.13, bf16[96,256]{1,0:T(8,128)(2,1)} %copy-done.14, bf16[96,256]{1,0:T(8,128)(2,1)} %copy-done.15, ...), custom_call_target="tpu_custom_call" | custom-call | flops 1000 | bytes 1000 | tf_op jit(solution)/shard_map/front/pallas_call | solution.py:193
  53.6 4.6 %project.7.refs_1_ = bf16[16,192,384]{2,1,0:T(8,128)(2,1)} custom-call(f32[192]{0:T(256)} %dynamic_slice.22.live_ref, bf16[96,96,128]{2,1,0:T(8,128)(2,1)} %get-tuple-element.31.normed_ref.refs_0_.refs_4_, f32[1,384]{1,0:T(1,128)} %broadcast_in_dim.7.cols_ref, bf16[256,128]{1,0:T(8,128)(2,1)} %bitcast.66), custom_call_target="tpu_custom_call" | custom-call | flops 1000 | bytes 1000 | tf_op jit(solution)/shard_map/project/pallas_call | solution.py:289
  58.2 4.2 project.6.refs_0_
  62.4 5.7 %all-to-all-start = ((bf16[16,192,384]{2,1,0:T(8,128)(2,1)}), bf16[16,192,384]{2,1,0:T(8,128)(2,1)S(1)}, u32[]{:S(2)}, u32[]{:S(2)}) async-start(bf16[16,192,384]{2,1,0:T(8,128)(2,1)} %get-tuple-element.32), calls=%async_computation | async-start | bytes 4718592 | tf_op jit(solution)/shard_map/all_to_all | solution.py:916
  68.2 15.3 %front.3 = (bf16[96,96,128]{2,1,0:T(8,128)(2,1)}, bf16[96,96,128]{2,1,0:T(8,128)(2,1)}) custom-call(s32[2]{0:T(128)} %pad_add_fusion.place_ref, bf16[96,256]{1,0:T(8,128)(2,1)} %copy-done.12, bf16[96,256]{1,0:T(8,128)(2,1)} %copy-done.13, bf16[96,256]{1,0:T(8,128)(2,1)} %copy-done.14, bf16[96,256]{1,0:T(8,128)(2,1)} %copy-done.15, ...), custom_call_target="tpu_custom_call" | custom-call | flops 1000 | bytes 1000 | tf_op jit(solution)/shard_map/front/pallas_call | solution.py:193
  83.5 4.7 %project.9.refs_1_ = bf16[16,192,384]{2,1,0:T(8,128)(2,1)} custom-call(f32[192]{0:T(256)} %dynamic_slice.22.live_ref, bf16[96,96,128]{2,1,0:T(8,128)(2,1)} %get-tuple-element.34.normed_ref.refs_1_.refs_5_, f32[1,384]{1,0:T(1,128)} %broadcast_in_dim.7.cols_ref, bf16[256,128]{1,0:T(8,128)(2,1)} %bitcast.67), custom_call_target="tpu_custom_call" | custom-call | flops 1000 | bytes 1000 | tf_op jit(solution)/shard_map/project/pallas_call | solution.py:289
  88.2 4.2 project.8.refs_0_
  92.4 4.2 project.10.refs_3_.refs_0_
  96.6 26.8 %collective-permute-done.11.refs_4_.refs_2_ = bf16[16,96,384]{2,1,0:T(8,128)(2,1)} collective-permute-done((bf16[16,96,384]{2,1,0:T(8,128)(2,1)S(1)}, bf16[16,96,384]{2,1,0:T(8,128)(2,1)}, u32[]{:S(2)}, u32[]{:S(2)}) %collective-permute-start.11) | collective-permute-done | bytes 1179680 | tf_op jit(solution)/shard_map/ppermute | solution.py:1008
  124.7 4.1 all-to-all-start.1
  128.8 3.5 collective-permute-start.12
  142.4 4.2 project.11.refs_4_.refs_1_
  146.6 9.6 %logit.1.logit_ref = f32[192,8,96]{2,1,0:T(8,128)} custom-call(f32[192]{0:T(256)} %dynamic_slice.22.live_ref, bf16[96,96,128]{2,1,0:T(8,128)(2,1)} %get-tuple-element.31.normed_ref.refs_0_.refs_4_, bf16[96,96,128]{2,1,0:T(8,128)(2,1)} %get-tuple-element.34.normed_ref.refs_1_.refs_5_, bf16[8,128]{1,0:T(8,128)(2,1)} %bitcast.87, ...), custom_call_target="tpu_custom_call" | custom-call | flops 1000 | bytes 1000 | tf_op jit(solution)/shard_map/logit/pallas_call | solution.py:334
  156.2 4.2 merge.2.refs_3_.refs_1_
  160.4 4.2 partial.1
  164.6 19.7 %all-to-all-done.1.refs_1_ = bf16[16,192,384]{2,1,0:T(8,128)(2,1)S(1)} async-done(((bf16[16,192,384]{2,1,0:T(8,128)(2,1)}), bf16[16,192,384]{2,1,0:T(8,128)(2,1)S(1)}, u32[]{:S(2)}, u32[]{:S(2)}) %all-to-all-start.1) | async-done | bytes 2359328 | tf_op jit(solution)/shard_map/all_to_all | solution.py:916
  185.7 9.4 %assemble_half.1 = (bf16[4,768,384]{2,1,0:T(8,128)(2,1)}, bf16[4,384,384]{2,1,0:T(8,128)(2,1)}, bf16[4,768,384]{2,1,0:T(8,128)(2,1)}) custom-call(s32[1]{0:T(128)} %bitcast.half_ref, bf16[16,192,384]{2,1,0:T(8,128)(2,1)} %copy-done, bf16[16,192,384]{2,1,0:T(8,128)(2,1)} %copy-done.2, f32[8,104,128]{2,1,0:T(8,128)} %get-tuple-element.38.refs_2_, ...), custom_call_target="tpu_custom_call" | custom-call | flops 1000 | bytes 1000 | tf_op jit(solution)/shard_map/assemble_half/pallas_call | solution.py:562
  197.5 4.7 %all-to-all-start.2 = ((bf16[16,384,384]{2,1,0:T(8,128)(2,1)}), bf16[16,384,384]{2,1,0:T(8,128)(2,1)}, u32[]{:S(2)}, u32[]{:S(2)}) async-start(bf16[16,384,384]{2,1,0:T(8,128)(2,1)} %get-tuple-element.48), calls=%async_computation.2 | async-start | bytes 9437184 | tf_op jit(solution)/shard_map/all_to_all | solution.py:916
  206.1 35.1 %collective-permute-done.13.refs_1_ = f32[8,104,128]{2,1,0:T(8,128)S(1)} collective-permute-done((f32[8,104,128]{2,1,0:T(8,128)S(1)}, f32[8,104,128]{2,1,0:T(8,128)S(1)}, u32[]{:S(2)}, u32[]{:S(2)}) %collective-permute-start.13) | collective-permute-done | bytes 426016 | tf_op jit(solution)/shard_map/ppermute | solution.py:962
  241.2 9.7 %collective-permute-done.15.refs_3_ = f32[8,104,128]{2,1,0:T(8,128)S(1)} collective-permute-done((f32[8,104,128]{2,1,0:T(8,128)S(1)}, f32[8,104,128]{2,1,0:T(8,128)S(1)}, u32[]{:S(2)}, u32[]{:S(2)}) %collective-permute-start.15) | collective-permute-done | bytes 426016 | tf_op jit(solution)/shard_map/ppermute | solution.py:962
  250.9 60.3 %collective-permute-done.16.recv_ref = bf16[4,768,384]{2,1,0:T(8,128)(2,1)} collective-permute-done((bf16[4,768,384]{2,1,0:T(8,128)(2,1)}, bf16[4,768,384]{2,1,0:T(8,128)(2,1)}, u32[]{:S(2)}, u32[]{:S(2)}) %collective-permute-start.16) | collective-permute-done | bytes 2359328 | tf_op jit(solution)/shard_map/ppermute | solution.py:1021
  311.2 6.8 %combine.1.refs_0_ = bf16[16,192,384]{2,1,0:T(8,128)(2,1)} custom-call(bf16[4,768,384]{2,1,0:T(8,128)(2,1)} %get-tuple-element.49.left_ref, bf16[4,384,384]{2,1,0:T(8,128)(2,1)} %get-tuple-element.50.own_ref, bf16[4,768,384]{2,1,0:T(8,128)(2,1)} %collective-permute-done.16.recv_ref, bf16[16,384,384]{2,1,0:T(8,128)(2,1)} %all-to-all-done.2.refs_0_.recv_ref, ...), custom_call_target="tpu_custom_call" | custom-call | flops 1000 | bytes 1000 | tf_op jit(solution)/shard_map/combine/pallas_call | solution.py:629
  318.0 4.1 all-to-all-start.3
  322.1 8.8 %assemble.1 = (bf16[2,16,48,768]{3,2,1,0:T(8,128)(2,1)}, bf16[2,4,1,192,768]{4,3,2,1,0:T(8,128)(2,1)}) custom-call(bf16[16,384,384]{2,1,0:T(8,128)(2,1)} %all-to-all-done.2.refs_0_.recv_ref, bf16[16,192,384]{2,1,0:T(8,128)(2,1)} %combine.1.refs_0_), custom_call_target="tpu_custom_call" | custom-call | flops 1000 | bytes 1000 | tf_op jit(solution)/shard_map/assemble/pallas_call | solution.py:400
  330.9 7.0 %multiply.13.refs_4_ = bf16[32,96,384]{2,1,0:T(8,128)(2,1)} custom-call(bf16[2,16,48,768]{3,2,1,0:T(8,128)(2,1)} %get-tuple-element.52.left_ref, bf16[2,768,768]{2,1,0:T(8,128)(2,1)} %bitcast.61), custom_call_target="tpu_custom_call" | custom-call | flops 1000 | bytes 1000 | tf_op jit(solution)/shard_map/multiply/pallas_call | solution.py:465
  337.9 14.7 %all-to-all-done.3.refs_0_ = bf16[16,192,384]{2,1,0:T(8,128)(2,1)S(1)} async-done(((bf16[16,192,384]{2,1,0:T(8,128)(2,1)}), bf16[16,192,384]{2,1,0:T(8,128)(2,1)S(1)}, u32[]{:S(2)}, u32[]{:S(2)}) %all-to-all-start.3) | async-done | bytes 2359328 | tf_op jit(solution)/shard_map/all_to_all | solution.py:916
  354.0 6.5 %all-to-all-start.4 = ((bf16[32,96,384]{2,1,0:T(8,128)(2,1)}), bf16[32,96,384]{2,1,0:T(8,128)(2,1)}, u32[]{:S(2)}, u32[]{:S(2)}) async-start(bf16[32,96,384]{2,1,0:T(8,128)(2,1)} %multiply.13.refs_4_), calls=%async_computation.4 | async-start | bytes 4718592 | tf_op jit(solution)/shard_map/all_to_all | solution.py:916
  367.2 4.7 %average.1 = bf16[96,256]{1,0:T(8,128)(2,1)} custom-call(f32[8,104,128]{2,1,0:T(8,128)} %get-tuple-element.54.refs_0_, f32[8,104,128]{2,1,0:T(8,128)} %get-tuple-element.55.refs_1_, f32[8,104,128]{2,1,0:T(8,128)} %get-tuple-element.56.refs_2_, f32[8,104,128]{2,1,0:T(8,128)} %get-tuple-element.57.refs_3_, f32[8,96,128]{2,1,0:T(8,128)} %copy.137.refs_4_, ...), custom_call_target="tpu_custom_call" | custom-call | flops 1000 | bytes 1000 | tf_op jit(solution)/shard_map/average/pallas_call | solution.py:751
  373.5 42.8 %all-to-all-done.4.refs_1_ = bf16[32,96,384]{2,1,0:T(8,128)(2,1)} async-done(((bf16[32,96,384]{2,1,0:T(8,128)(2,1)}), bf16[32,96,384]{2,1,0:T(8,128)(2,1)}, u32[]{:S(2)}, u32[]{:S(2)}) %all-to-all-start.4) | async-done | bytes 2359328 | tf_op jit(solution)/shard_map/all_to_all | solution.py:916
  416.3 13.0 %finish.1 = bf16[192,96,128]{2,1,0:T(8,128)(2,1)} custom-call(bf16[16,192,384]{2,1,0:T(8,128)(2,1)} %copy-done.1, bf16[32,96,384]{2,1,0:T(8,128)(2,1)} %all-to-all-done.4.refs_1_, bf16[96,96,128]{2,1,0:T(8,128)(2,1)} %get-tuple-element.58.refs_2_, bf16[96,96,128]{2,1,0:T(8,128)(2,1)} %get-tuple-element.59.refs_3_, ...), custom_call_target="tpu_custom_call" | custom-call | flops 1000 | bytes 1000 | tf_op jit(solution)/shard_map/finish/pallas_call | solution.py:816
  (168 shorter events, 59.3 us)
Async XLA Ops:
  0.6 18.1 %slice-start = ((bf16[64,576]{1,0:T(8,128)(2,1)}), bf16[64,32]{1,0:T(8,128)(2,1)S(1)}, s32[]{:S(2)}) async-start(bf16[64,576]{1,0:T(8,128)(2,1)} %param.14), calls=%async_computation.5 | async-start | bytes 32768 | tf_op jit(solution)/shard_map/slice | solution.py:887
  0.7 32.9 %copy-start.26 = (bf16[1024,128]{1,0:T(8,128)(2,1)S(1)}, bf16[1024,128]{1,0:T(8,128)(2,1)}, u32[]{:S(2)}) copy-start(bf16[1024,128]{1,0:T(8,128)(2,1)} %param.15) | copy-start | bytes 786436
  5.5 48.1 %copy-start.10 = (bf16[4,96,64]{1,2,0:T(8,128)(2,1)}, bf16[4,96,64]{1,2,0:T(8,128)(2,1)S(1)}, u32[]{:S(2)}) copy-start(bf16[4,96,64]{1,2,0:T(8,128)(2,1)S(1)} %fusion.7) | copy-start | bytes 147460
  6.4 30.7 %copy-start.9 = (bf16[4,96,32]{2,1,0:T(8,128)(2,1)}, bf16[4,96,32]{2,1,0:T(8,128)(2,1)S(1)}, u32[]{:S(2)}) copy-start(bf16[4,96,32]{2,1,0:T(8,128)(2,1)S(1)} %fusion.3.refs_8_) | copy-start | bytes 73732
  6.5 13.3 %collective-permute-start.10 = (bf16[4,96,32]{2,1,0:T(8,128)(2,1)S(1)}, bf16[4,96,32]{2,1,0:T(8,128)(2,1)S(1)}, u32[]{:S(2)}, u32[]{:S(2)}) collective-permute-start(bf16[4,96,32]{2,1,0:T(8,128)(2,1)S(1)} %fusion.3.refs_8_), channel_id=1, source_target_pairs={{0,8},{8,16},{16,24},{24,0},{1,9},{9,17},{17,25},{25,1},{2,10},{10... | collective-permute-start | bytes 73736 | tf_op jit(solution)/shard_map/ppermute | solution.py:901
  9.4 12.6 %collective-permute-start.8 = (bf16[4,96,32]{2,1,0:T(8,128)(2,1)S(1)}, bf16[4,96,32]{2,1,0:T(8,128)(2,1)S(1)}, u32[]{:S(2)}, u32[]{:S(2)}) collective-permute-start(bf16[4,96,32]{2,1,0:T(8,128)(2,1)S(1)} %fusion.3.refs_8_), channel_id=1, source_target_pairs={{0,24},{8,0},{16,8},{24,16},{1,25},{9,1},{17,9},{25,17},{2,26},{10... | collective-permute-start | bytes 73736 | tf_op jit(solution)/shard_map/ppermute | solution.py:901
  10.5 14.2 %collective-permute-start.9 = (bf16[4,96,32]{2,1,0:T(8,128)(2,1)S(1)}, bf16[4,96,32]{2,1,0:T(8,128)(2,1)S(1)}, u32[]{:S(2)}, u32[]{:S(2)}) collective-permute-start(bf16[4,96,32]{2,1,0:T(8,128)(2,1)S(1)} %fusion.3.refs_8_), channel_id=1, source_target_pairs={{0,16},{8,24},{16,0},{24,8},{1,17},{9,25},{17,1},{25,9},{2,18},{10... | collective-permute-start | bytes 73736 | tf_op jit(solution)/shard_map/ppermute | solution.py:901
  12.5 12.5 %collective-permute-start = (bf16[96,256]{1,0:T(8,128)(2,1)S(1)}, bf16[96,256]{1,0:T(8,128)(2,1)S(1)}, u32[]{:S(2)}, u32[]{:S(2)}) collective-permute-start(bf16[96,256]{1,0:T(8,128)(2,1)S(1)} %copy.110), channel_id=1, source_target_pairs={{0,0},{1,1},{2,8},{3,9},{4,16},{5,17},{6,24},{7,25},{8,2},{9,3},{1... | collective-permute-start | bytes 147464 | tf_op jit(solution)/shard_map/ppermute | solution.py:897
  13.2 14.7 %collective-permute-start.1 = (bf16[96,256]{1,0:T(8,128)(2,1)S(1)}, bf16[96,256]{1,0:T(8,128)(2,1)S(1)}, u32[]{:S(2)}, u32[]{:S(2)}) collective-permute-start(bf16[96,256]{1,0:T(8,128)(2,1)S(1)} %copy.110), channel_id=1, source_target_pairs={{0,7},{1,0},{2,15},{3,8},{4,23},{5,16},{6,31},{7,24},{8,1},{9,2},{... | collective-permute-start | bytes 147464 | tf_op jit(solution)/shard_map/ppermute | solution.py:897
  19.8 8.3 %collective-permute-start.2 = (bf16[96,256]{1,0:T(8,128)(2,1)S(1)}, bf16[96,256]{1,0:T(8,128)(2,1)S(1)}, u32[]{:S(2)}, u32[]{:S(2)}) collective-permute-start(bf16[96,256]{1,0:T(8,128)(2,1)S(1)} %copy.110), channel_id=1, source_target_pairs={{0,6},{1,7},{2,14},{3,15},{4,22},{5,23},{6,30},{7,31},{8,0},{9,1},... | collective-permute-start | bytes 147464 | tf_op jit(solution)/shard_map/ppermute | solution.py:897
  22.0 15.0 %collective-permute-start.3 = (bf16[96,256]{1,0:T(8,128)(2,1)S(1)}, bf16[96,256]{1,0:T(8,128)(2,1)S(1)}, u32[]{:S(2)}, u32[]{:S(2)}) collective-permute-start(bf16[96,256]{1,0:T(8,128)(2,1)S(1)} %copy.110), channel_id=1, source_target_pairs={{0,5},{1,6},{2,13},{3,14},{4,21},{5,22},{6,29},{7,30},{8,7},{9,0},... | collective-permute-start | bytes 147464 | tf_op jit(solution)/shard_map/ppermute | solution.py:897
  24.7 12.3 %collective-permute-start.4 = (bf16[96,256]{1,0:T(8,128)(2,1)S(1)}, bf16[96,256]{1,0:T(8,128)(2,1)S(1)}, u32[]{:S(2)}, u32[]{:S(2)}) collective-permute-start(bf16[96,256]{1,0:T(8,128)(2,1)S(1)} %copy.110), channel_id=1, source_target_pairs={{0,4},{1,5},{2,12},{3,13},{4,20},{5,21},{6,28},{7,29},{8,6},{9,7},... | collective-permute-start | bytes 147464 | tf_op jit(solution)/shard_map/ppermute | solution.py:897
  25.0 12.0 %collective-permute-start.5 = (bf16[96,256]{1,0:T(8,128)(2,1)S(1)}, bf16[96,256]{1,0:T(8,128)(2,1)S(1)}, u32[]{:S(2)}, u32[]{:S(2)}) collective-permute-start(bf16[96,256]{1,0:T(8,128)(2,1)S(1)} %copy.110), channel_id=1, source_target_pairs={{0,3},{1,4},{2,11},{3,12},{4,19},{5,20},{6,27},{7,28},{8,5},{9,6},... | collective-permute-start | bytes 147464 | tf_op jit(solution)/shard_map/ppermute | solution.py:897
  27.8 9.2 %collective-permute-start.6 = (bf16[96,256]{1,0:T(8,128)(2,1)S(1)}, bf16[96,256]{1,0:T(8,128)(2,1)S(1)}, u32[]{:S(2)}, u32[]{:S(2)}) collective-permute-start(bf16[96,256]{1,0:T(8,128)(2,1)S(1)} %copy.110), channel_id=1, source_target_pairs={{0,2},{1,3},{2,10},{3,11},{4,18},{5,19},{6,26},{7,27},{8,4},{9,5},... | collective-permute-start | bytes 147464 | tf_op jit(solution)/shard_map/ppermute | solution.py:897
  28.1 9.0 %collective-permute-start.7 = (bf16[96,256]{1,0:T(8,128)(2,1)S(1)}, bf16[96,256]{1,0:T(8,128)(2,1)S(1)}, u32[]{:S(2)}, u32[]{:S(2)}) collective-permute-start(bf16[96,256]{1,0:T(8,128)(2,1)S(1)} %copy.110), channel_id=1, source_target_pairs={{0,1},{1,2},{2,9},{3,10},{4,17},{5,18},{6,25},{7,26},{8,3},{9,4},{... | collective-permute-start | bytes 147464 | tf_op jit(solution)/shard_map/ppermute | solution.py:897
  62.4 60.9 %all-to-all-start = ((bf16[16,192,384]{2,1,0:T(8,128)(2,1)}), bf16[16,192,384]{2,1,0:T(8,128)(2,1)S(1)}, u32[]{:S(2)}, u32[]{:S(2)}) async-start(bf16[16,192,384]{2,1,0:T(8,128)(2,1)} %get-tuple-element.32), calls=%async_computation | async-start | bytes 4718592 | tf_op jit(solution)/shard_map/all_to_all | solution.py:916
  68.1 55.2 %collective-permute-start.11 = (bf16[16,96,384]{2,1,0:T(8,128)(2,1)S(1)}, bf16[16,96,384]{2,1,0:T(8,128)(2,1)}, u32[]{:S(2)}, u32[]{:S(2)}) collective-permute-start(bf16[16,96,384]{2,1,0:T(8,128)(2,1)S(1)} %copy-done.4), channel_id=1, source_target_pairs={{0,4},{4,0},{1,5},{5,1},{2,6},{6,2},{3,7},{7,3},{8,12},{12,8},{9,1... | collective-permute-start | bytes 3538952 | tf_op jit(solution)/shard_map/ppermute | solution.py:1008
  124.7 59.5 %all-to-all-start.1 = ((bf16[16,192,384]{2,1,0:T(8,128)(2,1)}), bf16[16,192,384]{2,1,0:T(8,128)(2,1)S(1)}, u32[]{:S(2)}, u32[]{:S(2)}) async-start(bf16[16,192,384]{2,1,0:T(8,128)(2,1)} %get-tuple-element.36), calls=%async_computation.1 | async-start | bytes 4718592 | tf_op jit(solution)/shard_map/all_to_all | solution.py:916
  128.8 66.3 %collective-permute-start.12 = (bf16[16,96,384]{2,1,0:T(8,128)(2,1)S(1)}, bf16[16,96,384]{2,1,0:T(8,128)(2,1)}, u32[]{:S(2)}, u32[]{:S(2)}) collective-permute-start(bf16[16,96,384]{2,1,0:T(8,128)(2,1)S(1)} %copy-done.3), channel_id=1, source_target_pairs={{0,4},{4,0},{1,5},{5,1},{2,6},{6,2},{3,7},{7,3},{8,12},{12,8},{9,1... | collective-permute-start | bytes 3538952 | tf_op jit(solution)/shard_map/ppermute | solution.py:1008
  197.5 113.7 %all-to-all-start.2 = ((bf16[16,384,384]{2,1,0:T(8,128)(2,1)}), bf16[16,384,384]{2,1,0:T(8,128)(2,1)}, u32[]{:S(2)}, u32[]{:S(2)}) async-start(bf16[16,384,384]{2,1,0:T(8,128)(2,1)} %get-tuple-element.48), calls=%async_computation.2 | async-start | bytes 9437184 | tf_op jit(solution)/shard_map/all_to_all | solution.py:916
  202.2 108.9 %collective-permute-start.16 = (bf16[4,768,384]{2,1,0:T(8,128)(2,1)}, bf16[4,768,384]{2,1,0:T(8,128)(2,1)}, u32[]{:S(2)}, u32[]{:S(2)}) collective-permute-start(bf16[4,768,384]{2,1,0:T(8,128)(2,1)} %get-tuple-element.51), channel_id=1, source_target_pairs={{0,4},{4,0},{1,5},{5,1},{2,6},{6,2},{3,7},{7,3},{8,12},{12,8},{9,1... | collective-permute-start | bytes 7077896 | tf_op jit(solution)/shard_map/ppermute | solution.py:1021
  202.3 38.9 %collective-permute-start.13 = (f32[8,104,128]{2,1,0:T(8,128)S(1)}, f32[8,104,128]{2,1,0:T(8,128)S(1)}, u32[]{:S(2)}, u32[]{:S(2)}) collective-permute-start(f32[8,104,128]{2,1,0:T(8,128)S(1)} %copy-done.20), channel_id=1, source_target_pairs={{0,24},{8,0},{16,8},{24,16},{1,25},{9,1},{17,9},{25,17},{2,26},{10... | collective-permute-start | bytes 1277960 | tf_op jit(solution)/shard_map/ppermute | solution.py:962
  205.0 36.2 %collective-permute-start.14 = (f32[8,104,128]{2,1,0:T(8,128)S(1)}, f32[8,104,128]{2,1,0:T(8,128)S(1)}, u32[]{:S(2)}, u32[]{:S(2)}) collective-permute-start(f32[8,104,128]{2,1,0:T(8,128)S(1)} %copy-done.21), channel_id=1, source_target_pairs={{0,16},{8,24},{16,0},{24,8},{1,17},{9,25},{17,1},{25,9},{2,18},{10... | collective-permute-start | bytes 1277960 | tf_op jit(solution)/shard_map/ppermute | solution.py:962
  205.5 45.4 %collective-permute-start.15 = (f32[8,104,128]{2,1,0:T(8,128)S(1)}, f32[8,104,128]{2,1,0:T(8,128)S(1)}, u32[]{:S(2)}, u32[]{:S(2)}) collective-permute-start(f32[8,104,128]{2,1,0:T(8,128)S(1)} %copy-done.22), channel_id=1, source_target_pairs={{0,8},{8,16},{16,24},{24,0},{1,9},{9,17},{17,25},{25,1},{2,10},{10... | collective-permute-start | bytes 1277960 | tf_op jit(solution)/shard_map/ppermute | solution.py:962
  241.2 70.0 %copy-start.5 = (f32[8,104,128]{2,1,0:T(8,128)}, f32[8,104,128]{2,1,0:T(8,128)S(1)}, u32[]{:S(2)}) copy-start(f32[8,104,128]{2,1,0:T(8,128)S(1)} %collective-permute-done.13.refs_1_) | copy-start | bytes 1277956
  241.2 70.0 %copy-start.6 = (f32[8,104,128]{2,1,0:T(8,128)}, f32[8,104,128]{2,1,0:T(8,128)S(1)}, u32[]{:S(2)}) copy-start(f32[8,104,128]{2,1,0:T(8,128)S(1)} %collective-permute-done.14.refs_2_) | copy-start | bytes 1277956
  250.9 60.3 %copy-start.7 = (f32[8,104,128]{2,1,0:T(8,128)}, f32[8,104,128]{2,1,0:T(8,128)S(1)}, u32[]{:S(2)}) copy-start(f32[8,104,128]{2,1,0:T(8,128)S(1)} %collective-permute-done.15.refs_3_) | copy-start | bytes 1277956
  318.0 34.6 %all-to-all-start.3 = ((bf16[16,192,384]{2,1,0:T(8,128)(2,1)}), bf16[16,192,384]{2,1,0:T(8,128)(2,1)S(1)}, u32[]{:S(2)}, u32[]{:S(2)}) async-start(bf16[16,192,384]{2,1,0:T(8,128)(2,1)} %combine.1.refs_0_), calls=%async_computation.3 | async-start | bytes 4718592 | tf_op jit(solution)/shard_map/all_to_all | solution.py:916
  337.9 24.0 %copy-start.30 = (bf16[128,128]{1,0:T(8,128)(2,1)S(1)}, bf16[128,128]{1,0:T(8,128)(2,1)}, u32[]{:S(2)}) copy-start(bf16[128,128]{1,0:T(8,128)(2,1)} %param.19) | copy-start | bytes 98308
  337.9 24.1 %copy-start.11 = (bf16[4,96,64]{1,2,0:T(8,128)(2,1)S(1)}, bf16[4,96,64]{1,2,0:T(8,128)(2,1)}, u32[]{:S(2)}) copy-start(bf16[4,96,64]{1,2,0:T(8,128)(2,1)} %copy-done.10) | copy-start | bytes 147460
  337.9 24.1 %copy-start.28 = (bf16[64,576]{1,0:T(8,128)(2,1)S(1)}, bf16[64,576]{1,0:T(8,128)(2,1)}, u32[]{:S(2)}) copy-start(bf16[64,576]{1,0:T(8,128)(2,1)} %param.14) | copy-start | bytes 221188
  354.0 62.3 %all-to-all-start.4 = ((bf16[32,96,384]{2,1,0:T(8,128)(2,1)}), bf16[32,96,384]{2,1,0:T(8,128)(2,1)}, u32[]{:S(2)}, u32[]{:S(2)}) async-start(bf16[32,96,384]{2,1,0:T(8,128)(2,1)} %multiply.13.refs_4_), calls=%async_computation.4 | async-start | bytes 4718592 | tf_op jit(solution)/shard_map/all_to_all | solution.py:916
  (26 other events, 150.1 us)

commit v11 on v10

--- a/solution.py
+++ b/solution.py
@@ -182,27 +182,27 @@
 
 
 def front(
-    chunk, chunks, place, lefts, rights, present_rows, coupling, w_tensor, present_cols, w_left, after
+    first_row, count, place, lefts, rights, present_rows, coupling, w_tensor, present_cols, w_left, after
 ):
     rows, cols, wide = coupling.shape
     seqs, width = present_rows.shape[0], w_left.shape[2]
     present_sides = present_rows.T
     block = 8
-    steps = rows // block // chunks
+    steps, offset = count // block, first_row // block
     tile = pl.BlockSpec((block, cols, wide), lambda i: (i, 0, 0))
     return pl.pallas_call(
         functools.partial(
             front_kernel,
             row_count=len(rights),
             col_count=len(lefts),
-            first_block=chunk * steps,
+            first_block=offset,
         ),
         grid=(steps,),
         in_specs=[pl.BlockSpec(memory_space=pltpu.SMEM)]
         + [whole(part.shape) for part in lefts + rights]
         + [
             whole(present_rows.shape),
-            pl.BlockSpec((block, cols, wide), lambda i: (i + chunk * steps, 0, 0)),
+            pl.BlockSpec((block, cols, wide), lambda i: (i + offset, 0, 0)),
             whole(w_tensor.shape),
             whole(present_cols.shape),
             whole(w_left.shape),
@@ -210,7 +210,7 @@
         ]
         + anywhere(after),
         out_specs=[tile, tile],
-        out_shape=[jax.ShapeDtypeStruct((rows // chunks, cols, wide), BF16)] * 2,
+        out_shape=[jax.ShapeDtypeStruct((count, cols, wide), BF16)] * 2,
         scratch_shapes=[
             pltpu.VMEM((rows * seqs, LANES), F32),
             pltpu.VMEM((cols, width * seqs), BF16),
@@ -304,10 +304,24 @@
     )(live_rows, normed, live_cols, weight)
 
 
-def logit_kernel(live_ref, *refs, chunks):
-    normeds, weight_ref, out_ref = refs[:chunks], refs[chunks], refs[-1]
+def at_chunk(steps, body, *groups):
+    start = 0
+    for chunk, count in enumerate(steps):
+        here = (pl.program_id(0) >= start) & (pl.program_id(0) < start + count)
+        pl.when(here)(functools.partial(body, *[group[chunk] for group in groups]))
+        start += count
+
+
+def chunk_tiles(shape, steps):
+    def tile(start, count):
+        return pl.BlockSpec(shape, lambda i: (jnp.clip(i - start, 0, count - 1), 0, 0))
+
+    return [tile(sum(steps[:chunk]), count) for chunk, count in enumerate(steps)]
+
+
+def logit_kernel(live_ref, *refs, steps):
+    normeds, weight_ref, out_ref = refs[: len(steps)], refs[len(steps)], refs[-1]
     block = out_ref.shape[0]
-    steps = pl.num_programs(0) // chunks
 
     def rows(normed_ref):
         for i in range(block):
@@ -316,30 +330,23 @@
                 weight_ref[...], normed_ref[i], NT, preferred_element_type=F32
             ) + MASK_PENALTY * (live - 1.0)
 
-    for chunk in range(chunks):
-        pl.when(pl.program_id(0) // steps == chunk)(functools.partial(rows, normeds[chunk]))
-
-
-def chunk_tiles(shape, chunks, steps):
-    def tile(chunk):
-        return pl.BlockSpec(shape, lambda i: (jnp.clip(i - chunk * steps, 0, steps - 1), 0, 0))
-
-    return [tile(chunk) for chunk in range(chunks)]
+    at_chunk(steps, rows, normeds)
 
 
 def logit(live_rows, normeds, weight, after):
-    rows, cols, wide = normeds[0].shape
-    block, chunks = 16, len(normeds)
+    _, cols, wide = normeds[0].shape
+    block = 16
+    steps = [normed.shape[0] // block for normed in normeds]
     heads = weight.shape[0]
     return pl.pallas_call(
-        functools.partial(logit_kernel, chunks=chunks),
-        grid=(rows // block * chunks,),
+        functools.partial(logit_kernel, steps=steps),
+        grid=(sum(steps),),
         in_specs=[pl.BlockSpec(memory_space=pltpu.SMEM)]
-        + chunk_tiles((block, cols, wide), chunks, rows // block)
+        + chunk_tiles((block, cols, wide), steps)
         + [whole(weight.shape)]
         + anywhere(after),
         out_specs=pl.BlockSpec((block, heads, cols), lambda i: (i, 0, 0)),
-        out_shape=jax.ShapeDtypeStruct((rows * chunks, heads, cols), F32),
+        out_shape=jax.ShapeDtypeStruct((sum(steps) * block, heads, cols), F32),
         compiler_params=params(),
         cost_estimate=LIGHT,
         name="logit",
@@ -644,22 +651,28 @@
     )(left, own, received, *after)
 
 
-def merge_kernel(*refs, parts):
-    for index, piece in enumerate(refs[:parts]):
-
-        @pl.when(pl.program_id(0) == index)
-        def _():
-            refs[-1][...] = piece[...]
-
-
-def merge(pieces, first, count, into):
-    sources, height, lanes = pieces[0].shape
-    return pl.pallas_call(
-        functools.partial(merge_kernel, parts=len(pieces)),
-        grid=(len(pieces),),
-        in_specs=[whole(piece.shape) for piece in pieces] + anywhere(into),
-        out_specs=pl.BlockSpec((sources, height, lanes), lambda i: (0, i + first, 0)),
-        out_shape=jax.ShapeDtypeStruct((sources, height * count, lanes), BF16),
+def merge_kernel(*refs, steps):
+    def put(piece):
+        refs[-1][...] = piece[...]
+
+    at_chunk(steps, put, refs[: len(steps)])
+
+
+def merge(pieces, first, height, unit, into):
+    sources, _, lanes = pieces[0].shape
+    steps = [piece.shape[1] // unit for piece in pieces]
+
+    def block(start, count):
+        return pl.BlockSpec(
+            (sources, unit, lanes), lambda i: (0, jnp.clip(i - start, 0, count - 1), 0)
+        )
+
+    return pl.pallas_call(
+        functools.partial(merge_kernel, steps=steps),
+        grid=(sum(steps),),
+        in_specs=[block(sum(steps[:at]), count) for at, count in enumerate(steps)] + anywhere(into),
+        out_specs=pl.BlockSpec((sources, unit, lanes), lambda i: (0, i + first // unit, 0)),
+        out_shape=jax.ShapeDtypeStruct((sources, height, lanes), BF16),
         input_output_aliases={len(pieces): 0} if into else {},
         compiler_params=params(),
         cost_estimate=LIGHT,
@@ -760,7 +773,8 @@
     )(*operands)
 
 
-def finish_kernel(*refs, parts, chunks):
+def finish_kernel(*refs, parts, steps):
+    chunks = len(steps)
     products = refs[:parts]
     mids = refs[parts : parts + chunks]
     normeds = refs[parts + chunks : parts + 2 * chunks]
@@ -796,25 +810,19 @@
                 gate = sigmoid(jnp.dot(normed_ref[i], gate_ref[...], preferred_element_type=F32))
                 out_ref[i] = (mid_ref[i].astype(F32) + gate * value).astype(BF16)
 
-    steps = pl.num_programs(0) // chunks
-    for chunk in range(chunks):
-        pl.when(pl.program_id(0) // steps == chunk)(
-            functools.partial(rows, mids[chunk], normeds[chunk])
-        )
+    at_chunk(steps, rows, mids, normeds)
 
 
 def finish(products, mids, normeds, w_gate, w_final):
-    rows, cols, wide = mids[0].shape
-    chunks = len(mids)
+    _, cols, wide = mids[0].shape
     lanes = products[0].shape[2]
-    total = rows * chunks // QUAD
+    total = sum(mid.shape[0] for mid in mids) // QUAD
     heights = [part.shape[1] // total for part in products]
     quads = max(8, 16 // min(heights))
-    steps = rows // QUAD // quads
-
-    tiles = chunk_tiles((quads * QUAD, cols, wide), chunks, steps)
-    return pl.pallas_call(
-        functools.partial(finish_kernel, parts=len(products), chunks=chunks),
+    steps = [mid.shape[0] // QUAD // quads for mid in mids]
+    tiles = chunk_tiles((quads * QUAD, cols, wide), steps)
+    return pl.pallas_call(
+        functools.partial(finish_kernel, parts=len(products), steps=steps),
         grid=(total // quads,),
         in_specs=[
             pl.BlockSpec((part.shape[0], quads * each, lanes), lambda i: (0, i, 0))
@@ -823,7 +831,7 @@
         + tiles * 2
         + [whole(w_gate.shape), whole(w_final.shape)],
         out_specs=pl.BlockSpec((quads * QUAD, cols, wide), lambda i: (i, 0, 0)),
-        out_shape=jax.ShapeDtypeStruct((rows * chunks, cols, wide), BF16),
+        out_shape=jax.ShapeDtypeStruct((total * QUAD, cols, wide), BF16),
         scratch_shapes=[
             pltpu.VMEM((lanes // LANES, part.shape[0] * quads * each, LANES), F32)
             for part, each in zip(products, heights)
@@ -915,10 +923,10 @@
     def exchange(block, axes):
         return lax.all_to_all(block, axes, split_axis=0, concat_axis=0, tiled=True)
 
-    def front_rows(chunk, chunks, after):
+    def front_rows(first_row, count, after):
         return front(
-            chunk,
-            chunks,
+            first_row,
+            count,
             place,
             lefts,
             rights,
@@ -930,8 +938,7 @@
             after,
         )
 
-    def project_rows(chunk, normed, weight, dests):
-        first_row = chunk * normed.shape[0]
+    def project_rows(first_row, normed, weight, dests):
         return project(first_row, live_rows, normed, live_packed, weight, dests)
 
     place = jnp.stack([row_index, col_index]).astype(jnp.int32)
@@ -971,8 +978,9 @@
         sent, sides = (), ()
         weight = side_weights(w_kinds.reshape(2, 2, devices, -1, wide))
         for chunk in range(row_chunks):
-            mid, normed = front_rows(chunk, row_chunks, sent)
-            block = project_rows(chunk, normed, weight, devices)
+            first_row = chunk * (rows // row_chunks)
+            mid, normed = front_rows(first_row, rows // row_chunks, sent)
+            block = project_rows(first_row, normed, weight, devices)
             sent = (block,)
             sides = assemble(chunk, row_chunks, 1, exchange(block, AXES), sides, (), *shape_of)
             mids.append(mid)
@@ -987,7 +995,7 @@
         orders = [(0, CTRI, devices)]
     else:
         cut = CTRI // 2
-        row_chunks = 2
+        row_chunks = [rows // 3, rows - rows // 3]
         w_half = side_weights(w_kinds[:, :, :cut].reshape(2, 2, group, -1, wide))
         w_both = w_kinds[:, :, cut:].reshape(2, 2, row_count, 2, pos_count, -1, wide)
 
@@ -998,26 +1006,29 @@
         w_own, w_other = half_weights(half), half_weights(1 - half)
         swap = [(0, 1), (1, 0)]
         received, crossed, kept, ahead = [], [], [], ()
-        for chunk in range(row_chunks):
-            mid, normed = front_rows(chunk, row_chunks, ahead)
+        for chunk, count in enumerate(row_chunks):
+            first_row = sum(row_chunks[:chunk])
+            mid, normed = front_rows(first_row, count, ahead)
             mids.append(mid)
             normeds.append(normed)
-            to_half = project_rows(chunk, normed, w_half, group)
-            to_other = project_rows(chunk, normed, w_other, group)
+            to_half = project_rows(first_row, normed, w_half, group)
+            to_other = project_rows(first_row, normed, w_other, group)
             to_other, to_half, w_own = fence([to_other, to_half, w_own], received + crossed)
             crossed.append(lax.ppermute(to_other, "half", swap))
             received.append(exchange(to_half, GROUP))
             ahead = (w_own,)
-            kept.append(project_rows(chunk, normed, w_own, group))
+            kept.append(project_rows(first_row, normed, w_own, group))
         half_scalar = half.astype(jnp.int32).reshape(1)
         logits = logit(live_rows, normeds, w_logit, tuple(kept))
         parts = partial_average(place, logits, lefts, w_value)
-        merged = merge(kept + crossed[:-1], 0, 2 * row_chunks, ())
+        height = 2 * sum(part.shape[1] for part in kept)
+        unit, last = kept[0].shape[1], height - kept[-1].shape[1]
+        merged = merge(kept + crossed[:-1], 0, height, unit, ())
         left, own, theirs = assemble_half(
             half_scalar, received, (parts[0], merged), *half_shape
         )
-        merged = merge(crossed[-1:], 2 * row_chunks - 1, 2 * row_chunks, (merged,))
-        theirs, merged, *parts = fence([theirs, merged, *parts], ())
+        merged = merge(crossed[-1:], last, height, unit, (merged,))
+        theirs, *parts = fence([theirs, *parts], ())
         partial = lax.ppermute(theirs, "half", swap)
         both = exchange(merged, GROUP)
         parts = gather_parts(parts)

time: 432 us -> 441 us (1.021)
  waiting for transfers between devices: 209 us -> 223 us
    ppermute x2, waiting for transfers between devices: 26.8 us -> 60.4 us  [on_device(): crossed.append(lax.ppermute(to_other, 'half', swap))]
    all_to_all x5, waiting for transfers between devices: 77.2 us -> 58.9 us  [exchange(): return lax.all_to_all(block, axes, split_axis=0, concat_axis=0, tiled=True)]
    ppermute x3, waiting for transfers between devices: 44.8 us -> 38.8 us  [gather_parts(): gathered.append(lax.ppermute(parts[t], 'row', pairs))]
    unnamed x72 -> x63, local copies, waits for them, and re-layouts: 8.15 us -> 10.9 us
  transfers between devices with their start and end apart: 22 -> 22, of which waited for: 7 -> 11; matrix products, arithmetic and copies ran while one was open for 6% -> 6% of each run, Pallas kernels for 19% -> 20%
where the time goes in v11:
time: 441 us; the launch traced here: 439 us
  waiting for transfers between devices  223 us (51%)
  Pallas kernels  125 us (28%)
  starting transfers between devices  54.5 us (12%)
  local copies, waits for them, and re-layouts  25.9 us (6%)
  other arithmetic  7.86 us (2%)
    ppermute x1, waiting for transfers between devices, on_device(): partial = lax.ppermute(theirs, 'half', swap)  60.6 us
    ppermute x2, waiting for transfers between devices, on_device(): crossed.append(lax.ppermute(to_other, 'half', swap))  60.4 us
    all_to_all x5, waiting for transfers between devices, exchange(): return lax.all_to_all(block, axes, split_axis=0, concat_axis=0, tiled=True)  58.9 us
    ppermute x3, waiting for transfers between devices, gather_parts(): gathered.append(lax.ppermute(parts[t], 'row', pairs))  38.8 us
    pallas_call x2, Pallas kernels, front(): pl.pallas_call(functools.partial(front_kernel, row_count=len(rights), col...  30.6 us
    all_to_all x5, starting transfers between devices, exchange(): return lax.all_to_all(block, axes, split_axis=0, concat_axis=0, tiled=True)  26.9 us
    pallas_call x6, Pallas kernels, project(): pl.pallas_call(functools.partial(project_kernel, first_row=first_row), gr...  24.1 us
    ppermute x8, starting transfers between devices, on_device(): lefts.append(lax.ppermute(own_rows, AXES, pairs))  14.8 us
  transfers between devices with their start and end apart: 22, of which 11 were waited for; matrix products, arithmetic and copies ran while one was open for 6% of the time, Pallas kernels for 20%

profile of v11, /device:TPU:0, one launch (start us, length us, event | category | flops | bytes accessed | tf_op | source)
XLA Modules:
  0.0 438.8 jit_solution(9623398048986920420)
XLA Ops:
  4.1 7.6 %collective-permute-start.1 = (bf16[96,256]{1,0:T(8,128)(2,1)S(1)}, bf16[96,256]{1,0:T(8,128)(2,1)S(1)}, u32[]{:S(2)}, u32[]{:S(2)}) collective-permute-start(bf16[96,256]{1,0:T(8,128)(2,1)S(1)} %copy.109), channel_id=1, source_target_pairs={{0,7},{1,0},{2,15},{3,8},{4,23},{5,16},{6,31},{7,24},{8,1},{9,2},{... | collective-permute-start | bytes 147464 | tf_op jit(solution)/shard_map/ppermute | solution.py:905
  24.5 3.4 collective-permute-done.10.refs_11_
  39.4 11.3 %front.2 = (bf16[64,96,128]{2,1,0:T(8,128)(2,1)}, bf16[64,96,128]{2,1,0:T(8,128)(2,1)}) custom-call(s32[2]{0:T(128)} %pad_add_fusion.place_ref, bf16[96,256]{1,0:T(8,128)(2,1)} %copy-done.10, bf16[96,256]{1,0:T(8,128)(2,1)} %copy-done.11, bf16[96,256]{1,0:T(8,128)(2,1)} %copy-done.12, bf16[96,256]{1,0:T(8,128)(2,1)} %copy-done.13, ...), custom_call_target="tpu_custom_call" | custom-call | flops 1000 | bytes 1000 | tf_op jit(solution)/shard_map/front/pallas_call | solution.py:193
  50.6 3.0 project.6.refs_0_
  53.6 3.2 project.7.refs_1_
  56.8 5.9 %all-to-all-start = ((bf16[16,128,384]{2,1,0:T(8,128)(2,1)}), bf16[16,128,384]{2,1,0:T(8,128)(2,1)S(1)}, u32[]{:S(2)}, u32[]{:S(2)}) async-start(bf16[16,128,384]{2,1,0:T(8,128)(2,1)} %get-tuple-element.31), calls=%async_computation | async-start | bytes 3145728 | tf_op jit(solution)/shard_map/all_to_all | solution.py:924
  63.5 3.0 project.10.refs_3_.refs_0_
  66.5 19.3 %front.3 = (bf16[128,96,128]{2,1,0:T(8,128)(2,1)}, bf16[128,96,128]{2,1,0:T(8,128)(2,1)}) custom-call(s32[2]{0:T(128)} %pad_add_fusion.place_ref, bf16[96,256]{1,0:T(8,128)(2,1)} %copy-done.10, bf16[96,256]{1,0:T(8,128)(2,1)} %copy-done.11, bf16[96,256]{1,0:T(8,128)(2,1)} %copy-done.12, bf16[96,256]{1,0:T(8,128)(2,1)} %copy-done.13, ...), custom_call_target="tpu_custom_call" | custom-call | flops 1000 | bytes 1000 | tf_op jit(solution)/shard_map/front/pallas_call | solution.py:193
  85.8 4.9 %project.8.refs_0_ = bf16[16,128,384]{2,1,0:T(8,128)(2,1)} custom-call(f32[192]{0:T(256)} %dynamic_slice.22.live_ref, bf16[128,96,128]{2,1,0:T(8,128)(2,1)} %get-tuple-element.33.normed_ref.refs_1_.refs_5_, f32[1,384]{1,0:T(1,128)} %broadcast_in_dim.7.cols_ref, bf16[128,128]{1,0:T(8,128)(2,1)} %bitcast.71), custom_call_target="tpu_custom_call" | custom-call | flops 1000 | bytes 1000 | tf_op jit(solution)/shard_map/project/pallas_call | solution.py:289
  90.6 5.3 %project.9.refs_1_ = bf16[16,256,384]{2,1,0:T(8,128)(2,1)} custom-call(f32[192]{0:T(256)} %dynamic_slice.22.live_ref, bf16[128,96,128]{2,1,0:T(8,128)(2,1)} %get-tuple-element.33.normed_ref.refs_1_.refs_5_, f32[1,384]{1,0:T(1,128)} %broadcast_in_dim.7.cols_ref, bf16[256,128]{1,0:T(8,128)(2,1)} %bitcast.67), custom_call_target="tpu_custom_call" | custom-call | flops 1000 | bytes 1000 | tf_op jit(solution)/shard_map/project/pallas_call | solution.py:289
  95.9 3.2 collective-permute-done.11.refs_4_.refs_2_
  101.9 4.6 %all-to-all-start.1 = ((bf16[16,256,384]{2,1,0:T(8,128)(2,1)}), bf16[16,256,384]{2,1,0:T(8,128)(2,1)S(1)}, u32[]{:S(2)}, u32[]{:S(2)}) async-start(bf16[16,256,384]{2,1,0:T(8,128)(2,1)} %get-tuple-element.35), calls=%async_computation.1 | async-start | bytes 6291456 | tf_op jit(solution)/shard_map/all_to_all | solution.py:924
  108.3 4.8 %project.11.refs_4_.refs_1_ = bf16[16,128,384]{2,1,0:T(8,128)(2,1)} custom-call(f32[192]{0:T(256)} %dynamic_slice.22.live_ref, bf16[128,96,128]{2,1,0:T(8,128)(2,1)} %get-tuple-element.33.normed_ref.refs_1_.refs_5_, f32[1,384]{1,0:T(1,128)} %broadcast_in_dim.7.cols_ref, bf16[128,128]{1,0:T(8,128)(2,1)} %get-tuple-element.36.weight_ref), custom_call_target="tpu_custom_call" | custom-call | flops 1000 | bytes 1000 | tf_op jit(solution)/shard_map/project/pallas_call | solution.py:289
  113.1 4.6 %merge.2.refs_3_ = bf16[16,384,384]{2,1,0:T(8,128)(2,1)} custom-call(bf16[16,64,384]{2,1,0:T(8,128)(2,1)} %project.10.refs_3_.refs_0_, bf16[16,128,384]{2,1,0:T(8,128)(2,1)} %project.11.refs_4_.refs_1_, bf16[16,64,384]{2,1,0:T(8,128)(2,1)} %copy-done.7), custom_call_target="tpu_custom_call" | custom-call | flops 1000 | bytes 1000 | tf_op jit(solution)/shard_map/merge/pallas_call | solution.py:670
  117.7 5.1 %copy.155.refs_1_ = bf16[16,384,384]{2,1,0:T(8,128)(2,1)} copy(bf16[16,384,384]{2,1,0:T(8,128)(2,1)} %merge.2.refs_3_) | data formatting | bytes 9437184
  122.9 57.2 %collective-permute-done.15.refs_0_ = bf16[16,128,384]{2,1,0:T(8,128)(2,1)} collective-permute-done((bf16[16,128,384]{2,1,0:T(8,128)(2,1)}, bf16[16,128,384]{2,1,0:T(8,128)(2,1)}, u32[]{:S(2)}, u32[]{:S(2)}) %collective-permute-start.15) | collective-permute-done | bytes 1572896 | tf_op jit(solution)/shard_map/ppermute | solution.py:1017
  184.2 5.8 %all-to-all-start.2 = ((bf16[16,384,384]{2,1,0:T(8,128)(2,1)}), bf16[16,384,384]{2,1,0:T(8,128)(2,1)}, u32[]{:S(2)}, u32[]{:S(2)}) async-start(bf16[16,384,384]{2,1,0:T(8,128)(2,1)} %merge.3), calls=%async_computation.2 | async-start | bytes 9437184 | tf_op jit(solution)/shard_map/all_to_all | solution.py:924
  192.4 9.5 %logit.1.logit_ref = f32[192,8,96]{2,1,0:T(8,128)} custom-call(f32[192]{0:T(256)} %dynamic_slice.22.live_ref, bf16[64,96,128]{2,1,0:T(8,128)(2,1)} %get-tuple-element.30.normed_ref.refs_0_.refs_4_, bf16[128,96,128]{2,1,0:T(8,128)(2,1)} %get-tuple-element.33.normed_ref.refs_1_.refs_5_, bf16[8,128]{1,0:T(8,128)(2,1)} %bitcast.87, ...), custom_call_target="tpu_custom_call" | custom-call | flops 1000 | bytes 1000 | tf_op jit(solution)/shard_map/logit/pallas_call | solution.py:341
  201.9 4.2 partial.1
  206.1 9.3 %assemble_half.1 = (bf16[4,768,384]{2,1,0:T(8,128)(2,1)}, bf16[4,384,384]{2,1,0:T(8,128)(2,1)}, bf16[4,768,384]{2,1,0:T(8,128)(2,1)}) custom-call(s32[1]{0:T(128)} %bitcast.half_ref, bf16[16,128,384]{2,1,0:T(8,128)(2,1)} %copy-done, bf16[16,256,384]{2,1,0:T(8,128)(2,1)} %copy-done.1, f32[8,104,128]{2,1,0:T(8,128)} %get-tuple-element.37.refs_2_.refs_1_, ...), custom_call_target="tpu_custom_call" | custom-call | flops 1000 | bytes 1000 | tf_op jit(solution)/shard_map/assemble_half/pallas_call | solution.py:569
  221.4 22.2 %collective-permute-done.12.refs_1_ = f32[8,104,128]{2,1,0:T(8,128)S(1)} collective-permute-done((f32[8,104,128]{2,1,0:T(8,128)}, f32[8,104,128]{2,1,0:T(8,128)S(1)}, u32[]{:S(2)}, u32[]{:S(2)}) %collective-permute-start.12) | collective-permute-done | bytes 426016 | tf_op jit(solution)/shard_map/ppermute | solution.py:969
  243.6 16.5 %collective-permute-done.14.refs_3_ = f32[8,104,128]{2,1,0:T(8,128)S(1)} collective-permute-done((f32[8,104,128]{2,1,0:T(8,128)}, f32[8,104,128]{2,1,0:T(8,128)S(1)}, u32[]{:S(2)}, u32[]{:S(2)}) %collective-permute-start.14) | collective-permute-done | bytes 426016 | tf_op jit(solution)/shard_map/ppermute | solution.py:969
  260.1 60.6 %collective-permute-done.16.recv_ref = bf16[4,768,384]{2,1,0:T(8,128)(2,1)} collective-permute-done((bf16[4,768,384]{2,1,0:T(8,128)(2,1)}, bf16[4,768,384]{2,1,0:T(8,128)(2,1)}, u32[]{:S(2)}, u32[]{:S(2)}) %collective-permute-start.16) | collective-permute-done | bytes 2359328 | tf_op jit(solution)/shard_map/ppermute | solution.py:1032
  320.7 6.8 %combine.1.refs_0_ = bf16[16,192,384]{2,1,0:T(8,128)(2,1)} custom-call(bf16[4,768,384]{2,1,0:T(8,128)(2,1)} %get-tuple-element.47.left_ref, bf16[4,384,384]{2,1,0:T(8,128)(2,1)} %get-tuple-element.48.own_ref, bf16[4,768,384]{2,1,0:T(8,128)(2,1)} %collective-permute-done.16.recv_ref, bf16[16,384,384]{2,1,0:T(8,128)(2,1)} %all-to-all-done.2.refs_0_.recv_ref, ...), custom_call_target="tpu_custom_call" | custom-call | flops 1000 | bytes 1000 | tf_op jit(solution)/shard_map/combine/pallas_call | solution.py:636
  327.6 4.0 all-to-all-start.3
  331.5 8.8 %assemble.1 = (bf16[2,16,48,768]{3,2,1,0:T(8,128)(2,1)}, bf16[2,4,1,192,768]{4,3,2,1,0:T(8,128)(2,1)}) custom-call(bf16[16,384,384]{2,1,0:T(8,128)(2,1)} %all-to-all-done.2.refs_0_.recv_ref, bf16[16,192,384]{2,1,0:T(8,128)(2,1)} %combine.1.refs_0_), custom_call_target="tpu_custom_call" | custom-call | flops 1000 | bytes 1000 | tf_op jit(solution)/shard_map/assemble/pallas_call | solution.py:407
  340.3 7.0 %multiply.13.refs_4_ = bf16[32,96,384]{2,1,0:T(8,128)(2,1)} custom-call(bf16[2,16,48,768]{3,2,1,0:T(8,128)(2,1)} %get-tuple-element.50.left_ref, bf16[2,768,768]{2,1,0:T(8,128)(2,1)} %bitcast.61), custom_call_target="tpu_custom_call" | custom-call | flops 1000 | bytes 1000 | tf_op jit(solution)/shard_map/multiply/pallas_call | solution.py:472
  347.3 14.7 %all-to-all-done.3.refs_0_ = bf16[16,192,384]{2,1,0:T(8,128)(2,1)S(1)} async-done(((bf16[16,192,384]{2,1,0:T(8,128)(2,1)}), bf16[16,192,384]{2,1,0:T(8,128)(2,1)S(1)}, u32[]{:S(2)}, u32[]{:S(2)}) %all-to-all-start.3) | async-done | bytes 2359328 | tf_op jit(solution)/shard_map/all_to_all | solution.py:924
  363.5 6.7 %all-to-all-start.4 = ((bf16[32,96,384]{2,1,0:T(8,128)(2,1)}), bf16[32,96,384]{2,1,0:T(8,128)(2,1)}, u32[]{:S(2)}, u32[]{:S(2)}) async-start(bf16[32,96,384]{2,1,0:T(8,128)(2,1)} %multiply.13.refs_4_), calls=%async_computation.4 | async-start | bytes 4718592 | tf_op jit(solution)/shard_map/all_to_all | solution.py:924
  377.0 4.7 %average.1 = bf16[96,256]{1,0:T(8,128)(2,1)} custom-call(f32[8,104,128]{2,1,0:T(8,128)} %get-tuple-element.52.refs_0_, f32[8,104,128]{2,1,0:T(8,128)} %get-tuple-element.53.refs_1_, f32[8,104,128]{2,1,0:T(8,128)} %get-tuple-element.54.refs_2_, f32[8,104,128]{2,1,0:T(8,128)} %get-tuple-element.55.refs_3_, f32[8,96,128]{2,1,0:T(8,128)} %copy.136.refs_4_, ...), custom_call_target="tpu_custom_call" | custom-call | flops 1000 | bytes 1000 | tf_op jit(solution)/shard_map/average/pallas_call | solution.py:764
  383.2 42.5 %all-to-all-done.4.refs_1_ = bf16[32,96,384]{2,1,0:T(8,128)(2,1)} async-done(((bf16[32,96,384]{2,1,0:T(8,128)(2,1)}), bf16[32,96,384]{2,1,0:T(8,128)(2,1)}, u32[]{:S(2)}, u32[]{:S(2)}) %all-to-all-start.4) | async-done | bytes 2359328 | tf_op jit(solution)/shard_map/all_to_all | solution.py:924
  425.8 13.0 %finish.1 = bf16[192,96,128]{2,1,0:T(8,128)(2,1)} custom-call(bf16[16,192,384]{2,1,0:T(8,128)(2,1)} %copy-done.2, bf16[32,96,384]{2,1,0:T(8,128)(2,1)} %all-to-all-done.4.refs_1_, bf16[64,96,128]{2,1,0:T(8,128)(2,1)} %get-tuple-element.56.refs_2_, bf16[128,96,128]{2,1,0:T(8,128)(2,1)} %get-tuple-element.57.refs_3_, ...), custom_call_target="tpu_custom_call" | custom-call | flops 1000 | bytes 1000 | tf_op jit(solution)/shard_map/finish/pallas_call | solution.py:824
  (159 shorter events, 54.9 us)
Async XLA Ops:
  0.6 18.8 %slice-start = ((bf16[64,576]{1,0:T(8,128)(2,1)}), bf16[64,32]{1,0:T(8,128)(2,1)S(1)}, s32[]{:S(2)}) async-start(bf16[64,576]{1,0:T(8,128)(2,1)} %param.14), calls=%async_computation.5 | async-start | bytes 32768 | tf_op jit(solution)/shard_map/slice | solution.py:895
  0.6 18.6 %copy-start.22 = (bf16[128,640]{1,0:T(8,128)(2,1)S(1)}, bf16[128,640]{1,0:T(8,128)(2,1)}, u32[]{:S(2)}) copy-start(bf16[128,640]{1,0:T(8,128)(2,1)} %param.18) | copy-start | bytes 491524
  0.7 33.9 %copy-start.21 = (bf16[1024,128]{1,0:T(8,128)(2,1)S(1)}, bf16[1024,128]{1,0:T(8,128)(2,1)}, u32[]{:S(2)}) copy-start(bf16[1024,128]{1,0:T(8,128)(2,1)} %param.15) | copy-start | bytes 786436
  3.5 25.3 %collective-permute-start = (bf16[96,256]{1,0:T(8,128)(2,1)S(1)}, bf16[96,256]{1,0:T(8,128)(2,1)S(1)}, u32[]{:S(2)}, u32[]{:S(2)}) collective-permute-start(bf16[96,256]{1,0:T(8,128)(2,1)S(1)} %copy.109), channel_id=1, source_target_pairs={{0,0},{1,1},{2,8},{3,9},{4,16},{5,17},{6,24},{7,25},{8,2},{9,3},{1... | collective-permute-start | bytes 147464 | tf_op jit(solution)/shard_map/ppermute | solution.py:905
  4.1 24.7 %collective-permute-start.1 = (bf16[96,256]{1,0:T(8,128)(2,1)S(1)}, bf16[96,256]{1,0:T(8,128)(2,1)S(1)}, u32[]{:S(2)}, u32[]{:S(2)}) collective-permute-start(bf16[96,256]{1,0:T(8,128)(2,1)S(1)} %copy.109), channel_id=1, source_target_pairs={{0,7},{1,0},{2,15},{3,8},{4,23},{5,16},{6,31},{7,24},{8,1},{9,2},{... | collective-permute-start | bytes 147464 | tf_op jit(solution)/shard_map/ppermute | solution.py:905
  11.7 19.1 %collective-permute-start.2 = (bf16[96,256]{1,0:T(8,128)(2,1)S(1)}, bf16[96,256]{1,0:T(8,128)(2,1)S(1)}, u32[]{:S(2)}, u32[]{:S(2)}) collective-permute-start(bf16[96,256]{1,0:T(8,128)(2,1)S(1)} %copy.109), channel_id=1, source_target_pairs={{0,6},{1,7},{2,14},{3,15},{4,22},{5,23},{6,30},{7,31},{8,0},{9,1},... | collective-permute-start | bytes 147464 | tf_op jit(solution)/shard_map/ppermute | solution.py:905
  15.7 22.5 %copy-start.9 = (bf16[4,96,32]{2,1,0:T(8,128)(2,1)}, bf16[4,96,32]{2,1,0:T(8,128)(2,1)S(1)}, u32[]{:S(2)}) copy-start(bf16[4,96,32]{2,1,0:T(8,128)(2,1)S(1)} %fusion.3.refs_8_) | copy-start | bytes 73732
  15.7 5.3 %collective-permute-start.8 = (bf16[4,96,32]{2,1,0:T(8,128)(2,1)S(1)}, bf16[4,96,32]{2,1,0:T(8,128)(2,1)S(1)}, u32[]{:S(2)}, u32[]{:S(2)}) collective-permute-start(bf16[4,96,32]{2,1,0:T(8,128)(2,1)S(1)} %fusion.3.refs_8_), channel_id=1, source_target_pairs={{0,24},{8,0},{16,8},{24,16},{1,25},{9,1},{17,9},{25,17},{2,26},{10... | collective-permute-start | bytes 73736 | tf_op jit(solution)/shard_map/ppermute | solution.py:909
  18.0 5.5 %collective-permute-start.9 = (bf16[4,96,32]{2,1,0:T(8,128)(2,1)S(1)}, bf16[4,96,32]{2,1,0:T(8,128)(2,1)S(1)}, u32[]{:S(2)}, u32[]{:S(2)}) collective-permute-start(bf16[4,96,32]{2,1,0:T(8,128)(2,1)S(1)} %fusion.3.refs_8_), channel_id=1, source_target_pairs={{0,16},{8,24},{16,0},{24,8},{1,17},{9,25},{17,1},{25,9},{2,18},{10... | collective-permute-start | bytes 73736 | tf_op jit(solution)/shard_map/ppermute | solution.py:909
  21.0 17.2 %copy-start.18 = (bf16[4,96,32]{2,1,0:T(8,128)(2,1)}, bf16[4,96,32]{2,1,0:T(8,128)(2,1)S(1)}, u32[]{:S(2)}) copy-start(bf16[4,96,32]{2,1,0:T(8,128)(2,1)S(1)} %collective-permute-done.8.refs_9_) | copy-start | bytes 73732
  21.0 6.9 %collective-permute-start.10 = (bf16[4,96,32]{2,1,0:T(8,128)(2,1)S(1)}, bf16[4,96,32]{2,1,0:T(8,128)(2,1)S(1)}, u32[]{:S(2)}, u32[]{:S(2)}) collective-permute-start(bf16[4,96,32]{2,1,0:T(8,128)(2,1)S(1)} %fusion.3.refs_8_), channel_id=1, source_target_pairs={{0,8},{8,16},{16,24},{24,0},{1,9},{9,17},{17,25},{25,1},{2,10},{10... | collective-permute-start | bytes 73736 | tf_op jit(solution)/shard_map/ppermute | solution.py:909
  23.5 14.6 %copy-start.19 = (bf16[4,96,32]{2,1,0:T(8,128)(2,1)}, bf16[4,96,32]{2,1,0:T(8,128)(2,1)S(1)}, u32[]{:S(2)}) copy-start(bf16[4,96,32]{2,1,0:T(8,128)(2,1)S(1)} %collective-permute-done.9.refs_10_) | copy-start | bytes 73732
  23.5 14.5 %collective-permute-start.3 = (bf16[96,256]{1,0:T(8,128)(2,1)S(1)}, bf16[96,256]{1,0:T(8,128)(2,1)S(1)}, u32[]{:S(2)}, u32[]{:S(2)}) collective-permute-start(bf16[96,256]{1,0:T(8,128)(2,1)S(1)} %copy.109), channel_id=1, source_target_pairs={{0,5},{1,6},{2,13},{3,14},{4,21},{5,22},{6,29},{7,30},{8,7},{9,0},... | collective-permute-start | bytes 147464 | tf_op jit(solution)/shard_map/ppermute | solution.py:905
  27.9 10.3 %copy-start.20 = (bf16[4,96,32]{2,1,0:T(8,128)(2,1)}, bf16[4,96,32]{2,1,0:T(8,128)(2,1)S(1)}, u32[]{:S(2)}) copy-start(bf16[4,96,32]{2,1,0:T(8,128)(2,1)S(1)} %collective-permute-done.10.refs_11_) | copy-start | bytes 73732
  27.9 10.2 %collective-permute-start.4 = (bf16[96,256]{1,0:T(8,128)(2,1)S(1)}, bf16[96,256]{1,0:T(8,128)(2,1)S(1)}, u32[]{:S(2)}, u32[]{:S(2)}) collective-permute-start(bf16[96,256]{1,0:T(8,128)(2,1)S(1)} %copy.109), channel_id=1, source_target_pairs={{0,4},{1,5},{2,12},{3,13},{4,20},{5,21},{6,28},{7,29},{8,6},{9,7},... | collective-permute-start | bytes 147464 | tf_op jit(solution)/shard_map/ppermute | solution.py:905
  28.7 9.4 %collective-permute-start.5 = (bf16[96,256]{1,0:T(8,128)(2,1)S(1)}, bf16[96,256]{1,0:T(8,128)(2,1)S(1)}, u32[]{:S(2)}, u32[]{:S(2)}) collective-permute-start(bf16[96,256]{1,0:T(8,128)(2,1)S(1)} %copy.109), channel_id=1, source_target_pairs={{0,3},{1,4},{2,11},{3,12},{4,19},{5,20},{6,27},{7,28},{8,5},{9,6},... | collective-permute-start | bytes 147464 | tf_op jit(solution)/shard_map/ppermute | solution.py:905
  28.9 9.3 %collective-permute-start.6 = (bf16[96,256]{1,0:T(8,128)(2,1)S(1)}, bf16[96,256]{1,0:T(8,128)(2,1)S(1)}, u32[]{:S(2)}, u32[]{:S(2)}) collective-permute-start(bf16[96,256]{1,0:T(8,128)(2,1)S(1)} %copy.109), channel_id=1, source_target_pairs={{0,2},{1,3},{2,10},{3,11},{4,18},{5,19},{6,26},{7,27},{8,4},{9,5},... | collective-permute-start | bytes 147464 | tf_op jit(solution)/shard_map/ppermute | solution.py:905
  30.8 7.3 %collective-permute-start.7 = (bf16[96,256]{1,0:T(8,128)(2,1)S(1)}, bf16[96,256]{1,0:T(8,128)(2,1)S(1)}, u32[]{:S(2)}, u32[]{:S(2)}) collective-permute-start(bf16[96,256]{1,0:T(8,128)(2,1)S(1)} %copy.109), channel_id=1, source_target_pairs={{0,1},{1,2},{2,9},{3,10},{4,17},{5,18},{6,25},{7,26},{8,3},{9,4},{... | collective-permute-start | bytes 147464 | tf_op jit(solution)/shard_map/ppermute | solution.py:905
  56.8 43.9 %all-to-all-start = ((bf16[16,128,384]{2,1,0:T(8,128)(2,1)}), bf16[16,128,384]{2,1,0:T(8,128)(2,1)S(1)}, u32[]{:S(2)}, u32[]{:S(2)}) async-start(bf16[16,128,384]{2,1,0:T(8,128)(2,1)} %get-tuple-element.31), calls=%async_computation | async-start | bytes 3145728 | tf_op jit(solution)/shard_map/all_to_all | solution.py:924
  62.7 36.3 %collective-permute-start.11 = (bf16[16,64,384]{2,1,0:T(8,128)(2,1)S(1)}, bf16[16,64,384]{2,1,0:T(8,128)(2,1)S(1)}, u32[]{:S(2)}, u32[]{:S(2)}) collective-permute-start(bf16[16,64,384]{2,1,0:T(8,128)(2,1)S(1)} %copy-done.6), channel_id=1, source_target_pairs={{0,4},{4,0},{1,5},{5,1},{2,6},{6,2},{3,7},{7,3},{8,12},{12,8},{9,1... | collective-permute-start | bytes 2359304 | tf_op jit(solution)/shard_map/ppermute | solution.py:1017
  101.9 80.7 %all-to-all-start.1 = ((bf16[16,256,384]{2,1,0:T(8,128)(2,1)}), bf16[16,256,384]{2,1,0:T(8,128)(2,1)S(1)}, u32[]{:S(2)}, u32[]{:S(2)}) async-start(bf16[16,256,384]{2,1,0:T(8,128)(2,1)} %get-tuple-element.35), calls=%async_computation.1 | async-start | bytes 6291456 | tf_op jit(solution)/shard_map/all_to_all | solution.py:924
  106.4 73.7 %collective-permute-start.15 = (bf16[16,128,384]{2,1,0:T(8,128)(2,1)}, bf16[16,128,384]{2,1,0:T(8,128)(2,1)}, u32[]{:S(2)}, u32[]{:S(2)}) collective-permute-start(bf16[16,128,384]{2,1,0:T(8,128)(2,1)} %get-tuple-element.46), channel_id=1, source_target_pairs={{0,4},{4,0},{1,5},{5,1},{2,6},{6,2},{3,7},{7,3},{8,12},{12,8},{9,1... | collective-permute-start | bytes 4718600 | tf_op jit(solution)/shard_map/ppermute | solution.py:1017
  184.2 136.5 %all-to-all-start.2 = ((bf16[16,384,384]{2,1,0:T(8,128)(2,1)}), bf16[16,384,384]{2,1,0:T(8,128)(2,1)}, u32[]{:S(2)}, u32[]{:S(2)}) async-start(bf16[16,384,384]{2,1,0:T(8,128)(2,1)} %merge.3), calls=%async_computation.2 | async-start | bytes 9437184 | tf_op jit(solution)/shard_map/all_to_all | solution.py:924
  215.4 105.3 %collective-permute-start.16 = (bf16[4,768,384]{2,1,0:T(8,128)(2,1)}, bf16[4,768,384]{2,1,0:T(8,128)(2,1)}, u32[]{:S(2)}, u32[]{:S(2)}) collective-permute-start(bf16[4,768,384]{2,1,0:T(8,128)(2,1)} %get-tuple-element.49), channel_id=1, source_target_pairs={{0,4},{4,0},{1,5},{5,1},{2,6},{6,2},{3,7},{7,3},{8,12},{12,8},{9,1... | collective-permute-start | bytes 7077896 | tf_op jit(solution)/shard_map/ppermute | solution.py:1032
  217.7 25.9 %collective-permute-start.12 = (f32[8,104,128]{2,1,0:T(8,128)}, f32[8,104,128]{2,1,0:T(8,128)S(1)}, u32[]{:S(2)}, u32[]{:S(2)}) collective-permute-start(f32[8,104,128]{2,1,0:T(8,128)} %get-tuple-element.43), channel_id=1, source_target_pairs={{0,24},{8,0},{16,8},{24,16},{1,25},{9,1},{17,9},{25,17},{2,26},{10... | collective-permute-start | bytes 1277960 | tf_op jit(solution)/shard_map/ppermute | solution.py:969
  220.3 23.3 %collective-permute-start.13 = (f32[8,104,128]{2,1,0:T(8,128)}, f32[8,104,128]{2,1,0:T(8,128)S(1)}, u32[]{:S(2)}, u32[]{:S(2)}) collective-permute-start(f32[8,104,128]{2,1,0:T(8,128)} %get-tuple-element.44), channel_id=1, source_target_pairs={{0,16},{8,24},{16,0},{24,8},{1,17},{9,25},{17,1},{25,9},{2,18},{10... | collective-permute-start | bytes 1277960 | tf_op jit(solution)/shard_map/ppermute | solution.py:969
  220.8 39.4 %collective-permute-start.14 = (f32[8,104,128]{2,1,0:T(8,128)}, f32[8,104,128]{2,1,0:T(8,128)S(1)}, u32[]{:S(2)}, u32[]{:S(2)}) collective-permute-start(f32[8,104,128]{2,1,0:T(8,128)} %get-tuple-element.45), channel_id=1, source_target_pairs={{0,8},{8,16},{16,24},{24,0},{1,9},{9,17},{17,25},{25,1},{2,10},{10... | collective-permute-start | bytes 1277960 | tf_op jit(solution)/shard_map/ppermute | solution.py:969
  243.6 77.1 %copy-start.3 = (f32[8,104,128]{2,1,0:T(8,128)}, f32[8,104,128]{2,1,0:T(8,128)S(1)}, u32[]{:S(2)}) copy-start(f32[8,104,128]{2,1,0:T(8,128)S(1)} %collective-permute-done.12.refs_1_) | copy-start | bytes 1277956
  243.6 77.1 %copy-start.4 = (f32[8,104,128]{2,1,0:T(8,128)}, f32[8,104,128]{2,1,0:T(8,128)S(1)}, u32[]{:S(2)}) copy-start(f32[8,104,128]{2,1,0:T(8,128)S(1)} %collective-permute-done.13.refs_2_) | copy-start | bytes 1277956
  260.1 60.6 %copy-start.5 = (f32[8,104,128]{2,1,0:T(8,128)}, f32[8,104,128]{2,1,0:T(8,128)S(1)}, u32[]{:S(2)}) copy-start(f32[8,104,128]{2,1,0:T(8,128)S(1)} %collective-permute-done.14.refs_3_) | copy-start | bytes 1277956
  327.6 34.5 %all-to-all-start.3 = ((bf16[16,192,384]{2,1,0:T(8,128)(2,1)}), bf16[16,192,384]{2,1,0:T(8,128)(2,1)S(1)}, u32[]{:S(2)}, u32[]{:S(2)}) async-start(bf16[16,192,384]{2,1,0:T(8,128)(2,1)} %combine.1.refs_0_), calls=%async_computation.3 | async-start | bytes 4718592 | tf_op jit(solution)/shard_map/all_to_all | solution.py:924
  363.5 62.3 %all-to-all-start.4 = ((bf16[32,96,384]{2,1,0:T(8,128)(2,1)}), bf16[32,96,384]{2,1,0:T(8,128)(2,1)}, u32[]{:S(2)}, u32[]{:S(2)}) async-start(bf16[32,96,384]{2,1,0:T(8,128)(2,1)} %multiply.13.refs_4_), calls=%async_computation.4 | async-start | bytes 4718592 | tf_op jit(solution)/shard_map/all_to_all | solution.py:924
  (21 other events, 71.1 us)

commit v12 on v11

--- a/solution.py
+++ b/solution.py
@@ -552,11 +552,9 @@
         own_ref[0, :, span] = right_ref[at, pl.ds(own, width), :].astype(BF16)
         theirs.append(right_ref[at, pl.ds(other, width), :].astype(BF16))
     theirs = jnp.concatenate(theirs, axis=1)
-    for row in range(row_count):
-        span = slice(row * QUAD * each, (row + 1) * QUAD * each)
-        send_ref[0, span] = lax.dot_general(
-            left_ref[0, span], theirs, NT, preferred_element_type=F32
-        ).astype(BF16)
+    send_ref[0] = lax.dot_general(
+        left_ref[0], theirs, NT, preferred_element_type=F32
+    ).astype(BF16)
 
 
 def assemble_half(half, received, after, row_count, pos_count, cols):
@@ -602,14 +600,14 @@
     each = left_ref.shape[1] // (row_count * QUAD)
     stride = out_ref.shape[1] // each
     tiles = lanes // LANES
-    for row in range(row_count):
-        for group in range(pos_count // 4):
-            cols = slice(group * lanes, (group + 1) * lanes)
+    for group in range(pos_count // 4):
+        cols = slice(group * lanes, (group + 1) * lanes)
+        whole_value = lax.dot_general(
+            left_ref[0], own_ref[0, cols], NT, preferred_element_type=F32
+        )
+        for row in range(row_count):
             span = slice(row * QUAD * each, (row + 1) * QUAD * each)
-            value = lax.dot_general(
-                left_ref[0, span], own_ref[0, cols], NT, preferred_element_type=F32
-            )
-            value = value + recv_ref[0, span, cols].astype(F32)
+            value = whole_value[span] + recv_ref[0, span, cols].astype(F32)
             blocks = [
                 [
                     value[a * each : (a + 1) * each, t * LANES : (t + 1) * LANES]
@@ -658,7 +656,7 @@
     at_chunk(steps, put, refs[: len(steps)])
 
 
-def merge(pieces, first, height, unit, into):
+def merge(pieces, first, height, unit, into, after):
     sources, _, lanes = pieces[0].shape
     steps = [piece.shape[1] // unit for piece in pieces]
 
@@ -670,14 +668,16 @@
     return pl.pallas_call(
         functools.partial(merge_kernel, steps=steps),
         grid=(sum(steps),),
-        in_specs=[block(sum(steps[:at]), count) for at, count in enumerate(steps)] + anywhere(into),
+        in_specs=[block(sum(steps[:at]), count) for at, count in enumerate(steps)]
+        + anywhere(into)
+        + anywhere(after),
         out_specs=pl.BlockSpec((sources, unit, lanes), lambda i: (0, i + first // unit, 0)),
         out_shape=jax.ShapeDtypeStruct((sources, height, lanes), BF16),
         input_output_aliases={len(pieces): 0} if into else {},
         compiler_params=params(),
         cost_estimate=LIGHT,
         name="merge",
-    )(*pieces, *into)
+    )(*pieces, *into, *after)
 
 
 def partial_kernel(place_ref, logit_ref, *refs, row_count, col_count):
@@ -791,6 +791,14 @@
                 tmp[t, src * height : (src + 1) * height] = value[:, t * LANES : (t + 1) * LANES]
 
     def rows(mid_ref, normed_ref):
+        count, cols, wide = normed_ref.shape
+        gates = sigmoid(
+            jnp.dot(
+                normed_ref[...].reshape(count * cols, wide),
+                gate_ref[...],
+                preferred_element_type=F32,
+            )
+        )
         for m in range(quads):
             pieces = []
             for product, tmp in zip(products, flat):
@@ -807,7 +815,7 @@
             out = lax.dot_general(normed, weight_ref[...], TN, preferred_element_type=F32)
             for a, value in enumerate(unpack_rows(out)):
                 i = QUAD * m + a
-                gate = sigmoid(jnp.dot(normed_ref[i], gate_ref[...], preferred_element_type=F32))
+                gate = gates[i * cols : (i + 1) * cols]
                 out_ref[i] = (mid_ref[i].astype(F32) + gate * value).astype(BF16)
 
     at_chunk(steps, rows, mids, normeds)
@@ -1023,11 +1031,11 @@
         parts = partial_average(place, logits, lefts, w_value)
         height = 2 * sum(part.shape[1] for part in kept)
         unit, last = kept[0].shape[1], height - kept[-1].shape[1]
-        merged = merge(kept + crossed[:-1], 0, height, unit, ())
+        merged = merge(kept + crossed[:-1], 0, height, unit, (), ())
         left, own, theirs = assemble_half(
             half_scalar, received, (parts[0], merged), *half_shape
         )
-        merged = merge(crossed[-1:], last, height, unit, (merged,))
+        merged = merge(crossed[-1:], last, height, unit, (merged,), (left,))
         theirs, *parts = fence([theirs, *parts], ())
         partial = lax.ppermute(theirs, "half", swap)
         both = exchange(merged, GROUP)

time: 441 us -> 425 us (0.964)
  waiting for transfers between devices: 223 us -> 208 us
    ppermute x2, waiting for transfers between devices: 60.4 us -> 5.29 us  [on_device(): crossed.append(lax.ppermute(to_other, 'half', swap))]
    all_to_all x5, waiting for transfers between devices: 58.9 us -> 97.8 us  [exchange(): return lax.all_to_all(block, axes, split_axis=0, concat_axis=0, tiled=True)]
    ppermute x3, waiting for transfers between devices: 38.8 us -> 44.8 us  [gather_parts(): gathered.append(lax.ppermute(parts[t], 'row', pairs))]
    unnamed x63 -> x62, local copies, waits for them, and re-layouts: 10.9 us -> 7.18 us
  transfers between devices with their start and end apart: 22 -> 22, of which waited for: 11 -> 7; matrix products, arithmetic and copies ran while one was open for 6% -> 5% of each run, Pallas kernels for 20% -> 20%
where the time goes in v12:
time: 425 us; the launch traced here: 423 us
  waiting for transfers between devices  208 us (49%)
  Pallas kernels  126 us (30%)
  starting transfers between devices  52.5 us (12%)
  local copies, waits for them, and re-layouts  25.3 us (6%)
  other arithmetic  8.81 us (2%)
    all_to_all x5, waiting for transfers between devices, exchange(): return lax.all_to_all(block, axes, split_axis=0, concat_axis=0, tiled=True)  97.8 us
    ppermute x1, waiting for transfers between devices, on_device(): partial = lax.ppermute(theirs, 'half', swap)  60.2 us
    ppermute x3, waiting for transfers between devices, gather_parts(): gathered.append(lax.ppermute(parts[t], 'row', pairs))  44.8 us
    pallas_call x2, Pallas kernels, front(): pl.pallas_call(functools.partial(front_kernel, row_count=len(rights), col...  30.6 us
    all_to_all x5, starting transfers between devices, exchange(): return lax.all_to_all(block, axes, split_axis=0, concat_axis=0, tiled=True)  25.2 us
    pallas_call x6, Pallas kernels, project(): pl.pallas_call(functools.partial(project_kernel, first_row=first_row), gr...  24.1 us
    ppermute x8, starting transfers between devices, on_device(): lefts.append(lax.ppermute(own_rows, AXES, pairs))  15.4 us
    pallas_call x1, Pallas kernels, finish(): pl.pallas_call(functools.partial(finish_kernel, parts=len(products), step...  12.9 us
  transfers between devices with their start and end apart: 22, of which 7 were waited for; matrix products, arithmetic and copies ran while one was open for 5% of the time, Pallas kernels for 20%

profile of v12, /device:TPU:0, one launch (start us, length us, event | category | flops | bytes accessed | tf_op | source)
XLA Modules:
  0.0 422.7 jit_solution(15152070064786461059)
XLA Ops:
  6.4 3.0 collective-permute-start.10
  13.1 3.5 collective-permute-start.1
  27.6 3.5 collective-permute-start.7
  37.9 11.3 %front.2 = (bf16[64,96,128]{2,1,0:T(8,128)(2,1)}, bf16[64,96,128]{2,1,0:T(8,128)(2,1)}) custom-call(s32[2]{0:T(128)} %pad_add_fusion.place_ref, bf16[96,256]{1,0:T(8,128)(2,1)} %copy-done.10, bf16[96,256]{1,0:T(8,128)(2,1)} %copy-done.11, bf16[96,256]{1,0:T(8,128)(2,1)} %copy-done.12, bf16[96,256]{1,0:T(8,128)(2,1)} %copy-done.13, ...), custom_call_target="tpu_custom_call" | custom-call | flops 1000 | bytes 1000 | tf_op jit(solution)/shard_map/front/pallas_call | solution.py:193
  49.2 3.2 project.7.refs_1_
  52.4 3.0 project.6.refs_0_
  55.4 5.7 %all-to-all-start = ((bf16[16,128,384]{2,1,0:T(8,128)(2,1)}), bf16[16,128,384]{2,1,0:T(8,128)(2,1)S(1)}, u32[]{:S(2)}, u32[]{:S(2)}) async-start(bf16[16,128,384]{2,1,0:T(8,128)(2,1)} %get-tuple-element.31), calls=%async_computation | async-start | bytes 3145728 | tf_op jit(solution)/shard_map/all_to_all | solution.py:932
  61.2 19.3 %front.3 = (bf16[128,96,128]{2,1,0:T(8,128)(2,1)}, bf16[128,96,128]{2,1,0:T(8,128)(2,1)}) custom-call(s32[2]{0:T(128)} %pad_add_fusion.place_ref, bf16[96,256]{1,0:T(8,128)(2,1)} %copy-done.10, bf16[96,256]{1,0:T(8,128)(2,1)} %copy-done.11, bf16[96,256]{1,0:T(8,128)(2,1)} %copy-done.12, bf16[96,256]{1,0:T(8,128)(2,1)} %copy-done.13, ...), custom_call_target="tpu_custom_call" | custom-call | flops 1000 | bytes 1000 | tf_op jit(solution)/shard_map/front/pallas_call | solution.py:193
  80.5 5.3 %project.9.refs_1_ = bf16[16,256,384]{2,1,0:T(8,128)(2,1)} custom-call(f32[192]{0:T(256)} %dynamic_slice.22.live_ref, bf16[128,96,128]{2,1,0:T(8,128)(2,1)} %get-tuple-element.33.normed_ref.refs_1_.refs_5_, f32[1,384]{1,0:T(1,128)} %broadcast_in_dim.7.cols_ref, bf16[256,128]{1,0:T(8,128)(2,1)} %bitcast.67), custom_call_target="tpu_custom_call" | custom-call | flops 1000 | bytes 1000 | tf_op jit(solution)/shard_map/project/pallas_call | solution.py:289
  85.8 4.9 %project.8.refs_0_ = bf16[16,128,384]{2,1,0:T(8,128)(2,1)} custom-call(f32[192]{0:T(256)} %dynamic_slice.22.live_ref, bf16[128,96,128]{2,1,0:T(8,128)(2,1)} %get-tuple-element.33.normed_ref.refs_1_.refs_5_, f32[1,384]{1,0:T(1,128)} %broadcast_in_dim.7.cols_ref, bf16[128,128]{1,0:T(8,128)(2,1)} %bitcast.71), custom_call_target="tpu_custom_call" | custom-call | flops 1000 | bytes 1000 | tf_op jit(solution)/shard_map/project/pallas_call | solution.py:289
  90.6 2.9 project.10.refs_3_.refs_0_
  93.5 5.3 %collective-permute-done.11.refs_4_.refs_2_ = bf16[16,64,384]{2,1,0:T(8,128)(2,1)S(1)} collective-permute-done((bf16[16,64,384]{2,1,0:T(8,128)(2,1)S(1)}, bf16[16,64,384]{2,1,0:T(8,128)(2,1)S(1)}, u32[]{:S(2)}, u32[]{:S(2)}) %collective-permute-start.11) | collective-permute-done | bytes 786464 | tf_op jit(solution)/shard_map/ppermute | solution.py:1025
  100.9 4.1 all-to-all-start.1
  113.5 4.9 %project.11.refs_4_.refs_1_ = bf16[16,128,384]{2,1,0:T(8,128)(2,1)} custom-call(f32[192]{0:T(256)} %dynamic_slice.22.live_ref, bf16[128,96,128]{2,1,0:T(8,128)(2,1)} %get-tuple-element.33.normed_ref.refs_1_.refs_5_, f32[1,384]{1,0:T(1,128)} %broadcast_in_dim.7.cols_ref, bf16[128,128]{1,0:T(8,128)(2,1)} %get-tuple-element.36.weight_ref), custom_call_target="tpu_custom_call" | custom-call | flops 1000 | bytes 1000 | tf_op jit(solution)/shard_map/project/pallas_call | solution.py:289
  118.3 9.5 %logit.1.logit_ref = f32[192,8,96]{2,1,0:T(8,128)} custom-call(f32[192]{0:T(256)} %dynamic_slice.22.live_ref, bf16[64,96,128]{2,1,0:T(8,128)(2,1)} %get-tuple-element.30.normed_ref.refs_0_.refs_4_, bf16[128,96,128]{2,1,0:T(8,128)(2,1)} %get-tuple-element.33.normed_ref.refs_1_.refs_5_, bf16[8,128]{1,0:T(8,128)(2,1)} %bitcast.87, ...), custom_call_target="tpu_custom_call" | custom-call | flops 1000 | bytes 1000 | tf_op jit(solution)/shard_map/logit/pallas_call | solution.py:341
  127.9 4.6 %merge.2.refs_3_.refs_1_ = bf16[16,384,384]{2,1,0:T(8,128)(2,1)} custom-call(bf16[16,64,384]{2,1,0:T(8,128)(2,1)} %project.10.refs_3_.refs_0_, bf16[16,128,384]{2,1,0:T(8,128)(2,1)} %project.11.refs_4_.refs_1_, bf16[16,64,384]{2,1,0:T(8,128)(2,1)} %copy-done.7), custom_call_target="tpu_custom_call" | custom-call | flops 1000 | bytes 1000 | tf_op jit(solution)/shard_map/merge/pallas_call | solution.py:668
  132.5 4.2 %partial.1 = (f32[8,104,128]{2,1,0:T(8,128)}, f32[8,104,128]{2,1,0:T(8,128)}, f32[8,104,128]{2,1,0:T(8,128)}, f32[8,104,128]{2,1,0:T(8,128)}) custom-call(s32[2]{0:T(128)} %pad_add_fusion.place_ref, f32[192,8,96]{2,1,0:T(8,128)} %logit.1.logit_ref, bf16[96,256]{1,0:T(8,128)(2,1)} %copy-done.10, bf16[96,256]{1,0:T(8,128)(2,1)} %copy-done.11, ...), custom_call_target="tpu_custom_call" | custom-call | flops 1000 | bytes 1000 | tf_op jit(solution)/shard_map/partial/pallas_call | solution.py:719
  136.7 40.6 %all-to-all-done.1.refs_1_ = bf16[16,256,384]{2,1,0:T(8,128)(2,1)S(1)} async-done(((bf16[16,256,384]{2,1,0:T(8,128)(2,1)}), bf16[16,256,384]{2,1,0:T(8,128)(2,1)S(1)}, u32[]{:S(2)}, u32[]{:S(2)}) %all-to-all-start.1) | async-done | bytes 3145760 | tf_op jit(solution)/shard_map/all_to_all | solution.py:932
  179.0 9.7 %assemble_half.1 = (bf16[4,768,384]{2,1,0:T(8,128)(2,1)}, bf16[4,384,384]{2,1,0:T(8,128)(2,1)}, bf16[4,768,384]{2,1,0:T(8,128)(2,1)}) custom-call(s32[1]{0:T(128)} %bitcast.half_ref, bf16[16,128,384]{2,1,0:T(8,128)(2,1)} %copy-done, bf16[16,256,384]{2,1,0:T(8,128)(2,1)} %copy-done.1, f32[8,104,128]{2,1,0:T(8,128)} %get-tuple-element.37.refs_2_.refs_1_, ...), custom_call_target="tpu_custom_call" | custom-call | flops 1000 | bytes 1000 | tf_op jit(solution)/shard_map/assemble_half/pallas_call | solution.py:567
  191.0 4.6 %all-to-all-start.2 = ((bf16[16,384,384]{2,1,0:T(8,128)(2,1)}), bf16[16,384,384]{2,1,0:T(8,128)(2,1)}, u32[]{:S(2)}, u32[]{:S(2)}) async-start(bf16[16,384,384]{2,1,0:T(8,128)(2,1)} %merge.3), calls=%async_computation.2 | async-start | bytes 9437184 | tf_op jit(solution)/shard_map/all_to_all | solution.py:932
  199.5 35.0 %collective-permute-done.12.refs_1_ = f32[8,104,128]{2,1,0:T(8,128)S(1)} collective-permute-done((f32[8,104,128]{2,1,0:T(8,128)}, f32[8,104,128]{2,1,0:T(8,128)S(1)}, u32[]{:S(2)}, u32[]{:S(2)}) %collective-permute-start.12) | collective-permute-done | bytes 426016 | tf_op jit(solution)/shard_map/ppermute | solution.py:977
  234.6 9.7 %collective-permute-done.14.refs_3_ = f32[8,104,128]{2,1,0:T(8,128)S(1)} collective-permute-done((f32[8,104,128]{2,1,0:T(8,128)}, f32[8,104,128]{2,1,0:T(8,128)S(1)}, u32[]{:S(2)}, u32[]{:S(2)}) %collective-permute-start.14) | collective-permute-done | bytes 426016 | tf_op jit(solution)/shard_map/ppermute | solution.py:977
  244.3 60.2 %collective-permute-done.16.recv_ref = bf16[4,768,384]{2,1,0:T(8,128)(2,1)} collective-permute-done((bf16[4,768,384]{2,1,0:T(8,128)(2,1)}, bf16[4,768,384]{2,1,0:T(8,128)(2,1)}, u32[]{:S(2)}, u32[]{:S(2)}) %collective-permute-start.16) | collective-permute-done | bytes 2359328 | tf_op jit(solution)/shard_map/ppermute | solution.py:1040
  304.5 7.0 %combine.1.refs_0_ = bf16[16,192,384]{2,1,0:T(8,128)(2,1)} custom-call(bf16[4,768,384]{2,1,0:T(8,128)(2,1)} %get-tuple-element.47.refs_2_.left_ref, bf16[4,384,384]{2,1,0:T(8,128)(2,1)} %get-tuple-element.48.own_ref, bf16[4,768,384]{2,1,0:T(8,128)(2,1)} %collective-permute-done.16.recv_ref, bf16[16,384,384]{2,1,0:T(8,128)(2,1)} %all-to-all-done.2.refs_0_.recv_ref, ...), custom_call_target="tpu_custom_call" | custom-call | flops 1000 | bytes 1000 | tf_op jit(solution)/shard_map/combine/pallas_call | solution.py:634
  311.5 3.9 all-to-all-start.3
  315.4 8.8 %assemble.1 = (bf16[2,16,48,768]{3,2,1,0:T(8,128)(2,1)}, bf16[2,4,1,192,768]{4,3,2,1,0:T(8,128)(2,1)}) custom-call(bf16[16,384,384]{2,1,0:T(8,128)(2,1)} %all-to-all-done.2.refs_0_.recv_ref, bf16[16,192,384]{2,1,0:T(8,128)(2,1)} %combine.1.refs_0_), custom_call_target="tpu_custom_call" | custom-call | flops 1000 | bytes 1000 | tf_op jit(solution)/shard_map/assemble/pallas_call | solution.py:407
  324.3 7.1 %multiply.13.refs_4_ = bf16[32,96,384]{2,1,0:T(8,128)(2,1)} custom-call(bf16[2,16,48,768]{3,2,1,0:T(8,128)(2,1)} %get-tuple-element.50.left_ref, bf16[2,768,768]{2,1,0:T(8,128)(2,1)} %bitcast.61), custom_call_target="tpu_custom_call" | custom-call | flops 1000 | bytes 1000 | tf_op jit(solution)/shard_map/multiply/pallas_call | solution.py:472
  331.4 14.3 %all-to-all-done.3.refs_0_ = bf16[16,192,384]{2,1,0:T(8,128)(2,1)S(1)} async-done(((bf16[16,192,384]{2,1,0:T(8,128)(2,1)}), bf16[16,192,384]{2,1,0:T(8,128)(2,1)S(1)}, u32[]{:S(2)}, u32[]{:S(2)}) %all-to-all-start.3) | async-done | bytes 2359328 | tf_op jit(solution)/shard_map/all_to_all | solution.py:932
  347.2 6.9 %all-to-all-start.4 = ((bf16[32,96,384]{2,1,0:T(8,128)(2,1)}), bf16[32,96,384]{2,1,0:T(8,128)(2,1)}, u32[]{:S(2)}, u32[]{:S(2)}) async-start(bf16[32,96,384]{2,1,0:T(8,128)(2,1)} %multiply.13.refs_4_), calls=%async_computation.4 | async-start | bytes 4718592 | tf_op jit(solution)/shard_map/all_to_all | solution.py:932
  360.7 4.7 %average.1 = bf16[96,256]{1,0:T(8,128)(2,1)} custom-call(f32[8,104,128]{2,1,0:T(8,128)} %get-tuple-element.52.refs_0_, f32[8,104,128]{2,1,0:T(8,128)} %get-tuple-element.53.refs_1_, f32[8,104,128]{2,1,0:T(8,128)} %get-tuple-element.54.refs_2_, f32[8,104,128]{2,1,0:T(8,128)} %get-tuple-element.55.refs_3_, f32[8,96,128]{2,1,0:T(8,128)} %copy.136.refs_4_, ...), custom_call_target="tpu_custom_call" | custom-call | flops 1000 | bytes 1000 | tf_op jit(solution)/shard_map/average/pallas_call | solution.py:764
  367.0 42.8 %all-to-all-done.4.refs_1_ = bf16[32,96,384]{2,1,0:T(8,128)(2,1)} async-done(((bf16[32,96,384]{2,1,0:T(8,128)(2,1)}), bf16[32,96,384]{2,1,0:T(8,128)(2,1)}, u32[]{:S(2)}, u32[]{:S(2)}) %all-to-all-start.4) | async-done | bytes 2359328 | tf_op jit(solution)/shard_map/all_to_all | solution.py:932
  409.8 12.9 %finish.1 = bf16[192,96,128]{2,1,0:T(8,128)(2,1)} custom-call(bf16[16,192,384]{2,1,0:T(8,128)(2,1)} %copy-done.2, bf16[32,96,384]{2,1,0:T(8,128)(2,1)} %all-to-all-done.4.refs_1_, bf16[64,96,128]{2,1,0:T(8,128)(2,1)} %get-tuple-element.56.refs_2_, bf16[128,96,128]{2,1,0:T(8,128)(2,1)} %get-tuple-element.57.refs_3_, ...), custom_call_target="tpu_custom_call" | custom-call | flops 1000 | bytes 1000 | tf_op jit(solution)/shard_map/finish/pallas_call | solution.py:832
  (158 shorter events, 55.1 us)
Async XLA Ops:
  0.6 17.7 %slice-start = ((bf16[64,576]{1,0:T(8,128)(2,1)}), bf16[64,32]{1,0:T(8,128)(2,1)S(1)}, s32[]{:S(2)}) async-start(bf16[64,576]{1,0:T(8,128)(2,1)} %param.14), calls=%async_computation.5 | async-start | bytes 32768 | tf_op jit(solution)/shard_map/slice | solution.py:903
  0.6 17.5 %copy-start.22 = (bf16[128,640]{1,0:T(8,128)(2,1)S(1)}, bf16[128,640]{1,0:T(8,128)(2,1)}, u32[]{:S(2)}) copy-start(bf16[128,640]{1,0:T(8,128)(2,1)} %param.18) | copy-start | bytes 491524
  0.7 32.5 %copy-start.21 = (bf16[1024,128]{1,0:T(8,128)(2,1)S(1)}, bf16[1024,128]{1,0:T(8,128)(2,1)}, u32[]{:S(2)}) copy-start(bf16[1024,128]{1,0:T(8,128)(2,1)} %param.15) | copy-start | bytes 786436
  6.4 30.3 %copy-start.9 = (bf16[4,96,32]{2,1,0:T(8,128)(2,1)}, bf16[4,96,32]{2,1,0:T(8,128)(2,1)S(1)}, u32[]{:S(2)}) copy-start(bf16[4,96,32]{2,1,0:T(8,128)(2,1)S(1)} %fusion.3.refs_8_) | copy-start | bytes 73732
  6.4 12.9 %collective-permute-start.10 = (bf16[4,96,32]{2,1,0:T(8,128)(2,1)S(1)}, bf16[4,96,32]{2,1,0:T(8,128)(2,1)S(1)}, u32[]{:S(2)}, u32[]{:S(2)}) collective-permute-start(bf16[4,96,32]{2,1,0:T(8,128)(2,1)S(1)} %fusion.3.refs_8_), channel_id=1, source_target_pairs={{0,8},{8,16},{16,24},{24,0},{1,9},{9,17},{17,25},{25,1},{2,10},{10... | collective-permute-start | bytes 73736 | tf_op jit(solution)/shard_map/ppermute | solution.py:917
  9.4 12.2 %collective-permute-start.8 = (bf16[4,96,32]{2,1,0:T(8,128)(2,1)S(1)}, bf16[4,96,32]{2,1,0:T(8,128)(2,1)S(1)}, u32[]{:S(2)}, u32[]{:S(2)}) collective-permute-start(bf16[4,96,32]{2,1,0:T(8,128)(2,1)S(1)} %fusion.3.refs_8_), channel_id=1, source_target_pairs={{0,24},{8,0},{16,8},{24,16},{1,25},{9,1},{17,9},{25,17},{2,26},{10... | collective-permute-start | bytes 73736 | tf_op jit(solution)/shard_map/ppermute | solution.py:917
  10.4 13.8 %collective-permute-start.9 = (bf16[4,96,32]{2,1,0:T(8,128)(2,1)S(1)}, bf16[4,96,32]{2,1,0:T(8,128)(2,1)S(1)}, u32[]{:S(2)}, u32[]{:S(2)}) collective-permute-start(bf16[4,96,32]{2,1,0:T(8,128)(2,1)S(1)} %fusion.3.refs_8_), channel_id=1, source_target_pairs={{0,16},{8,24},{16,0},{24,8},{1,17},{9,25},{17,1},{25,9},{2,18},{10... | collective-permute-start | bytes 73736 | tf_op jit(solution)/shard_map/ppermute | solution.py:917
  12.5 12.1 %collective-permute-start = (bf16[96,256]{1,0:T(8,128)(2,1)S(1)}, bf16[96,256]{1,0:T(8,128)(2,1)S(1)}, u32[]{:S(2)}, u32[]{:S(2)}) collective-permute-start(bf16[96,256]{1,0:T(8,128)(2,1)S(1)} %copy.109), channel_id=1, source_target_pairs={{0,0},{1,1},{2,8},{3,9},{4,16},{5,17},{6,24},{7,25},{8,2},{9,3},{1... | collective-permute-start | bytes 147464 | tf_op jit(solution)/shard_map/ppermute | solution.py:913
  13.1 14.3 %collective-permute-start.1 = (bf16[96,256]{1,0:T(8,128)(2,1)S(1)}, bf16[96,256]{1,0:T(8,128)(2,1)S(1)}, u32[]{:S(2)}, u32[]{:S(2)}) collective-permute-start(bf16[96,256]{1,0:T(8,128)(2,1)S(1)} %copy.109), channel_id=1, source_target_pairs={{0,7},{1,0},{2,15},{3,8},{4,23},{5,16},{6,31},{7,24},{8,1},{9,2},{... | collective-permute-start | bytes 147464 | tf_op jit(solution)/shard_map/ppermute | solution.py:913
  19.3 17.4 %copy-start.18 = (bf16[4,96,32]{2,1,0:T(8,128)(2,1)}, bf16[4,96,32]{2,1,0:T(8,128)(2,1)S(1)}, u32[]{:S(2)}) copy-start(bf16[4,96,32]{2,1,0:T(8,128)(2,1)S(1)} %collective-permute-done.10.refs_11_) | copy-start | bytes 73732
  19.3 8.3 %collective-permute-start.2 = (bf16[96,256]{1,0:T(8,128)(2,1)S(1)}, bf16[96,256]{1,0:T(8,128)(2,1)S(1)}, u32[]{:S(2)}, u32[]{:S(2)}) collective-permute-start(bf16[96,256]{1,0:T(8,128)(2,1)S(1)} %copy.109), channel_id=1, source_target_pairs={{0,6},{1,7},{2,14},{3,15},{4,22},{5,23},{6,30},{7,31},{8,0},{9,1},... | collective-permute-start | bytes 147464 | tf_op jit(solution)/shard_map/ppermute | solution.py:913
  21.6 15.1 %copy-start.19 = (bf16[4,96,32]{2,1,0:T(8,128)(2,1)}, bf16[4,96,32]{2,1,0:T(8,128)(2,1)S(1)}, u32[]{:S(2)}) copy-start(bf16[4,96,32]{2,1,0:T(8,128)(2,1)S(1)} %collective-permute-done.8.refs_9_) | copy-start | bytes 73732
  21.6 15.0 %collective-permute-start.3 = (bf16[96,256]{1,0:T(8,128)(2,1)S(1)}, bf16[96,256]{1,0:T(8,128)(2,1)S(1)}, u32[]{:S(2)}, u32[]{:S(2)}) collective-permute-start(bf16[96,256]{1,0:T(8,128)(2,1)S(1)} %copy.109), channel_id=1, source_target_pairs={{0,5},{1,6},{2,13},{3,14},{4,21},{5,22},{6,29},{7,30},{8,7},{9,0},... | collective-permute-start | bytes 147464 | tf_op jit(solution)/shard_map/ppermute | solution.py:913
  24.2 12.4 %collective-permute-start.4 = (bf16[96,256]{1,0:T(8,128)(2,1)S(1)}, bf16[96,256]{1,0:T(8,128)(2,1)S(1)}, u32[]{:S(2)}, u32[]{:S(2)}) collective-permute-start(bf16[96,256]{1,0:T(8,128)(2,1)S(1)} %copy.109), channel_id=1, source_target_pairs={{0,4},{1,5},{2,12},{3,13},{4,20},{5,21},{6,28},{7,29},{8,6},{9,7},... | collective-permute-start | bytes 147464 | tf_op jit(solution)/shard_map/ppermute | solution.py:913
  24.6 12.1 %collective-permute-start.5 = (bf16[96,256]{1,0:T(8,128)(2,1)S(1)}, bf16[96,256]{1,0:T(8,128)(2,1)S(1)}, u32[]{:S(2)}, u32[]{:S(2)}) collective-permute-start(bf16[96,256]{1,0:T(8,128)(2,1)S(1)} %copy.109), channel_id=1, source_target_pairs={{0,3},{1,4},{2,11},{3,12},{4,19},{5,20},{6,27},{7,28},{8,5},{9,6},... | collective-permute-start | bytes 147464 | tf_op jit(solution)/shard_map/ppermute | solution.py:913
  27.4 9.3 %collective-permute-start.6 = (bf16[96,256]{1,0:T(8,128)(2,1)S(1)}, bf16[96,256]{1,0:T(8,128)(2,1)S(1)}, u32[]{:S(2)}, u32[]{:S(2)}) collective-permute-start(bf16[96,256]{1,0:T(8,128)(2,1)S(1)} %copy.109), channel_id=1, source_target_pairs={{0,2},{1,3},{2,10},{3,11},{4,18},{5,19},{6,26},{7,27},{8,4},{9,5},... | collective-permute-start | bytes 147464 | tf_op jit(solution)/shard_map/ppermute | solution.py:913
  27.6 9.0 %collective-permute-start.7 = (bf16[96,256]{1,0:T(8,128)(2,1)S(1)}, bf16[96,256]{1,0:T(8,128)(2,1)S(1)}, u32[]{:S(2)}, u32[]{:S(2)}) collective-permute-start(bf16[96,256]{1,0:T(8,128)(2,1)S(1)} %copy.109), channel_id=1, source_target_pairs={{0,1},{1,2},{2,9},{3,10},{4,17},{5,18},{6,25},{7,26},{8,3},{9,4},{... | collective-permute-start | bytes 147464 | tf_op jit(solution)/shard_map/ppermute | solution.py:913
  55.4 43.5 %all-to-all-start = ((bf16[16,128,384]{2,1,0:T(8,128)(2,1)}), bf16[16,128,384]{2,1,0:T(8,128)(2,1)S(1)}, u32[]{:S(2)}, u32[]{:S(2)}) async-start(bf16[16,128,384]{2,1,0:T(8,128)(2,1)} %get-tuple-element.31), calls=%async_computation | async-start | bytes 3145728 | tf_op jit(solution)/shard_map/all_to_all | solution.py:932
  61.1 37.7 %collective-permute-start.11 = (bf16[16,64,384]{2,1,0:T(8,128)(2,1)S(1)}, bf16[16,64,384]{2,1,0:T(8,128)(2,1)S(1)}, u32[]{:S(2)}, u32[]{:S(2)}) collective-permute-start(bf16[16,64,384]{2,1,0:T(8,128)(2,1)S(1)} %copy-done.6), channel_id=1, source_target_pairs={{0,4},{4,0},{1,5},{5,1},{2,6},{6,2},{3,7},{7,3},{8,12},{12,8},{9,1... | collective-permute-start | bytes 2359304 | tf_op jit(solution)/shard_map/ppermute | solution.py:1025
  100.9 76.5 %all-to-all-start.1 = ((bf16[16,256,384]{2,1,0:T(8,128)(2,1)}), bf16[16,256,384]{2,1,0:T(8,128)(2,1)S(1)}, u32[]{:S(2)}, u32[]{:S(2)}) async-start(bf16[16,256,384]{2,1,0:T(8,128)(2,1)} %get-tuple-element.35), calls=%async_computation.1 | async-start | bytes 6291456 | tf_op jit(solution)/shard_map/all_to_all | solution.py:932
  105.0 83.6 %collective-permute-start.15 = (bf16[16,128,384]{2,1,0:T(8,128)(2,1)}, bf16[16,128,384]{2,1,0:T(8,128)(2,1)}, u32[]{:S(2)}, u32[]{:S(2)}) collective-permute-start(bf16[16,128,384]{2,1,0:T(8,128)(2,1)} %get-tuple-element.46), channel_id=1, source_target_pairs={{0,4},{4,0},{1,5},{5,1},{2,6},{6,2},{3,7},{7,3},{8,12},{12,8},{9,1... | collective-permute-start | bytes 4718600 | tf_op jit(solution)/shard_map/ppermute | solution.py:1025
  191.0 113.5 %all-to-all-start.2 = ((bf16[16,384,384]{2,1,0:T(8,128)(2,1)}), bf16[16,384,384]{2,1,0:T(8,128)(2,1)}, u32[]{:S(2)}, u32[]{:S(2)}) async-start(bf16[16,384,384]{2,1,0:T(8,128)(2,1)} %merge.3), calls=%async_computation.2 | async-start | bytes 9437184 | tf_op jit(solution)/shard_map/all_to_all | solution.py:932
  195.6 108.9 %collective-permute-start.16 = (bf16[4,768,384]{2,1,0:T(8,128)(2,1)}, bf16[4,768,384]{2,1,0:T(8,128)(2,1)}, u32[]{:S(2)}, u32[]{:S(2)}) collective-permute-start(bf16[4,768,384]{2,1,0:T(8,128)(2,1)} %get-tuple-element.49), channel_id=1, source_target_pairs={{0,4},{4,0},{1,5},{5,1},{2,6},{6,2},{3,7},{7,3},{8,12},{12,8},{9,1... | collective-permute-start | bytes 7077896 | tf_op jit(solution)/shard_map/ppermute | solution.py:1040
  195.7 38.9 %collective-permute-start.12 = (f32[8,104,128]{2,1,0:T(8,128)}, f32[8,104,128]{2,1,0:T(8,128)S(1)}, u32[]{:S(2)}, u32[]{:S(2)}) collective-permute-start(f32[8,104,128]{2,1,0:T(8,128)} %get-tuple-element.43), channel_id=1, source_target_pairs={{0,24},{8,0},{16,8},{24,16},{1,25},{9,1},{17,9},{25,17},{2,26},{10... | collective-permute-start | bytes 1277960 | tf_op jit(solution)/shard_map/ppermute | solution.py:977
  198.4 36.2 %collective-permute-start.13 = (f32[8,104,128]{2,1,0:T(8,128)}, f32[8,104,128]{2,1,0:T(8,128)S(1)}, u32[]{:S(2)}, u32[]{:S(2)}) collective-permute-start(f32[8,104,128]{2,1,0:T(8,128)} %get-tuple-element.44), channel_id=1, source_target_pairs={{0,16},{8,24},{16,0},{24,8},{1,17},{9,25},{17,1},{25,9},{2,18},{10... | collective-permute-start | bytes 1277960 | tf_op jit(solution)/shard_map/ppermute | solution.py:977
  198.9 45.4 %collective-permute-start.14 = (f32[8,104,128]{2,1,0:T(8,128)}, f32[8,104,128]{2,1,0:T(8,128)S(1)}, u32[]{:S(2)}, u32[]{:S(2)}) collective-permute-start(f32[8,104,128]{2,1,0:T(8,128)} %get-tuple-element.45), channel_id=1, source_target_pairs={{0,8},{8,16},{16,24},{24,0},{1,9},{9,17},{17,25},{25,1},{2,10},{10... | collective-permute-start | bytes 1277960 | tf_op jit(solution)/shard_map/ppermute | solution.py:977
  234.6 69.9 %copy-start.3 = (f32[8,104,128]{2,1,0:T(8,128)}, f32[8,104,128]{2,1,0:T(8,128)S(1)}, u32[]{:S(2)}) copy-start(f32[8,104,128]{2,1,0:T(8,128)S(1)} %collective-permute-done.12.refs_1_) | copy-start | bytes 1277956
  234.6 69.9 %copy-start.4 = (f32[8,104,128]{2,1,0:T(8,128)}, f32[8,104,128]{2,1,0:T(8,128)S(1)}, u32[]{:S(2)}) copy-start(f32[8,104,128]{2,1,0:T(8,128)S(1)} %collective-permute-done.13.refs_2_) | copy-start | bytes 1277956
  244.3 60.2 %copy-start.5 = (f32[8,104,128]{2,1,0:T(8,128)}, f32[8,104,128]{2,1,0:T(8,128)S(1)}, u32[]{:S(2)}) copy-start(f32[8,104,128]{2,1,0:T(8,128)S(1)} %collective-permute-done.14.refs_3_) | copy-start | bytes 1277956
  311.5 34.2 %all-to-all-start.3 = ((bf16[16,192,384]{2,1,0:T(8,128)(2,1)}), bf16[16,192,384]{2,1,0:T(8,128)(2,1)S(1)}, u32[]{:S(2)}, u32[]{:S(2)}) async-start(bf16[16,192,384]{2,1,0:T(8,128)(2,1)} %combine.1.refs_0_), calls=%async_computation.3 | async-start | bytes 4718592 | tf_op jit(solution)/shard_map/all_to_all | solution.py:932
  331.3 24.1 %copy-start.25 = (bf16[128,128]{1,0:T(8,128)(2,1)S(1)}, bf16[128,128]{1,0:T(8,128)(2,1)}, u32[]{:S(2)}) copy-start(bf16[128,128]{1,0:T(8,128)(2,1)} %param.19) | copy-start | bytes 98308
  347.2 62.6 %all-to-all-start.4 = ((bf16[32,96,384]{2,1,0:T(8,128)(2,1)}), bf16[32,96,384]{2,1,0:T(8,128)(2,1)}, u32[]{:S(2)}, u32[]{:S(2)}) async-start(bf16[32,96,384]{2,1,0:T(8,128)(2,1)} %multiply.13.refs_4_), calls=%async_computation.4 | async-start | bytes 4718592 | tf_op jit(solution)/shard_map/all_to_all | solution.py:932
  (21 other events, 78.6 us)

commit v13 on v12

--- a/solution.py
+++ b/solution.py
@@ -499,8 +499,26 @@
     tiles = lanes // LANES
     per_row = each * QUAD // cols
 
+    sorted_rows = stride == 8
+
+    def sort(src, carry):
+        start = 0
+        for recv in recvs:
+            for low in range(0, recv.shape[1], 64):
+                value = recv[src, low : low + 64].astype(F32)
+                values = exchange_rows([value[8 * i : 8 * i + 8] for i in range(8)])
+                for index, part in enumerate(values):
+                    at = index * each + start
+                    for t in range(tiles):
+                        flat_ref[src, t, at : at + 8] = part[:, t * LANES : (t + 1) * LANES]
+                start += 8
+        return carry
+
     @pl.when(channel == 0)
     def _():
+        if sorted_rows:
+            lax.fori_loop(0, row_count * pos_count, sort, 0)
+            return
         for src in range(row_count * pos_count):
             start = 0
             for recv in recvs:
@@ -511,12 +529,14 @@
                 start = end
 
     def block(row, group, index):
+        if sorted_rows:
+            place = pl.ds(pl.multiple_of(index * each, each), each)
+        else:
+            place = pl.ds(index, each, stride=stride)
         packed = []
         for p in range(4):
             src = row * pos_count + group * 4 + p
-            packed.append(
-                [flat_ref[src, t, pl.ds(index, each, stride=stride), :] for t in range(tiles)]
-            )
+            packed.append([flat_ref[src, t, place, :] for t in range(tiles)])
         return exchange_blocks(packed)
 
     for row in range(row_count):
@@ -778,17 +798,20 @@
     products = refs[:parts]
     mids = refs[parts : parts + chunks]
     normeds = refs[parts + chunks : parts + 2 * chunks]
-    gate_ref, weight_ref, out_ref = refs[parts + 2 * chunks : parts + 2 * chunks + 3]
-    flat = refs[parts + 2 * chunks + 3 :]
+    gate_ref, weight_ref, out_ref, tmp_ref = refs[parts + 2 * chunks :]
     quads = out_ref.shape[0] // QUAD
-    lanes = products[0].shape[2]
-    tiles = range(lanes // LANES)
-    for product, tmp in zip(products, flat):
+    total = tmp_ref.shape[0] // quads
+    first = 0
+    for product in products:
         sources, height, _ = product.shape
-        for src in range(sources):
-            value = product[src].astype(F32)
-            for t in tiles:
-                tmp[t, src * height : (src + 1) * height] = value[:, t * LANES : (t + 1) * LANES]
+        group = 8 // (height // quads)
+        for low in range(0, sources, group):
+            values = [product[src].astype(F32) for src in range(low, low + group)]
+            for b, value in enumerate(exchange_rows(values)):
+                for v in range(height // 8):
+                    start = (v * group + b) * total + first
+                    tmp_ref[start : start + 8] = value[8 * v : 8 * v + 8]
+            first += 8
 
     def rows(mid_ref, normed_ref):
         count, cols, wide = normed_ref.shape
@@ -800,18 +823,8 @@
             )
         )
         for m in range(quads):
-            pieces = []
-            for product, tmp in zip(products, flat):
-                sources, height, _ = product.shape
-                each = height // quads
-                for k in range(each):
-                    pieces.append(
-                        jnp.concatenate(
-                            [tmp[t, pl.ds(m * each + k, sources, stride=height), :] for t in tiles],
-                            axis=1,
-                        )
-                    )
-            normed = standardize_features(jnp.concatenate(pieces, axis=0), 0).astype(BF16)
+            product = tmp_ref[m * total : (m + 1) * total]
+            normed = standardize_features(product, 0).astype(BF16)
             out = lax.dot_general(normed, weight_ref[...], TN, preferred_element_type=F32)
             for a, value in enumerate(unpack_rows(out)):
                 i = QUAD * m + a
@@ -840,10 +853,7 @@
         + [whole(w_gate.shape), whole(w_final.shape)],
         out_specs=pl.BlockSpec((quads * QUAD, cols, wide), lambda i: (i, 0, 0)),
         out_shape=jax.ShapeDtypeStruct((total * QUAD, cols, wide), BF16),
-        scratch_shapes=[
-            pltpu.VMEM((lanes // LANES, part.shape[0] * quads * each, LANES), F32)
-            for part, each in zip(products, heights)
-        ],
+        scratch_shapes=[pltpu.VMEM((quads * w_final.shape[0], lanes), F32)],
         compiler_params=params(),
         cost_estimate=LIGHT,
         name="finish",
@@ -1000,7 +1010,6 @@
         logits = logit(live_rows, normeds, w_logit, ())
         parts = partial_average(place, logits, lefts, w_value)
         parts = gather_parts(fence(parts, (last,)))
-        orders = [(0, CTRI, devices)]
     else:
         cut = CTRI // 2
         row_chunks = [rows // 3, rows - rows // 3]
@@ -1046,21 +1055,14 @@
         right = right.reshape(right.shape[0], -1, right.shape[-1])
         last = multiply(left, right, (), *shape_of[1:])
         returned.append(exchange(last, AXES))
-        orders = [(0, cut, group), (cut, CTRI, devices)]
     parts = fence(parts, (last,))
     aligned = average(parts, sequence_gate, align, w_mean)
     alignment_updated_embedding = jnp.transpose(
         aligned.reshape(module_number, seq_each, feature_count), (1, 0, 2)
     )
-    w_final = jnp.concatenate(
-        [
-            jnp.transpose(
-                trimul_final_matrix[low:high].reshape(sources, -1, wide), (1, 0, 2)
-            ).reshape(-1, wide)
-            for low, high, sources in orders
-        ]
+    pair_output = finish(
+        returned, mids, normeds, trimul_matrices[:, 4 * CTRI :], trimul_final_matrix
     )
-    pair_output = finish(returned, mids, normeds, trimul_matrices[:, 4 * CTRI :], w_final)
     return (alignment_updated_embedding, pair_output)
 
 

time: 425 us -> 425 us (level)
  transfers between devices with their start and end apart: 22 -> 22, of which waited for: 7 -> 7; matrix products, arithmetic and copies ran while one was open for 5% -> 5% of each run, Pallas kernels for 20% -> 21%
where the time goes in v13:
time: 425 us; the launch traced here: 423 us
  waiting for transfers between devices  209 us (49%)
  Pallas kernels  125 us (29%)
  starting transfers between devices  52.3 us (12%)
  local copies, waits for them, and re-layouts  25.2 us (6%)
  other arithmetic  8.19 us (2%)
    all_to_all x5, waiting for transfers between devices, exchange(): return lax.all_to_all(block, axes, split_axis=0, concat_axis=0, tiled=True)  98.7 us
    ppermute x1, waiting for transfers between devices, on_device(): partial = lax.ppermute(theirs, 'half', swap)  60.2 us
    ppermute x3, waiting for transfers between devices, gather_parts(): gathered.append(lax.ppermute(parts[t], 'row', pairs))  44.8 us
    pallas_call x2, Pallas kernels, front(): pl.pallas_call(functools.partial(front_kernel, row_count=len(rights), col...  30.6 us
    all_to_all x5, starting transfers between devices, exchange(): return lax.all_to_all(block, axes, split_axis=0, concat_axis=0, tiled=True)  25 us
    pallas_call x6, Pallas kernels, project(): pl.pallas_call(functools.partial(project_kernel, first_row=first_row), gr...  24.1 us
    ppermute x8, starting transfers between devices, on_device(): lefts.append(lax.ppermute(own_rows, AXES, pairs))  15.4 us
    pallas_call x1, Pallas kernels, finish(): pl.pallas_call(functools.partial(finish_kernel, parts=len(products), step...  11.8 us
  transfers between devices with their start and end apart: 22, of which 7 were waited for; matrix products, arithmetic and copies ran while one was open for 5% of the time, Pallas kernels for 21%

profile of v13, /device:TPU:0, one launch (start us, length us, event | category | flops | bytes accessed | tf_op | source)
XLA Modules:
  0.0 422.6 jit_solution(3045829514479469703)
XLA Ops:
  6.4 3.0 collective-permute-start.10
  13.1 3.5 collective-permute-start.1
  27.7 3.5 collective-permute-start.7
  37.9 11.3 %front.2 = (bf16[64,96,128]{2,1,0:T(8,128)(2,1)}, bf16[64,96,128]{2,1,0:T(8,128)(2,1)}) custom-call(s32[2]{0:T(128)} %pad_add_fusion.place_ref, bf16[96,256]{1,0:T(8,128)(2,1)} %copy-done.10, bf16[96,256]{1,0:T(8,128)(2,1)} %copy-done.11, bf16[96,256]{1,0:T(8,128)(2,1)} %copy-done.12, bf16[96,256]{1,0:T(8,128)(2,1)} %copy-done.13, ...), custom_call_target="tpu_custom_call" | custom-call | flops 1000 | bytes 1000 | tf_op jit(solution)/shard_map/front/pallas_call | solution.py:193
  49.2 3.2 project.7.refs_1_
  52.4 2.9 project.6.refs_0_
  55.3 5.7 %all-to-all-start = ((bf16[16,128,384]{2,1,0:T(8,128)(2,1)}), bf16[16,128,384]{2,1,0:T(8,128)(2,1)S(1)}, u32[]{:S(2)}, u32[]{:S(2)}) async-start(bf16[16,128,384]{2,1,0:T(8,128)(2,1)} %get-tuple-element.31), calls=%async_computation | async-start | bytes 3145728 | tf_op jit(solution)/shard_map/all_to_all | solution.py:942
  61.1 19.3 %front.3 = (bf16[128,96,128]{2,1,0:T(8,128)(2,1)}, bf16[128,96,128]{2,1,0:T(8,128)(2,1)}) custom-call(s32[2]{0:T(128)} %pad_add_fusion.place_ref, bf16[96,256]{1,0:T(8,128)(2,1)} %copy-done.10, bf16[96,256]{1,0:T(8,128)(2,1)} %copy-done.11, bf16[96,256]{1,0:T(8,128)(2,1)} %copy-done.12, bf16[96,256]{1,0:T(8,128)(2,1)} %copy-done.13, ...), custom_call_target="tpu_custom_call" | custom-call | flops 1000 | bytes 1000 | tf_op jit(solution)/shard_map/front/pallas_call | solution.py:193
  80.4 5.3 %project.9.refs_1_ = bf16[16,256,384]{2,1,0:T(8,128)(2,1)} custom-call(f32[192]{0:T(256)} %dynamic_slice.22.live_ref, bf16[128,96,128]{2,1,0:T(8,128)(2,1)} %get-tuple-element.33.normed_ref.refs_1_.refs_5_, f32[1,384]{1,0:T(1,128)} %broadcast_in_dim.7.cols_ref, bf16[256,128]{1,0:T(8,128)(2,1)} %bitcast.59), custom_call_target="tpu_custom_call" | custom-call | flops 1000 | bytes 1000 | tf_op jit(solution)/shard_map/project/pallas_call | solution.py:289
  85.8 4.8 %project.8.refs_0_ = bf16[16,128,384]{2,1,0:T(8,128)(2,1)} custom-call(f32[192]{0:T(256)} %dynamic_slice.22.live_ref, bf16[128,96,128]{2,1,0:T(8,128)(2,1)} %get-tuple-element.33.normed_ref.refs_1_.refs_5_, f32[1,384]{1,0:T(1,128)} %broadcast_in_dim.7.cols_ref, bf16[128,128]{1,0:T(8,128)(2,1)} %bitcast.63), custom_call_target="tpu_custom_call" | custom-call | flops 1000 | bytes 1000 | tf_op jit(solution)/shard_map/project/pallas_call | solution.py:289
  90.6 2.9 project.10.refs_3_.refs_0_
  93.5 5.3 %collective-permute-done.11.refs_4_.refs_2_ = bf16[16,64,384]{2,1,0:T(8,128)(2,1)S(1)} collective-permute-done((bf16[16,64,384]{2,1,0:T(8,128)(2,1)S(1)}, bf16[16,64,384]{2,1,0:T(8,128)(2,1)S(1)}, u32[]{:S(2)}, u32[]{:S(2)}) %collective-permute-start.11) | collective-permute-done | bytes 786464 | tf_op jit(solution)/shard_map/ppermute | solution.py:1034
  100.8 4.1 all-to-all-start.1
  113.4 4.9 %project.11.refs_4_.refs_1_ = bf16[16,128,384]{2,1,0:T(8,128)(2,1)} custom-call(f32[192]{0:T(256)} %dynamic_slice.22.live_ref, bf16[128,96,128]{2,1,0:T(8,128)(2,1)} %get-tuple-element.33.normed_ref.refs_1_.refs_5_, f32[1,384]{1,0:T(1,128)} %broadcast_in_dim.7.cols_ref, bf16[128,128]{1,0:T(8,128)(2,1)} %get-tuple-element.36.weight_ref), custom_call_target="tpu_custom_call" | custom-call | flops 1000 | bytes 1000 | tf_op jit(solution)/shard_map/project/pallas_call | solution.py:289
  118.3 9.5 %logit.1.logit_ref = f32[192,8,96]{2,1,0:T(8,128)} custom-call(f32[192]{0:T(256)} %dynamic_slice.22.live_ref, bf16[64,96,128]{2,1,0:T(8,128)(2,1)} %get-tuple-element.30.normed_ref.refs_0_.refs_4_, bf16[128,96,128]{2,1,0:T(8,128)(2,1)} %get-tuple-element.33.normed_ref.refs_1_.refs_5_, bf16[8,128]{1,0:T(8,128)(2,1)} %bitcast.75, ...), custom_call_target="tpu_custom_call" | custom-call | flops 1000 | bytes 1000 | tf_op jit(solution)/shard_map/logit/pallas_call | solution.py:341
  127.8 4.6 %merge.2.refs_3_.refs_1_ = bf16[16,384,384]{2,1,0:T(8,128)(2,1)} custom-call(bf16[16,64,384]{2,1,0:T(8,128)(2,1)} %project.10.refs_3_.refs_0_, bf16[16,128,384]{2,1,0:T(8,128)(2,1)} %project.11.refs_4_.refs_1_, bf16[16,64,384]{2,1,0:T(8,128)(2,1)} %copy-done.7), custom_call_target="tpu_custom_call" | custom-call | flops 1000 | bytes 1000 | tf_op jit(solution)/shard_map/merge/pallas_call | solution.py:688
  132.4 4.2 %partial.1 = (f32[8,104,128]{2,1,0:T(8,128)}, f32[8,104,128]{2,1,0:T(8,128)}, f32[8,104,128]{2,1,0:T(8,128)}, f32[8,104,128]{2,1,0:T(8,128)}) custom-call(s32[2]{0:T(128)} %pad_add_fusion.place_ref, f32[192,8,96]{2,1,0:T(8,128)} %logit.1.logit_ref, bf16[96,256]{1,0:T(8,128)(2,1)} %copy-done.10, bf16[96,256]{1,0:T(8,128)(2,1)} %copy-done.11, ...), custom_call_target="tpu_custom_call" | custom-call | flops 1000 | bytes 1000 | tf_op jit(solution)/shard_map/partial/pallas_call | solution.py:739
  136.7 40.6 %all-to-all-done.1.refs_1_ = bf16[16,256,384]{2,1,0:T(8,128)(2,1)S(1)} async-done(((bf16[16,256,384]{2,1,0:T(8,128)(2,1)}), bf16[16,256,384]{2,1,0:T(8,128)(2,1)S(1)}, u32[]{:S(2)}, u32[]{:S(2)}) %all-to-all-start.1) | async-done | bytes 3145760 | tf_op jit(solution)/shard_map/all_to_all | solution.py:942
  178.9 10.7 %assemble_half.1 = (bf16[4,768,384]{2,1,0:T(8,128)(2,1)}, bf16[4,384,384]{2,1,0:T(8,128)(2,1)}, bf16[4,768,384]{2,1,0:T(8,128)(2,1)}) custom-call(s32[1]{0:T(128)} %bitcast.half_ref, bf16[16,128,384]{2,1,0:T(8,128)(2,1)} %copy-done, bf16[16,256,384]{2,1,0:T(8,128)(2,1)} %copy-done.1, f32[8,104,128]{2,1,0:T(8,128)} %get-tuple-element.37.refs_2_.refs_1_, ...), custom_call_target="tpu_custom_call" | custom-call | flops 1000 | bytes 1000 | tf_op jit(solution)/shard_map/assemble_half/pallas_call | solution.py:587
  191.9 4.6 %all-to-all-start.2 = ((bf16[16,384,384]{2,1,0:T(8,128)(2,1)}), bf16[16,384,384]{2,1,0:T(8,128)(2,1)}, u32[]{:S(2)}, u32[]{:S(2)}) async-start(bf16[16,384,384]{2,1,0:T(8,128)(2,1)} %merge.3), calls=%async_computation.2 | async-start | bytes 9437184 | tf_op jit(solution)/shard_map/all_to_all | solution.py:942
  200.5 35.0 %collective-permute-done.12.refs_1_ = f32[8,104,128]{2,1,0:T(8,128)S(1)} collective-permute-done((f32[8,104,128]{2,1,0:T(8,128)}, f32[8,104,128]{2,1,0:T(8,128)S(1)}, u32[]{:S(2)}, u32[]{:S(2)}) %collective-permute-start.12) | collective-permute-done | bytes 426016 | tf_op jit(solution)/shard_map/ppermute | solution.py:987
  235.6 9.7 %collective-permute-done.14.refs_3_ = f32[8,104,128]{2,1,0:T(8,128)S(1)} collective-permute-done((f32[8,104,128]{2,1,0:T(8,128)}, f32[8,104,128]{2,1,0:T(8,128)S(1)}, u32[]{:S(2)}, u32[]{:S(2)}) %collective-permute-start.14) | collective-permute-done | bytes 426016 | tf_op jit(solution)/shard_map/ppermute | solution.py:987
  245.3 60.2 %collective-permute-done.16.recv_ref = bf16[4,768,384]{2,1,0:T(8,128)(2,1)} collective-permute-done((bf16[4,768,384]{2,1,0:T(8,128)(2,1)}, bf16[4,768,384]{2,1,0:T(8,128)(2,1)}, u32[]{:S(2)}, u32[]{:S(2)}) %collective-permute-start.16) | collective-permute-done | bytes 2359328 | tf_op jit(solution)/shard_map/ppermute | solution.py:1049
  305.5 6.9 %combine.1.refs_0_ = bf16[16,192,384]{2,1,0:T(8,128)(2,1)} custom-call(bf16[4,768,384]{2,1,0:T(8,128)(2,1)} %get-tuple-element.47.refs_2_.left_ref, bf16[4,384,384]{2,1,0:T(8,128)(2,1)} %get-tuple-element.48.own_ref, bf16[4,768,384]{2,1,0:T(8,128)(2,1)} %collective-permute-done.16.recv_ref, bf16[16,384,384]{2,1,0:T(8,128)(2,1)} %all-to-all-done.2.refs_0_.recv_ref, ...), custom_call_target="tpu_custom_call" | custom-call | flops 1000 | bytes 1000 | tf_op jit(solution)/shard_map/combine/pallas_call | solution.py:654
  312.4 3.7 all-to-all-start.3
  316.2 8.8 %assemble.1 = (bf16[2,16,48,768]{3,2,1,0:T(8,128)(2,1)}, bf16[2,4,1,192,768]{4,3,2,1,0:T(8,128)(2,1)}) custom-call(bf16[16,384,384]{2,1,0:T(8,128)(2,1)} %all-to-all-done.2.refs_0_.recv_ref, bf16[16,192,384]{2,1,0:T(8,128)(2,1)} %combine.1.refs_0_), custom_call_target="tpu_custom_call" | custom-call | flops 1000 | bytes 1000 | tf_op jit(solution)/shard_map/assemble/pallas_call | solution.py:407
  325.0 7.1 %multiply.13.refs_4_ = bf16[32,96,384]{2,1,0:T(8,128)(2,1)} custom-call(bf16[2,16,48,768]{3,2,1,0:T(8,128)(2,1)} %get-tuple-element.50.left_ref, bf16[2,768,768]{2,1,0:T(8,128)(2,1)} %bitcast.53), custom_call_target="tpu_custom_call" | custom-call | flops 1000 | bytes 1000 | tf_op jit(solution)/shard_map/multiply/pallas_call | solution.py:472
  332.1 14.6 %all-to-all-done.3.refs_0_ = bf16[16,192,384]{2,1,0:T(8,128)(2,1)S(1)} async-done(((bf16[16,192,384]{2,1,0:T(8,128)(2,1)}), bf16[16,192,384]{2,1,0:T(8,128)(2,1)S(1)}, u32[]{:S(2)}, u32[]{:S(2)}) %all-to-all-start.3) | async-done | bytes 2359328 | tf_op jit(solution)/shard_map/all_to_all | solution.py:942
  348.1 6.9 %all-to-all-start.4 = ((bf16[32,96,384]{2,1,0:T(8,128)(2,1)}), bf16[32,96,384]{2,1,0:T(8,128)(2,1)}, u32[]{:S(2)}, u32[]{:S(2)}) async-start(bf16[32,96,384]{2,1,0:T(8,128)(2,1)} %multiply.13.refs_4_), calls=%async_computation.4 | async-start | bytes 4718592 | tf_op jit(solution)/shard_map/all_to_all | solution.py:942
  361.0 4.7 %average.1 = bf16[96,256]{1,0:T(8,128)(2,1)} custom-call(f32[8,104,128]{2,1,0:T(8,128)} %get-tuple-element.52.refs_0_, f32[8,104,128]{2,1,0:T(8,128)} %get-tuple-element.53.refs_1_, f32[8,104,128]{2,1,0:T(8,128)} %get-tuple-element.54.refs_2_, f32[8,104,128]{2,1,0:T(8,128)} %get-tuple-element.55.refs_3_, f32[8,96,128]{2,1,0:T(8,128)} %copy.130.refs_4_, ...), custom_call_target="tpu_custom_call" | custom-call | flops 1000 | bytes 1000 | tf_op jit(solution)/shard_map/average/pallas_call | solution.py:784
  367.3 43.5 %all-to-all-done.4.refs_1_ = bf16[32,96,384]{2,1,0:T(8,128)(2,1)} async-done(((bf16[32,96,384]{2,1,0:T(8,128)(2,1)}), bf16[32,96,384]{2,1,0:T(8,128)(2,1)}, u32[]{:S(2)}, u32[]{:S(2)}) %all-to-all-start.4) | async-done | bytes 2359328 | tf_op jit(solution)/shard_map/all_to_all | solution.py:942
  410.8 11.8 %finish.1 = bf16[192,96,128]{2,1,0:T(8,128)(2,1)} custom-call(bf16[16,192,384]{2,1,0:T(8,128)(2,1)} %copy-done.2, bf16[32,96,384]{2,1,0:T(8,128)(2,1)} %all-to-all-done.4.refs_1_, bf16[64,96,128]{2,1,0:T(8,128)(2,1)} %get-tuple-element.56.refs_2_, bf16[128,96,128]{2,1,0:T(8,128)(2,1)} %get-tuple-element.57.refs_3_, ...), custom_call_target="tpu_custom_call" | custom-call | flops 1000 | bytes 1000 | tf_op jit(solution)/shard_map/finish/pallas_call | solution.py:845
  (152 shorter events, 54.4 us)
Async XLA Ops:
  0.6 17.7 %slice-start = ((bf16[64,576]{1,0:T(8,128)(2,1)}), bf16[64,32]{1,0:T(8,128)(2,1)S(1)}, s32[]{:S(2)}) async-start(bf16[64,576]{1,0:T(8,128)(2,1)} %param.14), calls=%async_computation.5 | async-start | bytes 32768 | tf_op jit(solution)/shard_map/slice | solution.py:913
  0.6 17.5 %copy-start.22 = (bf16[128,640]{1,0:T(8,128)(2,1)S(1)}, bf16[128,640]{1,0:T(8,128)(2,1)}, u32[]{:S(2)}) copy-start(bf16[128,640]{1,0:T(8,128)(2,1)} %param.18) | copy-start | bytes 491524
  0.7 32.4 %copy-start.21 = (bf16[1024,128]{1,0:T(8,128)(2,1)S(1)}, bf16[1024,128]{1,0:T(8,128)(2,1)}, u32[]{:S(2)}) copy-start(bf16[1024,128]{1,0:T(8,128)(2,1)} %param.15) | copy-start | bytes 786436
  6.4 30.3 %copy-start.9 = (bf16[4,96,32]{2,1,0:T(8,128)(2,1)}, bf16[4,96,32]{2,1,0:T(8,128)(2,1)S(1)}, u32[]{:S(2)}) copy-start(bf16[4,96,32]{2,1,0:T(8,128)(2,1)S(1)} %fusion.3.refs_8_) | copy-start | bytes 73732
  6.4 12.9 %collective-permute-start.10 = (bf16[4,96,32]{2,1,0:T(8,128)(2,1)S(1)}, bf16[4,96,32]{2,1,0:T(8,128)(2,1)S(1)}, u32[]{:S(2)}, u32[]{:S(2)}) collective-permute-start(bf16[4,96,32]{2,1,0:T(8,128)(2,1)S(1)} %fusion.3.refs_8_), channel_id=1, source_target_pairs={{0,8},{8,16},{16,24},{24,0},{1,9},{9,17},{17,25},{25,1},{2,10},{10... | collective-permute-start | bytes 73736 | tf_op jit(solution)/shard_map/ppermute | solution.py:927
  9.4 12.2 %collective-permute-start.8 = (bf16[4,96,32]{2,1,0:T(8,128)(2,1)S(1)}, bf16[4,96,32]{2,1,0:T(8,128)(2,1)S(1)}, u32[]{:S(2)}, u32[]{:S(2)}) collective-permute-start(bf16[4,96,32]{2,1,0:T(8,128)(2,1)S(1)} %fusion.3.refs_8_), channel_id=1, source_target_pairs={{0,24},{8,0},{16,8},{24,16},{1,25},{9,1},{17,9},{25,17},{2,26},{10... | collective-permute-start | bytes 73736 | tf_op jit(solution)/shard_map/ppermute | solution.py:927
  10.4 13.8 %collective-permute-start.9 = (bf16[4,96,32]{2,1,0:T(8,128)(2,1)S(1)}, bf16[4,96,32]{2,1,0:T(8,128)(2,1)S(1)}, u32[]{:S(2)}, u32[]{:S(2)}) collective-permute-start(bf16[4,96,32]{2,1,0:T(8,128)(2,1)S(1)} %fusion.3.refs_8_), channel_id=1, source_target_pairs={{0,16},{8,24},{16,0},{24,8},{1,17},{9,25},{17,1},{25,9},{2,18},{10... | collective-permute-start | bytes 73736 | tf_op jit(solution)/shard_map/ppermute | solution.py:927
  12.5 12.1 %collective-permute-start = (bf16[96,256]{1,0:T(8,128)(2,1)S(1)}, bf16[96,256]{1,0:T(8,128)(2,1)S(1)}, u32[]{:S(2)}, u32[]{:S(2)}) collective-permute-start(bf16[96,256]{1,0:T(8,128)(2,1)S(1)} %copy.103), channel_id=1, source_target_pairs={{0,0},{1,1},{2,8},{3,9},{4,16},{5,17},{6,24},{7,25},{8,2},{9,3},{1... | collective-permute-start | bytes 147464 | tf_op jit(solution)/shard_map/ppermute | solution.py:923
  13.1 14.3 %collective-permute-start.1 = (bf16[96,256]{1,0:T(8,128)(2,1)S(1)}, bf16[96,256]{1,0:T(8,128)(2,1)S(1)}, u32[]{:S(2)}, u32[]{:S(2)}) collective-permute-start(bf16[96,256]{1,0:T(8,128)(2,1)S(1)} %copy.103), channel_id=1, source_target_pairs={{0,7},{1,0},{2,15},{3,8},{4,23},{5,16},{6,31},{7,24},{8,1},{9,2},{... | collective-permute-start | bytes 147464 | tf_op jit(solution)/shard_map/ppermute | solution.py:923
  19.3 17.3 %copy-start.18 = (bf16[4,96,32]{2,1,0:T(8,128)(2,1)}, bf16[4,96,32]{2,1,0:T(8,128)(2,1)S(1)}, u32[]{:S(2)}) copy-start(bf16[4,96,32]{2,1,0:T(8,128)(2,1)S(1)} %collective-permute-done.10.refs_11_) | copy-start | bytes 73732
  19.3 8.3 %collective-permute-start.2 = (bf16[96,256]{1,0:T(8,128)(2,1)S(1)}, bf16[96,256]{1,0:T(8,128)(2,1)S(1)}, u32[]{:S(2)}, u32[]{:S(2)}) collective-permute-start(bf16[96,256]{1,0:T(8,128)(2,1)S(1)} %copy.103), channel_id=1, source_target_pairs={{0,6},{1,7},{2,14},{3,15},{4,22},{5,23},{6,30},{7,31},{8,0},{9,1},... | collective-permute-start | bytes 147464 | tf_op jit(solution)/shard_map/ppermute | solution.py:923
  21.6 15.1 %copy-start.19 = (bf16[4,96,32]{2,1,0:T(8,128)(2,1)}, bf16[4,96,32]{2,1,0:T(8,128)(2,1)S(1)}, u32[]{:S(2)}) copy-start(bf16[4,96,32]{2,1,0:T(8,128)(2,1)S(1)} %collective-permute-done.8.refs_9_) | copy-start | bytes 73732
  21.6 15.0 %collective-permute-start.3 = (bf16[96,256]{1,0:T(8,128)(2,1)S(1)}, bf16[96,256]{1,0:T(8,128)(2,1)S(1)}, u32[]{:S(2)}, u32[]{:S(2)}) collective-permute-start(bf16[96,256]{1,0:T(8,128)(2,1)S(1)} %copy.103), channel_id=1, source_target_pairs={{0,5},{1,6},{2,13},{3,14},{4,21},{5,22},{6,29},{7,30},{8,7},{9,0},... | collective-permute-start | bytes 147464 | tf_op jit(solution)/shard_map/ppermute | solution.py:923
  24.3 12.4 %copy-start.20 = (bf16[4,96,32]{2,1,0:T(8,128)(2,1)}, bf16[4,96,32]{2,1,0:T(8,128)(2,1)S(1)}, u32[]{:S(2)}) copy-start(bf16[4,96,32]{2,1,0:T(8,128)(2,1)S(1)} %collective-permute-done.9.refs_10_) | copy-start | bytes 73732
  24.3 12.3 %collective-permute-start.4 = (bf16[96,256]{1,0:T(8,128)(2,1)S(1)}, bf16[96,256]{1,0:T(8,128)(2,1)S(1)}, u32[]{:S(2)}, u32[]{:S(2)}) collective-permute-start(bf16[96,256]{1,0:T(8,128)(2,1)S(1)} %copy.103), channel_id=1, source_target_pairs={{0,4},{1,5},{2,12},{3,13},{4,20},{5,21},{6,28},{7,29},{8,6},{9,7},... | collective-permute-start | bytes 147464 | tf_op jit(solution)/shard_map/ppermute | solution.py:923
  24.6 12.0 %collective-permute-start.5 = (bf16[96,256]{1,0:T(8,128)(2,1)S(1)}, bf16[96,256]{1,0:T(8,128)(2,1)S(1)}, u32[]{:S(2)}, u32[]{:S(2)}) collective-permute-start(bf16[96,256]{1,0:T(8,128)(2,1)S(1)} %copy.103), channel_id=1, source_target_pairs={{0,3},{1,4},{2,11},{3,12},{4,19},{5,20},{6,27},{7,28},{8,5},{9,6},... | collective-permute-start | bytes 147464 | tf_op jit(solution)/shard_map/ppermute | solution.py:923
  27.4 9.2 %collective-permute-start.6 = (bf16[96,256]{1,0:T(8,128)(2,1)S(1)}, bf16[96,256]{1,0:T(8,128)(2,1)S(1)}, u32[]{:S(2)}, u32[]{:S(2)}) collective-permute-start(bf16[96,256]{1,0:T(8,128)(2,1)S(1)} %copy.103), channel_id=1, source_target_pairs={{0,2},{1,3},{2,10},{3,11},{4,18},{5,19},{6,26},{7,27},{8,4},{9,5},... | collective-permute-start | bytes 147464 | tf_op jit(solution)/shard_map/ppermute | solution.py:923
  27.7 9.0 %collective-permute-start.7 = (bf16[96,256]{1,0:T(8,128)(2,1)S(1)}, bf16[96,256]{1,0:T(8,128)(2,1)S(1)}, u32[]{:S(2)}, u32[]{:S(2)}) collective-permute-start(bf16[96,256]{1,0:T(8,128)(2,1)S(1)} %copy.103), channel_id=1, source_target_pairs={{0,1},{1,2},{2,9},{3,10},{4,17},{5,18},{6,25},{7,26},{8,3},{9,4},{... | collective-permute-start | bytes 147464 | tf_op jit(solution)/shard_map/ppermute | solution.py:923
  55.3 43.5 %all-to-all-start = ((bf16[16,128,384]{2,1,0:T(8,128)(2,1)}), bf16[16,128,384]{2,1,0:T(8,128)(2,1)S(1)}, u32[]{:S(2)}, u32[]{:S(2)}) async-start(bf16[16,128,384]{2,1,0:T(8,128)(2,1)} %get-tuple-element.31), calls=%async_computation | async-start | bytes 3145728 | tf_op jit(solution)/shard_map/all_to_all | solution.py:942
  61.1 37.7 %collective-permute-start.11 = (bf16[16,64,384]{2,1,0:T(8,128)(2,1)S(1)}, bf16[16,64,384]{2,1,0:T(8,128)(2,1)S(1)}, u32[]{:S(2)}, u32[]{:S(2)}) collective-permute-start(bf16[16,64,384]{2,1,0:T(8,128)(2,1)S(1)} %copy-done.6), channel_id=1, source_target_pairs={{0,4},{4,0},{1,5},{5,1},{2,6},{6,2},{3,7},{7,3},{8,12},{12,8},{9,1... | collective-permute-start | bytes 2359304 | tf_op jit(solution)/shard_map/ppermute | solution.py:1034
  100.8 76.5 %all-to-all-start.1 = ((bf16[16,256,384]{2,1,0:T(8,128)(2,1)}), bf16[16,256,384]{2,1,0:T(8,128)(2,1)S(1)}, u32[]{:S(2)}, u32[]{:S(2)}) async-start(bf16[16,256,384]{2,1,0:T(8,128)(2,1)} %get-tuple-element.35), calls=%async_computation.1 | async-start | bytes 6291456 | tf_op jit(solution)/shard_map/all_to_all | solution.py:942
  105.0 84.6 %collective-permute-start.15 = (bf16[16,128,384]{2,1,0:T(8,128)(2,1)}, bf16[16,128,384]{2,1,0:T(8,128)(2,1)}, u32[]{:S(2)}, u32[]{:S(2)}) collective-permute-start(bf16[16,128,384]{2,1,0:T(8,128)(2,1)} %get-tuple-element.46), channel_id=1, source_target_pairs={{0,4},{4,0},{1,5},{5,1},{2,6},{6,2},{3,7},{7,3},{8,12},{12,8},{9,1... | collective-permute-start | bytes 4718600 | tf_op jit(solution)/shard_map/ppermute | solution.py:1034
  191.9 113.5 %all-to-all-start.2 = ((bf16[16,384,384]{2,1,0:T(8,128)(2,1)}), bf16[16,384,384]{2,1,0:T(8,128)(2,1)}, u32[]{:S(2)}, u32[]{:S(2)}) async-start(bf16[16,384,384]{2,1,0:T(8,128)(2,1)} %merge.3), calls=%async_computation.2 | async-start | bytes 9437184 | tf_op jit(solution)/shard_map/all_to_all | solution.py:942
  196.5 108.9 %collective-permute-start.16 = (bf16[4,768,384]{2,1,0:T(8,128)(2,1)}, bf16[4,768,384]{2,1,0:T(8,128)(2,1)}, u32[]{:S(2)}, u32[]{:S(2)}) collective-permute-start(bf16[4,768,384]{2,1,0:T(8,128)(2,1)} %get-tuple-element.49), channel_id=1, source_target_pairs={{0,4},{4,0},{1,5},{5,1},{2,6},{6,2},{3,7},{7,3},{8,12},{12,8},{9,1... | collective-permute-start | bytes 7077896 | tf_op jit(solution)/shard_map/ppermute | solution.py:1049
  196.6 38.9 %collective-permute-start.12 = (f32[8,104,128]{2,1,0:T(8,128)}, f32[8,104,128]{2,1,0:T(8,128)S(1)}, u32[]{:S(2)}, u32[]{:S(2)}) collective-permute-start(f32[8,104,128]{2,1,0:T(8,128)} %get-tuple-element.43), channel_id=1, source_target_pairs={{0,24},{8,0},{16,8},{24,16},{1,25},{9,1},{17,9},{25,17},{2,26},{10... | collective-permute-start | bytes 1277960 | tf_op jit(solution)/shard_map/ppermute | solution.py:987
  199.4 36.2 %collective-permute-start.13 = (f32[8,104,128]{2,1,0:T(8,128)}, f32[8,104,128]{2,1,0:T(8,128)S(1)}, u32[]{:S(2)}, u32[]{:S(2)}) collective-permute-start(f32[8,104,128]{2,1,0:T(8,128)} %get-tuple-element.44), channel_id=1, source_target_pairs={{0,16},{8,24},{16,0},{24,8},{1,17},{9,25},{17,1},{25,9},{2,18},{10... | collective-permute-start | bytes 1277960 | tf_op jit(solution)/shard_map/ppermute | solution.py:987
  199.9 45.4 %collective-permute-start.14 = (f32[8,104,128]{2,1,0:T(8,128)}, f32[8,104,128]{2,1,0:T(8,128)S(1)}, u32[]{:S(2)}, u32[]{:S(2)}) collective-permute-start(f32[8,104,128]{2,1,0:T(8,128)} %get-tuple-element.45), channel_id=1, source_target_pairs={{0,8},{8,16},{16,24},{24,0},{1,9},{9,17},{17,25},{25,1},{2,10},{10... | collective-permute-start | bytes 1277960 | tf_op jit(solution)/shard_map/ppermute | solution.py:987
  235.5 69.9 %copy-start.3 = (f32[8,104,128]{2,1,0:T(8,128)}, f32[8,104,128]{2,1,0:T(8,128)S(1)}, u32[]{:S(2)}) copy-start(f32[8,104,128]{2,1,0:T(8,128)S(1)} %collective-permute-done.12.refs_1_) | copy-start | bytes 1277956
  235.6 69.9 %copy-start.4 = (f32[8,104,128]{2,1,0:T(8,128)}, f32[8,104,128]{2,1,0:T(8,128)S(1)}, u32[]{:S(2)}) copy-start(f32[8,104,128]{2,1,0:T(8,128)S(1)} %collective-permute-done.13.refs_2_) | copy-start | bytes 1277956
  245.3 60.2 %copy-start.5 = (f32[8,104,128]{2,1,0:T(8,128)}, f32[8,104,128]{2,1,0:T(8,128)S(1)}, u32[]{:S(2)}) copy-start(f32[8,104,128]{2,1,0:T(8,128)S(1)} %collective-permute-done.14.refs_3_) | copy-start | bytes 1277956
  312.4 34.2 %all-to-all-start.3 = ((bf16[16,192,384]{2,1,0:T(8,128)(2,1)}), bf16[16,192,384]{2,1,0:T(8,128)(2,1)S(1)}, u32[]{:S(2)}, u32[]{:S(2)}) async-start(bf16[16,192,384]{2,1,0:T(8,128)(2,1)} %combine.1.refs_0_), calls=%async_computation.3 | async-start | bytes 4718592 | tf_op jit(solution)/shard_map/all_to_all | solution.py:942
  348.1 62.7 %all-to-all-start.4 = ((bf16[32,96,384]{2,1,0:T(8,128)(2,1)}), bf16[32,96,384]{2,1,0:T(8,128)(2,1)}, u32[]{:S(2)}, u32[]{:S(2)}) async-start(bf16[32,96,384]{2,1,0:T(8,128)(2,1)} %multiply.13.refs_4_), calls=%async_computation.4 | async-start | bytes 4718592 | tf_op jit(solution)/shard_map/all_to_all | solution.py:942
  (20 other events, 66.0 us)

commit v14 on v13

--- a/solution.py
+++ b/solution.py
@@ -212,7 +212,7 @@
         out_specs=[tile, tile],
         out_shape=[jax.ShapeDtypeStruct((count, cols, wide), BF16)] * 2,
         scratch_shapes=[
-            pltpu.VMEM((rows * seqs, LANES), F32),
+            pltpu.VMEM((rows * seqs + seqs, LANES), F32),
             pltpu.VMEM((cols, width * seqs), BF16),
             pltpu.VMEM((block // 2, width * seqs, 2 * wide), BF16),
         ],
@@ -368,7 +368,7 @@
         for src in range(row_count * pos_count):
             value = recv_ref[src].astype(F32)
             for t in range(tiles):
-                flat_ref[src, t] = value[:, t * LANES : (t + 1) * LANES]
+                flat_ref[src, t, : recv_ref.shape[1]] = value[:, t * LANES : (t + 1) * LANES]
 
     def block(row, group, index):
         packed = []
@@ -391,7 +391,7 @@
                     rows_ref[t, pl.ds(a, each, stride=QUAD), :] = right[a][t]
             for t in range(tiles):
                 at = slice(group * lanes + t * LANES, group * lanes + (t + 1) * LANES)
-                right_ref[0, row, 0, :, at] = rows_ref[t].astype(BF16)
+                right_ref[0, row, 0, :, at] = rows_ref[t, : QUAD * each].astype(BF16)
 
 
 def assemble(chunk, chunks, spans, received, sides, after, row_count, pos_count, cols):
@@ -417,8 +417,8 @@
         out_shape=[jax.ShapeDtypeStruct(shape, BF16) for shape in shapes],
         input_output_aliases={1: 0, 2: 1} if sides else {},
         scratch_shapes=[
-            pltpu.VMEM((sources, lanes // LANES, height, LANES), F32),
-            pltpu.VMEM((lanes // LANES, QUAD * each, LANES), F32),
+            pltpu.VMEM((sources, lanes // LANES, height + 16, LANES), F32),
+            pltpu.VMEM((lanes // LANES, QUAD * each + 8, LANES), F32),
         ],
         compiler_params=params(),
         cost_estimate=LIGHT,
@@ -462,7 +462,7 @@
     def _():
         for dest in range(row_count * pos_count):
             for t in range(tiles):
-                out_ref[dest, :, t * LANES : (t + 1) * LANES] = tmp_ref[dest, t].astype(BF16)
+                out_ref[dest, :, t * LANES : (t + 1) * LANES] = tmp_ref[dest, t, : out_ref.shape[1]].astype(BF16)
 
 
 def multiply(left, right, after, pos_count, cols):
@@ -479,7 +479,7 @@
         + anywhere(after),
         out_specs=whole(shape),
         out_shape=jax.ShapeDtypeStruct(shape, BF16),
-        scratch_shapes=[pltpu.VMEM((shape[0], lanes // LANES, shape[1], LANES), F32)],
+        scratch_shapes=[pltpu.VMEM((shape[0], lanes // LANES, shape[1] + 8, LANES), F32)],
         compiler_params=params(),
         cost_estimate=LIGHT,
         name="multiply",
@@ -603,8 +603,8 @@
             jax.ShapeDtypeStruct((channels, rows, depth), BF16),
         ],
         scratch_shapes=[
-            pltpu.VMEM((sources, lanes // LANES, height, LANES), F32),
-            pltpu.VMEM((depth // LANES, rows, LANES), F32),
+            pltpu.VMEM((sources, lanes // LANES, height + 16, LANES), F32),
+            pltpu.VMEM((depth // LANES, rows + 8, LANES), F32),
         ],
         compiler_params=params(),
         cost_estimate=LIGHT,
@@ -644,7 +644,7 @@
     def _():
         for dest in range(row_count * pos_count):
             for t in range(tiles):
-                out_ref[dest, :, t * LANES : (t + 1) * LANES] = tmp_ref[dest, t].astype(BF16)
+                out_ref[dest, :, t * LANES : (t + 1) * LANES] = tmp_ref[dest, t, : out_ref.shape[1]].astype(BF16)
 
 
 def combine(left, own, received, after, row_count, pos_count, cols):
@@ -662,7 +662,7 @@
         + anywhere(after),
         out_specs=whole(shape),
         out_shape=jax.ShapeDtypeStruct(shape, BF16),
-        scratch_shapes=[pltpu.VMEM((shape[0], shape[2] // LANES, shape[1], LANES), F32)],
+        scratch_shapes=[pltpu.VMEM((shape[0], shape[2] // LANES, shape[1] + 8, LANES), F32)],
         compiler_params=params(),
         cost_estimate=LIGHT,
         name="combine",
@@ -716,7 +716,7 @@
     top = jnp.max(logit_ref[...], axis=0)
     powers = jnp.exp(logit_ref[...] - top[None])
     total = jnp.sum(powers, axis=0)
-    exp_ref[:, 0:cols] = powers.reshape(rows * heads, cols)
+    exp_ref[: rows * heads, 0:cols] = powers.reshape(rows * heads, cols)
     for h in range(heads):
         weights = exp_ref[pl.ds(h, rows, stride=heads), :][:, :cols].astype(BF16)
         for t, out in enumerate(outs):
@@ -744,7 +744,7 @@
         out_specs=[whole(shape)] * row_count,
         out_shape=[jax.ShapeDtypeStruct(shape, F32)] * row_count,
         scratch_shapes=[
-            pltpu.VMEM((rows * heads, LANES), F32),
+            pltpu.VMEM((rows * heads + heads, LANES), F32),
             pltpu.VMEM((row_count, rows, w_value.shape[1]), BF16),
         ],
         compiler_params=params(),

time: 425 us -> 425 us (level)
  no operation moved by 1% of the time
where the time goes in v14:
time: 425 us; the launch traced here: 423 us
  waiting for transfers between devices  209 us (49%)
  Pallas kernels  125 us (29%)
  starting transfers between devices  52.3 us (12%)
  local copies, waits for them, and re-layouts  25.2 us (6%)
  other arithmetic  8.19 us (2%)
    all_to_all x5, waiting for transfers between devices, exchange(): return lax.all_to_all(block, axes, split_axis=0, concat_axis=0, tiled=True)  98.7 us
    ppermute x1, waiting for transfers between devices, on_device(): partial = lax.ppermute(theirs, 'half', swap)  60.2 us
    ppermute x3, waiting for transfers between devices, gather_parts(): gathered.append(lax.ppermute(parts[t], 'row', pairs))  44.8 us
    pallas_call x2, Pallas kernels, front(): pl.pallas_call(functools.partial(front_kernel, row_count=len(rights), col...  30.6 us
    all_to_all x5, starting transfers between devices, exchange(): return lax.all_to_all(block, axes, split_axis=0, concat_axis=0, tiled=True)  25 us
    pallas_call x6, Pallas kernels, project(): pl.pallas_call(functools.partial(project_kernel, first_row=first_row), gr...  24.1 us
    ppermute x8, starting transfers between devices, on_device(): lefts.append(lax.ppermute(own_rows, AXES, pairs))  15.4 us
    pallas_call x1, Pallas kernels, finish(): pl.pallas_call(functools.partial(finish_kernel, parts=len(products), step...  11.8 us
  transfers between devices with their start and end apart: 22, of which 7 were waited for; matrix products, arithmetic and copies ran while one was open for 5% of the time, Pallas kernels for 21%

profile of v14, /device:TPU:0, one launch (start us, length us, event | category | flops | bytes accessed | tf_op | source)
XLA Modules:
  0.0 422.6 jit_solution(3375176692095150673)
XLA Ops:
  6.4 3.0 collective-permute-start.10
  13.1 3.5 collective-permute-start.1
  27.7 3.5 collective-permute-start.7
  37.9 11.3 %front.2 = (bf16[64,96,128]{2,1,0:T(8,128)(2,1)}, bf16[64,96,128]{2,1,0:T(8,128)(2,1)}) custom-call(s32[2]{0:T(128)} %pad_add_fusion.place_ref, bf16[96,256]{1,0:T(8,128)(2,1)} %copy-done.10, bf16[96,256]{1,0:T(8,128)(2,1)} %copy-done.11, bf16[96,256]{1,0:T(8,128)(2,1)} %copy-done.12, bf16[96,256]{1,0:T(8,128)(2,1)} %copy-done.13, ...), custom_call_target="tpu_custom_call" | custom-call | flops 1000 | bytes 1000 | tf_op jit(solution)/shard_map/front/pallas_call | solution.py:193
  49.2 3.2 project.7.refs_1_
  52.4 2.9 project.6.refs_0_
  55.3 5.7 %all-to-all-start = ((bf16[16,128,384]{2,1,0:T(8,128)(2,1)}), bf16[16,128,384]{2,1,0:T(8,128)(2,1)S(1)}, u32[]{:S(2)}, u32[]{:S(2)}) async-start(bf16[16,128,384]{2,1,0:T(8,128)(2,1)} %get-tuple-element.31), calls=%async_computation | async-start | bytes 3145728 | tf_op jit(solution)/shard_map/all_to_all | solution.py:942
  61.1 19.3 %front.3 = (bf16[128,96,128]{2,1,0:T(8,128)(2,1)}, bf16[128,96,128]{2,1,0:T(8,128)(2,1)}) custom-call(s32[2]{0:T(128)} %pad_add_fusion.place_ref, bf16[96,256]{1,0:T(8,128)(2,1)} %copy-done.10, bf16[96,256]{1,0:T(8,128)(2,1)} %copy-done.11, bf16[96,256]{1,0:T(8,128)(2,1)} %copy-done.12, bf16[96,256]{1,0:T(8,128)(2,1)} %copy-done.13, ...), custom_call_target="tpu_custom_call" | custom-call | flops 1000 | bytes 1000 | tf_op jit(solution)/shard_map/front/pallas_call | solution.py:193
  80.4 5.3 %project.9.refs_1_ = bf16[16,256,384]{2,1,0:T(8,128)(2,1)} custom-call(f32[192]{0:T(256)} %dynamic_slice.22.live_ref, bf16[128,96,128]{2,1,0:T(8,128)(2,1)} %get-tuple-element.33.normed_ref.refs_1_.refs_5_, f32[1,384]{1,0:T(1,128)} %broadcast_in_dim.7.cols_ref, bf16[256,128]{1,0:T(8,128)(2,1)} %bitcast.59), custom_call_target="tpu_custom_call" | custom-call | flops 1000 | bytes 1000 | tf_op jit(solution)/shard_map/project/pallas_call | solution.py:289
  85.7 4.8 %project.8.refs_0_ = bf16[16,128,384]{2,1,0:T(8,128)(2,1)} custom-call(f32[192]{0:T(256)} %dynamic_slice.22.live_ref, bf16[128,96,128]{2,1,0:T(8,128)(2,1)} %get-tuple-element.33.normed_ref.refs_1_.refs_5_, f32[1,384]{1,0:T(1,128)} %broadcast_in_dim.7.cols_ref, bf16[128,128]{1,0:T(8,128)(2,1)} %bitcast.63), custom_call_target="tpu_custom_call" | custom-call | flops 1000 | bytes 1000 | tf_op jit(solution)/shard_map/project/pallas_call | solution.py:289
  90.6 2.9 project.10.refs_3_.refs_0_
  93.5 5.3 %collective-permute-done.11.refs_4_.refs_2_ = bf16[16,64,384]{2,1,0:T(8,128)(2,1)S(1)} collective-permute-done((bf16[16,64,384]{2,1,0:T(8,128)(2,1)S(1)}, bf16[16,64,384]{2,1,0:T(8,128)(2,1)S(1)}, u32[]{:S(2)}, u32[]{:S(2)}) %collective-permute-start.11) | collective-permute-done | bytes 786464 | tf_op jit(solution)/shard_map/ppermute | solution.py:1034
  100.8 4.1 all-to-all-start.1
  113.4 4.9 %project.11.refs_4_.refs_1_ = bf16[16,128,384]{2,1,0:T(8,128)(2,1)} custom-call(f32[192]{0:T(256)} %dynamic_slice.22.live_ref, bf16[128,96,128]{2,1,0:T(8,128)(2,1)} %get-tuple-element.33.normed_ref.refs_1_.refs_5_, f32[1,384]{1,0:T(1,128)} %broadcast_in_dim.7.cols_ref, bf16[128,128]{1,0:T(8,128)(2,1)} %get-tuple-element.36.weight_ref), custom_call_target="tpu_custom_call" | custom-call | flops 1000 | bytes 1000 | tf_op jit(solution)/shard_map/project/pallas_call | solution.py:289
  118.3 9.5 %logit.1.logit_ref = f32[192,8,96]{2,1,0:T(8,128)} custom-call(f32[192]{0:T(256)} %dynamic_slice.22.live_ref, bf16[64,96,128]{2,1,0:T(8,128)(2,1)} %get-tuple-element.30.normed_ref.refs_0_.refs_4_, bf16[128,96,128]{2,1,0:T(8,128)(2,1)} %get-tuple-element.33.normed_ref.refs_1_.refs_5_, bf16[8,128]{1,0:T(8,128)(2,1)} %bitcast.75, ...), custom_call_target="tpu_custom_call" | custom-call | flops 1000 | bytes 1000 | tf_op jit(solution)/shard_map/logit/pallas_call | solution.py:341
  127.8 4.6 %merge.2.refs_3_.refs_1_ = bf16[16,384,384]{2,1,0:T(8,128)(2,1)} custom-call(bf16[16,64,384]{2,1,0:T(8,128)(2,1)} %project.10.refs_3_.refs_0_, bf16[16,128,384]{2,1,0:T(8,128)(2,1)} %project.11.refs_4_.refs_1_, bf16[16,64,384]{2,1,0:T(8,128)(2,1)} %copy-done.7), custom_call_target="tpu_custom_call" | custom-call | flops 1000 | bytes 1000 | tf_op jit(solution)/shard_map/merge/pallas_call | solution.py:688
  132.4 4.2 %partial.1 = (f32[8,104,128]{2,1,0:T(8,128)}, f32[8,104,128]{2,1,0:T(8,128)}, f32[8,104,128]{2,1,0:T(8,128)}, f32[8,104,128]{2,1,0:T(8,128)}) custom-call(s32[2]{0:T(128)} %pad_add_fusion.place_ref, f32[192,8,96]{2,1,0:T(8,128)} %logit.1.logit_ref, bf16[96,256]{1,0:T(8,128)(2,1)} %copy-done.10, bf16[96,256]{1,0:T(8,128)(2,1)} %copy-done.11, ...), custom_call_target="tpu_custom_call" | custom-call | flops 1000 | bytes 1000 | tf_op jit(solution)/shard_map/partial/pallas_call | solution.py:739
  136.7 40.6 %all-to-all-done.1.refs_1_ = bf16[16,256,384]{2,1,0:T(8,128)(2,1)S(1)} async-done(((bf16[16,256,384]{2,1,0:T(8,128)(2,1)}), bf16[16,256,384]{2,1,0:T(8,128)(2,1)S(1)}, u32[]{:S(2)}, u32[]{:S(2)}) %all-to-all-start.1) | async-done | bytes 3145760 | tf_op jit(solution)/shard_map/all_to_all | solution.py:942
  178.9 10.7 %assemble_half.1 = (bf16[4,768,384]{2,1,0:T(8,128)(2,1)}, bf16[4,384,384]{2,1,0:T(8,128)(2,1)}, bf16[4,768,384]{2,1,0:T(8,128)(2,1)}) custom-call(s32[1]{0:T(128)} %bitcast.half_ref, bf16[16,128,384]{2,1,0:T(8,128)(2,1)} %copy-done, bf16[16,256,384]{2,1,0:T(8,128)(2,1)} %copy-done.1, f32[8,104,128]{2,1,0:T(8,128)} %get-tuple-element.37.refs_2_.refs_1_, ...), custom_call_target="tpu_custom_call" | custom-call | flops 1000 | bytes 1000 | tf_op jit(solution)/shard_map/assemble_half/pallas_call | solution.py:587
  191.9 4.6 %all-to-all-start.2 = ((bf16[16,384,384]{2,1,0:T(8,128)(2,1)}), bf16[16,384,384]{2,1,0:T(8,128)(2,1)}, u32[]{:S(2)}, u32[]{:S(2)}) async-start(bf16[16,384,384]{2,1,0:T(8,128)(2,1)} %merge.3), calls=%async_computation.2 | async-start | bytes 9437184 | tf_op jit(solution)/shard_map/all_to_all | solution.py:942
  200.5 35.0 %collective-permute-done.12.refs_1_ = f32[8,104,128]{2,1,0:T(8,128)S(1)} collective-permute-done((f32[8,104,128]{2,1,0:T(8,128)}, f32[8,104,128]{2,1,0:T(8,128)S(1)}, u32[]{:S(2)}, u32[]{:S(2)}) %collective-permute-start.12) | collective-permute-done | bytes 426016 | tf_op jit(solution)/shard_map/ppermute | solution.py:987
  235.5 9.7 %collective-permute-done.14.refs_3_ = f32[8,104,128]{2,1,0:T(8,128)S(1)} collective-permute-done((f32[8,104,128]{2,1,0:T(8,128)}, f32[8,104,128]{2,1,0:T(8,128)S(1)}, u32[]{:S(2)}, u32[]{:S(2)}) %collective-permute-start.14) | collective-permute-done | bytes 426016 | tf_op jit(solution)/shard_map/ppermute | solution.py:987
  245.3 60.2 %collective-permute-done.16.recv_ref = bf16[4,768,384]{2,1,0:T(8,128)(2,1)} collective-permute-done((bf16[4,768,384]{2,1,0:T(8,128)(2,1)}, bf16[4,768,384]{2,1,0:T(8,128)(2,1)}, u32[]{:S(2)}, u32[]{:S(2)}) %collective-permute-start.16) | collective-permute-done | bytes 2359328 | tf_op jit(solution)/shard_map/ppermute | solution.py:1049
  305.5 6.9 %combine.1.refs_0_ = bf16[16,192,384]{2,1,0:T(8,128)(2,1)} custom-call(bf16[4,768,384]{2,1,0:T(8,128)(2,1)} %get-tuple-element.47.refs_2_.left_ref, bf16[4,384,384]{2,1,0:T(8,128)(2,1)} %get-tuple-element.48.own_ref, bf16[4,768,384]{2,1,0:T(8,128)(2,1)} %collective-permute-done.16.recv_ref, bf16[16,384,384]{2,1,0:T(8,128)(2,1)} %all-to-all-done.2.refs_0_.recv_ref, ...), custom_call_target="tpu_custom_call" | custom-call | flops 1000 | bytes 1000 | tf_op jit(solution)/shard_map/combine/pallas_call | solution.py:654
  312.4 3.7 all-to-all-start.3
  316.2 8.8 %assemble.1 = (bf16[2,16,48,768]{3,2,1,0:T(8,128)(2,1)}, bf16[2,4,1,192,768]{4,3,2,1,0:T(8,128)(2,1)}) custom-call(bf16[16,384,384]{2,1,0:T(8,128)(2,1)} %all-to-all-done.2.refs_0_.recv_ref, bf16[16,192,384]{2,1,0:T(8,128)(2,1)} %combine.1.refs_0_), custom_call_target="tpu_custom_call" | custom-call | flops 1000 | bytes 1000 | tf_op jit(solution)/shard_map/assemble/pallas_call | solution.py:407
  325.0 7.1 %multiply.13.refs_4_ = bf16[32,96,384]{2,1,0:T(8,128)(2,1)} custom-call(bf16[2,16,48,768]{3,2,1,0:T(8,128)(2,1)} %get-tuple-element.50.left_ref, bf16[2,768,768]{2,1,0:T(8,128)(2,1)} %bitcast.53), custom_call_target="tpu_custom_call" | custom-call | flops 1000 | bytes 1000 | tf_op jit(solution)/shard_map/multiply/pallas_call | solution.py:472
  332.1 14.6 %all-to-all-done.3.refs_0_ = bf16[16,192,384]{2,1,0:T(8,128)(2,1)S(1)} async-done(((bf16[16,192,384]{2,1,0:T(8,128)(2,1)}), bf16[16,192,384]{2,1,0:T(8,128)(2,1)S(1)}, u32[]{:S(2)}, u32[]{:S(2)}) %all-to-all-start.3) | async-done | bytes 2359328 | tf_op jit(solution)/shard_map/all_to_all | solution.py:942
  348.1 6.9 %all-to-all-start.4 = ((bf16[32,96,384]{2,1,0:T(8,128)(2,1)}), bf16[32,96,384]{2,1,0:T(8,128)(2,1)}, u32[]{:S(2)}, u32[]{:S(2)}) async-start(bf16[32,96,384]{2,1,0:T(8,128)(2,1)} %multiply.13.refs_4_), calls=%async_computation.4 | async-start | bytes 4718592 | tf_op jit(solution)/shard_map/all_to_all | solution.py:942
  361.0 4.7 %average.1 = bf16[96,256]{1,0:T(8,128)(2,1)} custom-call(f32[8,104,128]{2,1,0:T(8,128)} %get-tuple-element.52.refs_0_, f32[8,104,128]{2,1,0:T(8,128)} %get-tuple-element.53.refs_1_, f32[8,104,128]{2,1,0:T(8,128)} %get-tuple-element.54.refs_2_, f32[8,104,128]{2,1,0:T(8,128)} %get-tuple-element.55.refs_3_, f32[8,96,128]{2,1,0:T(8,128)} %copy.130.refs_4_, ...), custom_call_target="tpu_custom_call" | custom-call | flops 1000 | bytes 1000 | tf_op jit(solution)/shard_map/average/pallas_call | solution.py:784
  367.3 43.5 %all-to-all-done.4.refs_1_ = bf16[32,96,384]{2,1,0:T(8,128)(2,1)} async-done(((bf16[32,96,384]{2,1,0:T(8,128)(2,1)}), bf16[32,96,384]{2,1,0:T(8,128)(2,1)}, u32[]{:S(2)}, u32[]{:S(2)}) %all-to-all-start.4) | async-done | bytes 2359328 | tf_op jit(solution)/shard_map/all_to_all | solution.py:942
  410.7 11.8 %finish.1 = bf16[192,96,128]{2,1,0:T(8,128)(2,1)} custom-call(bf16[16,192,384]{2,1,0:T(8,128)(2,1)} %copy-done.2, bf16[32,96,384]{2,1,0:T(8,128)(2,1)} %all-to-all-done.4.refs_1_, bf16[64,96,128]{2,1,0:T(8,128)(2,1)} %get-tuple-element.56.refs_2_, bf16[128,96,128]{2,1,0:T(8,128)(2,1)} %get-tuple-element.57.refs_3_, ...), custom_call_target="tpu_custom_call" | custom-call | flops 1000 | bytes 1000 | tf_op jit(solution)/shard_map/finish/pallas_call | solution.py:845
  (152 shorter events, 54.4 us)
Async XLA Ops:
  0.6 17.7 %slice-start = ((bf16[64,576]{1,0:T(8,128)(2,1)}), bf16[64,32]{1,0:T(8,128)(2,1)S(1)}, s32[]{:S(2)}) async-start(bf16[64,576]{1,0:T(8,128)(2,1)} %param.14), calls=%async_computation.5 | async-start | bytes 32768 | tf_op jit(solution)/shard_map/slice | solution.py:913
  0.6 17.5 %copy-start.22 = (bf16[128,640]{1,0:T(8,128)(2,1)S(1)}, bf16[128,640]{1,0:T(8,128)(2,1)}, u32[]{:S(2)}) copy-start(bf16[128,640]{1,0:T(8,128)(2,1)} %param.18) | copy-start | bytes 491524
  0.7 32.4 %copy-start.21 = (bf16[1024,128]{1,0:T(8,128)(2,1)S(1)}, bf16[1024,128]{1,0:T(8,128)(2,1)}, u32[]{:S(2)}) copy-start(bf16[1024,128]{1,0:T(8,128)(2,1)} %param.15) | copy-start | bytes 786436
  6.4 30.3 %copy-start.9 = (bf16[4,96,32]{2,1,0:T(8,128)(2,1)}, bf16[4,96,32]{2,1,0:T(8,128)(2,1)S(1)}, u32[]{:S(2)}) copy-start(bf16[4,96,32]{2,1,0:T(8,128)(2,1)S(1)} %fusion.3.refs_8_) | copy-start | bytes 73732
  6.4 12.9 %collective-permute-start.10 = (bf16[4,96,32]{2,1,0:T(8,128)(2,1)S(1)}, bf16[4,96,32]{2,1,0:T(8,128)(2,1)S(1)}, u32[]{:S(2)}, u32[]{:S(2)}) collective-permute-start(bf16[4,96,32]{2,1,0:T(8,128)(2,1)S(1)} %fusion.3.refs_8_), channel_id=1, source_target_pairs={{0,8},{8,16},{16,24},{24,0},{1,9},{9,17},{17,25},{25,1},{2,10},{10... | collective-permute-start | bytes 73736 | tf_op jit(solution)/shard_map/ppermute | solution.py:927
  9.4 12.2 %collective-permute-start.8 = (bf16[4,96,32]{2,1,0:T(8,128)(2,1)S(1)}, bf16[4,96,32]{2,1,0:T(8,128)(2,1)S(1)}, u32[]{:S(2)}, u32[]{:S(2)}) collective-permute-start(bf16[4,96,32]{2,1,0:T(8,128)(2,1)S(1)} %fusion.3.refs_8_), channel_id=1, source_target_pairs={{0,24},{8,0},{16,8},{24,16},{1,25},{9,1},{17,9},{25,17},{2,26},{10... | collective-permute-start | bytes 73736 | tf_op jit(solution)/shard_map/ppermute | solution.py:927
  10.4 13.8 %collective-permute-start.9 = (bf16[4,96,32]{2,1,0:T(8,128)(2,1)S(1)}, bf16[4,96,32]{2,1,0:T(8,128)(2,1)S(1)}, u32[]{:S(2)}, u32[]{:S(2)}) collective-permute-start(bf16[4,96,32]{2,1,0:T(8,128)(2,1)S(1)} %fusion.3.refs_8_), channel_id=1, source_target_pairs={{0,16},{8,24},{16,0},{24,8},{1,17},{9,25},{17,1},{25,9},{2,18},{10... | collective-permute-start | bytes 73736 | tf_op jit(solution)/shard_map/ppermute | solution.py:927
  12.5 12.1 %collective-permute-start = (bf16[96,256]{1,0:T(8,128)(2,1)S(1)}, bf16[96,256]{1,0:T(8,128)(2,1)S(1)}, u32[]{:S(2)}, u32[]{:S(2)}) collective-permute-start(bf16[96,256]{1,0:T(8,128)(2,1)S(1)} %copy.103), channel_id=1, source_target_pairs={{0,0},{1,1},{2,8},{3,9},{4,16},{5,17},{6,24},{7,25},{8,2},{9,3},{1... | collective-permute-start | bytes 147464 | tf_op jit(solution)/shard_map/ppermute | solution.py:923
  13.1 14.3 %collective-permute-start.1 = (bf16[96,256]{1,0:T(8,128)(2,1)S(1)}, bf16[96,256]{1,0:T(8,128)(2,1)S(1)}, u32[]{:S(2)}, u32[]{:S(2)}) collective-permute-start(bf16[96,256]{1,0:T(8,128)(2,1)S(1)} %copy.103), channel_id=1, source_target_pairs={{0,7},{1,0},{2,15},{3,8},{4,23},{5,16},{6,31},{7,24},{8,1},{9,2},{... | collective-permute-start | bytes 147464 | tf_op jit(solution)/shard_map/ppermute | solution.py:923
  19.3 17.3 %copy-start.18 = (bf16[4,96,32]{2,1,0:T(8,128)(2,1)}, bf16[4,96,32]{2,1,0:T(8,128)(2,1)S(1)}, u32[]{:S(2)}) copy-start(bf16[4,96,32]{2,1,0:T(8,128)(2,1)S(1)} %collective-permute-done.10.refs_11_) | copy-start | bytes 73732
  19.3 8.3 %collective-permute-start.2 = (bf16[96,256]{1,0:T(8,128)(2,1)S(1)}, bf16[96,256]{1,0:T(8,128)(2,1)S(1)}, u32[]{:S(2)}, u32[]{:S(2)}) collective-permute-start(bf16[96,256]{1,0:T(8,128)(2,1)S(1)} %copy.103), channel_id=1, source_target_pairs={{0,6},{1,7},{2,14},{3,15},{4,22},{5,23},{6,30},{7,31},{8,0},{9,1},... | collective-permute-start | bytes 147464 | tf_op jit(solution)/shard_map/ppermute | solution.py:923
  21.6 15.1 %copy-start.19 = (bf16[4,96,32]{2,1,0:T(8,128)(2,1)}, bf16[4,96,32]{2,1,0:T(8,128)(2,1)S(1)}, u32[]{:S(2)}) copy-start(bf16[4,96,32]{2,1,0:T(8,128)(2,1)S(1)} %collective-permute-done.8.refs_9_) | copy-start | bytes 73732
  21.6 15.0 %collective-permute-start.3 = (bf16[96,256]{1,0:T(8,128)(2,1)S(1)}, bf16[96,256]{1,0:T(8,128)(2,1)S(1)}, u32[]{:S(2)}, u32[]{:S(2)}) collective-permute-start(bf16[96,256]{1,0:T(8,128)(2,1)S(1)} %copy.103), channel_id=1, source_target_pairs={{0,5},{1,6},{2,13},{3,14},{4,21},{5,22},{6,29},{7,30},{8,7},{9,0},... | collective-permute-start | bytes 147464 | tf_op jit(solution)/shard_map/ppermute | solution.py:923
  24.3 12.4 %copy-start.20 = (bf16[4,96,32]{2,1,0:T(8,128)(2,1)}, bf16[4,96,32]{2,1,0:T(8,128)(2,1)S(1)}, u32[]{:S(2)}) copy-start(bf16[4,96,32]{2,1,0:T(8,128)(2,1)S(1)} %collective-permute-done.9.refs_10_) | copy-start | bytes 73732
  24.3 12.3 %collective-permute-start.4 = (bf16[96,256]{1,0:T(8,128)(2,1)S(1)}, bf16[96,256]{1,0:T(8,128)(2,1)S(1)}, u32[]{:S(2)}, u32[]{:S(2)}) collective-permute-start(bf16[96,256]{1,0:T(8,128)(2,1)S(1)} %copy.103), channel_id=1, source_target_pairs={{0,4},{1,5},{2,12},{3,13},{4,20},{5,21},{6,28},{7,29},{8,6},{9,7},... | collective-permute-start | bytes 147464 | tf_op jit(solution)/shard_map/ppermute | solution.py:923
  24.6 12.0 %collective-permute-start.5 = (bf16[96,256]{1,0:T(8,128)(2,1)S(1)}, bf16[96,256]{1,0:T(8,128)(2,1)S(1)}, u32[]{:S(2)}, u32[]{:S(2)}) collective-permute-start(bf16[96,256]{1,0:T(8,128)(2,1)S(1)} %copy.103), channel_id=1, source_target_pairs={{0,3},{1,4},{2,11},{3,12},{4,19},{5,20},{6,27},{7,28},{8,5},{9,6},... | collective-permute-start | bytes 147464 | tf_op jit(solution)/shard_map/ppermute | solution.py:923
  27.4 9.2 %collective-permute-start.6 = (bf16[96,256]{1,0:T(8,128)(2,1)S(1)}, bf16[96,256]{1,0:T(8,128)(2,1)S(1)}, u32[]{:S(2)}, u32[]{:S(2)}) collective-permute-start(bf16[96,256]{1,0:T(8,128)(2,1)S(1)} %copy.103), channel_id=1, source_target_pairs={{0,2},{1,3},{2,10},{3,11},{4,18},{5,19},{6,26},{7,27},{8,4},{9,5},... | collective-permute-start | bytes 147464 | tf_op jit(solution)/shard_map/ppermute | solution.py:923
  27.7 9.0 %collective-permute-start.7 = (bf16[96,256]{1,0:T(8,128)(2,1)S(1)}, bf16[96,256]{1,0:T(8,128)(2,1)S(1)}, u32[]{:S(2)}, u32[]{:S(2)}) collective-permute-start(bf16[96,256]{1,0:T(8,128)(2,1)S(1)} %copy.103), channel_id=1, source_target_pairs={{0,1},{1,2},{2,9},{3,10},{4,17},{5,18},{6,25},{7,26},{8,3},{9,4},{... | collective-permute-start | bytes 147464 | tf_op jit(solution)/shard_map/ppermute | solution.py:923
  55.3 43.5 %all-to-all-start = ((bf16[16,128,384]{2,1,0:T(8,128)(2,1)}), bf16[16,128,384]{2,1,0:T(8,128)(2,1)S(1)}, u32[]{:S(2)}, u32[]{:S(2)}) async-start(bf16[16,128,384]{2,1,0:T(8,128)(2,1)} %get-tuple-element.31), calls=%async_computation | async-start | bytes 3145728 | tf_op jit(solution)/shard_map/all_to_all | solution.py:942
  61.0 37.7 %collective-permute-start.11 = (bf16[16,64,384]{2,1,0:T(8,128)(2,1)S(1)}, bf16[16,64,384]{2,1,0:T(8,128)(2,1)S(1)}, u32[]{:S(2)}, u32[]{:S(2)}) collective-permute-start(bf16[16,64,384]{2,1,0:T(8,128)(2,1)S(1)} %copy-done.6), channel_id=1, source_target_pairs={{0,4},{4,0},{1,5},{5,1},{2,6},{6,2},{3,7},{7,3},{8,12},{12,8},{9,1... | collective-permute-start | bytes 2359304 | tf_op jit(solution)/shard_map/ppermute | solution.py:1034
  100.8 76.5 %all-to-all-start.1 = ((bf16[16,256,384]{2,1,0:T(8,128)(2,1)}), bf16[16,256,384]{2,1,0:T(8,128)(2,1)S(1)}, u32[]{:S(2)}, u32[]{:S(2)}) async-start(bf16[16,256,384]{2,1,0:T(8,128)(2,1)} %get-tuple-element.35), calls=%async_computation.1 | async-start | bytes 6291456 | tf_op jit(solution)/shard_map/all_to_all | solution.py:942
  104.9 84.6 %collective-permute-start.15 = (bf16[16,128,384]{2,1,0:T(8,128)(2,1)}, bf16[16,128,384]{2,1,0:T(8,128)(2,1)}, u32[]{:S(2)}, u32[]{:S(2)}) collective-permute-start(bf16[16,128,384]{2,1,0:T(8,128)(2,1)} %get-tuple-element.46), channel_id=1, source_target_pairs={{0,4},{4,0},{1,5},{5,1},{2,6},{6,2},{3,7},{7,3},{8,12},{12,8},{9,1... | collective-permute-start | bytes 4718600 | tf_op jit(solution)/shard_map/ppermute | solution.py:1034
  191.9 113.5 %all-to-all-start.2 = ((bf16[16,384,384]{2,1,0:T(8,128)(2,1)}), bf16[16,384,384]{2,1,0:T(8,128)(2,1)}, u32[]{:S(2)}, u32[]{:S(2)}) async-start(bf16[16,384,384]{2,1,0:T(8,128)(2,1)} %merge.3), calls=%async_computation.2 | async-start | bytes 9437184 | tf_op jit(solution)/shard_map/all_to_all | solution.py:942
  196.5 108.9 %collective-permute-start.16 = (bf16[4,768,384]{2,1,0:T(8,128)(2,1)}, bf16[4,768,384]{2,1,0:T(8,128)(2,1)}, u32[]{:S(2)}, u32[]{:S(2)}) collective-permute-start(bf16[4,768,384]{2,1,0:T(8,128)(2,1)} %get-tuple-element.49), channel_id=1, source_target_pairs={{0,4},{4,0},{1,5},{5,1},{2,6},{6,2},{3,7},{7,3},{8,12},{12,8},{9,1... | collective-permute-start | bytes 7077896 | tf_op jit(solution)/shard_map/ppermute | solution.py:1049
  196.6 38.9 %collective-permute-start.12 = (f32[8,104,128]{2,1,0:T(8,128)}, f32[8,104,128]{2,1,0:T(8,128)S(1)}, u32[]{:S(2)}, u32[]{:S(2)}) collective-permute-start(f32[8,104,128]{2,1,0:T(8,128)} %get-tuple-element.43), channel_id=1, source_target_pairs={{0,24},{8,0},{16,8},{24,16},{1,25},{9,1},{17,9},{25,17},{2,26},{10... | collective-permute-start | bytes 1277960 | tf_op jit(solution)/shard_map/ppermute | solution.py:987
  199.4 36.2 %collective-permute-start.13 = (f32[8,104,128]{2,1,0:T(8,128)}, f32[8,104,128]{2,1,0:T(8,128)S(1)}, u32[]{:S(2)}, u32[]{:S(2)}) collective-permute-start(f32[8,104,128]{2,1,0:T(8,128)} %get-tuple-element.44), channel_id=1, source_target_pairs={{0,16},{8,24},{16,0},{24,8},{1,17},{9,25},{17,1},{25,9},{2,18},{10... | collective-permute-start | bytes 1277960 | tf_op jit(solution)/shard_map/ppermute | solution.py:987
  199.9 45.4 %collective-permute-start.14 = (f32[8,104,128]{2,1,0:T(8,128)}, f32[8,104,128]{2,1,0:T(8,128)S(1)}, u32[]{:S(2)}, u32[]{:S(2)}) collective-permute-start(f32[8,104,128]{2,1,0:T(8,128)} %get-tuple-element.45), channel_id=1, source_target_pairs={{0,8},{8,16},{16,24},{24,0},{1,9},{9,17},{17,25},{25,1},{2,10},{10... | collective-permute-start | bytes 1277960 | tf_op jit(solution)/shard_map/ppermute | solution.py:987
  235.5 69.9 %copy-start.3 = (f32[8,104,128]{2,1,0:T(8,128)}, f32[8,104,128]{2,1,0:T(8,128)S(1)}, u32[]{:S(2)}) copy-start(f32[8,104,128]{2,1,0:T(8,128)S(1)} %collective-permute-done.12.refs_1_) | copy-start | bytes 1277956
  235.5 69.9 %copy-start.4 = (f32[8,104,128]{2,1,0:T(8,128)}, f32[8,104,128]{2,1,0:T(8,128)S(1)}, u32[]{:S(2)}) copy-start(f32[8,104,128]{2,1,0:T(8,128)S(1)} %collective-permute-done.13.refs_2_) | copy-start | bytes 1277956
  245.2 60.2 %copy-start.5 = (f32[8,104,128]{2,1,0:T(8,128)}, f32[8,104,128]{2,1,0:T(8,128)S(1)}, u32[]{:S(2)}) copy-start(f32[8,104,128]{2,1,0:T(8,128)S(1)} %collective-permute-done.14.refs_3_) | copy-start | bytes 1277956
  312.4 34.2 %all-to-all-start.3 = ((bf16[16,192,384]{2,1,0:T(8,128)(2,1)}), bf16[16,192,384]{2,1,0:T(8,128)(2,1)S(1)}, u32[]{:S(2)}, u32[]{:S(2)}) async-start(bf16[16,192,384]{2,1,0:T(8,128)(2,1)} %combine.1.refs_0_), calls=%async_computation.3 | async-start | bytes 4718592 | tf_op jit(solution)/shard_map/all_to_all | solution.py:942
  348.1 62.7 %all-to-all-start.4 = ((bf16[32,96,384]{2,1,0:T(8,128)(2,1)}), bf16[32,96,384]{2,1,0:T(8,128)(2,1)}, u32[]{:S(2)}, u32[]{:S(2)}) async-start(bf16[32,96,384]{2,1,0:T(8,128)(2,1)} %multiply.13.refs_4_), calls=%async_computation.4 | async-start | bytes 4718592 | tf_op jit(solution)/shard_map/all_to_all | solution.py:942
  (20 other events, 66.0 us)
